TPU v7x, 32 devices: a whole 2x2x4 slice. The times are simulated.
32 devices in a mesh: ctx: 8 (over y, x, core), tp: 4 (over z).
Axes of the slice: x: 2, y: 2, z: 4, core: 2. Of those that a mesh axis runs over, the one named last changes fastest.
Arguments:
- query: bfloat16 [2048, 4096], P('ctx', 'tp'), may hold values from -6 to 6
- keys: bfloat16 [2048, 4096], P('ctx', 'tp'), may hold values from -6 to 6
- values: bfloat16 [2048, 4096], P('ctx', 'tp'), may hold values from -6 to 6
- filt: float32 [2048, 4096], P('ctx', 'tp'), may hold values from -1 to 1
- direct: float32 [4096], P('tp'), may hold values from -4 to 4
- w_out: bfloat16 [4096, 4096], P('tp'), may hold values from -0.09375 to 0.09375
Outputs:
- output: bfloat16 [2048, 4096], P('ctx', 'tp')
All inputs are finite; a program needn't handle non-finite values.
Results may differ from a plain program's by a relative error of at most 0.0049.
Values sent between devices are 32-bit elements; how exact they have to be, the bound alone decides.
No kernel may reach another device: no remote copies, remote signals or barrier semaphores. Data moves between devices by JAX's collectives and lax.ppermute only.
A program may use at most 128 MiB of HBM per device.

v0:
```python
import math

import jax
import jax.numpy as jnp
from jax import lax
from jax.sharding import PartitionSpec as P


def dft_table(length, sign):
    steps = jnp.arange(length, dtype=jnp.int32)
    product = steps[:, None] * steps[None, :] % length
    angle = sign * 2.0 * math.pi / length * product.astype(jnp.float32)
    return (jnp.cos(angle), jnp.sin(angle))


def complex_dot(cosine, sine, real, imag):
    best = lax.Precision.HIGHEST
    out_real = jnp.dot(cosine, real, precision=best) - jnp.dot(sine, imag, precision=best)
    out_imag = jnp.dot(cosine, imag, precision=best) + jnp.dot(sine, real, precision=best)
    return (out_real, out_imag)


def rotate(real, imag, angle):
    cosine = jnp.cos(angle)
    sine = jnp.sin(angle)
    return (real * cosine - imag * sine, real * sine + imag * cosine)


def transform(real, imag, sign):
    length, width = real.shape
    factor = math.gcd(length, 64)
    if length <= 64 or factor == 1:
        cosine, sine = dft_table(length, sign)
        return complex_dot(cosine, sine, real, imag)
    others = length // factor
    cosine, sine = dft_table(factor, sign)
    real, imag = complex_dot(
        cosine, sine, real.reshape(factor, others * width), imag.reshape(factor, others * width)
    )
    first = jnp.arange(factor, dtype=jnp.int32)
    second = jnp.arange(others, dtype=jnp.int32)
    product = first[:, None] * second[None, :] % length
    angle = (sign * 2.0 * math.pi / length * product.astype(jnp.float32))[:, :, None]
    real, imag = rotate(
        real.reshape(factor, others, width), imag.reshape(factor, others, width), angle
    )
    real = jnp.transpose(real, (1, 0, 2)).reshape(others, factor * width)
    imag = jnp.transpose(imag, (1, 0, 2)).reshape(others, factor * width)
    real, imag = transform(real, imag, sign)
    return (real.reshape(length, width), imag.reshape(length, width))


def body(query, keys, values, filt, direct, w_out):
    signal = keys.astype(jnp.float32) * values.astype(jnp.float32)
    rows, chans = signal.shape
    count = lax.axis_size("ctx")
    total = 2 * rows * count
    me = lax.axis_index("ctx")
    piece = rows // count
    sig_part, flt_part = (
        lax.all_to_all(signal[None], "ctx", split_axis=1, concat_axis=0, tiled=True),
        lax.all_to_all(filt[None], "ctx", split_axis=1, concat_axis=0, tiled=True),
    )
    joined = jnp.concatenate([sig_part, flt_part], axis=2)
    joined = jnp.concatenate([joined, jnp.zeros_like(joined)], axis=0)
    flat = joined.reshape(2 * count, piece * 2 * chans)
    real, imag = transform(flat, jnp.zeros_like(flat), -1.0)
    freq = jnp.arange(2 * count, dtype=jnp.int32)
    lag = me * piece + jnp.arange(piece, dtype=jnp.int32)
    product = freq[:, None] * lag[None, :] % total
    turn = 2.0 * math.pi / total * product.astype(jnp.float32)
    real, imag = rotate(
        real.reshape(2 * count, piece, 2 * chans),
        imag.reshape(2 * count, piece, 2 * chans),
        -turn[:, :, None],
    )
    real, imag = (
        lax.all_to_all(real, "ctx", split_axis=0, concat_axis=1, tiled=True),
        lax.all_to_all(imag, "ctx", split_axis=0, concat_axis=1, tiled=True),
    )
    real = jnp.transpose(real, (1, 0, 2)).reshape(rows, 4 * chans)
    imag = jnp.transpose(imag, (1, 0, 2)).reshape(rows, 4 * chans)
    real, imag = transform(real, imag, -1.0)
    real = real.reshape(rows, 2, 2 * chans)
    imag = imag.reshape(rows, 2, 2 * chans)
    sig_re, flt_re = (real[:, :, :chans], real[:, :, chans:])
    sig_im, flt_im = (imag[:, :, :chans], imag[:, :, chans:])
    prod_re = sig_re * flt_re - sig_im * flt_im
    prod_im = sig_re * flt_im + sig_im * flt_re
    real, imag = transform(prod_re.reshape(rows, 2 * chans), prod_im.reshape(rows, 2 * chans), 1.0)
    real = jnp.transpose(real.reshape(rows, 2, chans), (1, 0, 2))
    imag = jnp.transpose(imag.reshape(rows, 2, chans), (1, 0, 2))
    real, imag = (
        lax.all_to_all(real, "ctx", split_axis=1, concat_axis=0, tiled=True),
        lax.all_to_all(imag, "ctx", split_axis=1, concat_axis=0, tiled=True),
    )
    real, imag = rotate(real, imag, turn[:, :, None])
    real, imag = transform(
        real.reshape(2 * count, piece * chans), imag.reshape(2 * count, piece * chans), 1.0
    )
    kept = real[:count].reshape(count, piece, chans) / total
    conv = lax.all_to_all(kept, "ctx", split_axis=0, concat_axis=1, tiled=True)[0]
    gated = (query.astype(jnp.float32) * (conv + direct[None, :] * signal)).astype(jnp.bfloat16)
    partial_terms = jnp.dot(gated, w_out, preferred_element_type=jnp.float32)
    return lax.psum_scatter(partial_terms, "tp", scatter_dimension=1, tiled=True).astype(
        jnp.bfloat16
    )


def solution(mesh):
    return jax.shard_map(
        body,
        mesh=mesh,
        in_specs=(
            P("ctx", "tp"),
            P("ctx", "tp"),
            P("ctx", "tp"),
            P("ctx", "tp"),
            P("tp"),
            P("tp", None),
        ),
        out_specs=P("ctx", "tp"),
        check_vma=False,
    )
```

profile of v0, /device:TPU:0, one launch (start us, length us, event | category | flops | bytes accessed | tf_op | source)
XLA Modules:
  0.0 521.1 jit_solution(16326412702973717459)
XLA Ops:
  9.7 5.2 all-to-all-start
  16.6 13.7 %all-to-all-done = f32[1,256,1024]{2,0,1:T(1,128)S(1)} async-done(((f32[1,256,1024]{2,0,1:T(1,128)}), f32[1,256,1024]{2,0,1:T(1,128)S(1)}, u32[]{:S(2)}, u32[]{:S(2)}) %all-to-all-start) | async-done | bytes 1048608 | tf_op jit(solution)/shard_map/all_to_all | solution.py:61
  30.3 3.6 all-to-all-start.1
  33.9 3.9 fusion.10
  38.0 11.2 %all-to-all-done.1 = f32[1,256,1024]{2,0,1:T(1,128)S(1)} async-done(((f32[1,256,1024]{2,0,1:T(1,128)}), f32[1,256,1024]{2,0,1:T(1,128)S(1)}, u32[]{:S(2)}, u32[]{:S(2)}) %all-to-all-start.1) | async-done | bytes 1048608 | tf_op jit(solution)/shard_map/all_to_all | solution.py:62
  49.9 2.4 copy.44
  52.3 3.7 fusion.56
  56.0 1.9 convolution_subtract_fusion.2
  58.0 2.4 copy.45
  60.4 3.9 convolution_add_fusion.2
  64.3 2.4 copy.46
  66.8 3.8 fusion
  70.6 52.3 %all_to_all.105 = f32[16,32,2048]{2,1,0:T(8,128)} all-to-all(f32[16,32,2048]{2,1,0:T(8,128)S(1)} %get-tuple-element.7), channel_id=1, replica_groups=mesh['ctx'=8,'tp'=4] {'ctx'}, dimensions={0} | all-to-all | bytes 8388608 | tf_op jit(solution)/shard_map/all_to_all | solution.py:78
  122.9 4.6 all-to-all-start.3
  128.1 2.5 copy.29
  130.6 5.2 %copy.30 = f32[256,2,2048]{2,1,0:T(2,128)} copy(f32[256,2,2048]{2,0,1:T(8,128)S(1)} %bitcast.111) | data formatting | bytes 8388608 | tf_op jit(solution)/shard_map/transpose | solution.py:81
  135.8 6.8 %reshape_reshape.24 = f32[64,16384]{1,0:T(8,128)} reshape(f32[256,2,2048]{2,1,0:T(2,128)} %copy.30) | data formatting | bytes 8388608 | tf_op jit(solution)/shard_map/reshape;reshape | solution.py:38
  142.6 8.0 %fusion.24 = f32[64,16384]{1,0:T(8,128)} fusion(f32[64,16384]{1,0:T(8,128)} %reshape_reshape.24), kind=kOutput, calls=%fused_computation.56 | convolution fusion | flops 805363712 | bytes 8388608 | tf_op jit(solution)/shard_map/dot_general | solution.py:18
  150.6 26.0 %all-to-all-done.3 = f32[16,32,2048]{2,1,0:T(8,128)} async-done(((f32[16,32,2048]{2,1,0:T(8,128)}), f32[16,32,2048]{2,1,0:T(8,128)}, u32[]{:S(2)}, u32[]{:S(2)}) %all-to-all-start.3) | async-done | bytes 4194336 | tf_op jit(solution)/shard_map/all_to_all | solution.py:79
  176.6 2.5 copy.31
  179.1 5.2 copy.32
  184.2 7.1 %reshape_reshape.25 = f32[64,16384]{1,0:T(8,128)} reshape(f32[256,2,2048]{2,1,0:T(2,128)} %copy.32) | data formatting | bytes 8388608 | tf_op jit(solution)/shard_map/reshape;reshape | solution.py:38
  191.4 8.1 %fusion.23 = f32[64,16384]{1,0:T(8,128)} fusion(f32[64,16384]{1,0:T(8,128)} %reshape_reshape.25), kind=kOutput, calls=%fused_computation.55 | convolution fusion | flops 805363712 | bytes 8388608 | tf_op jit(solution)/shard_map/dot_general | solution.py:19
  199.5 5.4 %convolution_subtract_fusion.3 = f32[64,16384]{1,0:T(8,128)} fusion(f32[64,16384]{1,0:T(8,128)S(1)} %copy-done.7, f32[64,16384]{1,0:T(8,128)S(1)} %copy-done.1), kind=kOutput, calls=%fused_computation.7 | convolution fusion | flops 806412288 | bytes 12582912 | tf_op jit(solution)/shard_map/dot_general | solution.py:18
  204.9 6.1 %reshape.218 = f32[64,4,4096]{2,1,0:T(4,128)} reshape(f32[64,16384]{1,0:T(8,128)} %convolution_subtract_fusion.3) | data formatting | bytes 8388608 | tf_op jit(solution)/shard_map/reshape | solution.py:45
  211.0 9.2 %convolution_add_fusion.3 = f32[64,16384]{1,0:T(8,128)} fusion(f32[64,16384]{1,0:T(8,128)} %fusion.23, f32[64,16384]{1,0:T(8,128)} %reshape_reshape.24), kind=kOutput, calls=%fused_computation.6 | convolution fusion | flops 806412288 | bytes 12582912 | tf_op jit(solution)/shard_map/dot_general | solution.py:19
  220.2 6.0 %reshape.219 = f32[64,4,4096]{2,1,0:T(4,128)} reshape(f32[64,16384]{1,0:T(8,128)} %convolution_add_fusion.3) | data formatting | bytes 8388608 | tf_op jit(solution)/shard_map/reshape | solution.py:45
  226.2 5.0 multiply_subtract_fusion
  231.2 8.0 %fusion.78 = f32[4,262144]{1,0:T(4,128)S(1)} fusion(f32[4,262144]{1,0:T(4,128)S(1)} %bitcast.89), kind=kOutput, calls=%fused_computation.120 | convolution fusion | flops 50331872 | bytes 8388608 | tf_op jit(solution)/shard_map/dot_general | solution.py:18
  239.3 8.7 %fusion.77 = f32[4,262144]{1,0:T(4,128)} fusion(f32[4,262144]{1,0:T(4,128)S(1)} %bitcast.91), kind=kOutput, calls=%fused_computation.119 | convolution fusion | flops 50331872 | bytes 8388608 | tf_op jit(solution)/shard_map/dot_general | solution.py:19
  248.0 9.2 %convolution_subtract_fusion = f32[4,262144]{1,0:T(4,128)} fusion(f32[4,262144]{1,0:T(4,128)S(1)} %fusion.78, f32[4,262144]{1,0:T(4,128)S(1)} %bitcast.92), kind=kOutput, calls=%fused_computation.1 | convolution fusion | flops 51380448 | bytes 12582912 | tf_op jit(solution)/shard_map/dot_general | solution.py:18
  257.2 8.4 %reshape_reshape.26 = f32[256,2,2048]{2,1,0:T(2,128)} reshape(f32[4,262144]{1,0:T(4,128)} %convolution_subtract_fusion) | data formatting | bytes 8388608 | tf_op jit(solution)/shard_map/reshape;reshape | solution.py:84
  265.7 12.0 %convolution_add_fusion = f32[4,262144]{1,0:T(4,128)} fusion(f32[4,262144]{1,0:T(4,128)} %fusion.77, f32[4,262144]{1,0:T(4,128)} %bitcast.90), kind=kOutput, calls=%fused_computation | convolution fusion | flops 51380448 | bytes 12582912 | tf_op jit(solution)/shard_map/dot_general | solution.py:19
  277.6 8.5 %reshape_reshape.27 = f32[256,2,2048]{2,1,0:T(2,128)} reshape(f32[4,262144]{1,0:T(4,128)} %convolution_add_fusion) | data formatting | bytes 8388608 | tf_op jit(solution)/shard_map/reshape;reshape | solution.py:85
  286.2 5.9 %multiply_subtract_fusion.2 = (f32[256,2,1024]{2,1,0:T(2,128)}, f32[256,2,1024]{2,1,0:T(2,128)}) fusion(f32[256,2,2048]{2,1,0:T(2,128)} %reshape_reshape.27, f32[256,2,2048]{2,1,0:T(2,128)} %reshape_reshape.26), kind=kLoop, calls=%fused_computation.31 | loop fusion | flops 3145728 | bytes 12582912 | tf_op jit(solution)/shard_map/sub | solution.py:88
  292.0 3.1 reshape_reshape.28
  295.1 3.4 fusion.22
  298.5 4.2 reshape_reshape.29
  302.7 5.1 fusion.21
  307.8 3.5 convolution_subtract_fusion.4
  311.4 3.6 reshape.222
  315.0 5.0 convolution_add_fusion.4
  320.0 3.7 reshape.223
  323.7 3.5 multiply_subtract_fusion.1
  327.2 3.7 fusion.76
  330.9 5.3 %convolution_subtract_fusion.1 = f32[4,131072]{1,0:T(4,128)} fusion(f32[4,131072]{1,0:T(4,128)S(1)} %fusion.76, f32[4,131072]{1,0:T(4,128)S(1)} %bitcast.105), kind=kOutput, calls=%fused_computation.3 | convolution fusion | flops 25690336 | bytes 6291456 | tf_op jit(solution)/shard_map/dot_general | solution.py:18
  336.2 5.1 reshape_reshape.30
  341.3 4.3 all-to-all-start.4
  345.7 5.4 %fusion.75 = f32[4,131072]{1,0:T(4,128)S(1)} fusion(f32[4,131072]{1,0:T(4,128)} %bitcast.106), kind=kOutput, calls=%fused_computation.117 | convolution fusion | flops 25166048 | bytes 4194304 | tf_op jit(solution)/shard_map/dot_general | solution.py:19
  351.1 5.0 convolution_add_fusion.1
  356.2 5.1 reshape_reshape.31
  361.2 11.1 %all-to-all-done.4 = f32[2,256,1024]{2,0,1:T(2,128)} async-done(((f32[2,256,1024]{2,0,1:T(2,128)}), f32[2,256,1024]{2,0,1:T(2,128)}, u32[]{:S(2)}, u32[]{:S(2)}) %all-to-all-start.4) | async-done | bytes 2097184 | tf_op jit(solution)/shard_map/all_to_all | solution.py:94
  372.3 4.3 all-to-all-start.5
  378.8 2.6 copy.50
  381.4 2.3 copy.37
  383.9 2.6 copy.47
  386.5 16.8 %all-to-all-done.5 = f32[2,256,1024]{2,0,1:T(2,128)} async-done(((f32[2,256,1024]{2,0,1:T(2,128)}), f32[2,256,1024]{2,0,1:T(2,128)}, u32[]{:S(2)}, u32[]{:S(2)}) %all-to-all-start.5) | async-done | bytes 2097184 | tf_op jit(solution)/shard_map/all_to_all | solution.py:95
  403.3 2.3 copy.39
  407.8 2.1 fusion.6
  409.9 2.1 fusion.2
  413.0 17.9 %all_to_all.106 = f32[8,32,1024]{2,1,0:T(8,128)S(1)} all-to-all(f32[8,32,1024]{2,1,0:T(8,128)S(1)} %copy.41), channel_id=1, replica_groups=mesh['ctx'=8,'tp'=4] {'ctx'}, dimensions={0} | all-to-all | bytes 2097152 | tf_op jit(solution)/shard_map/all_to_all | solution.py:102
  431.3 4.4 fusion.185
  435.7 76.3 %reduce-scatter.2.cloned.1.call-done = f32[256,1024]{1,0:T(8,128)} async-done(((f32[256,4096]{1,0:T(8,128)}), f32[256,1024]{1,0:T(8,128)}) %reduce-scatter.2.cloned.1.call-update) | async-done | bytes 1048592 | tf_op jit(solution)/shard_map/reduce_scatter | solution.py:105
  512.0 2.1 convert_element_type.121
  (60 shorter events, 12.3 us)
Async XLA Ops:
  6.5 8.3 %copy-start.11 = (f32[256,1024]{1,0:T(8,128)S(1)}, f32[256,1024]{1,0:T(8,128)}, u32[]{:S(2)}) copy-start(f32[256,1024]{1,0:T(8,128)} %param.9) | copy-start | bytes 3145732
  9.7 20.6 %all-to-all-start = ((f32[1,256,1024]{2,0,1:T(1,128)}), f32[1,256,1024]{2,0,1:T(1,128)S(1)}, u32[]{:S(2)}, u32[]{:S(2)}) async-start(f32[1,256,1024]{2,0,1:T(1,128)} %broadcast_in_dim.6), calls=%async_computation | async-start | bytes 2097152 | tf_op jit(solution)/shard_map/all_to_all | solution.py:61
  30.3 18.9 %all-to-all-start.1 = ((f32[1,256,1024]{2,0,1:T(1,128)}), f32[1,256,1024]{2,0,1:T(1,128)S(1)}, u32[]{:S(2)}, u32[]{:S(2)}) async-start(f32[1,256,1024]{2,0,1:T(1,128)} %broadcast_in_dim.7), calls=%async_computation.1 | async-start | bytes 2097152 | tf_op jit(solution)/shard_map/all_to_all | solution.py:62
  58.0 2.4 copy-start.6
  122.9 53.7 %all-to-all-start.3 = ((f32[16,32,2048]{2,1,0:T(8,128)}), f32[16,32,2048]{2,1,0:T(8,128)}, u32[]{:S(2)}, u32[]{:S(2)}) async-start(f32[16,32,2048]{2,1,0:T(8,128)} %get-tuple-element.8), calls=%async_computation.3 | async-start | bytes 8388608 | tf_op jit(solution)/shard_map/all_to_all | solution.py:79
  191.3 8.1 %copy-start.1 = (f32[64,16384]{1,0:T(8,128)S(1)}, f32[64,16384]{1,0:T(8,128)}, u32[]{:S(2)}) copy-start(f32[64,16384]{1,0:T(8,128)} %reshape_reshape.25) | copy-start | bytes 12582916
  191.3 8.1 %copy-start.7 = (f32[64,16384]{1,0:T(8,128)S(1)}, f32[64,16384]{1,0:T(8,128)}, u32[]{:S(2)}) copy-start(f32[64,16384]{1,0:T(8,128)} %fusion.24) | copy-start | bytes 12582916
  231.2 8.1 %copy-start = (f32[64,4,4096]{2,1,0:T(4,128)}, f32[64,4,4096]{2,1,0:T(4,128)S(1)}, u32[]{:S(2)}) copy-start(f32[64,4,4096]{2,1,0:T(4,128)S(1)} %get-tuple-element.5) | copy-start | bytes 12582916
  302.7 5.2 copy-start.4
  302.7 5.1 copy-start.8
  327.2 3.8 copy-start.5
  341.3 31.0 %all-to-all-start.4 = ((f32[2,256,1024]{2,0,1:T(2,128)}), f32[2,256,1024]{2,0,1:T(2,128)}, u32[]{:S(2)}, u32[]{:S(2)}) async-start(f32[2,256,1024]{2,0,1:T(2,128)} %bitcast.113), calls=%async_computation.4 | async-start | bytes 4194304 | tf_op jit(solution)/shard_map/all_to_all | solution.py:94
  372.3 31.0 %all-to-all-start.5 = ((f32[2,256,1024]{2,0,1:T(2,128)}), f32[2,256,1024]{2,0,1:T(2,128)}, u32[]{:S(2)}, u32[]{:S(2)}) async-start(f32[2,256,1024]{2,0,1:T(2,128)} %bitcast.23), calls=%async_computation.5 | async-start | bytes 4194304 | tf_op jit(solution)/shard_map/all_to_all | solution.py:95
  376.7 135.3 %reduce-scatter.2.cloned.1.call-start = ((), (), s32[]{:S(2)}) async-start(), calls=%async_computation.8 | async-start | bytes 5242880 | tf_op jit(solution)/shard_map/reduce_scatter | solution.py:105
  405.6 1.6 copy-start.2
  405.6 2.2 copy-start.3
  409.9 21.4 %slice-start = ((s8[8388608]{0:T(1024)(128)(4,1)}), s8[4194304]{0:T(1024)(128)(4,1)S(1)}, s32[]{:S(2)}) async-start(s8[8388608]{0:T(1024)(128)(4,1)} %bitcast.123), calls=%async_computation.9 | async-start | bytes 8388608
  412.0 18.9 %copy-start.9 = (bf16[256,1024]{1,0:T(8,128)(2,1)S(1)}, bf16[256,1024]{1,0:T(8,128)(2,1)}, u32[]{:S(2)}) copy-start(bf16[256,1024]{1,0:T(8,128)(2,1)} %param.8) | copy-start | bytes 1572868
  412.0 18.9 %copy-start.10 = (bf16[256,1024]{1,0:T(8,128)(2,1)S(1)}, bf16[256,1024]{1,0:T(8,128)(2,1)}, u32[]{:S(2)}) copy-start(bf16[256,1024]{1,0:T(8,128)(2,1)} %param.7) | copy-start | bytes 1572868
  412.1 18.9 %copy-start.12 = (bf16[256,1024]{1,0:T(8,128)(2,1)S(1)}, bf16[256,1024]{1,0:T(8,128)(2,1)}, u32[]{:S(2)}) copy-start(bf16[256,1024]{1,0:T(8,128)(2,1)} %param.6) | copy-start | bytes 1572868
  412.1 18.9 %copy-start.13 = (f32[1024]{0:T(1024)S(1)}, f32[1024]{0:T(1024)}, u32[]{:S(2)}) copy-start(f32[1024]{0:T(1024)} %param.10) | copy-start | bytes 12292
  412.1 19.2 %slice-start.1 = ((s8[8388608]{0:T(1024)(128)(4,1)}), s8[4194304]{0:T(1024)(128)(4,1)S(1)}, s32[]{:S(2)}) async-start(s8[8388608]{0:T(1024)(128)(4,1)} %bitcast.123), calls=%async_computation.10 | async-start | bytes 8388608
Sparse Core Ops, SparseCore 0:
  435.8 76.1 reduce-scatter.1
where the time goes:
time: 525 us; the launch traced here: 521 us
  waiting for transfers between devices  155 us (30%)
  matrix products  127 us (24%)
  local copies, waits for them, and re-layouts  109 us (21%)
  blocking collectives  70.2 us (13%)
  other arithmetic  22.9 us (4%)
  starting transfers between devices  22.4 us (4%)
  between operations  14.1 us (3%)
    reduce_scatter x1, waiting for transfers between devices, body(): lax.psum_scatter(partial_terms, 'tp', scatter_dimension=1, tiled=True)  76.3 us
    all_to_all x1, blocking collectives, body(): lax.all_to_all(real, 'ctx', split_axis=0, concat_axis=1, tiled=True)  52.3 us
    dot_general x5, matrix products, complex_dot(): jnp.dot(sine, real, precision=best)  35.2 us
    dot_general x5, matrix products, complex_dot(): jnp.dot(cosine, imag, precision=best) + jnp.dot(sine, real, precision=best)  31.2 us
    dot_general x6, matrix products, complex_dot(): jnp.dot(cosine, real, precision=best) - jnp.dot(sine, imag, precision=best)  29 us
    dot_general x6, matrix products, complex_dot(): jnp.dot(sine, imag, precision=best)  27.5 us
    all_to_all x1, waiting for transfers between devices, body(): lax.all_to_all(imag, 'ctx', split_axis=0, concat_axis=1, tiled=True)  26 us
    all_to_all x1, blocking collectives, body(): lax.all_to_all(kept, 'ctx', split_axis=0, concat_axis=1, tiled=True)[0]  17.9 us
  transfers between devices with their start and end apart: 6, of which 6 were waited for; matrix products, arithmetic and copies ran while one was open for 10% of the time, Pallas kernels for 0%

commit v1 on v0

v1 whole, which is shorter than its diff:
```python
import functools
import math

import jax
import jax.numpy as jnp
import ml_dtypes
import numpy as np
from jax import lax
from jax.experimental import pallas as pl
from jax.experimental.pallas import tpu as pltpu
from jax.sharding import PartitionSpec as P

F32 = jnp.float32
BF16 = jnp.bfloat16
VMEM_LIMIT = 56 * 1024 * 1024


def halves(table):
    high = table.astype(ml_dtypes.bfloat16)
    low = (table - high.astype(np.float64)).astype(ml_dtypes.bfloat16)
    return high, low


def tables(block):
    freq = 2 * np.arange(block, dtype=np.int64) + 1
    place = np.arange(block, dtype=np.int64)
    angle = 2.0 * math.pi / (4 * block) * (freq[:, None] * place[None, :] % (4 * block))
    forward = np.concatenate([np.cos(angle), -np.sin(angle)], axis=0)
    high, low = halves(forward)
    ahead = np.concatenate([high, high, low], axis=1)
    high, low = halves(forward.T / block)
    back = np.concatenate([high, high, low], axis=1)
    return ahead, back


def split3(value):
    high = value.astype(BF16)
    low = (value - high.astype(F32)).astype(BF16)
    return jnp.concatenate([high, low, high], axis=0)


def pack_kernel(place_ref, keys_ref, values_ref, filt_ref, *refs):
    outs, turned_ref = refs[:-1], refs[-1]
    chans = keys_ref.shape[1] // len(outs)
    for group in range(len(outs)):
        cols = slice(group * chans, (group + 1) * chans)
        slot = group ^ place_ref[0]
        turned_ref[slot, :, :chans] = keys_ref[:, cols].astype(F32) * values_ref[:, cols].astype(F32)
        turned_ref[slot, :, chans:] = filt_ref[:, cols]
    for turn, out in zip(turns(len(outs)), outs):
        out[...] = turned_ref[turn]


def pack(place, keys, values, filt, count):
    rows, width = keys.shape
    step = math.gcd(rows, 128)
    spec = pl.BlockSpec((step, width), lambda i: (i, 0))
    wide = 2 * width // count
    return pl.pallas_call(
        pack_kernel,
        grid=(rows // step,),
        in_specs=[pl.BlockSpec(memory_space=pltpu.SMEM), spec, spec, spec],
        out_specs=[pl.BlockSpec((step, wide), lambda i: (i, 0))] * count,
        out_shape=[jax.ShapeDtypeStruct((rows, wide), F32)] * count,
        scratch_shapes=[pltpu.VMEM((count, step, wide), F32)],
        compiler_params=pltpu.CompilerParams(vmem_limit_bytes=VMEM_LIMIT),
    )(place, keys, values, filt)


def turns(count):
    return [0, 1] + sorted(range(2, count), key=lambda d: (d & 1 and bin(d >> 1).count("1") == 1, -bin(d >> 1).count("1"), d))


def swap(arrays):
    count = len(arrays)
    pairs = [[(i, i ^ d) for i in range(count)] for d in turns(count)]
    return [arrays[0]] + [lax.ppermute(arrays[j], "ctx", pairs[j]) for j in range(1, count)]


def forward_kernel(ahead_ref, *refs):
    for j, x in enumerate(refs[:-1]):
        refs[-1][j] = jnp.dot(ahead_ref[...], split3(x[...]), preferred_element_type=F32)


def forward(xs, ahead):
    rows, width = xs[0].shape
    whole = pl.BlockSpec(memory_space=pltpu.VMEM)
    return pl.pallas_call(
        forward_kernel,
        in_specs=[whole] * (1 + len(xs)),
        out_specs=whole,
        out_shape=jax.ShapeDtypeStruct((len(xs), 2 * rows, width), F32),
        compiler_params=pltpu.CompilerParams(vmem_limit_bytes=VMEM_LIMIT),
    )(ahead, *xs)


def conv_kernel(place_ref, early_ref, *refs):
    first = early_ref.shape[0]
    count = (len(refs) - 4 + first) // 2
    xs, (ahead_ref, back_ref) = refs[: count - first], refs[count - first : count - first + 2]
    outs, (spec_ref, mix_ref) = refs[count - first + 2 : -2], refs[-2:]
    rows, width = xs[0].shape
    chans = width // 2
    place = place_ref[0]

    order = turns(count)
    for j, turn in enumerate(order):
        if j < first:
            spec_ref[turn ^ place] = early_ref[j]
        else:
            x = xs[j - first]
            spec_ref[turn ^ place] = jnp.dot(ahead_ref[...], split3(x[...]), preferred_element_type=F32)

    step = 8
    parity = lax.broadcasted_iota(jnp.int32, (step, chans), 0) % 2
    sign = (1 - 2 * parity).astype(F32)

    def combine(i, carry):
        real = pl.ds(pl.multiple_of(i * step, step), step)
        imag = pl.ds(pl.multiple_of(rows + i * step, step), step)
        flt = []
        last = None
        for j in range(count):
            here = (spec_ref[j, real, chans:], spec_ref[j, imag, chans:])
            if last is None:
                flt.append(here)
            else:
                flt.append((here[0] - sign * last[1], here[1] + sign * last[0]))
            last = here
        sig = [(spec_ref[j, real, :chans], spec_ref[j, imag, :chans]) for j in range(count)]
        for j in range(count):
            re = None
            for s in range(j + 1):
                a, b = sig[s]
                c, d = flt[j - s]
                if re is None:
                    re, im = a * c - b * d, a * d + b * c
                else:
                    re, im = re + (a * c - b * d), im + (a * d + b * c)
            mix_ref[j, real] = re
            mix_ref[j, imag] = im
        return carry

    lax.fori_loop(0, rows // step, combine, 0)

    for j in range(0, count, 2):
        pair = jnp.concatenate([mix_ref[order[j] ^ place], mix_ref[order[j + 1] ^ place]], axis=1)
        part = jnp.dot(back_ref[...], split3(pair), preferred_element_type=F32)
        outs[j][...] = part[:, :chans]
        outs[j + 1][...] = part[:, chans:]


def convolve(place, xs):
    count = len(xs)
    rows, width = xs[0].shape
    chans = width // 2
    ahead, back = (jnp.asarray(table) for table in tables(rows))
    first = count // 2
    early = forward(xs[:first], ahead)
    whole = pl.BlockSpec(memory_space=pltpu.VMEM)
    return pl.pallas_call(
        conv_kernel,
        in_specs=[pl.BlockSpec(memory_space=pltpu.SMEM)] + [whole] * (count - first + 3),
        out_specs=[whole] * count,
        out_shape=[jax.ShapeDtypeStruct((rows, chans), F32)] * count,
        scratch_shapes=[
            pltpu.VMEM((count, 2 * rows, width), F32),
            pltpu.VMEM((count, 2 * rows, chans), F32),
        ],
        compiler_params=pltpu.CompilerParams(vmem_limit_bytes=VMEM_LIMIT),
    )(place, early, *xs[first:], ahead, back)


CHAINS = 2


def gate_kernel(place_ref, q_ref, k_ref, v_ref, direct_ref, far_ref, *refs):
    convs, (gated_ref, *firsts), conv_ref = refs[: -2 - CHAINS], refs[-2 - CHAINS : -1], refs[-1]
    rows, chans = convs[0].shape
    for turn, ref in zip(turns(len(convs)), convs):
        conv_ref[turn ^ place_ref[0]] = ref[...]
    for group in range(len(convs)):
        cols = slice(group * chans, (group + 1) * chans)
        signal = k_ref[:, cols].astype(F32) * v_ref[:, cols].astype(F32)
        inner = conv_ref[group] + direct_ref[:, cols] * signal
        gated_ref[:, cols] = (q_ref[:, cols].astype(F32) * inner).astype(BF16)
    width = far_ref.shape[1] // CHAINS
    for k, out in enumerate(firsts):
        cols = slice(k * width, (k + 1) * width)
        out[...] = jnp.dot(gated_ref[...], far_ref[:, cols], preferred_element_type=F32)


def gate(place, query, keys, values, direct, far, convs):
    rows, width = query.shape
    whole = pl.BlockSpec(memory_space=pltpu.VMEM)
    first = jax.ShapeDtypeStruct((rows, far.shape[1] // CHAINS), F32)
    out = pl.pallas_call(
        gate_kernel,
        in_specs=[pl.BlockSpec(memory_space=pltpu.SMEM)] + [whole] * (5 + len(convs)),
        out_specs=[whole] * (1 + CHAINS),
        out_shape=[jax.ShapeDtypeStruct((rows, width), BF16)] + [first] * CHAINS,
        scratch_shapes=[pltpu.VMEM((len(convs),) + convs[0].shape, F32)],
        compiler_params=pltpu.CompilerParams(vmem_limit_bytes=VMEM_LIMIT),
    )(place, query, keys, values, direct, far, *convs)
    return out[0], out[1:]


def column_block(array, index, size):
    width = array.shape[1] // size
    return lax.dynamic_slice_in_dim(array, jnp.clip(index, 0, size - 1) * width, width, 1)


def pass_on(up, down, step, size):
    rise = [(z, z + 1) for z in range(min(step, size - 1))]
    fall = [(z, z - 1) for z in range(max(size - step, 1), size)]
    up, down = lax.optimization_barrier((up, down))
    up = lax.ppermute(up, "tp", rise)
    down = lax.ppermute(down, "tp", fall)
    return up, down


def first_step(value, size):
    place = lax.axis_index("tp")
    if size == 2:
        return pass_on(value, value, 1, size)
    got = lax.ppermute(value, "tp", [(0, 1), (size - 1, size - 2)])
    return jnp.where(place == 1, got, 0.0), jnp.where(place == size - 2, got, 0.0)


def scatter_dot(lhs, rhs, first):
    size = lax.axis_size("tp")
    place = lax.axis_index("tp")
    rows, width = first[0].shape
    lhs, first = lax.optimization_barrier((lhs, first))
    sums = [first_step(value, size) for value in first]
    terms = jnp.dot(lhs, rhs, preferred_element_type=F32)

    def own(index, k):
        start = jnp.clip(index, 0, size - 1) * (width * CHAINS) + k * width
        return lax.dynamic_slice_in_dim(terms, start, width, 1)

    for step in range(2, size):
        for k in range(CHAINS):
            up = sums[k][0] + own(place + size - step, k)
            down = sums[k][1] + own(place - size + step, k)
            up, down, terms = lax.optimization_barrier((up, down, terms))
            sums[k] = pass_on(up, down, step, size)
    out = jnp.zeros((rows, width * CHAINS), BF16)
    for k in range(CHAINS):
        part = (own(place, k) + sums[k][0] + sums[k][1]).astype(BF16)
        out = lax.dynamic_update_slice(out, part, (0, k * width))
        out, terms = lax.optimization_barrier((out, terms))
    return out


def body(query, keys, values, filt, direct, w_out):
    count = lax.axis_size("ctx")
    size = lax.axis_size("tp")
    place = lax.axis_index("ctx").reshape(1)
    xs = swap(pack(place, keys, values, filt, count))
    far = column_block(w_out, jnp.where(lax.axis_index("tp") == 0, size - 1, 0), size)
    xs[0], far = lax.optimization_barrier((xs[0], far))
    convs = swap(convolve(place, xs))
    gated, first = gate(place, query, keys, values, direct.reshape(1, -1), far, convs)
    return scatter_dot(gated, w_out, first)


def solution(mesh):
    return jax.shard_map(
        body,
        mesh=mesh,
        in_specs=(
            P("ctx", "tp"),
            P("ctx", "tp"),
            P("ctx", "tp"),
            P("ctx", "tp"),
            P("tp"),
            P("tp", None),
        ),
        out_specs=P("ctx", "tp"),
        check_vma=False,
    )
```

time: 525 us -> 133 us (0.25)
  matrix products: 127 us -> 5.9 us
  waiting for transfers between devices: 155 us -> 50 us
  local copies, waits for them, and re-layouts: 109 us -> 6.66 us
  blocking collectives: 70.2 us -> 0 us
  starting transfers between devices: 22.4 us -> 44.2 us
  Pallas kernels: 0 us -> 17.3 us
  other arithmetic: 22.9 us -> 8.17 us
  between operations: 14.1 us -> 0.19 us
    dot_general x23 -> x1, matrix products: 127 us -> 5.9 us  [scatter_dot(): terms = jnp.dot(lhs, rhs, preferred_element_type=F32)]
    all_to_all x5 -> x0, waiting for transfers between devices: 78.8 us -> none  [the longest x1 26 us: body(): lax.all_to_all(imag, 'ctx', split_axis=0, concat_axis=1, tiled=True)]
    reduce_scatter x1 -> x0, waiting for transfers between devices: 76.3 us -> none  [body(): lax.psum_scatter(partial_terms, 'tp', scatter_dimension=1, tiled=True)]
    all_to_all x2 -> x0, blocking collectives: 70.2 us -> none  [the longest x1 52.3 us: body(): lax.all_to_all(real, 'ctx', split_axis=0, concat_axis=1, tiled=True)]
    ppermute x0 -> x24, waiting for transfers between devices: none -> 50 us  [the longest x14 20.7 us: swap(): lax.ppermute(arrays[j], 'ctx', pairs[j])]
    another operation x8 -> x0, local copies, waits for them, and re-layouts: 48.3 us -> none  [the longest x2 11.3 us: transform(): imag.reshape(factor, others * width)]
    ppermute x0 -> x24, starting transfers between devices: none -> 44.2 us  [the longest x4 19.3 us: pass_on(): up = lax.ppermute(up, 'tp', rise)]
    all_to_all x5 -> x0, starting transfers between devices: 22 us -> none  [the longest x1 5.17 us: body(): lax.all_to_all(signal[None], 'ctx', split_axis=1, concat_axis=0, tiled=True)]
  transfers between devices with their start and end apart: 6 -> 24, of which waited for: 6 -> 15; matrix products, arithmetic and copies ran while one was open for 10% -> 12% of each run, Pallas kernels for 0% -> 3%
where the time goes in v1:
time: 133 us; the launch traced here: 132 us
  waiting for transfers between devices  50 us (38%)
  starting transfers between devices  44.2 us (33%)
  Pallas kernels  17.3 us (13%)
  other arithmetic  8.17 us (6%)
  local copies, waits for them, and re-layouts  6.66 us (5%)
  matrix products  5.9 us (4%)
    ppermute x14, waiting for transfers between devices, swap(): lax.ppermute(arrays[j], 'ctx', pairs[j])  20.7 us
    ppermute x4, starting transfers between devices, pass_on(): up = lax.ppermute(up, 'tp', rise)  19.3 us
    ppermute x4, waiting for transfers between devices, pass_on(): up = lax.ppermute(up, 'tp', rise)  18.7 us
    ppermute x14, starting transfers between devices, swap(): lax.ppermute(arrays[j], 'ctx', pairs[j])  14.4 us
    ppermute x2, waiting for transfers between devices, first_step(): got = lax.ppermute(value, 'tp', [(0, 1), (size - 1, size - 2)])  10.5 us
    pallas_call x1, Pallas kernels, convolve(): pl.pallas_call(conv_kernel, in_specs=[pl.BlockSpec(memory_space=pltpu.SME...  6.9 us
    dot_general x1, matrix products, scatter_dot(): terms = jnp.dot(lhs, rhs, preferred_element_type=F32)  5.9 us
    ppermute x2, starting transfers between devices, first_step(): got = lax.ppermute(value, 'tp', [(0, 1), (size - 1, size - 2)])  5.82 us
  transfers between devices with their start and end apart: 24, of which 15 were waited for; matrix products, arithmetic and copies ran while one was open for 12% of the time, Pallas kernels for 3%

profile of v1, /device:TPU:0, one launch (start us, length us, event | category | flops | bytes accessed | tf_op | source)
XLA Modules:
  0.0 132.4 jit_solution(5196896518550908439)
XLA Ops:
  0.0 2.6 %shard_map.82 = (f32[256,256]{1,0:T(8,128)}, f32[256,256]{1,0:T(8,128)}, f32[256,256]{1,0:T(8,128)}, f32[256,256]{1,0:T(8,128)}, f32[256,256]{1,0:T(8,128)}, /*i...) custom-call(s32[1]{0:T(128)} %bitcast.place_ref, bf16[256,1024]{1,0:T(8,128)(2,1)} %k_ref.1, ...), custom_call_target="tpu_custom_call" | custom-call | tf_op jit(solution)/shard_map/pallas_call | solution.py:59
  2.6 0.5 collective-permute-start
  3.1 3.5 %collective-permute-start.1 = (f32[256,256]{1,0:T(8,128)}, f32[256,256]{1,0:T(8,128)S(1)}, u32[]{:S(2)}, u32[]{:S(2)}) collective-permute-start(f32[256,256]{1,0:T(8,128)} %get-tuple-element.53), channel_id=1, source_target_pairs={{0,24},{4,28},{8,16},{12,20},{16,8},{20,12},{24,0},{28,4},{1,25},{... | collective-permute-start | bytes 786440 | tf_op jit(solution)/shard_map/ppermute | solution.py:77
  6.6 0.1 collective-permute-start.2
  6.7 1.7 %collective-permute-start.3 = (f32[256,256]{1,0:T(8,128)}, f32[256,256]{1,0:T(8,128)S(1)}, u32[]{:S(2)}, u32[]{:S(2)}) collective-permute-start(f32[256,256]{1,0:T(8,128)} %get-tuple-element.55), channel_id=1, source_target_pairs={{0,8},{4,12},{8,0},{12,4},{16,24},{20,28},{24,16},{28,20},{1,9},{5... | collective-permute-start | bytes 786440 | tf_op jit(solution)/shard_map/ppermute | solution.py:77
  8.4 1.5 %collective-permute-start.4 = (f32[256,256]{1,0:T(8,128)}, f32[256,256]{1,0:T(8,128)S(1)}, u32[]{:S(2)}, u32[]{:S(2)}) collective-permute-start(f32[256,256]{1,0:T(8,128)} %get-tuple-element.56), channel_id=1, source_target_pairs={{0,16},{4,20},{8,24},{12,28},{16,0},{20,4},{24,8},{28,12},{1,17},{... | collective-permute-start | bytes 786440 | tf_op jit(solution)/shard_map/ppermute | solution.py:77
  9.9 0.0 collective-permute-done.refs_1_
  9.9 0.0 collective-permute-start.5
  9.9 4.2 %collective-permute-done.1.refs_2_ = f32[256,256]{1,0:T(8,128)S(1)} collective-permute-done((f32[256,256]{1,0:T(8,128)}, f32[256,256]{1,0:T(8,128)S(1)}, u32[]{:S(2)}, u32[]{:S(2)}) %collective-permute-start.1) | collective-permute-done | bytes 262176 | tf_op jit(solution)/shard_map/ppermute | solution.py:77
  14.1 0.7 collective-permute-start.6
  14.8 3.1 %constant_dynamic-slice_fusion.far_ref = bf16[1024,1024]{1,0:T(8,128)(2,1)} fusion(bf16[1024,4096]{1,0:T(8,128)(2,1)} %param.13, s32[]{:T(128)S(6)} %select_n.61), kind=kLoop, calls=%fused_computation.11 | loop fusion | bytes 4194308 | tf_op jit(solution)/shard_map/dynamic_slice | solution.py:210
  17.9 1.3 %collective-permute-done.2.refs_3_ = f32[256,256]{1,0:T(8,128)S(1)} collective-permute-done((f32[256,256]{1,0:T(8,128)}, f32[256,256]{1,0:T(8,128)S(1)}, u32[]{:S(2)}, u32[]{:S(2)}) %collective-permute-start.2) | collective-permute-done | bytes 262176 | tf_op jit(solution)/shard_map/ppermute | solution.py:77
  19.2 0.7 copy-done.7
  19.9 3.8 %shard_map.83.early_ref = f32[4,512,256]{2,1,0:T(8,128)} custom-call(bf16[512,768]{1,0:T(8,128)(2,1)} %constant.47.clone.ahead_ref.refs_4_, f32[256,256]{1,0:T(8,128)} %get-tuple-element.51.refs_0_, f32[256,256]{1,0:T(8,128)} %copy-done.5, f32[256,256]{1,0:T(8,128)} %copy-done.6, f32[256,256]{1,0:T(8,128)} %copy-done.7), custom_call_target="tpu_custom_call" | custom-call | tf_op jit(solution)/shard_map/pallas_call | solution.py:88
  23.7 2.0 %collective-permute-done.3.refs_0_ = f32[256,256]{1,0:T(8,128)S(1)} collective-permute-done((f32[256,256]{1,0:T(8,128)}, f32[256,256]{1,0:T(8,128)S(1)}, u32[]{:S(2)}, u32[]{:S(2)}) %collective-permute-start.3) | collective-permute-done | bytes 262176 | tf_op jit(solution)/shard_map/ppermute | solution.py:77
  25.7 0.0 collective-permute-done.4.refs_1_
  25.7 4.7 %collective-permute-done.5.refs_2_ = f32[256,256]{1,0:T(8,128)S(1)} collective-permute-done((f32[256,256]{1,0:T(8,128)}, f32[256,256]{1,0:T(8,128)S(1)}, u32[]{:S(2)}, u32[]{:S(2)}) %collective-permute-start.5) | collective-permute-done | bytes 262176 | tf_op jit(solution)/shard_map/ppermute | solution.py:77
  30.4 0.1 collective-permute-done.6.refs_3_
  30.5 0.6 copy-done.3
  31.1 0.7 copy-done.4
  31.9 6.9 %shard_map.84 = (f32[256,128]{1,0:T(8,128)}, f32[256,128]{1,0:T(8,128)}, f32[256,128]{1,0:T(8,128)}, f32[256,128]{1,0:T(8,128)}, f32[256,128]{1,0:T(8,128)}, /*i...) custom-call(s32[1]{0:T(128)} %bitcast.place_ref, f32[4,512,256]{2,1,0:T(8,128)} %shard_map.83.early_ref, ...), custom_call_target="tpu_custom_call" | custom-call | tf_op jit(solution)/shard_map/pallas_call | solution.py:161
  38.8 1.5 %collective-permute-start.10 = (f32[256,128]{1,0:T(8,128)}, f32[256,128]{1,0:T(8,128)S(1)}, u32[]{:S(2)}, u32[]{:S(2)}) collective-permute-start(f32[256,128]{1,0:T(8,128)} %get-tuple-element.63), channel_id=1, source_target_pairs={{0,8},{4,12},{8,0},{12,4},{16,24},{20,28},{24,16},{28,20},{1,9},{5... | collective-permute-start | bytes 393224 | tf_op jit(solution)/shard_map/ppermute | solution.py:77
  40.3 1.1 collective-permute-start.11
  41.3 0.0 collective-permute-start.12
  41.3 1.2 collective-permute-start.13
  42.5 0.0 collective-permute-start.7
  42.5 2.1 %collective-permute-done.10.refs_4_ = f32[256,128]{1,0:T(8,128)S(1)} collective-permute-done((f32[256,128]{1,0:T(8,128)}, f32[256,128]{1,0:T(8,128)S(1)}, u32[]{:S(2)}, u32[]{:S(2)}) %collective-permute-start.10) | collective-permute-done | bytes 131104 | tf_op jit(solution)/shard_map/ppermute | solution.py:77
  44.7 2.7 %collective-permute-start.8 = (f32[256,128]{1,0:T(8,128)}, f32[256,128]{1,0:T(8,128)S(1)}, u32[]{:S(2)}, u32[]{:S(2)}) collective-permute-start(f32[256,128]{1,0:T(8,128)} %get-tuple-element.61), channel_id=1, source_target_pairs={{0,24},{4,28},{8,16},{12,20},{16,8},{20,12},{24,0},{28,4},{1,25},{... | collective-permute-start | bytes 393224 | tf_op jit(solution)/shard_map/ppermute | solution.py:77
  47.3 0.0 collective-permute-done.11.refs_5_
  47.3 0.0 collective-permute-start.9
  47.4 0.1 collective-permute-done.12.refs_6_
  47.4 5.5 %collective-permute-done.13.refs_7_ = f32[256,128]{1,0:T(8,128)S(1)} collective-permute-done((f32[256,128]{1,0:T(8,128)}, f32[256,128]{1,0:T(8,128)S(1)}, u32[]{:S(2)}, u32[]{:S(2)}) %collective-permute-start.13) | collective-permute-done | bytes 131104 | tf_op jit(solution)/shard_map/ppermute | solution.py:77
  52.9 0.0 collective-permute-done.7.refs_1_
  52.9 0.0 collective-permute-done.8.refs_2_
  52.9 0.7 collective-permute-done.9.refs_3_
  53.7 0.6 copy-done.14
  54.3 4.1 %shard_map.85 = (bf16[256,1024]{1,0:T(8,128)(2,1)}, f32[256,512]{1,0:T(8,128)}, f32[256,512]{1,0:T(8,128)}) custom-call(s32[1]{0:T(128)} %bitcast.place_ref, bf16[256,1024]{1,0:T(8,128)(2,1)} %q_ref.1, bf16[256,1024]{1,0:T(8,128)(2,1)} %k_ref.1, bf16[256,1024]{1,0:T(8,128)(2,1)} %v_ref.1, f32[1,1024]{1,0:T(1,128)} %bitcast.4, ...), custom_call_target="tpu_custom_call" | custom-call | tf_op jit(solution)/shard_map/pallas_call | solution.py:197
  58.3 3.7 %collective-permute-start.15 = (f32[256,512]{1,0:T(8,128)}, f32[256,512]{1,0:T(8,128)S(1)}, u32[]{:S(2)}, u32[]{:S(2)}) collective-permute-start(f32[256,512]{1,0:T(8,128)} %get-tuple-element.68), channel_id=1, source_target_pairs={{0,1},{3,2},{4,5},{7,6},{8,9},{11,10},{12,13},{15,14},{16,17},{19,... | collective-permute-start | bytes 1572872 | tf_op jit(solution)/shard_map/ppermute | solution.py:226
  62.0 2.1 %collective-permute-start.14 = (f32[256,512]{1,0:T(8,128)}, f32[256,512]{1,0:T(8,128)}, u32[]{:S(2)}, u32[]{:S(2)}) collective-permute-start(f32[256,512]{1,0:T(8,128)} %get-tuple-element.67), channel_id=1, source_target_pairs={{0,1},{3,2},{4,5},{7,6},{8,9},{11,10},{12,13},{15,14},{16,17},{19,... | collective-permute-start | bytes 1572872 | tf_op jit(solution)/shard_map/ppermute | solution.py:226
  64.1 5.9 %fusion.1 = f32[256,4096]{1,0:T(8,128)S(1)} fusion(bf16[256,1024]{1,0:T(8,128)(2,1)} %get-tuple-element.69, bf16[1024,4096]{1,0:T(8,128)(2,1)} %param.13), kind=kOutput, calls=%fused_computation.12 | convolution fusion | flops 2147483648 | bytes 13107200 | tf_op jit(solution)/shard_map/dot_general | solution.py:236
  70.1 4.5 %collective-permute-done.15 = f32[256,512]{1,0:T(8,128)S(1)} collective-permute-done((f32[256,512]{1,0:T(8,128)}, f32[256,512]{1,0:T(8,128)S(1)}, u32[]{:S(2)}, u32[]{:S(2)}) %collective-permute-start.15) | collective-permute-done | bytes 524320 | tf_op jit(solution)/shard_map/ppermute | solution.py:226
  74.5 0.2 dynamic-slice_add_fusion.6
  74.7 4.3 %collective-permute-start.17 = (f32[256,512]{1,0:T(8,128)S(1)}, f32[256,512]{1,0:T(8,128)S(1)}, u32[]{:S(2)}, u32[]{:S(2)}) collective-permute-start(f32[256,512]{1,0:T(8,128)S(1)} %get-tuple-element.76), channel_id=1, source_target_pairs={{0,1},{1,2},{4,5},{5,6},{8,9},{9,10},{12,13},{13,14},{16,17},{17,1... | collective-permute-start | bytes 1572872 | tf_op jit(solution)/shard_map/ppermute | solution.py:217
  79.1 0.7 collective-permute-start.18
  79.8 6.0 %collective-permute-done.14 = f32[256,512]{1,0:T(8,128)} collective-permute-done((f32[256,512]{1,0:T(8,128)}, f32[256,512]{1,0:T(8,128)}, u32[]{:S(2)}, u32[]{:S(2)}) %collective-permute-start.14) | collective-permute-done | bytes 524320 | tf_op jit(solution)/shard_map/ppermute | solution.py:226
  85.8 1.5 %dynamic-slice_add_fusion.4 = (f32[256,512]{1,0:T(8,128)S(1)}, f32[256,512]{1,0:T(8,128)S(1)}) fusion(f32[256,4096]{1,0:T(8,128)} %copy-done, s32[]{:T(128)S(6)} %select_n.70, f32[256,512]{1,0:T(8,128)} %collective-permute-done.14, pred[]{:T(512)S(6)} %eq.13, s32[]{:T(128)S(6)} %select_n.68, pred[]{:T(512)S(6)} %eq.11), kind=kLoop, calls=%fused_computation.6 | loop fusion | flops 524288 | bytes 2621450 | tf_op jit(solution)/shard_map/add | solution.py:245
  87.3 5.2 %collective-permute-start.16 = (f32[256,512]{1,0:T(8,128)S(1)}, f32[256,512]{1,0:T(8,128)}, u32[]{:S(2)}, u32[]{:S(2)}) collective-permute-start(f32[256,512]{1,0:T(8,128)S(1)} %get-tuple-element.73), channel_id=1, source_target_pairs={{0,1},{1,2},{4,5},{5,6},{8,9},{9,10},{12,13},{13,14},{16,17},{17,1... | collective-permute-start | bytes 1572872 | tf_op jit(solution)/shard_map/ppermute | solution.py:217
  92.5 1.5 %collective-permute-start.19 = (f32[256,512]{1,0:T(8,128)S(1)}, f32[256,512]{1,0:T(8,128)}, u32[]{:S(2)}, u32[]{:S(2)}) collective-permute-start(f32[256,512]{1,0:T(8,128)S(1)} %get-tuple-element.80), channel_id=1, source_target_pairs={{2,1},{3,2},{6,5},{7,6},{10,9},{11,10},{14,13},{15,14},{18,17},{19... | collective-permute-start | bytes 1572872 | tf_op jit(solution)/shard_map/ppermute | solution.py:218
  94.0 2.9 %collective-permute-done.17 = f32[256,512]{1,0:T(8,128)S(1)} collective-permute-done((f32[256,512]{1,0:T(8,128)S(1)}, f32[256,512]{1,0:T(8,128)S(1)}, u32[]{:S(2)}, u32[]{:S(2)}) %collective-permute-start.17) | collective-permute-done | bytes 524320 | tf_op jit(solution)/shard_map/ppermute | solution.py:217
  96.9 0.0 collective-permute-done.18
  96.9 1.4 %dynamic-slice_add_fusion.2 = (f32[256,512]{1,0:T(8,128)S(1)}, f32[256,512]{1,0:T(8,128)S(1)}) fusion(f32[256,512]{1,0:T(8,128)S(1)} %collective-permute-done.18, f32[256,4096]{1,0:T(8,128)} %copy-done, s32[]{:T(128)S(6)} %select_n.72, f32[256,512]{1,0:T(8,128)S(1)} %collective-permute-done.17, s32[]{:T(128)S(6)} %select_n.71), kind=kLoop, calls=%fused_computation.4 | loop fusion | flops 262144 | bytes 3145736 | tf_op jit(solution)/shard_map/add | solution.py:245
  98.3 4.4 %collective-permute-start.20 = (f32[256,512]{1,0:T(8,128)S(1)}, f32[256,512]{1,0:T(8,128)S(1)}, u32[]{:S(2)}, u32[]{:S(2)}) collective-permute-start(f32[256,512]{1,0:T(8,128)S(1)} %get-tuple-element.84), channel_id=1, source_target_pairs={{0,1},{1,2},{2,3},{4,5},{5,6},{6,7},{8,9},{9,10},{10,11},{12,13},{... | collective-permute-start | bytes 1572872 | tf_op jit(solution)/shard_map/ppermute | solution.py:217
  102.8 1.3 collective-permute-start.21
  104.1 4.1 %collective-permute-done.16 = f32[256,512]{1,0:T(8,128)} collective-permute-done((f32[256,512]{1,0:T(8,128)S(1)}, f32[256,512]{1,0:T(8,128)}, u32[]{:S(2)}, u32[]{:S(2)}) %collective-permute-start.16) | collective-permute-done | bytes 524320 | tf_op jit(solution)/shard_map/ppermute | solution.py:217
  108.2 1.7 %dynamic-slice_add_fusion = (f32[256,512]{1,0:T(8,128)S(1)}, f32[256,512]{1,0:T(8,128)S(1)}) fusion(f32[256,512]{1,0:T(8,128)} %collective-permute-done.19, f32[256,4096]{1,0:T(8,128)} %copy-done, s32[]{:T(128)S(6)} %select_n.74, f32[256,512]{1,0:T(8,128)} %collective-permute-done.16, s32[]{:T(128)S(6)} %select_n.73), kind=kLoop, calls=%fused_computation.2 | loop fusion | flops 262144 | bytes 3145736 | tf_op jit(solution)/shard_map/add | solution.py:245
  109.9 5.3 %collective-permute-start.22 = (f32[256,512]{1,0:T(8,128)S(1)}, f32[256,512]{1,0:T(8,128)}, u32[]{:S(2)}, u32[]{:S(2)}) collective-permute-start(f32[256,512]{1,0:T(8,128)S(1)} %get-tuple-element.90), channel_id=1, source_target_pairs={{0,1},{1,2},{2,3},{4,5},{5,6},{6,7},{8,9},{9,10},{10,11},{12,13},{... | collective-permute-start | bytes 1572872 | tf_op jit(solution)/shard_map/ppermute | solution.py:217
  115.2 1.3 collective-permute-start.23
  116.5 2.9 %collective-permute-done.20 = f32[256,512]{1,0:T(8,128)S(1)} collective-permute-done((f32[256,512]{1,0:T(8,128)S(1)}, f32[256,512]{1,0:T(8,128)S(1)}, u32[]{:S(2)}, u32[]{:S(2)}) %collective-permute-start.20) | collective-permute-done | bytes 524320 | tf_op jit(solution)/shard_map/ppermute | solution.py:217
  119.4 0.0 collective-permute-done.21
  119.4 1.2 add_convert_fusion.1
  120.5 0.9 dynamic_update_slice.6
  121.4 8.8 %collective-permute-done.22 = f32[256,512]{1,0:T(8,128)} collective-permute-done((f32[256,512]{1,0:T(8,128)S(1)}, f32[256,512]{1,0:T(8,128)}, u32[]{:S(2)}, u32[]{:S(2)}) %collective-permute-start.22) | collective-permute-done | bytes 524320 | tf_op jit(solution)/shard_map/ppermute | solution.py:217
  130.3 0.0 collective-permute-done.23
  130.3 2.2 %fusion = bf16[256,1024]{1,0:T(8,128)(2,1)} fusion(bf16[256,1024]{1,0:T(8,128)(2,1)} %dynamic_update_slice.6, f32[256,512]{1,0:T(8,128)} %collective-permute-done.23, f32[256,512]{1,0:T(8,128)} %collective-permute-done.22, f32[256,4096]{1,0:T(8,128)} %copy-done, s32[]{:T(128)S(6)} %select_n.76), kind=kLoop, calls=%fused_computation.10 | loop fusion | flops 393216 | bytes 1835012 | tf_op jit(solution)/shard_map/dynamic_update_slice | solution.py:251
  (27 shorter events, 0.1 us)
Async XLA Ops:
  2.6 7.3 %collective-permute-start = (f32[256,256]{1,0:T(8,128)}, f32[256,256]{1,0:T(8,128)S(1)}, u32[]{:S(2)}, u32[]{:S(2)}) collective-permute-start(f32[256,256]{1,0:T(8,128)} %get-tuple-element.52), channel_id=1, source_target_pairs={{0,4},{4,0},{8,12},{12,8},{16,20},{20,16},{24,28},{28,24},{1,5},{5... | collective-permute-start | bytes 786440 | tf_op jit(solution)/shard_map/ppermute | solution.py:77
  3.1 11.0 %collective-permute-start.1 = (f32[256,256]{1,0:T(8,128)}, f32[256,256]{1,0:T(8,128)S(1)}, u32[]{:S(2)}, u32[]{:S(2)}) collective-permute-start(f32[256,256]{1,0:T(8,128)} %get-tuple-element.53), channel_id=1, source_target_pairs={{0,24},{4,28},{8,16},{12,20},{16,8},{20,12},{24,0},{28,4},{1,25},{... | collective-permute-start | bytes 786440 | tf_op jit(solution)/shard_map/ppermute | solution.py:77
  6.6 12.6 %collective-permute-start.2 = (f32[256,256]{1,0:T(8,128)}, f32[256,256]{1,0:T(8,128)S(1)}, u32[]{:S(2)}, u32[]{:S(2)}) collective-permute-start(f32[256,256]{1,0:T(8,128)} %get-tuple-element.54), channel_id=1, source_target_pairs={{0,28},{4,24},{8,20},{12,16},{16,12},{20,8},{24,4},{28,0},{1,29},{... | collective-permute-start | bytes 786440 | tf_op jit(solution)/shard_map/ppermute | solution.py:77
  6.7 19.0 %collective-permute-start.3 = (f32[256,256]{1,0:T(8,128)}, f32[256,256]{1,0:T(8,128)S(1)}, u32[]{:S(2)}, u32[]{:S(2)}) collective-permute-start(f32[256,256]{1,0:T(8,128)} %get-tuple-element.55), channel_id=1, source_target_pairs={{0,8},{4,12},{8,0},{12,4},{16,24},{20,28},{24,16},{28,20},{1,9},{5... | collective-permute-start | bytes 786440 | tf_op jit(solution)/shard_map/ppermute | solution.py:77
  8.4 17.4 %collective-permute-start.4 = (f32[256,256]{1,0:T(8,128)}, f32[256,256]{1,0:T(8,128)S(1)}, u32[]{:S(2)}, u32[]{:S(2)}) collective-permute-start(f32[256,256]{1,0:T(8,128)} %get-tuple-element.56), channel_id=1, source_target_pairs={{0,16},{4,20},{8,24},{12,28},{16,0},{20,4},{24,8},{28,12},{1,17},{... | collective-permute-start | bytes 786440 | tf_op jit(solution)/shard_map/ppermute | solution.py:77
  9.9 9.3 %copy-start.5 = (f32[256,256]{1,0:T(8,128)}, f32[256,256]{1,0:T(8,128)S(1)}, u32[]{:S(2)}) copy-start(f32[256,256]{1,0:T(8,128)S(1)} %collective-permute-done.refs_1_) | copy-start | bytes 786436
  9.9 20.6 %collective-permute-start.5 = (f32[256,256]{1,0:T(8,128)}, f32[256,256]{1,0:T(8,128)S(1)}, u32[]{:S(2)}, u32[]{:S(2)}) collective-permute-start(f32[256,256]{1,0:T(8,128)} %get-tuple-element.57), channel_id=1, source_target_pairs={{0,12},{4,8},{8,4},{12,0},{16,28},{20,24},{24,20},{28,16},{1,13},{... | collective-permute-start | bytes 786440 | tf_op jit(solution)/shard_map/ppermute | solution.py:77
  14.1 5.1 %copy-start.6 = (f32[256,256]{1,0:T(8,128)}, f32[256,256]{1,0:T(8,128)S(1)}, u32[]{:S(2)}) copy-start(f32[256,256]{1,0:T(8,128)S(1)} %collective-permute-done.1.refs_2_) | copy-start | bytes 786436
  14.1 16.4 %collective-permute-start.6 = (f32[256,256]{1,0:T(8,128)}, f32[256,256]{1,0:T(8,128)S(1)}, u32[]{:S(2)}, u32[]{:S(2)}) collective-permute-start(f32[256,256]{1,0:T(8,128)} %get-tuple-element.58), channel_id=1, source_target_pairs={{0,20},{4,16},{8,28},{12,24},{16,4},{20,0},{24,12},{28,8},{1,21},{... | collective-permute-start | bytes 786440 | tf_op jit(solution)/shard_map/ppermute | solution.py:77
  19.2 0.7 copy-start.7
  25.7 4.8 %copy-start.1 = (f32[256,256]{1,0:T(8,128)}, f32[256,256]{1,0:T(8,128)S(1)}, u32[]{:S(2)}) copy-start(f32[256,256]{1,0:T(8,128)S(1)} %collective-permute-done.3.refs_0_) | copy-start | bytes 786436
  25.7 4.8 %copy-start.2 = (f32[256,256]{1,0:T(8,128)}, f32[256,256]{1,0:T(8,128)S(1)}, u32[]{:S(2)}) copy-start(f32[256,256]{1,0:T(8,128)S(1)} %collective-permute-done.4.refs_1_) | copy-start | bytes 786436
  30.4 0.7 copy-start.3
  31.1 0.7 copy-start.4
  38.8 5.9 %collective-permute-start.10 = (f32[256,128]{1,0:T(8,128)}, f32[256,128]{1,0:T(8,128)S(1)}, u32[]{:S(2)}, u32[]{:S(2)}) collective-permute-start(f32[256,128]{1,0:T(8,128)} %get-tuple-element.63), channel_id=1, source_target_pairs={{0,8},{4,12},{8,0},{12,4},{16,24},{20,28},{24,16},{28,20},{1,9},{5... | collective-permute-start | bytes 393224 | tf_op jit(solution)/shard_map/ppermute | solution.py:77
  40.3 7.1 %collective-permute-start.11 = (f32[256,128]{1,0:T(8,128)}, f32[256,128]{1,0:T(8,128)S(1)}, u32[]{:S(2)}, u32[]{:S(2)}) collective-permute-start(f32[256,128]{1,0:T(8,128)} %get-tuple-element.64), channel_id=1, source_target_pairs={{0,16},{4,20},{8,24},{12,28},{16,0},{20,4},{24,8},{28,12},{1,17},{... | collective-permute-start | bytes 393224 | tf_op jit(solution)/shard_map/ppermute | solution.py:77
  41.3 6.1 %collective-permute-start.12 = (f32[256,128]{1,0:T(8,128)}, f32[256,128]{1,0:T(8,128)S(1)}, u32[]{:S(2)}, u32[]{:S(2)}) collective-permute-start(f32[256,128]{1,0:T(8,128)} %get-tuple-element.65), channel_id=1, source_target_pairs={{0,12},{4,8},{8,4},{12,0},{16,28},{20,24},{24,20},{28,16},{1,13},{... | collective-permute-start | bytes 393224 | tf_op jit(solution)/shard_map/ppermute | solution.py:77
  41.3 11.5 %collective-permute-start.13 = (f32[256,128]{1,0:T(8,128)}, f32[256,128]{1,0:T(8,128)S(1)}, u32[]{:S(2)}, u32[]{:S(2)}) collective-permute-start(f32[256,128]{1,0:T(8,128)} %get-tuple-element.66), channel_id=1, source_target_pairs={{0,20},{4,16},{8,28},{12,24},{16,4},{20,0},{24,12},{28,8},{1,21},{... | collective-permute-start | bytes 393224 | tf_op jit(solution)/shard_map/ppermute | solution.py:77
  42.5 10.3 %collective-permute-start.7 = (f32[256,128]{1,0:T(8,128)}, f32[256,128]{1,0:T(8,128)S(1)}, u32[]{:S(2)}, u32[]{:S(2)}) collective-permute-start(f32[256,128]{1,0:T(8,128)} %get-tuple-element.60), channel_id=1, source_target_pairs={{0,4},{4,0},{8,12},{12,8},{16,20},{20,16},{24,28},{28,24},{1,5},{5... | collective-permute-start | bytes 393224 | tf_op jit(solution)/shard_map/ppermute | solution.py:77
  44.7 8.9 %copy-start.8 = (f32[256,128]{1,0:T(8,128)}, f32[256,128]{1,0:T(8,128)S(1)}, u32[]{:S(2)}) copy-start(f32[256,128]{1,0:T(8,128)S(1)} %collective-permute-done.10.refs_4_) | copy-start | bytes 393220
  44.7 8.2 %collective-permute-start.8 = (f32[256,128]{1,0:T(8,128)}, f32[256,128]{1,0:T(8,128)S(1)}, u32[]{:S(2)}, u32[]{:S(2)}) collective-permute-start(f32[256,128]{1,0:T(8,128)} %get-tuple-element.61), channel_id=1, source_target_pairs={{0,24},{4,28},{8,16},{12,20},{16,8},{20,12},{24,0},{28,4},{1,25},{... | collective-permute-start | bytes 393224 | tf_op jit(solution)/shard_map/ppermute | solution.py:77
  47.3 6.3 %copy-start.9 = (f32[256,128]{1,0:T(8,128)}, f32[256,128]{1,0:T(8,128)S(1)}, u32[]{:S(2)}) copy-start(f32[256,128]{1,0:T(8,128)S(1)} %collective-permute-done.11.refs_5_) | copy-start | bytes 393220
  47.3 6.3 %collective-permute-start.9 = (f32[256,128]{1,0:T(8,128)}, f32[256,128]{1,0:T(8,128)S(1)}, u32[]{:S(2)}, u32[]{:S(2)}) collective-permute-start(f32[256,128]{1,0:T(8,128)} %get-tuple-element.62), channel_id=1, source_target_pairs={{0,28},{4,24},{8,20},{12,16},{16,12},{20,8},{24,4},{28,0},{1,29},{... | collective-permute-start | bytes 393224 | tf_op jit(solution)/shard_map/ppermute | solution.py:77
  47.4 6.2 %copy-start.10 = (f32[256,128]{1,0:T(8,128)}, f32[256,128]{1,0:T(8,128)S(1)}, u32[]{:S(2)}) copy-start(f32[256,128]{1,0:T(8,128)S(1)} %collective-permute-done.12.refs_6_) | copy-start | bytes 393220
  52.9 0.8 copy-start.11
  52.9 0.8 copy-start.12
  52.9 0.8 copy-start.13
  53.6 0.6 copy-start.14
  58.3 16.2 %collective-permute-start.15 = (f32[256,512]{1,0:T(8,128)}, f32[256,512]{1,0:T(8,128)S(1)}, u32[]{:S(2)}, u32[]{:S(2)}) collective-permute-start(f32[256,512]{1,0:T(8,128)} %get-tuple-element.68), channel_id=1, source_target_pairs={{0,1},{3,2},{4,5},{7,6},{8,9},{11,10},{12,13},{15,14},{16,17},{19,... | collective-permute-start | bytes 1572872 | tf_op jit(solution)/shard_map/ppermute | solution.py:226
  62.0 23.7 %collective-permute-start.14 = (f32[256,512]{1,0:T(8,128)}, f32[256,512]{1,0:T(8,128)}, u32[]{:S(2)}, u32[]{:S(2)}) collective-permute-start(f32[256,512]{1,0:T(8,128)} %get-tuple-element.67), channel_id=1, source_target_pairs={{0,1},{3,2},{4,5},{7,6},{8,9},{11,10},{12,13},{15,14},{16,17},{19,... | collective-permute-start | bytes 1572872 | tf_op jit(solution)/shard_map/ppermute | solution.py:226
  70.1 4.5 %copy-start = (f32[256,4096]{1,0:T(8,128)}, f32[256,4096]{1,0:T(8,128)S(1)}, u32[]{:S(2)}) copy-start(f32[256,4096]{1,0:T(8,128)S(1)} %fusion.1) | copy-start | bytes 12582916
  74.7 22.2 %collective-permute-start.17 = (f32[256,512]{1,0:T(8,128)S(1)}, f32[256,512]{1,0:T(8,128)S(1)}, u32[]{:S(2)}, u32[]{:S(2)}) collective-permute-start(f32[256,512]{1,0:T(8,128)S(1)} %get-tuple-element.76), channel_id=1, source_target_pairs={{0,1},{1,2},{4,5},{5,6},{8,9},{9,10},{12,13},{13,14},{16,17},{17,1... | collective-permute-start | bytes 1572872 | tf_op jit(solution)/shard_map/ppermute | solution.py:217
  79.1 17.9 %collective-permute-start.18 = (f32[256,512]{1,0:T(8,128)S(1)}, f32[256,512]{1,0:T(8,128)S(1)}, u32[]{:S(2)}, u32[]{:S(2)}) collective-permute-start(f32[256,512]{1,0:T(8,128)S(1)} %get-tuple-element.78), channel_id=1, source_target_pairs={{2,1},{3,2},{6,5},{7,6},{10,9},{11,10},{14,13},{15,14},{18,17},{19... | collective-permute-start | bytes 1572872 | tf_op jit(solution)/shard_map/ppermute | solution.py:218
  87.3 20.8 %collective-permute-start.16 = (f32[256,512]{1,0:T(8,128)S(1)}, f32[256,512]{1,0:T(8,128)}, u32[]{:S(2)}, u32[]{:S(2)}) collective-permute-start(f32[256,512]{1,0:T(8,128)S(1)} %get-tuple-element.73), channel_id=1, source_target_pairs={{0,1},{1,2},{4,5},{5,6},{8,9},{9,10},{12,13},{13,14},{16,17},{17,1... | collective-permute-start | bytes 1572872 | tf_op jit(solution)/shard_map/ppermute | solution.py:217
  92.5 15.6 %collective-permute-start.19 = (f32[256,512]{1,0:T(8,128)S(1)}, f32[256,512]{1,0:T(8,128)}, u32[]{:S(2)}, u32[]{:S(2)}) collective-permute-start(f32[256,512]{1,0:T(8,128)S(1)} %get-tuple-element.80), channel_id=1, source_target_pairs={{2,1},{3,2},{6,5},{7,6},{10,9},{11,10},{14,13},{15,14},{18,17},{19... | collective-permute-start | bytes 1572872 | tf_op jit(solution)/shard_map/ppermute | solution.py:218
  98.3 21.1 %collective-permute-start.20 = (f32[256,512]{1,0:T(8,128)S(1)}, f32[256,512]{1,0:T(8,128)S(1)}, u32[]{:S(2)}, u32[]{:S(2)}) collective-permute-start(f32[256,512]{1,0:T(8,128)S(1)} %get-tuple-element.84), channel_id=1, source_target_pairs={{0,1},{1,2},{2,3},{4,5},{5,6},{6,7},{8,9},{9,10},{10,11},{12,13},{... | collective-permute-start | bytes 1572872 | tf_op jit(solution)/shard_map/ppermute | solution.py:217
  102.8 16.6 %collective-permute-start.21 = (f32[256,512]{1,0:T(8,128)S(1)}, f32[256,512]{1,0:T(8,128)S(1)}, u32[]{:S(2)}, u32[]{:S(2)}) collective-permute-start(f32[256,512]{1,0:T(8,128)S(1)} %get-tuple-element.85), channel_id=1, source_target_pairs={{1,0},{2,1},{3,2},{5,4},{6,5},{7,6},{9,8},{10,9},{11,10},{13,12},{... | collective-permute-start | bytes 1572872 | tf_op jit(solution)/shard_map/ppermute | solution.py:218
  109.9 20.4 %collective-permute-start.22 = (f32[256,512]{1,0:T(8,128)S(1)}, f32[256,512]{1,0:T(8,128)}, u32[]{:S(2)}, u32[]{:S(2)}) collective-permute-start(f32[256,512]{1,0:T(8,128)S(1)} %get-tuple-element.90), channel_id=1, source_target_pairs={{0,1},{1,2},{2,3},{4,5},{5,6},{6,7},{8,9},{9,10},{10,11},{12,13},{... | collective-permute-start | bytes 1572872 | tf_op jit(solution)/shard_map/ppermute | solution.py:217
  115.2 15.0 %collective-permute-start.23 = (f32[256,512]{1,0:T(8,128)S(1)}, f32[256,512]{1,0:T(8,128)}, u32[]{:S(2)}, u32[]{:S(2)}) collective-permute-start(f32[256,512]{1,0:T(8,128)S(1)} %get-tuple-element.91), channel_id=1, source_target_pairs={{1,0},{2,1},{3,2},{5,4},{6,5},{7,6},{9,8},{10,9},{11,10},{13,12},{... | collective-permute-start | bytes 1572872 | tf_op jit(solution)/shard_map/ppermute | solution.py:218

commit v2 on v1

--- a/solution.py
+++ b/solution.py
@@ -12,7 +12,14 @@
 
 F32 = jnp.float32
 BF16 = jnp.bfloat16
-VMEM_LIMIT = 56 * 1024 * 1024
+
+
+def room(*shapes):
+    total = 0
+    for shape in shapes:
+        lanes = -(-shape[-1] // 128) * 128
+        total += 4 * lanes * math.prod(shape[:-1])
+    return pltpu.CompilerParams(vmem_limit_bytes=total + total // 4 + 4 * 1024 * 1024)
 
 
 def halves(table):
@@ -63,7 +70,7 @@
         out_specs=[pl.BlockSpec((step, wide), lambda i: (i, 0))] * count,
         out_shape=[jax.ShapeDtypeStruct((rows, wide), F32)] * count,
         scratch_shapes=[pltpu.VMEM((count, step, wide), F32)],
-        compiler_params=pltpu.CompilerParams(vmem_limit_bytes=VMEM_LIMIT),
+        compiler_params=pltpu.CompilerParams(vmem_limit_bytes=56 * 1024 * 1024),
     )(place, keys, values, filt)
 
 
@@ -90,15 +97,17 @@
         in_specs=[whole] * (1 + len(xs)),
         out_specs=whole,
         out_shape=jax.ShapeDtypeStruct((len(xs), 2 * rows, width), F32),
-        compiler_params=pltpu.CompilerParams(vmem_limit_bytes=VMEM_LIMIT),
+        compiler_params=room((len(xs), 2 * rows, width), (len(xs), rows, width), (4 * rows, 3 * rows)),
     )(ahead, *xs)
 
 
 def conv_kernel(place_ref, early_ref, *refs):
     first = early_ref.shape[0]
-    count = (len(refs) - 4 + first) // 2
-    xs, (ahead_ref, back_ref) = refs[: count - first], refs[count - first : count - first + 2]
-    outs, (spec_ref, mix_ref) = refs[count - first + 2 : -2], refs[-2:]
+    count = (len(refs) - 6 + first) // 2
+    xs, (ahead_ref, back_hbm) = refs[: count - first], refs[count - first : count - first + 2]
+    outs, (spec_ref, mix_ref, back_ref, back_sem) = refs[count - first + 2 : -4], refs[-4:]
+    back_in = pltpu.make_async_copy(back_hbm, back_ref, back_sem)
+    back_in.start()
     rows, width = xs[0].shape
     chans = width // 2
     place = place_ref[0]
@@ -118,31 +127,26 @@
     def combine(i, carry):
         real = pl.ds(pl.multiple_of(i * step, step), step)
         imag = pl.ds(pl.multiple_of(rows + i * step, step), step)
-        flt = []
+        sig = [(spec_ref[j, real, :chans], spec_ref[j, imag, :chans]) for j in range(count)]
+        sums = [None] * count
         last = None
+        for lag in range(count):
+            here = (spec_ref[lag, real, chans:], spec_ref[lag, imag, chans:])
+            c, d = here
+            if last is not None:
+                c, d = c - sign * last[1], d + sign * last[0]
+            last = here
+            for j in range(lag, count):
+                a, b = sig[j - lag]
+                re, im = a * c - b * d, a * d + b * c
+                sums[j] = (re, im) if lag == 0 else (sums[j][0] + re, sums[j][1] + im)
         for j in range(count):
-            here = (spec_ref[j, real, chans:], spec_ref[j, imag, chans:])
-            if last is None:
-                flt.append(here)
-            else:
-                flt.append((here[0] - sign * last[1], here[1] + sign * last[0]))
-            last = here
-        sig = [(spec_ref[j, real, :chans], spec_ref[j, imag, :chans]) for j in range(count)]
-        for j in range(count):
-            re = None
-            for s in range(j + 1):
-                a, b = sig[s]
-                c, d = flt[j - s]
-                if re is None:
-                    re, im = a * c - b * d, a * d + b * c
-                else:
-                    re, im = re + (a * c - b * d), im + (a * d + b * c)
-            mix_ref[j, real] = re
-            mix_ref[j, imag] = im
+            mix_ref[j, real], mix_ref[j, imag] = sums[j]
         return carry
 
     lax.fori_loop(0, rows // step, combine, 0)
 
+    back_in.wait()
     for j in range(0, count, 2):
         pair = jnp.concatenate([mix_ref[order[j] ^ place], mix_ref[order[j + 1] ^ place]], axis=1)
         part = jnp.dot(back_ref[...], split3(pair), preferred_element_type=F32)
@@ -160,48 +164,86 @@
     whole = pl.BlockSpec(memory_space=pltpu.VMEM)
     return pl.pallas_call(
         conv_kernel,
-        in_specs=[pl.BlockSpec(memory_space=pltpu.SMEM)] + [whole] * (count - first + 3),
+        in_specs=[pl.BlockSpec(memory_space=pltpu.SMEM)]
+        + [whole] * (count - first + 2)
+        + [pl.BlockSpec(memory_space=pl.ANY)],
         out_specs=[whole] * count,
         out_shape=[jax.ShapeDtypeStruct((rows, chans), F32)] * count,
         scratch_shapes=[
             pltpu.VMEM((count, 2 * rows, width), F32),
             pltpu.VMEM((count, 2 * rows, chans), F32),
+            pltpu.VMEM(back.shape, BF16),
+            pltpu.SemaphoreType.DMA,
         ],
-        compiler_params=pltpu.CompilerParams(vmem_limit_bytes=VMEM_LIMIT),
+        compiler_params=room(
+            *[(count, 2 * rows, width)] * 2, *[(count, 2 * rows, chans)] * 2, (4 * rows, 3 * rows)
+        ),
     )(place, early, *xs[first:], ahead, back)
 
 
 CHAINS = 2
 
 
-def gate_kernel(place_ref, q_ref, k_ref, v_ref, direct_ref, far_ref, *refs):
-    convs, (gated_ref, *firsts), conv_ref = refs[: -2 - CHAINS], refs[-2 - CHAINS : -1], refs[-1]
-    rows, chans = convs[0].shape
-    for turn, ref in zip(turns(len(convs)), convs):
-        conv_ref[turn ^ place_ref[0]] = ref[...]
-    for group in range(len(convs)):
+def gate_kernel(place_ref, direct_ref, q_hbm, k_hbm, v_hbm, far_hbm, *refs):
+    count = len(refs) - 10 - CHAINS
+    convs, gated_hbm, firsts = refs[:count], refs[count], refs[count + 1 : -9]
+    q_ref, k_ref, v_ref, far_ref, conv_ref, gated_ref, first_ref, in_sem, out_sem = refs[-9:]
+    chans = convs[0].shape[1]
+    width = far_ref.shape[1] // CHAINS
+
+    into = [
+        pltpu.make_async_copy(conv, conv_ref.at[turn ^ place_ref[0]], in_sem.at[4 + j])
+        for j, (turn, conv) in enumerate(zip(turns(count), convs))
+    ]
+    pairs = ((q_hbm, q_ref), (k_hbm, k_ref), (v_hbm, v_ref), (far_hbm, far_ref))
+    into += [pltpu.make_async_copy(src, dst, in_sem.at[j]) for j, (src, dst) in enumerate(pairs)]
+    for copy in into:
+        copy.start()
+    for copy in into[:-1]:
+        copy.wait()
+    for group in range(count):
         cols = slice(group * chans, (group + 1) * chans)
         signal = k_ref[:, cols].astype(F32) * v_ref[:, cols].astype(F32)
         inner = conv_ref[group] + direct_ref[:, cols] * signal
         gated_ref[:, cols] = (q_ref[:, cols].astype(F32) * inner).astype(BF16)
-    width = far_ref.shape[1] // CHAINS
+    away = [pltpu.make_async_copy(gated_ref, gated_hbm, out_sem.at[CHAINS])]
+    away[0].start()
+    into[-1].wait()
     for k, out in enumerate(firsts):
         cols = slice(k * width, (k + 1) * width)
-        out[...] = jnp.dot(gated_ref[...], far_ref[:, cols], preferred_element_type=F32)
+        first_ref[k] = jnp.dot(gated_ref[...], far_ref[:, cols], preferred_element_type=F32)
+        away.append(pltpu.make_async_copy(first_ref.at[k], out, out_sem.at[k]))
+        away[-1].start()
+    for copy in away:
+        copy.wait()
 
 
 def gate(place, query, keys, values, direct, far, convs):
     rows, width = query.shape
-    whole = pl.BlockSpec(memory_space=pltpu.VMEM)
-    first = jax.ShapeDtypeStruct((rows, far.shape[1] // CHAINS), F32)
+    count = len(convs)
+    there = pl.BlockSpec(memory_space=pl.ANY)
+    part = (rows, far.shape[1] // CHAINS)
+    blocks = (count,) + convs[0].shape
     out = pl.pallas_call(
         gate_kernel,
-        in_specs=[pl.BlockSpec(memory_space=pltpu.SMEM)] + [whole] * (5 + len(convs)),
-        out_specs=[whole] * (1 + CHAINS),
-        out_shape=[jax.ShapeDtypeStruct((rows, width), BF16)] + [first] * CHAINS,
-        scratch_shapes=[pltpu.VMEM((len(convs),) + convs[0].shape, F32)],
-        compiler_params=pltpu.CompilerParams(vmem_limit_bytes=VMEM_LIMIT),
-    )(place, query, keys, values, direct, far, *convs)
+        in_specs=[pl.BlockSpec(memory_space=pltpu.SMEM), pl.BlockSpec(memory_space=pltpu.VMEM)]
+        + [there] * (4 + count),
+        out_specs=[there] * (1 + CHAINS),
+        out_shape=[jax.ShapeDtypeStruct((rows, width), BF16)]
+        + [jax.ShapeDtypeStruct(part, F32)] * CHAINS,
+        scratch_shapes=[
+            pltpu.VMEM((rows, width), BF16),
+            pltpu.VMEM((rows, width), BF16),
+            pltpu.VMEM((rows, width), BF16),
+            pltpu.VMEM(far.shape, BF16),
+            pltpu.VMEM(blocks, F32),
+            pltpu.VMEM((rows, width), BF16),
+            pltpu.VMEM((CHAINS,) + part, F32),
+            pltpu.SemaphoreType.DMA((4 + count,)),
+            pltpu.SemaphoreType.DMA((CHAINS + 1,)),
+        ],
+        compiler_params=pltpu.CompilerParams(vmem_limit_bytes=56 * 1024 * 1024),
+    )(place, direct, query, keys, values, far, *convs)
     return out[0], out[1:]
 
 

time: 133 us -> 130 us (0.977)
  Pallas kernels: 17.3 us -> 13.2 us
  waiting for transfers between devices: 50 us -> 51.7 us
  local copies, waits for them, and re-layouts: 6.66 us -> 5.28 us
    pallas_call x1, Pallas kernels: 6.9 us -> 3.75 us  [convolve(): pl.pallas_call(conv_kernel, in_specs=[pl.BlockSpec(memory_space=pltpu.SME...]
    ppermute x14, waiting for transfers between devices: 20.7 us -> 22.8 us  [swap(): lax.ppermute(arrays[j], 'ctx', pairs[j])]
    pallas_call x1, Pallas kernels: 3.75 us -> 1.94 us  [forward(): pl.pallas_call(forward_kernel, in_specs=[whole] * (1 + len(xs)), out_spec...]
    unnamed x30 -> x24, local copies, waits for them, and re-layouts: 2.69 us -> 1.29 us
  transfers between devices with their start and end apart: 24 -> 24, of which waited for: 15 -> 14; matrix products, arithmetic and copies ran while one was open for 12% -> 12% of each run, Pallas kernels for 3% -> 1%
where the time goes in v2:
time: 130 us; the launch traced here: 129 us
  waiting for transfers between devices  51.7 us (40%)
  starting transfers between devices  44.8 us (34%)
  Pallas kernels  13.2 us (10%)
  other arithmetic  8.17 us (6%)
  matrix products  5.9 us (5%)
  local copies, waits for them, and re-layouts  5.28 us (4%)
    ppermute x14, waiting for transfers between devices, swap(): lax.ppermute(arrays[j], 'ctx', pairs[j])  22.8 us
    ppermute x4, starting transfers between devices, pass_on(): up = lax.ppermute(up, 'tp', rise)  19.3 us
    ppermute x4, waiting for transfers between devices, pass_on(): up = lax.ppermute(up, 'tp', rise)  18.4 us
    ppermute x14, starting transfers between devices, swap(): lax.ppermute(arrays[j], 'ctx', pairs[j])  15.2 us
    ppermute x2, waiting for transfers between devices, first_step(): got = lax.ppermute(value, 'tp', [(0, 1), (size - 1, size - 2)])  10.5 us
    dot_general x1, matrix products, scatter_dot(): terms = jnp.dot(lhs, rhs, preferred_element_type=F32)  5.9 us
    ppermute x2, starting transfers between devices, first_step(): got = lax.ppermute(value, 'tp', [(0, 1), (size - 1, size - 2)])  5.6 us
    pallas_call x1, Pallas kernels, gate(): pl.pallas_call(gate_kernel, in_specs=[pl.BlockSpec(memory_space=pltpu.SME...  4.86 us
  transfers between devices with their start and end apart: 24, of which 14 were waited for; matrix products, arithmetic and copies ran while one was open for 12% of the time, Pallas kernels for 1%

profile of v2, /device:TPU:0, one launch (start us, length us, event | category | flops | bytes accessed | tf_op | source)
XLA Modules:
  0.0 129.4 jit_solution(14647202222217750938)
XLA Ops:
  0.0 2.7 %shard_map.82 = (f32[256,256]{1,0:T(8,128)}, f32[256,256]{1,0:T(8,128)}, f32[256,256]{1,0:T(8,128)}, f32[256,256]{1,0:T(8,128)}, f32[256,256]{1,0:T(8,128)}, /*i...) custom-call(s32[1]{0:T(128)} %bitcast.place_ref, bf16[256,1024]{1,0:T(8,128)(2,1)} %k_hbm.1, ...), custom_call_target="tpu_custom_call" | custom-call | tf_op jit(solution)/shard_map/pallas_call | solution.py:66
  2.7 0.0 copy-start.1
  2.7 0.5 collective-permute-start
  3.2 3.5 %collective-permute-start.1 = (f32[256,256]{1,0:T(8,128)}, f32[256,256]{1,0:T(8,128)S(1)}, u32[]{:S(2)}, u32[]{:S(2)}) collective-permute-start(f32[256,256]{1,0:T(8,128)} %get-tuple-element.53), channel_id=1, source_target_pairs={{0,24},{4,28},{8,16},{12,20},{16,8},{20,12},{24,0},{28,4},{1,25},{... | collective-permute-start | bytes 786440 | tf_op jit(solution)/shard_map/ppermute | solution.py:84
  6.7 0.1 collective-permute-start.2
  6.8 1.7 %collective-permute-start.3 = (f32[256,256]{1,0:T(8,128)}, f32[256,256]{1,0:T(8,128)S(1)}, u32[]{:S(2)}, u32[]{:S(2)}) collective-permute-start(f32[256,256]{1,0:T(8,128)} %get-tuple-element.55), channel_id=1, source_target_pairs={{0,8},{4,12},{8,0},{12,4},{16,24},{20,28},{24,16},{28,20},{1,9},{5... | collective-permute-start | bytes 786440 | tf_op jit(solution)/shard_map/ppermute | solution.py:84
  8.5 1.5 %collective-permute-start.4 = (f32[256,256]{1,0:T(8,128)}, f32[256,256]{1,0:T(8,128)S(1)}, u32[]{:S(2)}, u32[]{:S(2)}) collective-permute-start(f32[256,256]{1,0:T(8,128)} %get-tuple-element.56), channel_id=1, source_target_pairs={{0,16},{4,20},{8,24},{12,28},{16,0},{20,4},{24,8},{28,12},{1,17},{... | collective-permute-start | bytes 786440 | tf_op jit(solution)/shard_map/ppermute | solution.py:84
  10.0 0.0 collective-permute-done.refs_1_
  10.0 0.0 collective-permute-start.5
  10.0 4.2 %collective-permute-done.1.refs_2_ = f32[256,256]{1,0:T(8,128)S(1)} collective-permute-done((f32[256,256]{1,0:T(8,128)}, f32[256,256]{1,0:T(8,128)S(1)}, u32[]{:S(2)}, u32[]{:S(2)}) %collective-permute-start.1) | collective-permute-done | bytes 262176 | tf_op jit(solution)/shard_map/ppermute | solution.py:84
  14.2 0.7 collective-permute-start.6
  14.9 3.1 %constant_dynamic-slice_fusion.far_hbm = bf16[1024,1024]{1,0:T(8,128)(2,1)} fusion(bf16[1024,4096]{1,0:T(8,128)(2,1)} %param.13, s32[]{:T(128)S(6)} %select_n.61), kind=kLoop, calls=%fused_computation.11 | loop fusion | bytes 4194308 | tf_op jit(solution)/shard_map/dynamic_slice | solution.py:252
  18.0 1.4 %collective-permute-done.2.refs_3_ = f32[256,256]{1,0:T(8,128)} collective-permute-done((f32[256,256]{1,0:T(8,128)}, f32[256,256]{1,0:T(8,128)}, u32[]{:S(2)}, u32[]{:S(2)}) %collective-permute-start.2) | collective-permute-done | bytes 262176 | tf_op jit(solution)/shard_map/ppermute | solution.py:84
  19.4 1.9 %shard_map.83.early_ref = f32[4,512,256]{2,1,0:T(8,128)S(1)} custom-call(bf16[512,768]{1,0:T(8,128)(2,1)S(1)} %copy-done, f32[256,256]{1,0:T(8,128)S(1)} %copy-done.2, f32[256,256]{1,0:T(8,128)S(1)} %collective-permute-done.refs_1_, f32[256,256]{1,0:T(8,128)S(1)} %collective-permute-done.1.refs_2_, f32[256,256]{1,0:T(8,128)} %collective-permute-done.2.refs_3_), custom_call_target="tpu_custom_call" | custom-call | tf_op jit(solution)/shard_map/pallas_call | solution.py:95
  21.4 4.5 %collective-permute-done.3.refs_0_ = f32[256,256]{1,0:T(8,128)S(1)} collective-permute-done((f32[256,256]{1,0:T(8,128)}, f32[256,256]{1,0:T(8,128)S(1)}, u32[]{:S(2)}, u32[]{:S(2)}) %collective-permute-start.3) | collective-permute-done | bytes 262176 | tf_op jit(solution)/shard_map/ppermute | solution.py:84
  25.8 0.0 collective-permute-done.4.refs_1_
  25.9 4.7 %collective-permute-done.5.refs_2_ = f32[256,256]{1,0:T(8,128)S(1)} collective-permute-done((f32[256,256]{1,0:T(8,128)}, f32[256,256]{1,0:T(8,128)S(1)}, u32[]{:S(2)}, u32[]{:S(2)}) %collective-permute-start.5) | collective-permute-done | bytes 262176 | tf_op jit(solution)/shard_map/ppermute | solution.py:84
  30.6 0.1 collective-permute-done.6.refs_3_
  30.6 3.8 %shard_map.84 = (f32[256,128]{1,0:T(8,128)S(1)}, f32[256,128]{1,0:T(8,128)S(1)}, f32[256,128]{1,0:T(8,128)S(1)}, f32[256,128]{1,0:T(8,128)S(1)}, f32[256,128]{1,...) custom-call(s32[1]{0:T(128)} %bitcast.place_ref, ...), custom_call_target="tpu_custom_call" | custom-call | tf_op jit(solution)/shard_map/pallas_call | solution.py:165
  34.4 0.6 copy-done.3
  35.0 1.7 %collective-permute-start.10 = (f32[256,128]{1,0:T(8,128)S(1)}, f32[256,128]{1,0:T(8,128)S(1)}, u32[]{:S(2)}, u32[]{:S(2)}) collective-permute-start(f32[256,128]{1,0:T(8,128)S(1)} %get-tuple-element.63), channel_id=1, source_target_pairs={{0,8},{4,12},{8,0},{12,4},{16,24},{20,28},{24,16},{28,20},{1,9},{5... | collective-permute-start | bytes 393224 | tf_op jit(solution)/shard_map/ppermute | solution.py:84
  36.7 1.5 %collective-permute-start.11 = (f32[256,128]{1,0:T(8,128)S(1)}, f32[256,128]{1,0:T(8,128)S(1)}, u32[]{:S(2)}, u32[]{:S(2)}) collective-permute-start(f32[256,128]{1,0:T(8,128)S(1)} %get-tuple-element.64), channel_id=1, source_target_pairs={{0,16},{4,20},{8,24},{12,28},{16,0},{20,4},{24,8},{28,12},{1,17},{... | collective-permute-start | bytes 393224 | tf_op jit(solution)/shard_map/ppermute | solution.py:84
  38.2 0.0 collective-permute-start.12
  38.2 0.6 collective-permute-start.13
  38.8 0.1 collective-permute-start.7
  38.9 1.8 %collective-permute-done.10.refs_4_ = f32[256,128]{1,0:T(8,128)S(1)} collective-permute-done((f32[256,128]{1,0:T(8,128)S(1)}, f32[256,128]{1,0:T(8,128)S(1)}, u32[]{:S(2)}, u32[]{:S(2)}) %collective-permute-start.10) | collective-permute-done | bytes 131104 | tf_op jit(solution)/shard_map/ppermute | solution.py:84
  40.7 3.4 %collective-permute-start.8 = (f32[256,128]{1,0:T(8,128)S(1)}, f32[256,128]{1,0:T(8,128)S(1)}, u32[]{:S(2)}, u32[]{:S(2)}) collective-permute-start(f32[256,128]{1,0:T(8,128)S(1)} %get-tuple-element.61), channel_id=1, source_target_pairs={{0,24},{4,28},{8,16},{12,20},{16,8},{20,12},{24,0},{28,4},{1,25},{... | collective-permute-start | bytes 393224 | tf_op jit(solution)/shard_map/ppermute | solution.py:84
  44.0 0.0 collective-permute-done.11.refs_5_
  44.0 0.0 collective-permute-start.9
  44.1 0.0 collective-permute-done.12.refs_6_
  44.1 5.4 %collective-permute-done.13.refs_7_ = f32[256,128]{1,0:T(8,128)S(1)} collective-permute-done((f32[256,128]{1,0:T(8,128)S(1)}, f32[256,128]{1,0:T(8,128)S(1)}, u32[]{:S(2)}, u32[]{:S(2)}) %collective-permute-start.13) | collective-permute-done | bytes 131104 | tf_op jit(solution)/shard_map/ppermute | solution.py:84
  49.5 0.0 collective-permute-done.7.refs_1_
  49.5 0.0 collective-permute-done.8.refs_2_
  49.5 0.8 collective-permute-done.9.refs_3_
  50.3 0.6 copy-done.11
  50.9 4.9 %shard_map.85 = (bf16[256,1024]{1,0:T(8,128)(2,1)}, f32[256,512]{1,0:T(8,128)}, f32[256,512]{1,0:T(8,128)}) custom-call(s32[1]{0:T(128)} %bitcast.place_ref, f32[1,1024]{1,0:T(1,128)} %bitcast.4, bf16[256,1024]{1,0:T(8,128)(2,1)} %q_hbm.1, bf16[256,1024]{1,0:T(8,128)(2,1)} %k_hbm.1, bf16[256,1024]{1,0:T(8,128)(2,1)} %v_hbm.1, ...), custom_call_target="tpu_custom_call" | custom-call | tf_op jit(solution)/shard_map/pallas_call | solution.py:227
  55.8 3.5 %collective-permute-start.15 = (f32[256,512]{1,0:T(8,128)}, f32[256,512]{1,0:T(8,128)S(1)}, u32[]{:S(2)}, u32[]{:S(2)}) collective-permute-start(f32[256,512]{1,0:T(8,128)} %get-tuple-element.68), channel_id=1, source_target_pairs={{0,1},{3,2},{4,5},{7,6},{8,9},{11,10},{12,13},{15,14},{16,17},{19,... | collective-permute-start | bytes 1572872 | tf_op jit(solution)/shard_map/ppermute | solution.py:268
  59.3 2.1 %collective-permute-start.14 = (f32[256,512]{1,0:T(8,128)}, f32[256,512]{1,0:T(8,128)}, u32[]{:S(2)}, u32[]{:S(2)}) collective-permute-start(f32[256,512]{1,0:T(8,128)} %get-tuple-element.67), channel_id=1, source_target_pairs={{0,1},{3,2},{4,5},{7,6},{8,9},{11,10},{12,13},{15,14},{16,17},{19,... | collective-permute-start | bytes 1572872 | tf_op jit(solution)/shard_map/ppermute | solution.py:268
  61.4 5.9 %fusion.1 = f32[256,4096]{1,0:T(8,128)S(1)} fusion(bf16[256,1024]{1,0:T(8,128)(2,1)} %get-tuple-element.69, bf16[1024,4096]{1,0:T(8,128)(2,1)} %param.13), kind=kOutput, calls=%fused_computation.12 | convolution fusion | flops 2147483648 | bytes 13107200 | tf_op jit(solution)/shard_map/dot_general | solution.py:278
  67.3 4.5 %collective-permute-done.15 = f32[256,512]{1,0:T(8,128)S(1)} collective-permute-done((f32[256,512]{1,0:T(8,128)}, f32[256,512]{1,0:T(8,128)S(1)}, u32[]{:S(2)}, u32[]{:S(2)}) %collective-permute-start.15) | collective-permute-done | bytes 524320 | tf_op jit(solution)/shard_map/ppermute | solution.py:268
  71.8 0.2 dynamic-slice_add_fusion.6
  72.0 4.3 %collective-permute-start.17 = (f32[256,512]{1,0:T(8,128)S(1)}, f32[256,512]{1,0:T(8,128)S(1)}, u32[]{:S(2)}, u32[]{:S(2)}) collective-permute-start(f32[256,512]{1,0:T(8,128)S(1)} %get-tuple-element.76), channel_id=1, source_target_pairs={{0,1},{1,2},{4,5},{5,6},{8,9},{9,10},{12,13},{13,14},{16,17},{17,1... | collective-permute-start | bytes 1572872 | tf_op jit(solution)/shard_map/ppermute | solution.py:259
  76.3 0.7 collective-permute-start.18
  77.0 6.0 %collective-permute-done.14 = f32[256,512]{1,0:T(8,128)} collective-permute-done((f32[256,512]{1,0:T(8,128)}, f32[256,512]{1,0:T(8,128)}, u32[]{:S(2)}, u32[]{:S(2)}) %collective-permute-start.14) | collective-permute-done | bytes 524320 | tf_op jit(solution)/shard_map/ppermute | solution.py:268
  83.1 1.5 %dynamic-slice_add_fusion.4 = (f32[256,512]{1,0:T(8,128)S(1)}, f32[256,512]{1,0:T(8,128)S(1)}) fusion(f32[256,4096]{1,0:T(8,128)} %copy-done.4, s32[]{:T(128)S(6)} %select_n.70, f32[256,512]{1,0:T(8,128)} %collective-permute-done.14, pred[]{:T(512)S(6)} %eq.13, s32[]{:T(128)S(6)} %select_n.68, pred[]{:T(512)S(6)} %eq.11), kind=kLoop, calls=%fused_computation.6 | loop fusion | flops 524288 | bytes 2621450 | tf_op jit(solution)/shard_map/add | solution.py:287
  84.6 5.2 %collective-permute-start.16 = (f32[256,512]{1,0:T(8,128)S(1)}, f32[256,512]{1,0:T(8,128)}, u32[]{:S(2)}, u32[]{:S(2)}) collective-permute-start(f32[256,512]{1,0:T(8,128)S(1)} %get-tuple-element.73), channel_id=1, source_target_pairs={{0,1},{1,2},{4,5},{5,6},{8,9},{9,10},{12,13},{13,14},{16,17},{17,1... | collective-permute-start | bytes 1572872 | tf_op jit(solution)/shard_map/ppermute | solution.py:259
  89.8 1.5 %collective-permute-start.19 = (f32[256,512]{1,0:T(8,128)S(1)}, f32[256,512]{1,0:T(8,128)}, u32[]{:S(2)}, u32[]{:S(2)}) collective-permute-start(f32[256,512]{1,0:T(8,128)S(1)} %get-tuple-element.80), channel_id=1, source_target_pairs={{2,1},{3,2},{6,5},{7,6},{10,9},{11,10},{14,13},{15,14},{18,17},{19... | collective-permute-start | bytes 1572872 | tf_op jit(solution)/shard_map/ppermute | solution.py:260
  91.3 2.9 %collective-permute-done.17 = f32[256,512]{1,0:T(8,128)S(1)} collective-permute-done((f32[256,512]{1,0:T(8,128)S(1)}, f32[256,512]{1,0:T(8,128)S(1)}, u32[]{:S(2)}, u32[]{:S(2)}) %collective-permute-start.17) | collective-permute-done | bytes 524320 | tf_op jit(solution)/shard_map/ppermute | solution.py:259
  94.2 0.0 collective-permute-done.18
  94.2 1.4 %dynamic-slice_add_fusion.2 = (f32[256,512]{1,0:T(8,128)S(1)}, f32[256,512]{1,0:T(8,128)S(1)}) fusion(f32[256,512]{1,0:T(8,128)S(1)} %collective-permute-done.18, f32[256,4096]{1,0:T(8,128)} %copy-done.4, s32[]{:T(128)S(6)} %select_n.72, f32[256,512]{1,0:T(8,128)S(1)} %collective-permute-done.17, s32[]{:T(128)S(6)} %select_n.71), kind=kLoop, calls=%fused_computation.4 | loop fusion | flops 262144 | bytes 3145736 | tf_op jit(solution)/shard_map/add | solution.py:287
  95.6 4.4 %collective-permute-start.20 = (f32[256,512]{1,0:T(8,128)S(1)}, f32[256,512]{1,0:T(8,128)S(1)}, u32[]{:S(2)}, u32[]{:S(2)}) collective-permute-start(f32[256,512]{1,0:T(8,128)S(1)} %get-tuple-element.84), channel_id=1, source_target_pairs={{0,1},{1,2},{2,3},{4,5},{5,6},{6,7},{8,9},{9,10},{10,11},{12,13},{... | collective-permute-start | bytes 1572872 | tf_op jit(solution)/shard_map/ppermute | solution.py:259
  100.0 1.3 collective-permute-start.21
  101.3 4.1 %collective-permute-done.16 = f32[256,512]{1,0:T(8,128)} collective-permute-done((f32[256,512]{1,0:T(8,128)S(1)}, f32[256,512]{1,0:T(8,128)}, u32[]{:S(2)}, u32[]{:S(2)}) %collective-permute-start.16) | collective-permute-done | bytes 524320 | tf_op jit(solution)/shard_map/ppermute | solution.py:259
  105.4 0.0 collective-permute-done.19
  105.4 1.7 %dynamic-slice_add_fusion = (f32[256,512]{1,0:T(8,128)S(1)}, f32[256,512]{1,0:T(8,128)S(1)}) fusion(f32[256,512]{1,0:T(8,128)} %collective-permute-done.19, f32[256,4096]{1,0:T(8,128)} %copy-done.4, s32[]{:T(128)S(6)} %select_n.74, f32[256,512]{1,0:T(8,128)} %collective-permute-done.16, s32[]{:T(128)S(6)} %select_n.73), kind=kLoop, calls=%fused_computation.2 | loop fusion | flops 262144 | bytes 3145736 | tf_op jit(solution)/shard_map/add | solution.py:287
  107.2 5.3 %collective-permute-start.22 = (f32[256,512]{1,0:T(8,128)S(1)}, f32[256,512]{1,0:T(8,128)}, u32[]{:S(2)}, u32[]{:S(2)}) collective-permute-start(f32[256,512]{1,0:T(8,128)S(1)} %get-tuple-element.90), channel_id=1, source_target_pairs={{0,1},{1,2},{2,3},{4,5},{5,6},{6,7},{8,9},{9,10},{10,11},{12,13},{... | collective-permute-start | bytes 1572872 | tf_op jit(solution)/shard_map/ppermute | solution.py:259
  112.5 1.3 collective-permute-start.23
  113.8 2.9 %collective-permute-done.20 = f32[256,512]{1,0:T(8,128)S(1)} collective-permute-done((f32[256,512]{1,0:T(8,128)S(1)}, f32[256,512]{1,0:T(8,128)S(1)}, u32[]{:S(2)}, u32[]{:S(2)}) %collective-permute-start.20) | collective-permute-done | bytes 524320 | tf_op jit(solution)/shard_map/ppermute | solution.py:259
  116.7 0.0 collective-permute-done.21
  116.7 1.2 add_convert_fusion.1
  117.8 0.9 dynamic_update_slice.6
  118.7 8.5 %collective-permute-done.22 = f32[256,512]{1,0:T(8,128)} collective-permute-done((f32[256,512]{1,0:T(8,128)S(1)}, f32[256,512]{1,0:T(8,128)}, u32[]{:S(2)}, u32[]{:S(2)}) %collective-permute-start.22) | collective-permute-done | bytes 524320 | tf_op jit(solution)/shard_map/ppermute | solution.py:259
  127.2 0.0 collective-permute-done.23
  127.2 2.2 %fusion = bf16[256,1024]{1,0:T(8,128)(2,1)} fusion(bf16[256,1024]{1,0:T(8,128)(2,1)} %dynamic_update_slice.6, f32[256,512]{1,0:T(8,128)} %collective-permute-done.23, f32[256,512]{1,0:T(8,128)} %collective-permute-done.22, f32[256,4096]{1,0:T(8,128)} %copy-done.4, s32[]{:T(128)S(6)} %select_n.76), kind=kLoop, calls=%fused_computation.10 | loop fusion | flops 393216 | bytes 1835012 | tf_op jit(solution)/shard_map/dynamic_update_slice | solution.py:293
  (21 shorter events, 0.0 us)
Async XLA Ops:
  0.0 19.4 %copy-start = (bf16[512,768]{1,0:T(8,128)(2,1)S(1)}, bf16[512,768]{1,0:T(8,128)(2,1)}, u32[]{:S(2)}) copy-start(bf16[512,768]{1,0:T(8,128)(2,1)} %constant.47.clone.ahead_ref.refs_4_) | copy-start | bytes 2359300
  2.7 16.7 %copy-start.2 = (f32[256,256]{1,0:T(8,128)S(1)}, f32[256,256]{1,0:T(8,128)}, u32[]{:S(2)}) copy-start(f32[256,256]{1,0:T(8,128)} %get-tuple-element.51.refs_0_) | copy-start | bytes 786436
  2.7 27.9 %copy-start.1 = (bf16[256,1536]{1,0:T(8,128)(2,1)S(1)}, bf16[256,1536]{1,0:T(8,128)(2,1)}, u32[]{:S(2)}) copy-start(bf16[256,1536]{1,0:T(8,128)(2,1)} %constant.48.clone.refs_5_) | copy-start | bytes 2359300
  2.7 7.3 %collective-permute-start = (f32[256,256]{1,0:T(8,128)}, f32[256,256]{1,0:T(8,128)S(1)}, u32[]{:S(2)}, u32[]{:S(2)}) collective-permute-start(f32[256,256]{1,0:T(8,128)} %get-tuple-element.52), channel_id=1, source_target_pairs={{0,4},{4,0},{8,12},{12,8},{16,20},{20,16},{24,28},{28,24},{1,5},{5... | collective-permute-start | bytes 786440 | tf_op jit(solution)/shard_map/ppermute | solution.py:84
  3.2 11.0 %collective-permute-start.1 = (f32[256,256]{1,0:T(8,128)}, f32[256,256]{1,0:T(8,128)S(1)}, u32[]{:S(2)}, u32[]{:S(2)}) collective-permute-start(f32[256,256]{1,0:T(8,128)} %get-tuple-element.53), channel_id=1, source_target_pairs={{0,24},{4,28},{8,16},{12,20},{16,8},{20,12},{24,0},{28,4},{1,25},{... | collective-permute-start | bytes 786440 | tf_op jit(solution)/shard_map/ppermute | solution.py:84
  6.7 12.7 %collective-permute-start.2 = (f32[256,256]{1,0:T(8,128)}, f32[256,256]{1,0:T(8,128)}, u32[]{:S(2)}, u32[]{:S(2)}) collective-permute-start(f32[256,256]{1,0:T(8,128)} %get-tuple-element.54), channel_id=1, source_target_pairs={{0,28},{4,24},{8,20},{12,16},{16,12},{20,8},{24,4},{28,0},{1,29},{... | collective-permute-start | bytes 786440 | tf_op jit(solution)/shard_map/ppermute | solution.py:84
  6.8 19.0 %collective-permute-start.3 = (f32[256,256]{1,0:T(8,128)}, f32[256,256]{1,0:T(8,128)S(1)}, u32[]{:S(2)}, u32[]{:S(2)}) collective-permute-start(f32[256,256]{1,0:T(8,128)} %get-tuple-element.55), channel_id=1, source_target_pairs={{0,8},{4,12},{8,0},{12,4},{16,24},{20,28},{24,16},{28,20},{1,9},{5... | collective-permute-start | bytes 786440 | tf_op jit(solution)/shard_map/ppermute | solution.py:84
  8.5 17.4 %collective-permute-start.4 = (f32[256,256]{1,0:T(8,128)}, f32[256,256]{1,0:T(8,128)S(1)}, u32[]{:S(2)}, u32[]{:S(2)}) collective-permute-start(f32[256,256]{1,0:T(8,128)} %get-tuple-element.56), channel_id=1, source_target_pairs={{0,16},{4,20},{8,24},{12,28},{16,0},{20,4},{24,8},{28,12},{1,17},{... | collective-permute-start | bytes 786440 | tf_op jit(solution)/shard_map/ppermute | solution.py:84
  10.0 20.6 %collective-permute-start.5 = (f32[256,256]{1,0:T(8,128)}, f32[256,256]{1,0:T(8,128)S(1)}, u32[]{:S(2)}, u32[]{:S(2)}) collective-permute-start(f32[256,256]{1,0:T(8,128)} %get-tuple-element.57), channel_id=1, source_target_pairs={{0,12},{4,8},{8,4},{12,0},{16,28},{20,24},{24,20},{28,16},{1,13},{... | collective-permute-start | bytes 786440 | tf_op jit(solution)/shard_map/ppermute | solution.py:84
  14.2 16.4 %collective-permute-start.6 = (f32[256,256]{1,0:T(8,128)}, f32[256,256]{1,0:T(8,128)S(1)}, u32[]{:S(2)}, u32[]{:S(2)}) collective-permute-start(f32[256,256]{1,0:T(8,128)} %get-tuple-element.58), channel_id=1, source_target_pairs={{0,20},{4,16},{8,28},{12,24},{16,4},{20,0},{24,12},{28,8},{1,21},{... | collective-permute-start | bytes 786440 | tf_op jit(solution)/shard_map/ppermute | solution.py:84
  34.4 0.7 copy-start.3
  35.0 5.6 %collective-permute-start.10 = (f32[256,128]{1,0:T(8,128)S(1)}, f32[256,128]{1,0:T(8,128)S(1)}, u32[]{:S(2)}, u32[]{:S(2)}) collective-permute-start(f32[256,128]{1,0:T(8,128)S(1)} %get-tuple-element.63), channel_id=1, source_target_pairs={{0,8},{4,12},{8,0},{12,4},{16,24},{20,28},{24,16},{28,20},{1,9},{5... | collective-permute-start | bytes 393224 | tf_op jit(solution)/shard_map/ppermute | solution.py:84
  36.7 7.3 %collective-permute-start.11 = (f32[256,128]{1,0:T(8,128)S(1)}, f32[256,128]{1,0:T(8,128)S(1)}, u32[]{:S(2)}, u32[]{:S(2)}) collective-permute-start(f32[256,128]{1,0:T(8,128)S(1)} %get-tuple-element.64), channel_id=1, source_target_pairs={{0,16},{4,20},{8,24},{12,28},{16,0},{20,4},{24,8},{28,12},{1,17},{... | collective-permute-start | bytes 393224 | tf_op jit(solution)/shard_map/ppermute | solution.py:84
  38.2 5.8 %collective-permute-start.12 = (f32[256,128]{1,0:T(8,128)S(1)}, f32[256,128]{1,0:T(8,128)S(1)}, u32[]{:S(2)}, u32[]{:S(2)}) collective-permute-start(f32[256,128]{1,0:T(8,128)S(1)} %get-tuple-element.65), channel_id=1, source_target_pairs={{0,12},{4,8},{8,4},{12,0},{16,28},{20,24},{24,20},{28,16},{1,13},{... | collective-permute-start | bytes 393224 | tf_op jit(solution)/shard_map/ppermute | solution.py:84
  38.2 11.2 %collective-permute-start.13 = (f32[256,128]{1,0:T(8,128)S(1)}, f32[256,128]{1,0:T(8,128)S(1)}, u32[]{:S(2)}, u32[]{:S(2)}) collective-permute-start(f32[256,128]{1,0:T(8,128)S(1)} %get-tuple-element.66), channel_id=1, source_target_pairs={{0,20},{4,16},{8,28},{12,24},{16,4},{20,0},{24,12},{28,8},{1,21},{... | collective-permute-start | bytes 393224 | tf_op jit(solution)/shard_map/ppermute | solution.py:84
  38.8 10.7 %collective-permute-start.7 = (f32[256,128]{1,0:T(8,128)S(1)}, f32[256,128]{1,0:T(8,128)S(1)}, u32[]{:S(2)}, u32[]{:S(2)}) collective-permute-start(f32[256,128]{1,0:T(8,128)S(1)} %get-tuple-element.60), channel_id=1, source_target_pairs={{0,4},{4,0},{8,12},{12,8},{16,20},{20,16},{24,28},{28,24},{1,5},{5... | collective-permute-start | bytes 393224 | tf_op jit(solution)/shard_map/ppermute | solution.py:84
  40.7 9.6 %copy-start.5 = (f32[256,128]{1,0:T(8,128)}, f32[256,128]{1,0:T(8,128)S(1)}, u32[]{:S(2)}) copy-start(f32[256,128]{1,0:T(8,128)S(1)} %collective-permute-done.10.refs_4_) | copy-start | bytes 393220
  40.7 8.8 %collective-permute-start.8 = (f32[256,128]{1,0:T(8,128)S(1)}, f32[256,128]{1,0:T(8,128)S(1)}, u32[]{:S(2)}, u32[]{:S(2)}) collective-permute-start(f32[256,128]{1,0:T(8,128)S(1)} %get-tuple-element.61), channel_id=1, source_target_pairs={{0,24},{4,28},{8,16},{12,20},{16,8},{20,12},{24,0},{28,4},{1,25},{... | collective-permute-start | bytes 393224 | tf_op jit(solution)/shard_map/ppermute | solution.py:84
  44.0 6.2 %copy-start.6 = (f32[256,128]{1,0:T(8,128)}, f32[256,128]{1,0:T(8,128)S(1)}, u32[]{:S(2)}) copy-start(f32[256,128]{1,0:T(8,128)S(1)} %collective-permute-done.11.refs_5_) | copy-start | bytes 393220
  44.0 6.2 %collective-permute-start.9 = (f32[256,128]{1,0:T(8,128)S(1)}, f32[256,128]{1,0:T(8,128)S(1)}, u32[]{:S(2)}, u32[]{:S(2)}) collective-permute-start(f32[256,128]{1,0:T(8,128)S(1)} %get-tuple-element.62), channel_id=1, source_target_pairs={{0,28},{4,24},{8,20},{12,16},{16,12},{20,8},{24,4},{28,0},{1,29},{... | collective-permute-start | bytes 393224 | tf_op jit(solution)/shard_map/ppermute | solution.py:84
  44.1 6.2 %copy-start.7 = (f32[256,128]{1,0:T(8,128)}, f32[256,128]{1,0:T(8,128)S(1)}, u32[]{:S(2)}) copy-start(f32[256,128]{1,0:T(8,128)S(1)} %collective-permute-done.12.refs_6_) | copy-start | bytes 393220
  49.5 0.8 copy-start.8
  49.5 0.8 copy-start.9
  49.5 0.8 copy-start.10
  50.3 0.6 copy-start.11
  55.8 16.1 %collective-permute-start.15 = (f32[256,512]{1,0:T(8,128)}, f32[256,512]{1,0:T(8,128)S(1)}, u32[]{:S(2)}, u32[]{:S(2)}) collective-permute-start(f32[256,512]{1,0:T(8,128)} %get-tuple-element.68), channel_id=1, source_target_pairs={{0,1},{3,2},{4,5},{7,6},{8,9},{11,10},{12,13},{15,14},{16,17},{19,... | collective-permute-start | bytes 1572872 | tf_op jit(solution)/shard_map/ppermute | solution.py:268
  59.3 23.8 %collective-permute-start.14 = (f32[256,512]{1,0:T(8,128)}, f32[256,512]{1,0:T(8,128)}, u32[]{:S(2)}, u32[]{:S(2)}) collective-permute-start(f32[256,512]{1,0:T(8,128)} %get-tuple-element.67), channel_id=1, source_target_pairs={{0,1},{3,2},{4,5},{7,6},{8,9},{11,10},{12,13},{15,14},{16,17},{19,... | collective-permute-start | bytes 1572872 | tf_op jit(solution)/shard_map/ppermute | solution.py:268
  67.3 4.5 %copy-start.4 = (f32[256,4096]{1,0:T(8,128)}, f32[256,4096]{1,0:T(8,128)S(1)}, u32[]{:S(2)}) copy-start(f32[256,4096]{1,0:T(8,128)S(1)} %fusion.1) | copy-start | bytes 12582916
  72.0 22.2 %collective-permute-start.17 = (f32[256,512]{1,0:T(8,128)S(1)}, f32[256,512]{1,0:T(8,128)S(1)}, u32[]{:S(2)}, u32[]{:S(2)}) collective-permute-start(f32[256,512]{1,0:T(8,128)S(1)} %get-tuple-element.76), channel_id=1, source_target_pairs={{0,1},{1,2},{4,5},{5,6},{8,9},{9,10},{12,13},{13,14},{16,17},{17,1... | collective-permute-start | bytes 1572872 | tf_op jit(solution)/shard_map/ppermute | solution.py:259
  76.3 17.9 %collective-permute-start.18 = (f32[256,512]{1,0:T(8,128)S(1)}, f32[256,512]{1,0:T(8,128)S(1)}, u32[]{:S(2)}, u32[]{:S(2)}) collective-permute-start(f32[256,512]{1,0:T(8,128)S(1)} %get-tuple-element.78), channel_id=1, source_target_pairs={{2,1},{3,2},{6,5},{7,6},{10,9},{11,10},{14,13},{15,14},{18,17},{19... | collective-permute-start | bytes 1572872 | tf_op jit(solution)/shard_map/ppermute | solution.py:260
  84.6 20.8 %collective-permute-start.16 = (f32[256,512]{1,0:T(8,128)S(1)}, f32[256,512]{1,0:T(8,128)}, u32[]{:S(2)}, u32[]{:S(2)}) collective-permute-start(f32[256,512]{1,0:T(8,128)S(1)} %get-tuple-element.73), channel_id=1, source_target_pairs={{0,1},{1,2},{4,5},{5,6},{8,9},{9,10},{12,13},{13,14},{16,17},{17,1... | collective-permute-start | bytes 1572872 | tf_op jit(solution)/shard_map/ppermute | solution.py:259
  89.8 15.6 %collective-permute-start.19 = (f32[256,512]{1,0:T(8,128)S(1)}, f32[256,512]{1,0:T(8,128)}, u32[]{:S(2)}, u32[]{:S(2)}) collective-permute-start(f32[256,512]{1,0:T(8,128)S(1)} %get-tuple-element.80), channel_id=1, source_target_pairs={{2,1},{3,2},{6,5},{7,6},{10,9},{11,10},{14,13},{15,14},{18,17},{19... | collective-permute-start | bytes 1572872 | tf_op jit(solution)/shard_map/ppermute | solution.py:260
  95.6 21.1 %collective-permute-start.20 = (f32[256,512]{1,0:T(8,128)S(1)}, f32[256,512]{1,0:T(8,128)S(1)}, u32[]{:S(2)}, u32[]{:S(2)}) collective-permute-start(f32[256,512]{1,0:T(8,128)S(1)} %get-tuple-element.84), channel_id=1, source_target_pairs={{0,1},{1,2},{2,3},{4,5},{5,6},{6,7},{8,9},{9,10},{10,11},{12,13},{... | collective-permute-start | bytes 1572872 | tf_op jit(solution)/shard_map/ppermute | solution.py:259
  100.0 16.6 %collective-permute-start.21 = (f32[256,512]{1,0:T(8,128)S(1)}, f32[256,512]{1,0:T(8,128)S(1)}, u32[]{:S(2)}, u32[]{:S(2)}) collective-permute-start(f32[256,512]{1,0:T(8,128)S(1)} %get-tuple-element.85), channel_id=1, source_target_pairs={{1,0},{2,1},{3,2},{5,4},{6,5},{7,6},{9,8},{10,9},{11,10},{13,12},{... | collective-permute-start | bytes 1572872 | tf_op jit(solution)/shard_map/ppermute | solution.py:260
  107.2 20.0 %collective-permute-start.22 = (f32[256,512]{1,0:T(8,128)S(1)}, f32[256,512]{1,0:T(8,128)}, u32[]{:S(2)}, u32[]{:S(2)}) collective-permute-start(f32[256,512]{1,0:T(8,128)S(1)} %get-tuple-element.90), channel_id=1, source_target_pairs={{0,1},{1,2},{2,3},{4,5},{5,6},{6,7},{8,9},{9,10},{10,11},{12,13},{... | collective-permute-start | bytes 1572872 | tf_op jit(solution)/shard_map/ppermute | solution.py:259
  112.5 14.7 %collective-permute-start.23 = (f32[256,512]{1,0:T(8,128)S(1)}, f32[256,512]{1,0:T(8,128)}, u32[]{:S(2)}, u32[]{:S(2)}) collective-permute-start(f32[256,512]{1,0:T(8,128)S(1)} %get-tuple-element.91), channel_id=1, source_target_pairs={{1,0},{2,1},{3,2},{5,4},{6,5},{7,6},{9,8},{10,9},{11,10},{13,12},{... | collective-permute-start | bytes 1572872 | tf_op jit(solution)/shard_map/ppermute | solution.py:260

commit v3 on v2

--- a/solution.py
+++ b/solution.py
@@ -46,19 +46,23 @@
     return jnp.concatenate([high, low, high], axis=0)
 
 
-def pack_kernel(place_ref, keys_ref, values_ref, filt_ref, *refs):
+def pack_kernel(place_ref, keys_ref, values_ref, filt_ref, direct_ref, *refs):
     outs, turned_ref = refs[:-1], refs[-1]
     chans = keys_ref.shape[1] // len(outs)
+    origin = jnp.logical_and(place_ref[0] == 0, pl.program_id(0) == 0)
+    rows = lax.broadcasted_iota(jnp.int32, (8, chans), 0)
     for group in range(len(outs)):
         cols = slice(group * chans, (group + 1) * chans)
         slot = group ^ place_ref[0]
         turned_ref[slot, :, :chans] = keys_ref[:, cols].astype(F32) * values_ref[:, cols].astype(F32)
         turned_ref[slot, :, chans:] = filt_ref[:, cols]
+        here = jnp.where(jnp.logical_and(rows == 0, origin), direct_ref[:, cols], 0.0)
+        turned_ref[slot, :8, chans:] = filt_ref[:8, cols] + here
     for turn, out in zip(turns(len(outs)), outs):
         out[...] = turned_ref[turn]
 
 
-def pack(place, keys, values, filt, count):
+def pack(place, keys, values, filt, direct, count):
     rows, width = keys.shape
     step = math.gcd(rows, 128)
     spec = pl.BlockSpec((step, width), lambda i: (i, 0))
@@ -66,12 +70,13 @@
     return pl.pallas_call(
         pack_kernel,
         grid=(rows // step,),
-        in_specs=[pl.BlockSpec(memory_space=pltpu.SMEM), spec, spec, spec],
+        in_specs=[pl.BlockSpec(memory_space=pltpu.SMEM), spec, spec, spec]
+        + [pl.BlockSpec((1, width), lambda i: (0, 0))],
         out_specs=[pl.BlockSpec((step, wide), lambda i: (i, 0))] * count,
         out_shape=[jax.ShapeDtypeStruct((rows, wide), F32)] * count,
         scratch_shapes=[pltpu.VMEM((count, step, wide), F32)],
         compiler_params=pltpu.CompilerParams(vmem_limit_bytes=56 * 1024 * 1024),
-    )(place, keys, values, filt)
+    )(place, keys, values, filt, direct)
 
 
 def turns(count):
@@ -176,7 +181,7 @@
             pltpu.SemaphoreType.DMA,
         ],
         compiler_params=room(
-            *[(count, 2 * rows, width)] * 2, *[(count, 2 * rows, chans)] * 2, (4 * rows, 3 * rows)
+            (count, 2 * rows, width), *[(count, 2 * rows, chans)] * 2, (count, rows, width)
         ),
     )(place, early, *xs[first:], ahead, back)
 
@@ -184,66 +189,48 @@
 CHAINS = 2
 
 
-def gate_kernel(place_ref, direct_ref, q_hbm, k_hbm, v_hbm, far_hbm, *refs):
-    count = len(refs) - 10 - CHAINS
-    convs, gated_hbm, firsts = refs[:count], refs[count], refs[count + 1 : -9]
-    q_ref, k_ref, v_ref, far_ref, conv_ref, gated_ref, first_ref, in_sem, out_sem = refs[-9:]
+def gate_kernel(place_ref, far_ref, q_hbm, *refs):
+    count = len(refs) - 4 - CHAINS
+    convs, (gated_ref, *firsts), (q_ref, conv_ref, in_sem) = refs[:count], refs[count:-3], refs[-3:]
     chans = convs[0].shape[1]
     width = far_ref.shape[1] // CHAINS
-
-    into = [
-        pltpu.make_async_copy(conv, conv_ref.at[turn ^ place_ref[0]], in_sem.at[4 + j])
+    into = [pltpu.make_async_copy(q_hbm, q_ref, in_sem.at[count])]
+    into += [
+        pltpu.make_async_copy(conv, conv_ref.at[turn ^ place_ref[0]], in_sem.at[j])
         for j, (turn, conv) in enumerate(zip(turns(count), convs))
     ]
-    pairs = ((q_hbm, q_ref), (k_hbm, k_ref), (v_hbm, v_ref), (far_hbm, far_ref))
-    into += [pltpu.make_async_copy(src, dst, in_sem.at[j]) for j, (src, dst) in enumerate(pairs)]
     for copy in into:
         copy.start()
-    for copy in into[:-1]:
+    for copy in into:
         copy.wait()
     for group in range(count):
         cols = slice(group * chans, (group + 1) * chans)
-        signal = k_ref[:, cols].astype(F32) * v_ref[:, cols].astype(F32)
-        inner = conv_ref[group] + direct_ref[:, cols] * signal
-        gated_ref[:, cols] = (q_ref[:, cols].astype(F32) * inner).astype(BF16)
-    away = [pltpu.make_async_copy(gated_ref, gated_hbm, out_sem.at[CHAINS])]
-    away[0].start()
-    into[-1].wait()
+        gated_ref[:, cols] = (q_ref[:, cols].astype(F32) * conv_ref[group]).astype(BF16)
     for k, out in enumerate(firsts):
         cols = slice(k * width, (k + 1) * width)
-        first_ref[k] = jnp.dot(gated_ref[...], far_ref[:, cols], preferred_element_type=F32)
-        away.append(pltpu.make_async_copy(first_ref.at[k], out, out_sem.at[k]))
-        away[-1].start()
-    for copy in away:
-        copy.wait()
-
-
-def gate(place, query, keys, values, direct, far, convs):
+        out[...] = jnp.dot(gated_ref[...], far_ref[:, cols], preferred_element_type=F32)
+
+
+def gate(place, query, far, convs):
     rows, width = query.shape
     count = len(convs)
+    here = pl.BlockSpec(memory_space=pltpu.VMEM)
     there = pl.BlockSpec(memory_space=pl.ANY)
     part = (rows, far.shape[1] // CHAINS)
     blocks = (count,) + convs[0].shape
     out = pl.pallas_call(
         gate_kernel,
-        in_specs=[pl.BlockSpec(memory_space=pltpu.SMEM), pl.BlockSpec(memory_space=pltpu.VMEM)]
-        + [there] * (4 + count),
-        out_specs=[there] * (1 + CHAINS),
+        in_specs=[pl.BlockSpec(memory_space=pltpu.SMEM), here] + [there] * (1 + count),
+        out_specs=[here] * (1 + CHAINS),
         out_shape=[jax.ShapeDtypeStruct((rows, width), BF16)]
         + [jax.ShapeDtypeStruct(part, F32)] * CHAINS,
         scratch_shapes=[
             pltpu.VMEM((rows, width), BF16),
-            pltpu.VMEM((rows, width), BF16),
-            pltpu.VMEM((rows, width), BF16),
-            pltpu.VMEM(far.shape, BF16),
             pltpu.VMEM(blocks, F32),
-            pltpu.VMEM((rows, width), BF16),
-            pltpu.VMEM((CHAINS,) + part, F32),
-            pltpu.SemaphoreType.DMA((4 + count,)),
-            pltpu.SemaphoreType.DMA((CHAINS + 1,)),
+            pltpu.SemaphoreType.DMA((count + 1,)),
         ],
-        compiler_params=pltpu.CompilerParams(vmem_limit_bytes=56 * 1024 * 1024),
-    )(place, direct, query, keys, values, far, *convs)
+        compiler_params=room(*[(rows, width)] * 2, far.shape, blocks, (CHAINS,) + part),
+    )(place, far, query, *convs)
     return out[0], out[1:]
 
 
@@ -299,11 +286,11 @@
     count = lax.axis_size("ctx")
     size = lax.axis_size("tp")
     place = lax.axis_index("ctx").reshape(1)
-    xs = swap(pack(place, keys, values, filt, count))
+    xs = swap(pack(place, keys, values, filt, direct.reshape(1, -1), count))
     far = column_block(w_out, jnp.where(lax.axis_index("tp") == 0, size - 1, 0), size)
     xs[0], far = lax.optimization_barrier((xs[0], far))
     convs = swap(convolve(place, xs))
-    gated, first = gate(place, query, keys, values, direct.reshape(1, -1), far, convs)
+    gated, first = gate(place, query, far, convs)
     return scatter_dot(gated, w_out, first)
 
 

time: 130 us -> 130 us (level)
    pallas_call x1, Pallas kernels: 3.75 us -> 5.61 us  [convolve(): pl.pallas_call(conv_kernel, in_specs=[pl.BlockSpec(memory_space=pltpu.SME...]
    pallas_call x1, Pallas kernels: 4.86 us -> 3.07 us  [gate(): pl.pallas_call(gate_kernel, in_specs=[pl.BlockSpec(memory_space=pltpu.SME...]
  transfers between devices with their start and end apart: 24 -> 24, of which waited for: 14 -> 14; matrix products, arithmetic and copies ran while one was open for 12% -> 11% of each run, Pallas kernels for 1% -> 2%
where the time goes in v3:
time: 130 us; the launch traced here: 129 us
  waiting for transfers between devices  51.6 us (40%)
  starting transfers between devices  45 us (35%)
  Pallas kernels  13.3 us (10%)
  other arithmetic  8.17 us (6%)
  matrix products  5.73 us (4%)
  local copies, waits for them, and re-layouts  5.24 us (4%)
    ppermute x14, waiting for transfers between devices, swap(): lax.ppermute(arrays[j], 'ctx', pairs[j])  22.9 us
    ppermute x4, starting transfers between devices, pass_on(): up = lax.ppermute(up, 'tp', rise)  19.4 us
    ppermute x4, waiting for transfers between devices, pass_on(): up = lax.ppermute(up, 'tp', rise)  18.3 us
    ppermute x14, starting transfers between devices, swap(): lax.ppermute(arrays[j], 'ctx', pairs[j])  15.3 us
    ppermute x2, waiting for transfers between devices, first_step(): got = lax.ppermute(value, 'tp', [(0, 1), (size - 1, size - 2)])  10.4 us
    dot_general x1, matrix products, scatter_dot(): terms = jnp.dot(lhs, rhs, preferred_element_type=F32)  5.73 us
    ppermute x2, starting transfers between devices, first_step(): got = lax.ppermute(value, 'tp', [(0, 1), (size - 1, size - 2)])  5.61 us
    pallas_call x1, Pallas kernels, convolve(): pl.pallas_call(conv_kernel, in_specs=[pl.BlockSpec(memory_space=pltpu.SME...  5.61 us
  transfers between devices with their start and end apart: 24, of which 14 were waited for; matrix products, arithmetic and copies ran while one was open for 11% of the time, Pallas kernels for 2%

profile of v3, /device:TPU:0, one launch (start us, length us, event | category | flops | bytes accessed | tf_op | source)
XLA Modules:
  0.0 129.2 jit_solution(1037050327294725219)
XLA Ops:
  0.0 2.7 %shard_map.82 = (f32[256,256]{1,0:T(8,128)}, f32[256,256]{1,0:T(8,128)}, f32[256,256]{1,0:T(8,128)}, f32[256,256]{1,0:T(8,128)}, f32[256,256]{1,0:T(8,128)}, /*i...) custom-call(s32[1]{0:T(128)} %bitcast.place_ref, bf16[256,1024]{1,0:T(8,128)(2,1)} %keys_ref.1, ...), custom_call_target="tpu_custom_call" | custom-call | tf_op jit(solution)/shard_map/pallas_call | solution.py:70
  2.7 0.5 collective-permute-start
  3.2 3.5 %collective-permute-start.1 = (f32[256,256]{1,0:T(8,128)}, f32[256,256]{1,0:T(8,128)S(1)}, u32[]{:S(2)}, u32[]{:S(2)}) collective-permute-start(f32[256,256]{1,0:T(8,128)} %get-tuple-element.53), channel_id=1, source_target_pairs={{0,24},{4,28},{8,16},{12,20},{16,8},{20,12},{24,0},{28,4},{1,25},{... | collective-permute-start | bytes 786440 | tf_op jit(solution)/shard_map/ppermute | solution.py:89
  6.7 0.1 collective-permute-start.2
  6.8 1.7 %collective-permute-start.3 = (f32[256,256]{1,0:T(8,128)}, f32[256,256]{1,0:T(8,128)}, u32[]{:S(2)}, u32[]{:S(2)}) collective-permute-start(f32[256,256]{1,0:T(8,128)} %get-tuple-element.55), channel_id=1, source_target_pairs={{0,8},{4,12},{8,0},{12,4},{16,24},{20,28},{24,16},{28,20},{1,9},{5... | collective-permute-start | bytes 786440 | tf_op jit(solution)/shard_map/ppermute | solution.py:89
  8.4 1.5 %collective-permute-start.4 = (f32[256,256]{1,0:T(8,128)}, f32[256,256]{1,0:T(8,128)}, u32[]{:S(2)}, u32[]{:S(2)}) collective-permute-start(f32[256,256]{1,0:T(8,128)} %get-tuple-element.56), channel_id=1, source_target_pairs={{0,16},{4,20},{8,24},{12,28},{16,0},{20,4},{24,8},{28,12},{1,17},{... | collective-permute-start | bytes 786440 | tf_op jit(solution)/shard_map/ppermute | solution.py:89
  10.0 0.0 collective-permute-done.refs_1_
  10.0 0.7 copy-done.4
  10.7 0.0 collective-permute-start.5
  10.7 3.5 %collective-permute-done.1.refs_2_ = f32[256,256]{1,0:T(8,128)S(1)} collective-permute-done((f32[256,256]{1,0:T(8,128)}, f32[256,256]{1,0:T(8,128)S(1)}, u32[]{:S(2)}, u32[]{:S(2)}) %collective-permute-start.1) | collective-permute-done | bytes 262176 | tf_op jit(solution)/shard_map/ppermute | solution.py:89
  14.2 0.7 copy-done.6
  14.9 0.7 collective-permute-start.6
  15.5 1.8 %constant_dynamic-slice_fusion.far_ref = bf16[1024,1024]{1,0:T(8,128)(2,1)S(1)} fusion(bf16[1024,4096]{1,0:T(8,128)(2,1)} %param.13, s32[]{:T(128)S(6)} %select_n.61), kind=kLoop, calls=%fused_computation.11 | loop fusion | bytes 4194308 | tf_op jit(solution)/shard_map/dynamic_slice | solution.py:239
  17.4 0.0 copy-start.2
  17.4 2.0 %collective-permute-done.2.refs_3_ = f32[256,256]{1,0:T(8,128)} collective-permute-done((f32[256,256]{1,0:T(8,128)}, f32[256,256]{1,0:T(8,128)}, u32[]{:S(2)}, u32[]{:S(2)}) %collective-permute-start.2) | collective-permute-done | bytes 262176 | tf_op jit(solution)/shard_map/ppermute | solution.py:89
  19.4 2.0 %shard_map.83.early_ref = f32[4,512,256]{2,1,0:T(8,128)S(1)} custom-call(bf16[512,768]{1,0:T(8,128)(2,1)S(1)} %copy-done, f32[256,256]{1,0:T(8,128)S(1)} %copy-done.3, f32[256,256]{1,0:T(8,128)S(1)} %copy-done.5, f32[256,256]{1,0:T(8,128)S(1)} %copy-done.7, f32[256,256]{1,0:T(8,128)} %collective-permute-done.2.refs_3_), custom_call_target="tpu_custom_call" | custom-call | tf_op jit(solution)/shard_map/pallas_call | solution.py:100
  21.4 4.6 %collective-permute-done.3.refs_0_ = f32[256,256]{1,0:T(8,128)} collective-permute-done((f32[256,256]{1,0:T(8,128)}, f32[256,256]{1,0:T(8,128)}, u32[]{:S(2)}, u32[]{:S(2)}) %collective-permute-start.3) | collective-permute-done | bytes 262176 | tf_op jit(solution)/shard_map/ppermute | solution.py:89
  25.9 0.0 collective-permute-done.4.refs_1_
  25.9 4.7 %collective-permute-done.5.refs_2_ = f32[256,256]{1,0:T(8,128)} collective-permute-done((f32[256,256]{1,0:T(8,128)}, f32[256,256]{1,0:T(8,128)}, u32[]{:S(2)}, u32[]{:S(2)}) %collective-permute-start.5) | collective-permute-done | bytes 262176 | tf_op jit(solution)/shard_map/ppermute | solution.py:89
  30.6 0.1 collective-permute-done.6.refs_3_
  30.7 1.1 copy-done.1
  31.8 5.6 %shard_map.84 = (f32[256,128]{1,0:T(8,128)S(1)}, f32[256,128]{1,0:T(8,128)}, f32[256,128]{1,0:T(8,128)}, f32[256,128]{1,0:T(8,128)}, f32[256,128]{1,0:T(8,128)S(...) custom-call(s32[1]{0:T(128)} %bitcast.place_ref, f32[4,512,256]{2,1,0:T(8,128)S(1)} %shard_map.83.early_ref, ...), custom_call_target="tpu_custom_call" | custom-call | tf_op jit(solution)/shard_map/pallas_call | solution.py:170
  37.4 1.8 %collective-permute-start.10 = (f32[256,128]{1,0:T(8,128)S(1)}, f32[256,128]{1,0:T(8,128)S(1)}, u32[]{:S(2)}, u32[]{:S(2)}) collective-permute-start(f32[256,128]{1,0:T(8,128)S(1)} %get-tuple-element.63), channel_id=1, source_target_pairs={{0,8},{4,12},{8,0},{12,4},{16,24},{20,28},{24,16},{28,20},{1,9},{5... | collective-permute-start | bytes 393224 | tf_op jit(solution)/shard_map/ppermute | solution.py:89
  39.2 1.5 %collective-permute-start.11 = (f32[256,128]{1,0:T(8,128)S(1)}, f32[256,128]{1,0:T(8,128)S(1)}, u32[]{:S(2)}, u32[]{:S(2)}) collective-permute-start(f32[256,128]{1,0:T(8,128)S(1)} %get-tuple-element.64), channel_id=1, source_target_pairs={{0,16},{4,20},{8,24},{12,28},{16,0},{20,4},{24,8},{28,12},{1,17},{... | collective-permute-start | bytes 393224 | tf_op jit(solution)/shard_map/ppermute | solution.py:89
  40.7 0.0 collective-permute-start.12
  40.7 0.5 collective-permute-start.13
  41.3 0.1 collective-permute-start.7
  41.4 1.7 %collective-permute-done.10.refs_4_ = f32[256,128]{1,0:T(8,128)S(1)} collective-permute-done((f32[256,128]{1,0:T(8,128)S(1)}, f32[256,128]{1,0:T(8,128)S(1)}, u32[]{:S(2)}, u32[]{:S(2)}) %collective-permute-start.10) | collective-permute-done | bytes 131104 | tf_op jit(solution)/shard_map/ppermute | solution.py:89
  43.1 3.4 %collective-permute-start.8 = (f32[256,128]{1,0:T(8,128)}, f32[256,128]{1,0:T(8,128)S(1)}, u32[]{:S(2)}, u32[]{:S(2)}) collective-permute-start(f32[256,128]{1,0:T(8,128)} %get-tuple-element.61), channel_id=1, source_target_pairs={{0,24},{4,28},{8,16},{12,20},{16,8},{20,12},{24,0},{28,4},{1,25},{... | collective-permute-start | bytes 393224 | tf_op jit(solution)/shard_map/ppermute | solution.py:89
  46.5 0.0 collective-permute-done.11.refs_5_
  46.5 0.0 collective-permute-start.9
  46.5 0.0 collective-permute-done.12.refs_6_
  46.5 5.5 %collective-permute-done.13.refs_7_ = f32[256,128]{1,0:T(8,128)S(1)} collective-permute-done((f32[256,128]{1,0:T(8,128)}, f32[256,128]{1,0:T(8,128)S(1)}, u32[]{:S(2)}, u32[]{:S(2)}) %collective-permute-start.13) | collective-permute-done | bytes 131104 | tf_op jit(solution)/shard_map/ppermute | solution.py:89
  52.1 0.0 collective-permute-done.7.refs_1_
  52.1 0.0 collective-permute-done.8.refs_2_
  52.1 0.8 collective-permute-done.9.refs_3_
  52.8 3.1 %shard_map.85 = (bf16[256,1024]{1,0:T(8,128)(2,1)S(1)}, f32[256,512]{1,0:T(8,128)S(1)}, f32[256,512]{1,0:T(8,128)}) custom-call(s32[1]{0:T(128)} %bitcast.place_ref, bf16[1024,1024]{1,0:T(8,128)(2,1)S(1)} %constant_dynamic-slice_fusion.far_ref, bf16[256,1024]{1,0:T(8,128)(2,1)S(1)} %copy-done.2, f32[256,128]{1,0:T(8,128)S(1)} %get-tuple-element.59.refs_0_, ...), custom_call_target="tpu_custom_call" | custom-call | tf_op jit(solution)/shard_map/pallas_call | solution.py:221
  55.9 3.5 %collective-permute-start.15 = (f32[256,512]{1,0:T(8,128)S(1)}, f32[256,512]{1,0:T(8,128)S(1)}, u32[]{:S(2)}, u32[]{:S(2)}) collective-permute-start(f32[256,512]{1,0:T(8,128)S(1)} %get-tuple-element.68), channel_id=1, source_target_pairs={{0,1},{3,2},{4,5},{7,6},{8,9},{11,10},{12,13},{15,14},{16,17},{19,... | collective-permute-start | bytes 1572872 | tf_op jit(solution)/shard_map/ppermute | solution.py:255
  59.4 2.1 %collective-permute-start.14 = (f32[256,512]{1,0:T(8,128)}, f32[256,512]{1,0:T(8,128)}, u32[]{:S(2)}, u32[]{:S(2)}) collective-permute-start(f32[256,512]{1,0:T(8,128)} %get-tuple-element.67), channel_id=1, source_target_pairs={{0,1},{3,2},{4,5},{7,6},{8,9},{11,10},{12,13},{15,14},{16,17},{19,... | collective-permute-start | bytes 1572872 | tf_op jit(solution)/shard_map/ppermute | solution.py:255
  61.5 5.7 %fusion.1 = f32[256,4096]{1,0:T(8,128)S(1)} fusion(bf16[256,1024]{1,0:T(8,128)(2,1)S(1)} %get-tuple-element.69, bf16[1024,4096]{1,0:T(8,128)(2,1)} %param.13), kind=kOutput, calls=%fused_computation.12 | convolution fusion | flops 2147483648 | bytes 13107200 | tf_op jit(solution)/shard_map/dot_general | solution.py:265
  67.3 4.4 %collective-permute-done.15 = f32[256,512]{1,0:T(8,128)S(1)} collective-permute-done((f32[256,512]{1,0:T(8,128)S(1)}, f32[256,512]{1,0:T(8,128)S(1)}, u32[]{:S(2)}, u32[]{:S(2)}) %collective-permute-start.15) | collective-permute-done | bytes 524320 | tf_op jit(solution)/shard_map/ppermute | solution.py:255
  71.7 0.2 dynamic-slice_add_fusion.6
  71.9 4.4 %collective-permute-start.17 = (f32[256,512]{1,0:T(8,128)S(1)}, f32[256,512]{1,0:T(8,128)S(1)}, u32[]{:S(2)}, u32[]{:S(2)}) collective-permute-start(f32[256,512]{1,0:T(8,128)S(1)} %get-tuple-element.76), channel_id=1, source_target_pairs={{0,1},{1,2},{4,5},{5,6},{8,9},{9,10},{12,13},{13,14},{16,17},{17,1... | collective-permute-start | bytes 1572872 | tf_op jit(solution)/shard_map/ppermute | solution.py:246
  76.3 0.7 collective-permute-start.18
  77.0 6.0 %collective-permute-done.14 = f32[256,512]{1,0:T(8,128)} collective-permute-done((f32[256,512]{1,0:T(8,128)}, f32[256,512]{1,0:T(8,128)}, u32[]{:S(2)}, u32[]{:S(2)}) %collective-permute-start.14) | collective-permute-done | bytes 524320 | tf_op jit(solution)/shard_map/ppermute | solution.py:255
  83.0 1.5 %dynamic-slice_add_fusion.4 = (f32[256,512]{1,0:T(8,128)S(1)}, f32[256,512]{1,0:T(8,128)S(1)}) fusion(f32[256,4096]{1,0:T(8,128)} %copy-done.8, s32[]{:T(128)S(6)} %select_n.70, f32[256,512]{1,0:T(8,128)} %collective-permute-done.14, pred[]{:T(512)S(6)} %eq.13, s32[]{:T(128)S(6)} %select_n.68, pred[]{:T(512)S(6)} %eq.11), kind=kLoop, calls=%fused_computation.6 | loop fusion | flops 524288 | bytes 2621450 | tf_op jit(solution)/shard_map/add | solution.py:274
  84.6 5.2 %collective-permute-start.16 = (f32[256,512]{1,0:T(8,128)S(1)}, f32[256,512]{1,0:T(8,128)}, u32[]{:S(2)}, u32[]{:S(2)}) collective-permute-start(f32[256,512]{1,0:T(8,128)S(1)} %get-tuple-element.73), channel_id=1, source_target_pairs={{0,1},{1,2},{4,5},{5,6},{8,9},{9,10},{12,13},{13,14},{16,17},{17,1... | collective-permute-start | bytes 1572872 | tf_op jit(solution)/shard_map/ppermute | solution.py:246
  89.8 1.5 %collective-permute-start.19 = (f32[256,512]{1,0:T(8,128)S(1)}, f32[256,512]{1,0:T(8,128)}, u32[]{:S(2)}, u32[]{:S(2)}) collective-permute-start(f32[256,512]{1,0:T(8,128)S(1)} %get-tuple-element.80), channel_id=1, source_target_pairs={{2,1},{3,2},{6,5},{7,6},{10,9},{11,10},{14,13},{15,14},{18,17},{19... | collective-permute-start | bytes 1572872 | tf_op jit(solution)/shard_map/ppermute | solution.py:247
  91.2 2.9 %collective-permute-done.17 = f32[256,512]{1,0:T(8,128)S(1)} collective-permute-done((f32[256,512]{1,0:T(8,128)S(1)}, f32[256,512]{1,0:T(8,128)S(1)}, u32[]{:S(2)}, u32[]{:S(2)}) %collective-permute-start.17) | collective-permute-done | bytes 524320 | tf_op jit(solution)/shard_map/ppermute | solution.py:246
  94.2 0.0 collective-permute-done.18
  94.2 1.4 %dynamic-slice_add_fusion.2 = (f32[256,512]{1,0:T(8,128)S(1)}, f32[256,512]{1,0:T(8,128)S(1)}) fusion(f32[256,512]{1,0:T(8,128)S(1)} %collective-permute-done.18, f32[256,4096]{1,0:T(8,128)} %copy-done.8, s32[]{:T(128)S(6)} %select_n.72, f32[256,512]{1,0:T(8,128)S(1)} %collective-permute-done.17, s32[]{:T(128)S(6)} %select_n.71), kind=kLoop, calls=%fused_computation.4 | loop fusion | flops 262144 | bytes 3145736 | tf_op jit(solution)/shard_map/add | solution.py:274
  95.6 4.4 %collective-permute-start.20 = (f32[256,512]{1,0:T(8,128)S(1)}, f32[256,512]{1,0:T(8,128)S(1)}, u32[]{:S(2)}, u32[]{:S(2)}) collective-permute-start(f32[256,512]{1,0:T(8,128)S(1)} %get-tuple-element.84), channel_id=1, source_target_pairs={{0,1},{1,2},{2,3},{4,5},{5,6},{6,7},{8,9},{9,10},{10,11},{12,13},{... | collective-permute-start | bytes 1572872 | tf_op jit(solution)/shard_map/ppermute | solution.py:246
  100.0 1.3 %collective-permute-start.21 = (f32[256,512]{1,0:T(8,128)S(1)}, f32[256,512]{1,0:T(8,128)S(1)}, u32[]{:S(2)}, u32[]{:S(2)}) collective-permute-start(f32[256,512]{1,0:T(8,128)S(1)} %get-tuple-element.85), channel_id=1, source_target_pairs={{1,0},{2,1},{3,2},{5,4},{6,5},{7,6},{9,8},{10,9},{11,10},{13,12},{... | collective-permute-start | bytes 1572872 | tf_op jit(solution)/shard_map/ppermute | solution.py:247
  101.3 4.1 %collective-permute-done.16 = f32[256,512]{1,0:T(8,128)} collective-permute-done((f32[256,512]{1,0:T(8,128)S(1)}, f32[256,512]{1,0:T(8,128)}, u32[]{:S(2)}, u32[]{:S(2)}) %collective-permute-start.16) | collective-permute-done | bytes 524320 | tf_op jit(solution)/shard_map/ppermute | solution.py:246
  105.4 1.7 %dynamic-slice_add_fusion = (f32[256,512]{1,0:T(8,128)S(1)}, f32[256,512]{1,0:T(8,128)S(1)}) fusion(f32[256,512]{1,0:T(8,128)} %collective-permute-done.19, f32[256,4096]{1,0:T(8,128)} %copy-done.8, s32[]{:T(128)S(6)} %select_n.74, f32[256,512]{1,0:T(8,128)} %collective-permute-done.16, s32[]{:T(128)S(6)} %select_n.73), kind=kLoop, calls=%fused_computation.2 | loop fusion | flops 262144 | bytes 3145736 | tf_op jit(solution)/shard_map/add | solution.py:274
  107.1 5.3 %collective-permute-start.22 = (f32[256,512]{1,0:T(8,128)S(1)}, f32[256,512]{1,0:T(8,128)}, u32[]{:S(2)}, u32[]{:S(2)}) collective-permute-start(f32[256,512]{1,0:T(8,128)S(1)} %get-tuple-element.90), channel_id=1, source_target_pairs={{0,1},{1,2},{2,3},{4,5},{5,6},{6,7},{8,9},{9,10},{10,11},{12,13},{... | collective-permute-start | bytes 1572872 | tf_op jit(solution)/shard_map/ppermute | solution.py:246
  112.5 1.3 collective-permute-start.23
  113.8 2.9 %collective-permute-done.20 = f32[256,512]{1,0:T(8,128)S(1)} collective-permute-done((f32[256,512]{1,0:T(8,128)S(1)}, f32[256,512]{1,0:T(8,128)S(1)}, u32[]{:S(2)}, u32[]{:S(2)}) %collective-permute-start.20) | collective-permute-done | bytes 524320 | tf_op jit(solution)/shard_map/ppermute | solution.py:246
  116.6 0.0 collective-permute-done.21
  116.6 1.2 add_convert_fusion.1
  117.8 0.9 dynamic_update_slice.6
  118.6 8.3 %collective-permute-done.22 = f32[256,512]{1,0:T(8,128)} collective-permute-done((f32[256,512]{1,0:T(8,128)S(1)}, f32[256,512]{1,0:T(8,128)}, u32[]{:S(2)}, u32[]{:S(2)}) %collective-permute-start.22) | collective-permute-done | bytes 524320 | tf_op jit(solution)/shard_map/ppermute | solution.py:246
  127.0 0.0 collective-permute-done.23
  127.0 2.2 %fusion = bf16[256,1024]{1,0:T(8,128)(2,1)} fusion(bf16[256,1024]{1,0:T(8,128)(2,1)} %dynamic_update_slice.6, f32[256,512]{1,0:T(8,128)} %collective-permute-done.23, f32[256,512]{1,0:T(8,128)} %collective-permute-done.22, f32[256,4096]{1,0:T(8,128)} %copy-done.8, s32[]{:T(128)S(6)} %select_n.76), kind=kLoop, calls=%fused_computation.10 | loop fusion | flops 393216 | bytes 1835012 | tf_op jit(solution)/shard_map/dynamic_update_slice | solution.py:280
  (15 shorter events, 0.0 us)
Async XLA Ops:
  0.0 19.4 %copy-start = (bf16[512,768]{1,0:T(8,128)(2,1)S(1)}, bf16[512,768]{1,0:T(8,128)(2,1)}, u32[]{:S(2)}) copy-start(bf16[512,768]{1,0:T(8,128)(2,1)} %constant.47.clone.ahead_ref.refs_4_) | copy-start | bytes 2359300
  2.7 7.3 %collective-permute-start = (f32[256,256]{1,0:T(8,128)}, f32[256,256]{1,0:T(8,128)S(1)}, u32[]{:S(2)}, u32[]{:S(2)}) collective-permute-start(f32[256,256]{1,0:T(8,128)} %get-tuple-element.52), channel_id=1, source_target_pairs={{0,4},{4,0},{8,12},{12,8},{16,20},{20,16},{24,28},{28,24},{1,5},{5... | collective-permute-start | bytes 786440 | tf_op jit(solution)/shard_map/ppermute | solution.py:89
  3.2 11.0 %collective-permute-start.1 = (f32[256,256]{1,0:T(8,128)}, f32[256,256]{1,0:T(8,128)S(1)}, u32[]{:S(2)}, u32[]{:S(2)}) collective-permute-start(f32[256,256]{1,0:T(8,128)} %get-tuple-element.53), channel_id=1, source_target_pairs={{0,24},{4,28},{8,16},{12,20},{16,8},{20,12},{24,0},{28,4},{1,25},{... | collective-permute-start | bytes 786440 | tf_op jit(solution)/shard_map/ppermute | solution.py:89
  6.7 12.7 %collective-permute-start.2 = (f32[256,256]{1,0:T(8,128)}, f32[256,256]{1,0:T(8,128)}, u32[]{:S(2)}, u32[]{:S(2)}) collective-permute-start(f32[256,256]{1,0:T(8,128)} %get-tuple-element.54), channel_id=1, source_target_pairs={{0,28},{4,24},{8,20},{12,16},{16,12},{20,8},{24,4},{28,0},{1,29},{... | collective-permute-start | bytes 786440 | tf_op jit(solution)/shard_map/ppermute | solution.py:89
  6.8 19.1 %collective-permute-start.3 = (f32[256,256]{1,0:T(8,128)}, f32[256,256]{1,0:T(8,128)}, u32[]{:S(2)}, u32[]{:S(2)}) collective-permute-start(f32[256,256]{1,0:T(8,128)} %get-tuple-element.55), channel_id=1, source_target_pairs={{0,8},{4,12},{8,0},{12,4},{16,24},{20,28},{24,16},{28,20},{1,9},{5... | collective-permute-start | bytes 786440 | tf_op jit(solution)/shard_map/ppermute | solution.py:89
  8.4 17.5 %collective-permute-start.4 = (f32[256,256]{1,0:T(8,128)}, f32[256,256]{1,0:T(8,128)}, u32[]{:S(2)}, u32[]{:S(2)}) collective-permute-start(f32[256,256]{1,0:T(8,128)} %get-tuple-element.56), channel_id=1, source_target_pairs={{0,16},{4,20},{8,24},{12,28},{16,0},{20,4},{24,8},{28,12},{1,17},{... | collective-permute-start | bytes 786440 | tf_op jit(solution)/shard_map/ppermute | solution.py:89
  10.0 0.7 copy-start.4
  10.7 20.0 %collective-permute-start.5 = (f32[256,256]{1,0:T(8,128)}, f32[256,256]{1,0:T(8,128)}, u32[]{:S(2)}, u32[]{:S(2)}) collective-permute-start(f32[256,256]{1,0:T(8,128)} %get-tuple-element.57), channel_id=1, source_target_pairs={{0,12},{4,8},{8,4},{12,0},{16,28},{20,24},{24,20},{28,16},{1,13},{... | collective-permute-start | bytes 786440 | tf_op jit(solution)/shard_map/ppermute | solution.py:89
  14.2 0.7 copy-start.6
  14.9 15.8 %collective-permute-start.6 = (f32[256,256]{1,0:T(8,128)}, f32[256,256]{1,0:T(8,128)}, u32[]{:S(2)}, u32[]{:S(2)}) collective-permute-start(f32[256,256]{1,0:T(8,128)} %get-tuple-element.58), channel_id=1, source_target_pairs={{0,20},{4,16},{8,28},{12,24},{16,4},{20,0},{24,12},{28,8},{1,21},{... | collective-permute-start | bytes 786440 | tf_op jit(solution)/shard_map/ppermute | solution.py:89
  15.5 3.8 %copy-start.3 = (f32[256,256]{1,0:T(8,128)S(1)}, f32[256,256]{1,0:T(8,128)}, u32[]{:S(2)}) copy-start(f32[256,256]{1,0:T(8,128)} %get-tuple-element.51.refs_0_) | copy-start | bytes 786436
  15.5 3.8 %copy-start.5 = (f32[256,256]{1,0:T(8,128)S(1)}, f32[256,256]{1,0:T(8,128)}, u32[]{:S(2)}) copy-start(f32[256,256]{1,0:T(8,128)} %copy-done.4) | copy-start | bytes 786436
  15.5 3.8 %copy-start.7 = (f32[256,256]{1,0:T(8,128)S(1)}, f32[256,256]{1,0:T(8,128)}, u32[]{:S(2)}) copy-start(f32[256,256]{1,0:T(8,128)} %copy-done.6) | copy-start | bytes 786436
  17.4 35.4 %copy-start.2 = (bf16[256,1024]{1,0:T(8,128)(2,1)S(1)}, bf16[256,1024]{1,0:T(8,128)(2,1)}, u32[]{:S(2)}) copy-start(bf16[256,1024]{1,0:T(8,128)(2,1)} %q_hbm.1) | copy-start | bytes 1572868
  30.7 1.1 copy-start.1
  37.4 5.7 %collective-permute-start.10 = (f32[256,128]{1,0:T(8,128)S(1)}, f32[256,128]{1,0:T(8,128)S(1)}, u32[]{:S(2)}, u32[]{:S(2)}) collective-permute-start(f32[256,128]{1,0:T(8,128)S(1)} %get-tuple-element.63), channel_id=1, source_target_pairs={{0,8},{4,12},{8,0},{12,4},{16,24},{20,28},{24,16},{28,20},{1,9},{5... | collective-permute-start | bytes 393224 | tf_op jit(solution)/shard_map/ppermute | solution.py:89
  39.2 7.3 %collective-permute-start.11 = (f32[256,128]{1,0:T(8,128)S(1)}, f32[256,128]{1,0:T(8,128)S(1)}, u32[]{:S(2)}, u32[]{:S(2)}) collective-permute-start(f32[256,128]{1,0:T(8,128)S(1)} %get-tuple-element.64), channel_id=1, source_target_pairs={{0,16},{4,20},{8,24},{12,28},{16,0},{20,4},{24,8},{28,12},{1,17},{... | collective-permute-start | bytes 393224 | tf_op jit(solution)/shard_map/ppermute | solution.py:89
  40.7 5.8 %collective-permute-start.12 = (f32[256,128]{1,0:T(8,128)}, f32[256,128]{1,0:T(8,128)S(1)}, u32[]{:S(2)}, u32[]{:S(2)}) collective-permute-start(f32[256,128]{1,0:T(8,128)} %get-tuple-element.65), channel_id=1, source_target_pairs={{0,12},{4,8},{8,4},{12,0},{16,28},{20,24},{24,20},{28,16},{1,13},{... | collective-permute-start | bytes 393224 | tf_op jit(solution)/shard_map/ppermute | solution.py:89
  40.7 11.3 %collective-permute-start.13 = (f32[256,128]{1,0:T(8,128)}, f32[256,128]{1,0:T(8,128)S(1)}, u32[]{:S(2)}, u32[]{:S(2)}) collective-permute-start(f32[256,128]{1,0:T(8,128)} %get-tuple-element.66), channel_id=1, source_target_pairs={{0,20},{4,16},{8,28},{12,24},{16,4},{20,0},{24,12},{28,8},{1,21},{... | collective-permute-start | bytes 393224 | tf_op jit(solution)/shard_map/ppermute | solution.py:89
  41.3 10.8 %collective-permute-start.7 = (f32[256,128]{1,0:T(8,128)}, f32[256,128]{1,0:T(8,128)S(1)}, u32[]{:S(2)}, u32[]{:S(2)}) collective-permute-start(f32[256,128]{1,0:T(8,128)} %get-tuple-element.60), channel_id=1, source_target_pairs={{0,4},{4,0},{8,12},{12,8},{16,20},{20,16},{24,28},{28,24},{1,5},{5... | collective-permute-start | bytes 393224 | tf_op jit(solution)/shard_map/ppermute | solution.py:89
  43.1 8.9 %collective-permute-start.8 = (f32[256,128]{1,0:T(8,128)}, f32[256,128]{1,0:T(8,128)S(1)}, u32[]{:S(2)}, u32[]{:S(2)}) collective-permute-start(f32[256,128]{1,0:T(8,128)} %get-tuple-element.61), channel_id=1, source_target_pairs={{0,24},{4,28},{8,16},{12,20},{16,8},{20,12},{24,0},{28,4},{1,25},{... | collective-permute-start | bytes 393224 | tf_op jit(solution)/shard_map/ppermute | solution.py:89
  46.5 6.3 %collective-permute-start.9 = (f32[256,128]{1,0:T(8,128)}, f32[256,128]{1,0:T(8,128)}, u32[]{:S(2)}, u32[]{:S(2)}) collective-permute-start(f32[256,128]{1,0:T(8,128)} %get-tuple-element.62), channel_id=1, source_target_pairs={{0,28},{4,24},{8,20},{12,16},{16,12},{20,8},{24,4},{28,0},{1,29},{... | collective-permute-start | bytes 393224 | tf_op jit(solution)/shard_map/ppermute | solution.py:89
  55.9 15.8 %collective-permute-start.15 = (f32[256,512]{1,0:T(8,128)S(1)}, f32[256,512]{1,0:T(8,128)S(1)}, u32[]{:S(2)}, u32[]{:S(2)}) collective-permute-start(f32[256,512]{1,0:T(8,128)S(1)} %get-tuple-element.68), channel_id=1, source_target_pairs={{0,1},{3,2},{4,5},{7,6},{8,9},{11,10},{12,13},{15,14},{16,17},{19,... | collective-permute-start | bytes 1572872 | tf_op jit(solution)/shard_map/ppermute | solution.py:255
  59.4 23.6 %collective-permute-start.14 = (f32[256,512]{1,0:T(8,128)}, f32[256,512]{1,0:T(8,128)}, u32[]{:S(2)}, u32[]{:S(2)}) collective-permute-start(f32[256,512]{1,0:T(8,128)} %get-tuple-element.67), channel_id=1, source_target_pairs={{0,1},{3,2},{4,5},{7,6},{8,9},{11,10},{12,13},{15,14},{16,17},{19,... | collective-permute-start | bytes 1572872 | tf_op jit(solution)/shard_map/ppermute | solution.py:255
  67.3 4.4 %copy-start.8 = (f32[256,4096]{1,0:T(8,128)}, f32[256,4096]{1,0:T(8,128)S(1)}, u32[]{:S(2)}) copy-start(f32[256,4096]{1,0:T(8,128)S(1)} %fusion.1) | copy-start | bytes 12582916
  71.9 22.3 %collective-permute-start.17 = (f32[256,512]{1,0:T(8,128)S(1)}, f32[256,512]{1,0:T(8,128)S(1)}, u32[]{:S(2)}, u32[]{:S(2)}) collective-permute-start(f32[256,512]{1,0:T(8,128)S(1)} %get-tuple-element.76), channel_id=1, source_target_pairs={{0,1},{1,2},{4,5},{5,6},{8,9},{9,10},{12,13},{13,14},{16,17},{17,1... | collective-permute-start | bytes 1572872 | tf_op jit(solution)/shard_map/ppermute | solution.py:246
  76.3 17.9 %collective-permute-start.18 = (f32[256,512]{1,0:T(8,128)S(1)}, f32[256,512]{1,0:T(8,128)S(1)}, u32[]{:S(2)}, u32[]{:S(2)}) collective-permute-start(f32[256,512]{1,0:T(8,128)S(1)} %get-tuple-element.78), channel_id=1, source_target_pairs={{2,1},{3,2},{6,5},{7,6},{10,9},{11,10},{14,13},{15,14},{18,17},{19... | collective-permute-start | bytes 1572872 | tf_op jit(solution)/shard_map/ppermute | solution.py:247
  84.6 20.8 %collective-permute-start.16 = (f32[256,512]{1,0:T(8,128)S(1)}, f32[256,512]{1,0:T(8,128)}, u32[]{:S(2)}, u32[]{:S(2)}) collective-permute-start(f32[256,512]{1,0:T(8,128)S(1)} %get-tuple-element.73), channel_id=1, source_target_pairs={{0,1},{1,2},{4,5},{5,6},{8,9},{9,10},{12,13},{13,14},{16,17},{17,1... | collective-permute-start | bytes 1572872 | tf_op jit(solution)/shard_map/ppermute | solution.py:246
  89.8 15.6 %collective-permute-start.19 = (f32[256,512]{1,0:T(8,128)S(1)}, f32[256,512]{1,0:T(8,128)}, u32[]{:S(2)}, u32[]{:S(2)}) collective-permute-start(f32[256,512]{1,0:T(8,128)S(1)} %get-tuple-element.80), channel_id=1, source_target_pairs={{2,1},{3,2},{6,5},{7,6},{10,9},{11,10},{14,13},{15,14},{18,17},{19... | collective-permute-start | bytes 1572872 | tf_op jit(solution)/shard_map/ppermute | solution.py:247
  95.6 21.1 %collective-permute-start.20 = (f32[256,512]{1,0:T(8,128)S(1)}, f32[256,512]{1,0:T(8,128)S(1)}, u32[]{:S(2)}, u32[]{:S(2)}) collective-permute-start(f32[256,512]{1,0:T(8,128)S(1)} %get-tuple-element.84), channel_id=1, source_target_pairs={{0,1},{1,2},{2,3},{4,5},{5,6},{6,7},{8,9},{9,10},{10,11},{12,13},{... | collective-permute-start | bytes 1572872 | tf_op jit(solution)/shard_map/ppermute | solution.py:246
  100.0 16.6 %collective-permute-start.21 = (f32[256,512]{1,0:T(8,128)S(1)}, f32[256,512]{1,0:T(8,128)S(1)}, u32[]{:S(2)}, u32[]{:S(2)}) collective-permute-start(f32[256,512]{1,0:T(8,128)S(1)} %get-tuple-element.85), channel_id=1, source_target_pairs={{1,0},{2,1},{3,2},{5,4},{6,5},{7,6},{9,8},{10,9},{11,10},{13,12},{... | collective-permute-start | bytes 1572872 | tf_op jit(solution)/shard_map/ppermute | solution.py:247
  107.1 19.9 %collective-permute-start.22 = (f32[256,512]{1,0:T(8,128)S(1)}, f32[256,512]{1,0:T(8,128)}, u32[]{:S(2)}, u32[]{:S(2)}) collective-permute-start(f32[256,512]{1,0:T(8,128)S(1)} %get-tuple-element.90), channel_id=1, source_target_pairs={{0,1},{1,2},{2,3},{4,5},{5,6},{6,7},{8,9},{9,10},{10,11},{12,13},{... | collective-permute-start | bytes 1572872 | tf_op jit(solution)/shard_map/ppermute | solution.py:246
  112.5 14.5 %collective-permute-start.23 = (f32[256,512]{1,0:T(8,128)S(1)}, f32[256,512]{1,0:T(8,128)}, u32[]{:S(2)}, u32[]{:S(2)}) collective-permute-start(f32[256,512]{1,0:T(8,128)S(1)} %get-tuple-element.91), channel_id=1, source_target_pairs={{1,0},{2,1},{3,2},{5,4},{6,5},{7,6},{9,8},{10,9},{11,10},{13,12},{... | collective-permute-start | bytes 1572872 | tf_op jit(solution)/shard_map/ppermute | solution.py:247

commit v4 on v3

--- a/solution.py
+++ b/solution.py
@@ -12,6 +12,10 @@
 
 F32 = jnp.float32
 BF16 = jnp.bfloat16
+
+
+def stay(array):
+    return pltpu.with_memory_space_constraint(array, pltpu.MemorySpace.HBM)
 
 
 def room(*shapes):
@@ -76,7 +80,7 @@
         out_shape=[jax.ShapeDtypeStruct((rows, wide), F32)] * count,
         scratch_shapes=[pltpu.VMEM((count, step, wide), F32)],
         compiler_params=pltpu.CompilerParams(vmem_limit_bytes=56 * 1024 * 1024),
-    )(place, keys, values, filt, direct)
+    )(place, stay(keys), stay(values), stay(filt), stay(direct))
 
 
 def turns(count):
@@ -106,24 +110,27 @@
     )(ahead, *xs)
 
 
-def conv_kernel(place_ref, early_ref, *refs):
+def conv_kernel(place_ref, early_ref, ahead_ref, back_hbm, *refs):
     first = early_ref.shape[0]
-    count = (len(refs) - 6 + first) // 2
-    xs, (ahead_ref, back_hbm) = refs[: count - first], refs[count - first : count - first + 2]
-    outs, (spec_ref, mix_ref, back_ref, back_sem) = refs[count - first + 2 : -4], refs[-4:]
-    back_in = pltpu.make_async_copy(back_hbm, back_ref, back_sem)
-    back_in.start()
+    spec_ref, mix_ref, x_ref, out_ref, back_ref, x_sem, out_sem, back_sem = refs[-8:]
+    count = spec_ref.shape[0]
+    xs, outs = refs[: count - first], refs[count - first : -8]
     rows, width = xs[0].shape
     chans = width // 2
     place = place_ref[0]
-
     order = turns(count)
+
+    blocks_in = [pltpu.make_async_copy(x, x_ref.at[j], x_sem.at[j]) for j, x in enumerate(xs)]
+    for copy in blocks_in:
+        copy.start()
+    back_in = pltpu.make_async_copy(back_hbm, back_ref, back_sem)
+    back_in.start()
     for j, turn in enumerate(order):
         if j < first:
             spec_ref[turn ^ place] = early_ref[j]
         else:
-            x = xs[j - first]
-            spec_ref[turn ^ place] = jnp.dot(ahead_ref[...], split3(x[...]), preferred_element_type=F32)
+            blocks_in[j - first].wait()
+            spec_ref[turn ^ place] = jnp.dot(ahead_ref[...], split3(x_ref[j - first]), preferred_element_type=F32)
 
     step = 8
     parity = lax.broadcasted_iota(jnp.int32, (step, chans), 0) % 2
@@ -152,11 +159,16 @@
     lax.fori_loop(0, rows // step, combine, 0)
 
     back_in.wait()
+    blocks_out = [pltpu.make_async_copy(out_ref.at[j], out, out_sem.at[j]) for j, out in enumerate(outs)]
     for j in range(0, count, 2):
         pair = jnp.concatenate([mix_ref[order[j] ^ place], mix_ref[order[j + 1] ^ place]], axis=1)
         part = jnp.dot(back_ref[...], split3(pair), preferred_element_type=F32)
-        outs[j][...] = part[:, :chans]
-        outs[j + 1][...] = part[:, chans:]
+        out_ref[j] = part[:, :chans]
+        out_ref[j + 1] = part[:, chans:]
+        blocks_out[j].start()
+        blocks_out[j + 1].start()
+    for copy in blocks_out:
+        copy.wait()
 
 
 def convolve(place, xs):
@@ -167,23 +179,27 @@
     first = count // 2
     early = forward(xs[:first], ahead)
     whole = pl.BlockSpec(memory_space=pltpu.VMEM)
+    there = pl.BlockSpec(memory_space=pl.ANY)
+    scratch = [
+        (count, 2 * rows, width),
+        (count, 2 * rows, chans),
+        (count - first, rows, width),
+        (count, rows, chans),
+    ]
     return pl.pallas_call(
         conv_kernel,
-        in_specs=[pl.BlockSpec(memory_space=pltpu.SMEM)]
-        + [whole] * (count - first + 2)
-        + [pl.BlockSpec(memory_space=pl.ANY)],
-        out_specs=[whole] * count,
+        in_specs=[pl.BlockSpec(memory_space=pltpu.SMEM), whole, whole] + [there] * (count - first + 1),
+        out_specs=[there] * count,
         out_shape=[jax.ShapeDtypeStruct((rows, chans), F32)] * count,
-        scratch_shapes=[
-            pltpu.VMEM((count, 2 * rows, width), F32),
-            pltpu.VMEM((count, 2 * rows, chans), F32),
+        scratch_shapes=[pltpu.VMEM(shape, F32) for shape in scratch]
+        + [
             pltpu.VMEM(back.shape, BF16),
+            pltpu.SemaphoreType.DMA((count - first,)),
+            pltpu.SemaphoreType.DMA((count,)),
             pltpu.SemaphoreType.DMA,
         ],
-        compiler_params=room(
-            (count, 2 * rows, width), *[(count, 2 * rows, chans)] * 2, (count, rows, width)
-        ),
-    )(place, early, *xs[first:], ahead, back)
+        compiler_params=room(*scratch, scratch[1]),
+    )(place, early, ahead, stay(back), *xs[first:])
 
 
 CHAINS = 2
@@ -222,15 +238,14 @@
         gate_kernel,
         in_specs=[pl.BlockSpec(memory_space=pltpu.SMEM), here] + [there] * (1 + count),
         out_specs=[here] * (1 + CHAINS),
-        out_shape=[jax.ShapeDtypeStruct((rows, width), BF16)]
-        + [jax.ShapeDtypeStruct(part, F32)] * CHAINS,
+        out_shape=[pltpu.VMEM((rows, width), BF16)] + [pltpu.VMEM(part, F32)] * CHAINS,
         scratch_shapes=[
             pltpu.VMEM((rows, width), BF16),
             pltpu.VMEM(blocks, F32),
             pltpu.SemaphoreType.DMA((count + 1,)),
         ],
         compiler_params=room(*[(rows, width)] * 2, far.shape, blocks, (CHAINS,) + part),
-    )(place, far, query, *convs)
+    )(place, far, stay(query), *convs)
     return out[0], out[1:]
 
 

time: 130 us -> 130 us (level)
    pallas_call x1, Pallas kernels: 5.61 us -> 6.97 us  [convolve(): pl.pallas_call(conv_kernel, in_specs=[pl.BlockSpec(memory_space=pltpu.SME...]
where the time goes in v4:
time: 130 us; the launch traced here: 129 us
  waiting for transfers between devices  51.5 us (40%)
  starting transfers between devices  45 us (35%)
  Pallas kernels  14.6 us (11%)
  other arithmetic  8.17 us (6%)
  matrix products  5.73 us (4%)
  local copies, waits for them, and re-layouts  4.12 us (3%)
    ppermute x14, waiting for transfers between devices, swap(): lax.ppermute(arrays[j], 'ctx', pairs[j])  22.7 us
    ppermute x4, starting transfers between devices, pass_on(): up = lax.ppermute(up, 'tp', rise)  19.3 us
    ppermute x4, waiting for transfers between devices, pass_on(): up = lax.ppermute(up, 'tp', rise)  18.3 us
    ppermute x14, starting transfers between devices, swap(): lax.ppermute(arrays[j], 'ctx', pairs[j])  15.3 us
    ppermute x2, waiting for transfers between devices, first_step(): got = lax.ppermute(value, 'tp', [(0, 1), (size - 1, size - 2)])  10.4 us
    pallas_call x1, Pallas kernels, convolve(): pl.pallas_call(conv_kernel, in_specs=[pl.BlockSpec(memory_space=pltpu.SME...  6.97 us
    dot_general x1, matrix products, scatter_dot(): terms = jnp.dot(lhs, rhs, preferred_element_type=F32)  5.73 us
    ppermute x2, starting transfers between devices, first_step(): got = lax.ppermute(value, 'tp', [(0, 1), (size - 1, size - 2)])  5.62 us
  transfers between devices with their start and end apart: 24, of which 14 were waited for; matrix products, arithmetic and copies ran while one was open for 11% of the time, Pallas kernels for 2%

profile of v4, /device:TPU:0, one launch (start us, length us, event | category | flops | bytes accessed | tf_op | source)
XLA Modules:
  0.0 129.2 jit_solution(15917324624602337669)
XLA Ops:
  0.0 2.7 %shard_map.82 = (f32[256,256]{1,0:T(8,128)}, f32[256,256]{1,0:T(8,128)}, f32[256,256]{1,0:T(8,128)}, f32[256,256]{1,0:T(8,128)}, f32[256,256]{1,0:T(8,128)}, /*i...) custom-call(s32[1]{0:T(128)} %bitcast.place_ref, bf16[256,1024]{1,0:T(8,128)(2,1)} %keys_ref.1, ...), custom_call_target="tpu_custom_call" | custom-call | tf_op jit(solution)/shard_map/pallas_call | solution.py:74
  2.7 0.5 collective-permute-start
  3.2 3.5 %collective-permute-start.1 = (f32[256,256]{1,0:T(8,128)}, f32[256,256]{1,0:T(8,128)S(1)}, u32[]{:S(2)}, u32[]{:S(2)}) collective-permute-start(f32[256,256]{1,0:T(8,128)} %get-tuple-element.53), channel_id=1, source_target_pairs={{0,24},{4,28},{8,16},{12,20},{16,8},{20,12},{24,0},{28,4},{1,25},{... | collective-permute-start | bytes 786440 | tf_op jit(solution)/shard_map/ppermute | solution.py:93
  6.7 0.1 collective-permute-start.2
  6.8 1.7 %collective-permute-start.3 = (f32[256,256]{1,0:T(8,128)}, f32[256,256]{1,0:T(8,128)S(1)}, u32[]{:S(2)}, u32[]{:S(2)}) collective-permute-start(f32[256,256]{1,0:T(8,128)} %get-tuple-element.55), channel_id=1, source_target_pairs={{0,8},{4,12},{8,0},{12,4},{16,24},{20,28},{24,16},{28,20},{1,9},{5... | collective-permute-start | bytes 786440 | tf_op jit(solution)/shard_map/ppermute | solution.py:93
  8.4 1.5 %collective-permute-start.4 = (f32[256,256]{1,0:T(8,128)}, f32[256,256]{1,0:T(8,128)S(1)}, u32[]{:S(2)}, u32[]{:S(2)}) collective-permute-start(f32[256,256]{1,0:T(8,128)} %get-tuple-element.56), channel_id=1, source_target_pairs={{0,16},{4,20},{8,24},{12,28},{16,0},{20,4},{24,8},{28,12},{1,17},{... | collective-permute-start | bytes 786440 | tf_op jit(solution)/shard_map/ppermute | solution.py:93
  10.0 0.0 collective-permute-done.refs_1_
  10.0 0.7 copy-done.2
  10.7 0.0 collective-permute-start.5
  10.7 3.5 %collective-permute-done.1.refs_2_ = f32[256,256]{1,0:T(8,128)S(1)} collective-permute-done((f32[256,256]{1,0:T(8,128)}, f32[256,256]{1,0:T(8,128)S(1)}, u32[]{:S(2)}, u32[]{:S(2)}) %collective-permute-start.1) | collective-permute-done | bytes 262176 | tf_op jit(solution)/shard_map/ppermute | solution.py:93
  14.2 0.7 copy-done.4
  14.9 0.7 collective-permute-start.6
  15.6 1.8 %constant_dynamic-slice_fusion.far_ref = bf16[1024,1024]{1,0:T(8,128)(2,1)S(1)} fusion(bf16[1024,4096]{1,0:T(8,128)(2,1)} %param.13, s32[]{:T(128)S(6)} %select_n.61), kind=kLoop, calls=%fused_computation.11 | loop fusion | bytes 4194308 | tf_op jit(solution)/shard_map/dynamic_slice | solution.py:254
  17.4 2.0 %collective-permute-done.2.refs_3_ = f32[256,256]{1,0:T(8,128)} collective-permute-done((f32[256,256]{1,0:T(8,128)}, f32[256,256]{1,0:T(8,128)}, u32[]{:S(2)}, u32[]{:S(2)}) %collective-permute-start.2) | collective-permute-done | bytes 262176 | tf_op jit(solution)/shard_map/ppermute | solution.py:93
  19.4 0.0 copy-done
  19.4 2.0 %shard_map.83.early_ref = f32[4,512,256]{2,1,0:T(8,128)S(1)} custom-call(bf16[512,768]{1,0:T(8,128)(2,1)S(1)} %copy-done, f32[256,256]{1,0:T(8,128)S(1)} %copy-done.1, f32[256,256]{1,0:T(8,128)S(1)} %copy-done.3, f32[256,256]{1,0:T(8,128)S(1)} %copy-done.5, f32[256,256]{1,0:T(8,128)} %collective-permute-done.2.refs_3_), custom_call_target="tpu_custom_call" | custom-call | tf_op jit(solution)/shard_map/pallas_call | solution.py:104
  21.4 4.5 %collective-permute-done.3.refs_0_ = f32[256,256]{1,0:T(8,128)S(1)} collective-permute-done((f32[256,256]{1,0:T(8,128)}, f32[256,256]{1,0:T(8,128)S(1)}, u32[]{:S(2)}, u32[]{:S(2)}) %collective-permute-start.3) | collective-permute-done | bytes 262176 | tf_op jit(solution)/shard_map/ppermute | solution.py:93
  25.8 0.0 collective-permute-done.4.refs_1_
  25.8 4.8 %collective-permute-done.5.refs_2_ = f32[256,256]{1,0:T(8,128)} collective-permute-done((f32[256,256]{1,0:T(8,128)}, f32[256,256]{1,0:T(8,128)}, u32[]{:S(2)}, u32[]{:S(2)}) %collective-permute-start.5) | collective-permute-done | bytes 262176 | tf_op jit(solution)/shard_map/ppermute | solution.py:93
  30.6 0.1 collective-permute-done.6.refs_3_
  30.7 7.0 %shard_map.84 = (f32[256,128]{1,0:T(8,128)S(1)}, f32[256,128]{1,0:T(8,128)}, f32[256,128]{1,0:T(8,128)}, f32[256,128]{1,0:T(8,128)}, f32[256,128]{1,0:T(8,128)S(...) custom-call(s32[1]{0:T(128)} %bitcast.place_ref, f32[4,512,256]{2,1,0:T(8,128)S(1)} %shard_map.83.early_ref, ...), custom_call_target="tpu_custom_call" | custom-call | tf_op jit(solution)/shard_map/pallas_call | solution.py:189
  37.7 1.8 %collective-permute-start.10 = (f32[256,128]{1,0:T(8,128)S(1)}, f32[256,128]{1,0:T(8,128)S(1)}, u32[]{:S(2)}, u32[]{:S(2)}) collective-permute-start(f32[256,128]{1,0:T(8,128)S(1)} %get-tuple-element.63), channel_id=1, source_target_pairs={{0,8},{4,12},{8,0},{12,4},{16,24},{20,28},{24,16},{28,20},{1,9},{5... | collective-permute-start | bytes 393224 | tf_op jit(solution)/shard_map/ppermute | solution.py:93
  39.4 1.5 %collective-permute-start.11 = (f32[256,128]{1,0:T(8,128)S(1)}, f32[256,128]{1,0:T(8,128)S(1)}, u32[]{:S(2)}, u32[]{:S(2)}) collective-permute-start(f32[256,128]{1,0:T(8,128)S(1)} %get-tuple-element.64), channel_id=1, source_target_pairs={{0,16},{4,20},{8,24},{12,28},{16,0},{20,4},{24,8},{28,12},{1,17},{... | collective-permute-start | bytes 393224 | tf_op jit(solution)/shard_map/ppermute | solution.py:93
  40.9 0.0 collective-permute-start.12
  41.0 0.6 collective-permute-start.13
  41.5 0.1 collective-permute-start.7
  41.6 1.7 %collective-permute-done.10.refs_4_ = f32[256,128]{1,0:T(8,128)S(1)} collective-permute-done((f32[256,128]{1,0:T(8,128)S(1)}, f32[256,128]{1,0:T(8,128)S(1)}, u32[]{:S(2)}, u32[]{:S(2)}) %collective-permute-start.10) | collective-permute-done | bytes 131104 | tf_op jit(solution)/shard_map/ppermute | solution.py:93
  43.3 3.4 %collective-permute-start.8 = (f32[256,128]{1,0:T(8,128)}, f32[256,128]{1,0:T(8,128)S(1)}, u32[]{:S(2)}, u32[]{:S(2)}) collective-permute-start(f32[256,128]{1,0:T(8,128)} %get-tuple-element.61), channel_id=1, source_target_pairs={{0,24},{4,28},{8,16},{12,20},{16,8},{20,12},{24,0},{28,4},{1,25},{... | collective-permute-start | bytes 393224 | tf_op jit(solution)/shard_map/ppermute | solution.py:93
  46.7 0.0 collective-permute-done.11.refs_5_
  46.7 0.0 collective-permute-start.9
  46.7 0.0 collective-permute-done.12.refs_6_
  46.7 5.5 %collective-permute-done.13.refs_7_ = f32[256,128]{1,0:T(8,128)S(1)} collective-permute-done((f32[256,128]{1,0:T(8,128)}, f32[256,128]{1,0:T(8,128)S(1)}, u32[]{:S(2)}, u32[]{:S(2)}) %collective-permute-start.13) | collective-permute-done | bytes 131104 | tf_op jit(solution)/shard_map/ppermute | solution.py:93
  52.3 0.0 collective-permute-done.7.refs_1_
  52.3 0.0 collective-permute-done.8.refs_2_
  52.3 0.7 collective-permute-done.9.refs_3_
  52.9 3.0 %shard_map.85 = (bf16[256,1024]{1,0:T(8,128)(2,1)S(1)}, f32[256,512]{1,0:T(8,128)S(1)}, f32[256,512]{1,0:T(8,128)}) custom-call(s32[1]{0:T(128)} %bitcast.place_ref, bf16[1024,1024]{1,0:T(8,128)(2,1)S(1)} %constant_dynamic-slice_fusion.far_ref, bf16[256,1024]{1,0:T(8,128)(2,1)} %q_hbm.1, f32[256,128]{1,0:T(8,128)S(1)} %get-tuple-element.59.refs_0_, ...), custom_call_target="tpu_custom_call" | custom-call | tf_op jit(solution)/shard_map/pallas_call | solution.py:237
  55.9 3.5 %collective-permute-start.15 = (f32[256,512]{1,0:T(8,128)S(1)}, f32[256,512]{1,0:T(8,128)S(1)}, u32[]{:S(2)}, u32[]{:S(2)}) collective-permute-start(f32[256,512]{1,0:T(8,128)S(1)} %get-tuple-element.68), channel_id=1, source_target_pairs={{0,1},{3,2},{4,5},{7,6},{8,9},{11,10},{12,13},{15,14},{16,17},{19,... | collective-permute-start | bytes 1572872 | tf_op jit(solution)/shard_map/ppermute | solution.py:270
  59.4 2.1 %collective-permute-start.14 = (f32[256,512]{1,0:T(8,128)}, f32[256,512]{1,0:T(8,128)}, u32[]{:S(2)}, u32[]{:S(2)}) collective-permute-start(f32[256,512]{1,0:T(8,128)} %get-tuple-element.67), channel_id=1, source_target_pairs={{0,1},{3,2},{4,5},{7,6},{8,9},{11,10},{12,13},{15,14},{16,17},{19,... | collective-permute-start | bytes 1572872 | tf_op jit(solution)/shard_map/ppermute | solution.py:270
  61.5 5.7 %fusion.1 = f32[256,4096]{1,0:T(8,128)S(1)} fusion(bf16[256,1024]{1,0:T(8,128)(2,1)S(1)} %get-tuple-element.69, bf16[1024,4096]{1,0:T(8,128)(2,1)} %param.13), kind=kOutput, calls=%fused_computation.12 | convolution fusion | flops 2147483648 | bytes 13107200 | tf_op jit(solution)/shard_map/dot_general | solution.py:280
  67.3 4.4 %collective-permute-done.15 = f32[256,512]{1,0:T(8,128)S(1)} collective-permute-done((f32[256,512]{1,0:T(8,128)S(1)}, f32[256,512]{1,0:T(8,128)S(1)}, u32[]{:S(2)}, u32[]{:S(2)}) %collective-permute-start.15) | collective-permute-done | bytes 524320 | tf_op jit(solution)/shard_map/ppermute | solution.py:270
  71.7 0.2 dynamic-slice_add_fusion.6
  71.9 4.4 %collective-permute-start.17 = (f32[256,512]{1,0:T(8,128)S(1)}, f32[256,512]{1,0:T(8,128)S(1)}, u32[]{:S(2)}, u32[]{:S(2)}) collective-permute-start(f32[256,512]{1,0:T(8,128)S(1)} %get-tuple-element.76), channel_id=1, source_target_pairs={{0,1},{1,2},{4,5},{5,6},{8,9},{9,10},{12,13},{13,14},{16,17},{17,1... | collective-permute-start | bytes 1572872 | tf_op jit(solution)/shard_map/ppermute | solution.py:261
  76.3 0.7 collective-permute-start.18
  77.0 6.0 %collective-permute-done.14 = f32[256,512]{1,0:T(8,128)} collective-permute-done((f32[256,512]{1,0:T(8,128)}, f32[256,512]{1,0:T(8,128)}, u32[]{:S(2)}, u32[]{:S(2)}) %collective-permute-start.14) | collective-permute-done | bytes 524320 | tf_op jit(solution)/shard_map/ppermute | solution.py:270
  83.0 1.5 %dynamic-slice_add_fusion.4 = (f32[256,512]{1,0:T(8,128)S(1)}, f32[256,512]{1,0:T(8,128)S(1)}) fusion(f32[256,4096]{1,0:T(8,128)} %copy-done.6, s32[]{:T(128)S(6)} %select_n.70, f32[256,512]{1,0:T(8,128)} %collective-permute-done.14, pred[]{:T(512)S(6)} %eq.13, s32[]{:T(128)S(6)} %select_n.68, pred[]{:T(512)S(6)} %eq.11), kind=kLoop, calls=%fused_computation.6 | loop fusion | flops 524288 | bytes 2621450 | tf_op jit(solution)/shard_map/add | solution.py:289
  84.5 5.2 %collective-permute-start.16 = (f32[256,512]{1,0:T(8,128)S(1)}, f32[256,512]{1,0:T(8,128)}, u32[]{:S(2)}, u32[]{:S(2)}) collective-permute-start(f32[256,512]{1,0:T(8,128)S(1)} %get-tuple-element.73), channel_id=1, source_target_pairs={{0,1},{1,2},{4,5},{5,6},{8,9},{9,10},{12,13},{13,14},{16,17},{17,1... | collective-permute-start | bytes 1572872 | tf_op jit(solution)/shard_map/ppermute | solution.py:261
  89.7 1.5 %collective-permute-start.19 = (f32[256,512]{1,0:T(8,128)S(1)}, f32[256,512]{1,0:T(8,128)}, u32[]{:S(2)}, u32[]{:S(2)}) collective-permute-start(f32[256,512]{1,0:T(8,128)S(1)} %get-tuple-element.80), channel_id=1, source_target_pairs={{2,1},{3,2},{6,5},{7,6},{10,9},{11,10},{14,13},{15,14},{18,17},{19... | collective-permute-start | bytes 1572872 | tf_op jit(solution)/shard_map/ppermute | solution.py:262
  91.2 2.9 %collective-permute-done.17 = f32[256,512]{1,0:T(8,128)S(1)} collective-permute-done((f32[256,512]{1,0:T(8,128)S(1)}, f32[256,512]{1,0:T(8,128)S(1)}, u32[]{:S(2)}, u32[]{:S(2)}) %collective-permute-start.17) | collective-permute-done | bytes 524320 | tf_op jit(solution)/shard_map/ppermute | solution.py:261
  94.1 0.0 collective-permute-done.18
  94.1 1.4 %dynamic-slice_add_fusion.2 = (f32[256,512]{1,0:T(8,128)S(1)}, f32[256,512]{1,0:T(8,128)S(1)}) fusion(f32[256,512]{1,0:T(8,128)S(1)} %collective-permute-done.18, f32[256,4096]{1,0:T(8,128)} %copy-done.6, s32[]{:T(128)S(6)} %select_n.72, f32[256,512]{1,0:T(8,128)S(1)} %collective-permute-done.17, s32[]{:T(128)S(6)} %select_n.71), kind=kLoop, calls=%fused_computation.4 | loop fusion | flops 262144 | bytes 3145736 | tf_op jit(solution)/shard_map/add | solution.py:289
  95.6 4.4 %collective-permute-start.20 = (f32[256,512]{1,0:T(8,128)S(1)}, f32[256,512]{1,0:T(8,128)S(1)}, u32[]{:S(2)}, u32[]{:S(2)}) collective-permute-start(f32[256,512]{1,0:T(8,128)S(1)} %get-tuple-element.84), channel_id=1, source_target_pairs={{0,1},{1,2},{2,3},{4,5},{5,6},{6,7},{8,9},{9,10},{10,11},{12,13},{... | collective-permute-start | bytes 1572872 | tf_op jit(solution)/shard_map/ppermute | solution.py:261
  100.0 1.3 %collective-permute-start.21 = (f32[256,512]{1,0:T(8,128)S(1)}, f32[256,512]{1,0:T(8,128)S(1)}, u32[]{:S(2)}, u32[]{:S(2)}) collective-permute-start(f32[256,512]{1,0:T(8,128)S(1)} %get-tuple-element.85), channel_id=1, source_target_pairs={{1,0},{2,1},{3,2},{5,4},{6,5},{7,6},{9,8},{10,9},{11,10},{13,12},{... | collective-permute-start | bytes 1572872 | tf_op jit(solution)/shard_map/ppermute | solution.py:262
  101.3 4.1 %collective-permute-done.16 = f32[256,512]{1,0:T(8,128)} collective-permute-done((f32[256,512]{1,0:T(8,128)S(1)}, f32[256,512]{1,0:T(8,128)}, u32[]{:S(2)}, u32[]{:S(2)}) %collective-permute-start.16) | collective-permute-done | bytes 524320 | tf_op jit(solution)/shard_map/ppermute | solution.py:261
  105.4 0.0 collective-permute-done.19
  105.4 1.7 %dynamic-slice_add_fusion = (f32[256,512]{1,0:T(8,128)S(1)}, f32[256,512]{1,0:T(8,128)S(1)}) fusion(f32[256,512]{1,0:T(8,128)} %collective-permute-done.19, f32[256,4096]{1,0:T(8,128)} %copy-done.6, s32[]{:T(128)S(6)} %select_n.74, f32[256,512]{1,0:T(8,128)} %collective-permute-done.16, s32[]{:T(128)S(6)} %select_n.73), kind=kLoop, calls=%fused_computation.2 | loop fusion | flops 262144 | bytes 3145736 | tf_op jit(solution)/shard_map/add | solution.py:289
  107.1 5.3 %collective-permute-start.22 = (f32[256,512]{1,0:T(8,128)S(1)}, f32[256,512]{1,0:T(8,128)}, u32[]{:S(2)}, u32[]{:S(2)}) collective-permute-start(f32[256,512]{1,0:T(8,128)S(1)} %get-tuple-element.90), channel_id=1, source_target_pairs={{0,1},{1,2},{2,3},{4,5},{5,6},{6,7},{8,9},{9,10},{10,11},{12,13},{... | collective-permute-start | bytes 1572872 | tf_op jit(solution)/shard_map/ppermute | solution.py:261
  112.4 1.3 collective-permute-start.23
  113.7 2.9 %collective-permute-done.20 = f32[256,512]{1,0:T(8,128)S(1)} collective-permute-done((f32[256,512]{1,0:T(8,128)S(1)}, f32[256,512]{1,0:T(8,128)S(1)}, u32[]{:S(2)}, u32[]{:S(2)}) %collective-permute-start.20) | collective-permute-done | bytes 524320 | tf_op jit(solution)/shard_map/ppermute | solution.py:261
  116.6 0.0 collective-permute-done.21
  116.6 1.2 add_convert_fusion.1
  117.8 0.9 dynamic_update_slice.6
  118.6 8.4 %collective-permute-done.22 = f32[256,512]{1,0:T(8,128)} collective-permute-done((f32[256,512]{1,0:T(8,128)S(1)}, f32[256,512]{1,0:T(8,128)}, u32[]{:S(2)}, u32[]{:S(2)}) %collective-permute-start.22) | collective-permute-done | bytes 524320 | tf_op jit(solution)/shard_map/ppermute | solution.py:261
  127.0 0.0 collective-permute-done.23
  127.0 2.2 %fusion = bf16[256,1024]{1,0:T(8,128)(2,1)} fusion(bf16[256,1024]{1,0:T(8,128)(2,1)} %dynamic_update_slice.6, f32[256,512]{1,0:T(8,128)} %collective-permute-done.23, f32[256,512]{1,0:T(8,128)} %collective-permute-done.22, f32[256,4096]{1,0:T(8,128)} %copy-done.6, s32[]{:T(128)S(6)} %select_n.76), kind=kLoop, calls=%fused_computation.10 | loop fusion | flops 393216 | bytes 1835012 | tf_op jit(solution)/shard_map/dynamic_update_slice | solution.py:295
  (11 shorter events, 0.0 us)
Async XLA Ops:
  0.0 19.4 %copy-start = (bf16[512,768]{1,0:T(8,128)(2,1)S(1)}, bf16[512,768]{1,0:T(8,128)(2,1)}, u32[]{:S(2)}) copy-start(bf16[512,768]{1,0:T(8,128)(2,1)} %constant.47.clone.ahead_ref) | copy-start | bytes 2359300
  2.7 7.3 %collective-permute-start = (f32[256,256]{1,0:T(8,128)}, f32[256,256]{1,0:T(8,128)S(1)}, u32[]{:S(2)}, u32[]{:S(2)}) collective-permute-start(f32[256,256]{1,0:T(8,128)} %get-tuple-element.52), channel_id=1, source_target_pairs={{0,4},{4,0},{8,12},{12,8},{16,20},{20,16},{24,28},{28,24},{1,5},{5... | collective-permute-start | bytes 786440 | tf_op jit(solution)/shard_map/ppermute | solution.py:93
  3.2 11.0 %collective-permute-start.1 = (f32[256,256]{1,0:T(8,128)}, f32[256,256]{1,0:T(8,128)S(1)}, u32[]{:S(2)}, u32[]{:S(2)}) collective-permute-start(f32[256,256]{1,0:T(8,128)} %get-tuple-element.53), channel_id=1, source_target_pairs={{0,24},{4,28},{8,16},{12,20},{16,8},{20,12},{24,0},{28,4},{1,25},{... | collective-permute-start | bytes 786440 | tf_op jit(solution)/shard_map/ppermute | solution.py:93
  6.7 12.7 %collective-permute-start.2 = (f32[256,256]{1,0:T(8,128)}, f32[256,256]{1,0:T(8,128)}, u32[]{:S(2)}, u32[]{:S(2)}) collective-permute-start(f32[256,256]{1,0:T(8,128)} %get-tuple-element.54), channel_id=1, source_target_pairs={{0,28},{4,24},{8,20},{12,16},{16,12},{20,8},{24,4},{28,0},{1,29},{... | collective-permute-start | bytes 786440 | tf_op jit(solution)/shard_map/ppermute | solution.py:93
  6.8 19.0 %collective-permute-start.3 = (f32[256,256]{1,0:T(8,128)}, f32[256,256]{1,0:T(8,128)S(1)}, u32[]{:S(2)}, u32[]{:S(2)}) collective-permute-start(f32[256,256]{1,0:T(8,128)} %get-tuple-element.55), channel_id=1, source_target_pairs={{0,8},{4,12},{8,0},{12,4},{16,24},{20,28},{24,16},{28,20},{1,9},{5... | collective-permute-start | bytes 786440 | tf_op jit(solution)/shard_map/ppermute | solution.py:93
  8.4 17.4 %collective-permute-start.4 = (f32[256,256]{1,0:T(8,128)}, f32[256,256]{1,0:T(8,128)S(1)}, u32[]{:S(2)}, u32[]{:S(2)}) collective-permute-start(f32[256,256]{1,0:T(8,128)} %get-tuple-element.56), channel_id=1, source_target_pairs={{0,16},{4,20},{8,24},{12,28},{16,0},{20,4},{24,8},{28,12},{1,17},{... | collective-permute-start | bytes 786440 | tf_op jit(solution)/shard_map/ppermute | solution.py:93
  10.0 0.7 copy-start.2
  10.7 19.9 %collective-permute-start.5 = (f32[256,256]{1,0:T(8,128)}, f32[256,256]{1,0:T(8,128)}, u32[]{:S(2)}, u32[]{:S(2)}) collective-permute-start(f32[256,256]{1,0:T(8,128)} %get-tuple-element.57), channel_id=1, source_target_pairs={{0,12},{4,8},{8,4},{12,0},{16,28},{20,24},{24,20},{28,16},{1,13},{... | collective-permute-start | bytes 786440 | tf_op jit(solution)/shard_map/ppermute | solution.py:93
  14.2 0.7 copy-start.4
  14.9 15.8 %collective-permute-start.6 = (f32[256,256]{1,0:T(8,128)}, f32[256,256]{1,0:T(8,128)}, u32[]{:S(2)}, u32[]{:S(2)}) collective-permute-start(f32[256,256]{1,0:T(8,128)} %get-tuple-element.58), channel_id=1, source_target_pairs={{0,20},{4,16},{8,28},{12,24},{16,4},{20,0},{24,12},{28,8},{1,21},{... | collective-permute-start | bytes 786440 | tf_op jit(solution)/shard_map/ppermute | solution.py:93
  15.6 3.8 %copy-start.1 = (f32[256,256]{1,0:T(8,128)S(1)}, f32[256,256]{1,0:T(8,128)}, u32[]{:S(2)}) copy-start(f32[256,256]{1,0:T(8,128)} %get-tuple-element.51.refs_0_) | copy-start | bytes 786436
  15.6 3.8 %copy-start.3 = (f32[256,256]{1,0:T(8,128)S(1)}, f32[256,256]{1,0:T(8,128)}, u32[]{:S(2)}) copy-start(f32[256,256]{1,0:T(8,128)} %copy-done.2) | copy-start | bytes 786436
  15.6 3.8 %copy-start.5 = (f32[256,256]{1,0:T(8,128)S(1)}, f32[256,256]{1,0:T(8,128)}, u32[]{:S(2)}) copy-start(f32[256,256]{1,0:T(8,128)} %copy-done.4) | copy-start | bytes 786436
  37.7 5.7 %collective-permute-start.10 = (f32[256,128]{1,0:T(8,128)S(1)}, f32[256,128]{1,0:T(8,128)S(1)}, u32[]{:S(2)}, u32[]{:S(2)}) collective-permute-start(f32[256,128]{1,0:T(8,128)S(1)} %get-tuple-element.63), channel_id=1, source_target_pairs={{0,8},{4,12},{8,0},{12,4},{16,24},{20,28},{24,16},{28,20},{1,9},{5... | collective-permute-start | bytes 393224 | tf_op jit(solution)/shard_map/ppermute | solution.py:93
  39.4 7.3 %collective-permute-start.11 = (f32[256,128]{1,0:T(8,128)S(1)}, f32[256,128]{1,0:T(8,128)S(1)}, u32[]{:S(2)}, u32[]{:S(2)}) collective-permute-start(f32[256,128]{1,0:T(8,128)S(1)} %get-tuple-element.64), channel_id=1, source_target_pairs={{0,16},{4,20},{8,24},{12,28},{16,0},{20,4},{24,8},{28,12},{1,17},{... | collective-permute-start | bytes 393224 | tf_op jit(solution)/shard_map/ppermute | solution.py:93
  40.9 5.8 %collective-permute-start.12 = (f32[256,128]{1,0:T(8,128)}, f32[256,128]{1,0:T(8,128)S(1)}, u32[]{:S(2)}, u32[]{:S(2)}) collective-permute-start(f32[256,128]{1,0:T(8,128)} %get-tuple-element.65), channel_id=1, source_target_pairs={{0,12},{4,8},{8,4},{12,0},{16,28},{20,24},{24,20},{28,16},{1,13},{... | collective-permute-start | bytes 393224 | tf_op jit(solution)/shard_map/ppermute | solution.py:93
  41.0 11.3 %collective-permute-start.13 = (f32[256,128]{1,0:T(8,128)}, f32[256,128]{1,0:T(8,128)S(1)}, u32[]{:S(2)}, u32[]{:S(2)}) collective-permute-start(f32[256,128]{1,0:T(8,128)} %get-tuple-element.66), channel_id=1, source_target_pairs={{0,20},{4,16},{8,28},{12,24},{16,4},{20,0},{24,12},{28,8},{1,21},{... | collective-permute-start | bytes 393224 | tf_op jit(solution)/shard_map/ppermute | solution.py:93
  41.5 10.8 %collective-permute-start.7 = (f32[256,128]{1,0:T(8,128)}, f32[256,128]{1,0:T(8,128)S(1)}, u32[]{:S(2)}, u32[]{:S(2)}) collective-permute-start(f32[256,128]{1,0:T(8,128)} %get-tuple-element.60), channel_id=1, source_target_pairs={{0,4},{4,0},{8,12},{12,8},{16,20},{20,16},{24,28},{28,24},{1,5},{5... | collective-permute-start | bytes 393224 | tf_op jit(solution)/shard_map/ppermute | solution.py:93
  43.3 8.9 %collective-permute-start.8 = (f32[256,128]{1,0:T(8,128)}, f32[256,128]{1,0:T(8,128)S(1)}, u32[]{:S(2)}, u32[]{:S(2)}) collective-permute-start(f32[256,128]{1,0:T(8,128)} %get-tuple-element.61), channel_id=1, source_target_pairs={{0,24},{4,28},{8,16},{12,20},{16,8},{20,12},{24,0},{28,4},{1,25},{... | collective-permute-start | bytes 393224 | tf_op jit(solution)/shard_map/ppermute | solution.py:93
  46.7 6.2 %collective-permute-start.9 = (f32[256,128]{1,0:T(8,128)}, f32[256,128]{1,0:T(8,128)S(1)}, u32[]{:S(2)}, u32[]{:S(2)}) collective-permute-start(f32[256,128]{1,0:T(8,128)} %get-tuple-element.62), channel_id=1, source_target_pairs={{0,28},{4,24},{8,20},{12,16},{16,12},{20,8},{24,4},{28,0},{1,29},{... | collective-permute-start | bytes 393224 | tf_op jit(solution)/shard_map/ppermute | solution.py:93
  55.9 15.8 %collective-permute-start.15 = (f32[256,512]{1,0:T(8,128)S(1)}, f32[256,512]{1,0:T(8,128)S(1)}, u32[]{:S(2)}, u32[]{:S(2)}) collective-permute-start(f32[256,512]{1,0:T(8,128)S(1)} %get-tuple-element.68), channel_id=1, source_target_pairs={{0,1},{3,2},{4,5},{7,6},{8,9},{11,10},{12,13},{15,14},{16,17},{19,... | collective-permute-start | bytes 1572872 | tf_op jit(solution)/shard_map/ppermute | solution.py:270
  59.4 23.6 %collective-permute-start.14 = (f32[256,512]{1,0:T(8,128)}, f32[256,512]{1,0:T(8,128)}, u32[]{:S(2)}, u32[]{:S(2)}) collective-permute-start(f32[256,512]{1,0:T(8,128)} %get-tuple-element.67), channel_id=1, source_target_pairs={{0,1},{3,2},{4,5},{7,6},{8,9},{11,10},{12,13},{15,14},{16,17},{19,... | collective-permute-start | bytes 1572872 | tf_op jit(solution)/shard_map/ppermute | solution.py:270
  67.3 4.4 %copy-start.6 = (f32[256,4096]{1,0:T(8,128)}, f32[256,4096]{1,0:T(8,128)S(1)}, u32[]{:S(2)}) copy-start(f32[256,4096]{1,0:T(8,128)S(1)} %fusion.1) | copy-start | bytes 12582916
  71.9 22.3 %collective-permute-start.17 = (f32[256,512]{1,0:T(8,128)S(1)}, f32[256,512]{1,0:T(8,128)S(1)}, u32[]{:S(2)}, u32[]{:S(2)}) collective-permute-start(f32[256,512]{1,0:T(8,128)S(1)} %get-tuple-element.76), channel_id=1, source_target_pairs={{0,1},{1,2},{4,5},{5,6},{8,9},{9,10},{12,13},{13,14},{16,17},{17,1... | collective-permute-start | bytes 1572872 | tf_op jit(solution)/shard_map/ppermute | solution.py:261
  76.3 17.9 %collective-permute-start.18 = (f32[256,512]{1,0:T(8,128)S(1)}, f32[256,512]{1,0:T(8,128)S(1)}, u32[]{:S(2)}, u32[]{:S(2)}) collective-permute-start(f32[256,512]{1,0:T(8,128)S(1)} %get-tuple-element.78), channel_id=1, source_target_pairs={{2,1},{3,2},{6,5},{7,6},{10,9},{11,10},{14,13},{15,14},{18,17},{19... | collective-permute-start | bytes 1572872 | tf_op jit(solution)/shard_map/ppermute | solution.py:262
  84.5 20.8 %collective-permute-start.16 = (f32[256,512]{1,0:T(8,128)S(1)}, f32[256,512]{1,0:T(8,128)}, u32[]{:S(2)}, u32[]{:S(2)}) collective-permute-start(f32[256,512]{1,0:T(8,128)S(1)} %get-tuple-element.73), channel_id=1, source_target_pairs={{0,1},{1,2},{4,5},{5,6},{8,9},{9,10},{12,13},{13,14},{16,17},{17,1... | collective-permute-start | bytes 1572872 | tf_op jit(solution)/shard_map/ppermute | solution.py:261
  89.7 15.6 %collective-permute-start.19 = (f32[256,512]{1,0:T(8,128)S(1)}, f32[256,512]{1,0:T(8,128)}, u32[]{:S(2)}, u32[]{:S(2)}) collective-permute-start(f32[256,512]{1,0:T(8,128)S(1)} %get-tuple-element.80), channel_id=1, source_target_pairs={{2,1},{3,2},{6,5},{7,6},{10,9},{11,10},{14,13},{15,14},{18,17},{19... | collective-permute-start | bytes 1572872 | tf_op jit(solution)/shard_map/ppermute | solution.py:262
  95.6 21.1 %collective-permute-start.20 = (f32[256,512]{1,0:T(8,128)S(1)}, f32[256,512]{1,0:T(8,128)S(1)}, u32[]{:S(2)}, u32[]{:S(2)}) collective-permute-start(f32[256,512]{1,0:T(8,128)S(1)} %get-tuple-element.84), channel_id=1, source_target_pairs={{0,1},{1,2},{2,3},{4,5},{5,6},{6,7},{8,9},{9,10},{10,11},{12,13},{... | collective-permute-start | bytes 1572872 | tf_op jit(solution)/shard_map/ppermute | solution.py:261
  100.0 16.6 %collective-permute-start.21 = (f32[256,512]{1,0:T(8,128)S(1)}, f32[256,512]{1,0:T(8,128)S(1)}, u32[]{:S(2)}, u32[]{:S(2)}) collective-permute-start(f32[256,512]{1,0:T(8,128)S(1)} %get-tuple-element.85), channel_id=1, source_target_pairs={{1,0},{2,1},{3,2},{5,4},{6,5},{7,6},{9,8},{10,9},{11,10},{13,12},{... | collective-permute-start | bytes 1572872 | tf_op jit(solution)/shard_map/ppermute | solution.py:262
  107.1 19.9 %collective-permute-start.22 = (f32[256,512]{1,0:T(8,128)S(1)}, f32[256,512]{1,0:T(8,128)}, u32[]{:S(2)}, u32[]{:S(2)}) collective-permute-start(f32[256,512]{1,0:T(8,128)S(1)} %get-tuple-element.90), channel_id=1, source_target_pairs={{0,1},{1,2},{2,3},{4,5},{5,6},{6,7},{8,9},{9,10},{10,11},{12,13},{... | collective-permute-start | bytes 1572872 | tf_op jit(solution)/shard_map/ppermute | solution.py:261
  112.4 14.6 %collective-permute-start.23 = (f32[256,512]{1,0:T(8,128)S(1)}, f32[256,512]{1,0:T(8,128)}, u32[]{:S(2)}, u32[]{:S(2)}) collective-permute-start(f32[256,512]{1,0:T(8,128)S(1)} %get-tuple-element.91), channel_id=1, source_target_pairs={{1,0},{2,1},{3,2},{5,4},{6,5},{7,6},{9,8},{10,9},{11,10},{13,12},{... | collective-permute-start | bytes 1572872 | tf_op jit(solution)/shard_map/ppermute | solution.py:262

commit v5 on v3

--- a/solution.py
+++ b/solution.py
@@ -12,6 +12,10 @@
 
 F32 = jnp.float32
 BF16 = jnp.bfloat16
+
+
+def stay(array):
+    return pltpu.with_memory_space_constraint(array, pltpu.MemorySpace.HBM)
 
 
 def room(*shapes):
@@ -76,7 +80,7 @@
         out_shape=[jax.ShapeDtypeStruct((rows, wide), F32)] * count,
         scratch_shapes=[pltpu.VMEM((count, step, wide), F32)],
         compiler_params=pltpu.CompilerParams(vmem_limit_bytes=56 * 1024 * 1024),
-    )(place, keys, values, filt, direct)
+    )(place, stay(keys), stay(values), stay(filt), stay(direct))
 
 
 def turns(count):
@@ -164,7 +168,7 @@
     rows, width = xs[0].shape
     chans = width // 2
     ahead, back = (jnp.asarray(table) for table in tables(rows))
-    first = count // 2
+    first = max(1, count - 2)
     early = forward(xs[:first], ahead)
     whole = pl.BlockSpec(memory_space=pltpu.VMEM)
     return pl.pallas_call(
@@ -173,7 +177,7 @@
         + [whole] * (count - first + 2)
         + [pl.BlockSpec(memory_space=pl.ANY)],
         out_specs=[whole] * count,
-        out_shape=[jax.ShapeDtypeStruct((rows, chans), F32)] * count,
+        out_shape=[pltpu.VMEM((rows, chans), F32)] * count,
         scratch_shapes=[
             pltpu.VMEM((count, 2 * rows, width), F32),
             pltpu.VMEM((count, 2 * rows, chans), F32),
@@ -183,17 +187,16 @@
         compiler_params=room(
             (count, 2 * rows, width), *[(count, 2 * rows, chans)] * 2, (count, rows, width)
         ),
-    )(place, early, *xs[first:], ahead, back)
+    )(place, early, *xs[first:], ahead, stay(back))
 
 
 CHAINS = 2
 
 
 def gate_kernel(place_ref, far_ref, q_hbm, *refs):
-    count = len(refs) - 4 - CHAINS
-    convs, (gated_ref, *firsts), (q_ref, conv_ref, in_sem) = refs[:count], refs[count:-3], refs[-3:]
+    count = len(refs) - 5
+    convs, (gated_ref, first_ref), (q_ref, conv_ref, in_sem) = refs[:count], refs[count:-3], refs[-3:]
     chans = convs[0].shape[1]
-    width = far_ref.shape[1] // CHAINS
     into = [pltpu.make_async_copy(q_hbm, q_ref, in_sem.at[count])]
     into += [
         pltpu.make_async_copy(conv, conv_ref.at[turn ^ place_ref[0]], in_sem.at[j])
@@ -206,9 +209,7 @@
     for group in range(count):
         cols = slice(group * chans, (group + 1) * chans)
         gated_ref[:, cols] = (q_ref[:, cols].astype(F32) * conv_ref[group]).astype(BF16)
-    for k, out in enumerate(firsts):
-        cols = slice(k * width, (k + 1) * width)
-        out[...] = jnp.dot(gated_ref[...], far_ref[:, cols], preferred_element_type=F32)
+    first_ref[...] = jnp.dot(gated_ref[...], far_ref[...], preferred_element_type=F32)
 
 
 def gate(place, query, far, convs):
@@ -216,27 +217,20 @@
     count = len(convs)
     here = pl.BlockSpec(memory_space=pltpu.VMEM)
     there = pl.BlockSpec(memory_space=pl.ANY)
-    part = (rows, far.shape[1] // CHAINS)
+    part = (rows, far.shape[1])
     blocks = (count,) + convs[0].shape
-    out = pl.pallas_call(
+    return pl.pallas_call(
         gate_kernel,
         in_specs=[pl.BlockSpec(memory_space=pltpu.SMEM), here] + [there] * (1 + count),
-        out_specs=[here] * (1 + CHAINS),
-        out_shape=[jax.ShapeDtypeStruct((rows, width), BF16)]
-        + [jax.ShapeDtypeStruct(part, F32)] * CHAINS,
+        out_specs=[here, here],
+        out_shape=[pltpu.VMEM((rows, width), BF16), pltpu.VMEM(part, F32)],
         scratch_shapes=[
             pltpu.VMEM((rows, width), BF16),
             pltpu.VMEM(blocks, F32),
             pltpu.SemaphoreType.DMA((count + 1,)),
         ],
-        compiler_params=room(*[(rows, width)] * 2, far.shape, blocks, (CHAINS,) + part),
-    )(place, far, query, *convs)
-    return out[0], out[1:]
-
-
-def column_block(array, index, size):
-    width = array.shape[1] // size
-    return lax.dynamic_slice_in_dim(array, jnp.clip(index, 0, size - 1) * width, width, 1)
+        compiler_params=room(*[(rows, width)] * 2, far.shape, blocks, part),
+    )(place, far, stay(query), *convs)
 
 
 def pass_on(up, down, step, size):
@@ -256,18 +250,24 @@
     return jnp.where(place == 1, got, 0.0), jnp.where(place == size - 2, got, 0.0)
 
 
+def far_end(size):
+    return jnp.where(lax.axis_index("tp") == 0, size - 1, 0)
+
+
 def scatter_dot(lhs, rhs, first):
     size = lax.axis_size("tp")
     place = lax.axis_index("tp")
-    rows, width = first[0].shape
+    rows, width = first.shape
     lhs, first = lax.optimization_barrier((lhs, first))
-    sums = [first_step(value, size) for value in first]
     terms = jnp.dot(lhs, rhs, preferred_element_type=F32)
 
     def own(index, k):
         start = jnp.clip(index, 0, size - 1) * (width * CHAINS) + k * width
         return lax.dynamic_slice_in_dim(terms, start, width, 1)
 
+    firsts = [first] + [own(far_end(size), k) for k in range(1, CHAINS)]
+    firsts[1:], terms = lax.optimization_barrier((firsts[1:], terms))
+    sums = [first_step(value, size) for value in firsts]
     for step in range(2, size):
         for k in range(CHAINS):
             up = sums[k][0] + own(place + size - step, k)
@@ -287,7 +287,8 @@
     size = lax.axis_size("tp")
     place = lax.axis_index("ctx").reshape(1)
     xs = swap(pack(place, keys, values, filt, direct.reshape(1, -1), count))
-    far = column_block(w_out, jnp.where(lax.axis_index("tp") == 0, size - 1, 0), size)
+    part = w_out.shape[1] // (size * CHAINS)
+    far = lax.dynamic_slice_in_dim(w_out, far_end(size) * (part * CHAINS), part, 1)
     xs[0], far = lax.optimization_barrier((xs[0], far))
     convs = swap(convolve(place, xs))
     gated, first = gate(place, query, far, convs)

time: 130 us -> 125 us (0.962)
  Pallas kernels: 13.3 us -> 10.2 us
  waiting for transfers between devices: 51.6 us -> 48.7 us
    ppermute x2, waiting for transfers between devices: 10.4 us -> 7.13 us  [first_step(): got = lax.ppermute(value, 'tp', [(0, 1), (size - 1, size - 2)])]
    pallas_call x1, Pallas kernels: 5.61 us -> 3.29 us  [convolve(): pl.pallas_call(conv_kernel, in_specs=[pl.BlockSpec(memory_space=pltpu.SME...]
    unnamed x18 -> x6, local copies, waits for them, and re-layouts: 2.54 us -> 2.9 us
  transfers between devices with their start and end apart: 24 -> 24, of which waited for: 14 -> 14; matrix products, arithmetic and copies ran while one was open for 11% -> 12% of each run, Pallas kernels for 2% -> 2%
where the time goes in v5:
time: 125 us; the launch traced here: 124 us
  waiting for transfers between devices  48.7 us (39%)
  starting transfers between devices  45.1 us (36%)
  Pallas kernels  10.2 us (8%)
  other arithmetic  9.36 us (7%)
  matrix products  5.72 us (5%)
  local copies, waits for them, and re-layouts  5.09 us (4%)
    ppermute x14, waiting for transfers between devices, swap(): lax.ppermute(arrays[j], 'ctx', pairs[j])  23.3 us
    ppermute x4, starting transfers between devices, pass_on(): up = lax.ppermute(up, 'tp', rise)  19.5 us
    ppermute x4, waiting for transfers between devices, pass_on(): up = lax.ppermute(up, 'tp', rise)  18.3 us
    ppermute x14, starting transfers between devices, swap(): lax.ppermute(arrays[j], 'ctx', pairs[j])  15.3 us
    ppermute x2, waiting for transfers between devices, first_step(): got = lax.ppermute(value, 'tp', [(0, 1), (size - 1, size - 2)])  7.13 us
    add x4, other arithmetic, scatter_dot(): down = sums[k][1] + own(place - size + step, k)  6.03 us
    dot_general x1, matrix products, scatter_dot(): terms = jnp.dot(lhs, rhs, preferred_element_type=F32)  5.72 us
    ppermute x2, starting transfers between devices, first_step(): got = lax.ppermute(value, 'tp', [(0, 1), (size - 1, size - 2)])  5.62 us
  transfers between devices with their start and end apart: 24, of which 14 were waited for; matrix products, arithmetic and copies ran while one was open for 12% of the time, Pallas kernels for 2%

profile of v5, /device:TPU:0, one launch (start us, length us, event | category | flops | bytes accessed | tf_op | source)
XLA Modules:
  0.0 124.3 jit_solution(1866509172682104928)
XLA Ops:
  0.0 2.7 %shard_map.82 = (f32[256,256]{1,0:T(8,128)}, f32[256,256]{1,0:T(8,128)}, f32[256,256]{1,0:T(8,128)}, f32[256,256]{1,0:T(8,128)}, f32[256,256]{1,0:T(8,128)}, /*i...) custom-call(s32[1]{0:T(128)} %bitcast.place_ref, bf16[256,1024]{1,0:T(8,128)(2,1)} %keys_ref.1, ...), custom_call_target="tpu_custom_call" | custom-call | tf_op jit(solution)/shard_map/pallas_call | solution.py:74
  2.7 0.5 collective-permute-start
  3.2 3.5 %collective-permute-start.1 = (f32[256,256]{1,0:T(8,128)}, f32[256,256]{1,0:T(8,128)S(1)}, u32[]{:S(2)}, u32[]{:S(2)}) collective-permute-start(f32[256,256]{1,0:T(8,128)} %get-tuple-element.54), channel_id=1, source_target_pairs={{0,24},{4,28},{8,16},{12,20},{16,8},{20,12},{24,0},{28,4},{1,25},{... | collective-permute-start | bytes 786440 | tf_op jit(solution)/shard_map/ppermute | solution.py:93
  6.7 0.1 collective-permute-start.2
  6.8 1.7 %collective-permute-start.3 = (f32[256,256]{1,0:T(8,128)}, f32[256,256]{1,0:T(8,128)S(1)}, u32[]{:S(2)}, u32[]{:S(2)}) collective-permute-start(f32[256,256]{1,0:T(8,128)} %get-tuple-element.56), channel_id=1, source_target_pairs={{0,8},{4,12},{8,0},{12,4},{16,24},{20,28},{24,16},{28,20},{1,9},{5... | collective-permute-start | bytes 786440 | tf_op jit(solution)/shard_map/ppermute | solution.py:93
  8.5 1.5 %collective-permute-start.4 = (f32[256,256]{1,0:T(8,128)}, f32[256,256]{1,0:T(8,128)}, u32[]{:S(2)}, u32[]{:S(2)}) collective-permute-start(f32[256,256]{1,0:T(8,128)} %get-tuple-element.57), channel_id=1, source_target_pairs={{0,16},{4,20},{8,24},{12,28},{16,0},{20,4},{24,8},{28,12},{1,17},{... | collective-permute-start | bytes 786440 | tf_op jit(solution)/shard_map/ppermute | solution.py:93
  10.0 0.0 collective-permute-done.refs_1_
  10.0 0.0 collective-permute-start.5
  10.0 4.2 %collective-permute-done.1.refs_2_ = f32[256,256]{1,0:T(8,128)S(1)} collective-permute-done((f32[256,256]{1,0:T(8,128)}, f32[256,256]{1,0:T(8,128)S(1)}, u32[]{:S(2)}, u32[]{:S(2)}) %collective-permute-start.1) | collective-permute-done | bytes 262176 | tf_op jit(solution)/shard_map/ppermute | solution.py:93
  14.2 0.7 collective-permute-start.6
  14.9 1.3 %constant_dynamic-slice_fusion.1.far_ref = bf16[1024,512]{1,0:T(8,128)(2,1)S(1)} fusion(bf16[1024,4096]{1,0:T(8,128)(2,1)} %param.13, s32[]{:T(128)S(6)} %select_n.67), kind=kLoop, calls=%fused_computation.12 | loop fusion | bytes 2097156 | tf_op jit(solution)/shard_map/dynamic_slice | solution.py:291
  16.2 3.2 %collective-permute-done.2.refs_3_ = f32[256,256]{1,0:T(8,128)S(1)} collective-permute-done((f32[256,256]{1,0:T(8,128)}, f32[256,256]{1,0:T(8,128)S(1)}, u32[]{:S(2)}, u32[]{:S(2)}) %collective-permute-start.2) | collective-permute-done | bytes 262176 | tf_op jit(solution)/shard_map/ppermute | solution.py:93
  19.3 6.5 %collective-permute-done.3.refs_4_ = f32[256,256]{1,0:T(8,128)S(1)} collective-permute-done((f32[256,256]{1,0:T(8,128)}, f32[256,256]{1,0:T(8,128)S(1)}, u32[]{:S(2)}, u32[]{:S(2)}) %collective-permute-start.3) | collective-permute-done | bytes 262176 | tf_op jit(solution)/shard_map/ppermute | solution.py:93
  25.8 0.0 collective-permute-done.4.refs_5_
  25.8 0.0 copy-done
  25.8 0.9 copy-done.1
  26.8 2.3 %shard_map.83.early_ref = f32[6,512,256]{2,1,0:T(8,128)S(1)} custom-call(bf16[512,768]{1,0:T(8,128)(2,1)S(1)} %copy-done, f32[256,256]{1,0:T(8,128)S(1)} %copy-done.1, f32[256,256]{1,0:T(8,128)S(1)} %collective-permute-done.refs_1_, f32[256,256]{1,0:T(8,128)S(1)} %collective-permute-done.1.refs_2_, f32[256,256]{1,0:T(8,128)S(1)} %collective-permute-done.2.refs_3_, ...), custom_call_target="tpu_custom_call" | custom-call | tf_op jit(solution)/shard_map/pallas_call | solution.py:104
  29.1 1.4 %collective-permute-done.5.refs_0_ = f32[256,256]{1,0:T(8,128)S(1)} collective-permute-done((f32[256,256]{1,0:T(8,128)}, f32[256,256]{1,0:T(8,128)S(1)}, u32[]{:S(2)}, u32[]{:S(2)}) %collective-permute-start.5) | collective-permute-done | bytes 262176 | tf_op jit(solution)/shard_map/ppermute | solution.py:93
  30.5 0.1 collective-permute-done.6.refs_1_
  30.6 3.3 %shard_map.84 = (f32[256,128]{1,0:T(8,128)S(1)}, f32[256,128]{1,0:T(8,128)S(1)}, f32[256,128]{1,0:T(8,128)S(1)}, f32[256,128]{1,0:T(8,128)S(1)}, f32[256,128]{1,...) custom-call(s32[1]{0:T(128)} %bitcast.place_ref, ...), custom_call_target="tpu_custom_call" | custom-call | tf_op jit(solution)/shard_map/pallas_call | solution.py:174
  33.9 1.8 %collective-permute-start.10 = (f32[256,128]{1,0:T(8,128)S(1)}, f32[256,128]{1,0:T(8,128)S(1)}, u32[]{:S(2)}, u32[]{:S(2)}) collective-permute-start(f32[256,128]{1,0:T(8,128)S(1)} %get-tuple-element.64), channel_id=1, source_target_pairs={{0,8},{4,12},{8,0},{12,4},{16,24},{20,28},{24,16},{28,20},{1,9},{5... | collective-permute-start | bytes 393224 | tf_op jit(solution)/shard_map/ppermute | solution.py:93
  35.6 1.5 %collective-permute-start.11 = (f32[256,128]{1,0:T(8,128)S(1)}, f32[256,128]{1,0:T(8,128)S(1)}, u32[]{:S(2)}, u32[]{:S(2)}) collective-permute-start(f32[256,128]{1,0:T(8,128)S(1)} %get-tuple-element.65), channel_id=1, source_target_pairs={{0,16},{4,20},{8,24},{12,28},{16,0},{20,4},{24,8},{28,12},{1,17},{... | collective-permute-start | bytes 393224 | tf_op jit(solution)/shard_map/ppermute | solution.py:93
  37.2 0.0 collective-permute-start.12
  37.2 0.6 collective-permute-start.13
  37.7 0.1 collective-permute-start.7
  37.8 1.7 %collective-permute-done.10.refs_4_ = f32[256,128]{1,0:T(8,128)S(1)} collective-permute-done((f32[256,128]{1,0:T(8,128)S(1)}, f32[256,128]{1,0:T(8,128)S(1)}, u32[]{:S(2)}, u32[]{:S(2)}) %collective-permute-start.10) | collective-permute-done | bytes 131104 | tf_op jit(solution)/shard_map/ppermute | solution.py:93
  39.6 3.4 %collective-permute-start.8 = (f32[256,128]{1,0:T(8,128)S(1)}, f32[256,128]{1,0:T(8,128)S(1)}, u32[]{:S(2)}, u32[]{:S(2)}) collective-permute-start(f32[256,128]{1,0:T(8,128)S(1)} %get-tuple-element.62), channel_id=1, source_target_pairs={{0,24},{4,28},{8,16},{12,20},{16,8},{20,12},{24,0},{28,4},{1,25},{... | collective-permute-start | bytes 393224 | tf_op jit(solution)/shard_map/ppermute | solution.py:93
  43.0 0.0 collective-permute-done.11.refs_5_
  43.0 0.0 collective-permute-start.9
  43.0 0.0 collective-permute-done.12.refs_6_
  43.0 5.4 %collective-permute-done.13.refs_7_ = f32[256,128]{1,0:T(8,128)S(1)} collective-permute-done((f32[256,128]{1,0:T(8,128)S(1)}, f32[256,128]{1,0:T(8,128)S(1)}, u32[]{:S(2)}, u32[]{:S(2)}) %collective-permute-start.13) | collective-permute-done | bytes 131104 | tf_op jit(solution)/shard_map/ppermute | solution.py:93
  48.4 0.0 collective-permute-done.7.refs_1_
  48.4 0.0 collective-permute-done.8.refs_2_
  48.4 0.8 collective-permute-done.9.refs_3_
  49.2 1.9 %shard_map.85 = (bf16[256,1024]{1,0:T(8,128)(2,1)S(1)}, f32[256,512]{1,0:T(8,128)S(1)}) custom-call(s32[1]{0:T(128)} %bitcast.place_ref, bf16[1024,512]{1,0:T(8,128)(2,1)S(1)} %constant_dynamic-slice_fusion.1.far_ref, bf16[256,1024]{1,0:T(8,128)(2,1)} %q_hbm.1, f32[256,128]{1,0:T(8,128)S(1)} %get-tuple-element.60.refs_0_, ...), custom_call_target="tpu_custom_call" | custom-call | tf_op jit(solution)/shard_map/pallas_call | solution.py:222
  51.1 3.5 %collective-permute-start.15 = (f32[256,512]{1,0:T(8,128)S(1)}, f32[256,512]{1,0:T(8,128)S(1)}, u32[]{:S(2)}, u32[]{:S(2)}) collective-permute-start(f32[256,512]{1,0:T(8,128)S(1)} %get-tuple-element.70), channel_id=1, source_target_pairs={{0,1},{3,2},{4,5},{7,6},{8,9},{11,10},{12,13},{15,14},{16,17},{19,... | collective-permute-start | bytes 1572872 | tf_op jit(solution)/shard_map/ppermute | solution.py:249
  54.6 5.7 %fusion.1 = f32[256,4096]{1,0:T(8,128)S(1)} fusion(bf16[256,1024]{1,0:T(8,128)(2,1)S(1)} %get-tuple-element.68, bf16[1024,4096]{1,0:T(8,128)(2,1)} %param.13), kind=kOutput, calls=%fused_computation.13 | convolution fusion | flops 2147483648 | bytes 13107200 | tf_op jit(solution)/shard_map/dot_general | solution.py:262
  60.3 1.9 %copy-done.2 = f32[256,4096]{1,0:T(8,128)} copy-done((f32[256,4096]{1,0:T(8,128)}, f32[256,4096]{1,0:T(8,128)S(1)}, u32[]{:S(2)}) %copy-start.2) | copy-done | bytes 4194328
  62.3 2.1 %collective-permute-start.14 = (f32[256,512]{1,0:T(8,128)S(1)}, f32[256,512]{1,0:T(8,128)}, u32[]{:S(2)}, u32[]{:S(2)}) collective-permute-start(f32[256,512]{1,0:T(8,128)S(1)} %constant_dynamic-slice_fusion), channel_id=1, source_target_pairs={{0,1},{3,2},{4,5},{7,6},{8,9},{11,10},{12,13},{15,14},{16,17},{19,... | collective-permute-start | bytes 1572872 | tf_op jit(solution)/shard_map/ppermute | solution.py:249
  64.4 2.4 %collective-permute-done.15 = f32[256,512]{1,0:T(8,128)S(1)} collective-permute-done((f32[256,512]{1,0:T(8,128)S(1)}, f32[256,512]{1,0:T(8,128)S(1)}, u32[]{:S(2)}, u32[]{:S(2)}) %collective-permute-start.15) | collective-permute-done | bytes 524320 | tf_op jit(solution)/shard_map/ppermute | solution.py:249
  66.8 1.4 %dynamic-slice_add_fusion.6 = (f32[256,512]{1,0:T(8,128)S(1)}, f32[256,512]{1,0:T(8,128)S(1)}) fusion(f32[256,4096]{1,0:T(8,128)} %copy-done.2, s32[]{:T(128)S(6)} %select_n.74, f32[256,512]{1,0:T(8,128)S(1)} %collective-permute-done.15, pred[]{:T(512)S(6)} %eq.14, s32[]{:T(128)S(6)} %select_n.71, pred[]{:T(512)S(6)} %eq.12), kind=kLoop, calls=%fused_computation.8 | loop fusion | flops 524288 | bytes 2621450 | tf_op jit(solution)/shard_map/add | solution.py:274
  68.2 4.4 %collective-permute-start.17 = (f32[256,512]{1,0:T(8,128)S(1)}, f32[256,512]{1,0:T(8,128)S(1)}, u32[]{:S(2)}, u32[]{:S(2)}) collective-permute-start(f32[256,512]{1,0:T(8,128)S(1)} %get-tuple-element.78), channel_id=1, source_target_pairs={{0,1},{1,2},{4,5},{5,6},{8,9},{9,10},{12,13},{13,14},{16,17},{17,1... | collective-permute-start | bytes 1572872 | tf_op jit(solution)/shard_map/ppermute | solution.py:240
  72.6 0.7 collective-permute-start.18
  73.3 4.7 %collective-permute-done.14 = f32[256,512]{1,0:T(8,128)} collective-permute-done((f32[256,512]{1,0:T(8,128)S(1)}, f32[256,512]{1,0:T(8,128)}, u32[]{:S(2)}, u32[]{:S(2)}) %collective-permute-start.14) | collective-permute-done | bytes 524320 | tf_op jit(solution)/shard_map/ppermute | solution.py:249
  78.0 1.5 %dynamic-slice_add_fusion.4 = (f32[256,512]{1,0:T(8,128)S(1)}, f32[256,512]{1,0:T(8,128)S(1)}) fusion(f32[256,4096]{1,0:T(8,128)} %copy-done.2, s32[]{:T(128)S(6)} %select_n.77, f32[256,512]{1,0:T(8,128)} %collective-permute-done.14, pred[]{:T(512)S(6)} %eq.14, s32[]{:T(128)S(6)} %select_n.75, pred[]{:T(512)S(6)} %eq.12), kind=kLoop, calls=%fused_computation.6 | loop fusion | flops 524288 | bytes 2621450 | tf_op jit(solution)/shard_map/add | solution.py:274
  79.6 5.3 %collective-permute-start.16 = (f32[256,512]{1,0:T(8,128)S(1)}, f32[256,512]{1,0:T(8,128)}, u32[]{:S(2)}, u32[]{:S(2)}) collective-permute-start(f32[256,512]{1,0:T(8,128)S(1)} %get-tuple-element.75), channel_id=1, source_target_pairs={{0,1},{1,2},{4,5},{5,6},{8,9},{9,10},{12,13},{13,14},{16,17},{17,1... | collective-permute-start | bytes 1572872 | tf_op jit(solution)/shard_map/ppermute | solution.py:240
  84.9 1.5 %collective-permute-start.19 = (f32[256,512]{1,0:T(8,128)S(1)}, f32[256,512]{1,0:T(8,128)}, u32[]{:S(2)}, u32[]{:S(2)}) collective-permute-start(f32[256,512]{1,0:T(8,128)S(1)} %get-tuple-element.82), channel_id=1, source_target_pairs={{2,1},{3,2},{6,5},{7,6},{10,9},{11,10},{14,13},{15,14},{18,17},{19... | collective-permute-start | bytes 1572872 | tf_op jit(solution)/shard_map/ppermute | solution.py:241
  86.4 2.9 %collective-permute-done.17 = f32[256,512]{1,0:T(8,128)S(1)} collective-permute-done((f32[256,512]{1,0:T(8,128)S(1)}, f32[256,512]{1,0:T(8,128)S(1)}, u32[]{:S(2)}, u32[]{:S(2)}) %collective-permute-start.17) | collective-permute-done | bytes 524320 | tf_op jit(solution)/shard_map/ppermute | solution.py:240
  89.3 0.0 collective-permute-done.18
  89.3 1.4 %dynamic-slice_add_fusion.2 = (f32[256,512]{1,0:T(8,128)S(1)}, f32[256,512]{1,0:T(8,128)S(1)}) fusion(f32[256,512]{1,0:T(8,128)S(1)} %collective-permute-done.18, f32[256,4096]{1,0:T(8,128)} %copy-done.2, s32[]{:T(128)S(6)} %select_n.79, f32[256,512]{1,0:T(8,128)S(1)} %collective-permute-done.17, s32[]{:T(128)S(6)} %select_n.78), kind=kLoop, calls=%fused_computation.4 | loop fusion | flops 262144 | bytes 3145736 | tf_op jit(solution)/shard_map/add | solution.py:274
  90.7 4.4 %collective-permute-start.20 = (f32[256,512]{1,0:T(8,128)S(1)}, f32[256,512]{1,0:T(8,128)S(1)}, u32[]{:S(2)}, u32[]{:S(2)}) collective-permute-start(f32[256,512]{1,0:T(8,128)S(1)} %get-tuple-element.86), channel_id=1, source_target_pairs={{0,1},{1,2},{2,3},{4,5},{5,6},{6,7},{8,9},{9,10},{10,11},{12,13},{... | collective-permute-start | bytes 1572872 | tf_op jit(solution)/shard_map/ppermute | solution.py:240
  95.1 1.3 %collective-permute-start.21 = (f32[256,512]{1,0:T(8,128)S(1)}, f32[256,512]{1,0:T(8,128)S(1)}, u32[]{:S(2)}, u32[]{:S(2)}) collective-permute-start(f32[256,512]{1,0:T(8,128)S(1)} %get-tuple-element.87), channel_id=1, source_target_pairs={{1,0},{2,1},{3,2},{5,4},{6,5},{7,6},{9,8},{10,9},{11,10},{13,12},{... | collective-permute-start | bytes 1572872 | tf_op jit(solution)/shard_map/ppermute | solution.py:241
  96.4 4.1 %collective-permute-done.16 = f32[256,512]{1,0:T(8,128)} collective-permute-done((f32[256,512]{1,0:T(8,128)S(1)}, f32[256,512]{1,0:T(8,128)}, u32[]{:S(2)}, u32[]{:S(2)}) %collective-permute-start.16) | collective-permute-done | bytes 524320 | tf_op jit(solution)/shard_map/ppermute | solution.py:240
  100.5 0.0 collective-permute-done.19
  100.5 1.7 %dynamic-slice_add_fusion = (f32[256,512]{1,0:T(8,128)S(1)}, f32[256,512]{1,0:T(8,128)S(1)}) fusion(f32[256,512]{1,0:T(8,128)} %collective-permute-done.19, f32[256,4096]{1,0:T(8,128)} %copy-done.2, s32[]{:T(128)S(6)} %select_n.81, f32[256,512]{1,0:T(8,128)} %collective-permute-done.16, s32[]{:T(128)S(6)} %select_n.80), kind=kLoop, calls=%fused_computation.2 | loop fusion | flops 262144 | bytes 3145736 | tf_op jit(solution)/shard_map/add | solution.py:274
  102.3 5.3 %collective-permute-start.22 = (f32[256,512]{1,0:T(8,128)S(1)}, f32[256,512]{1,0:T(8,128)}, u32[]{:S(2)}, u32[]{:S(2)}) collective-permute-start(f32[256,512]{1,0:T(8,128)S(1)} %get-tuple-element.92), channel_id=1, source_target_pairs={{0,1},{1,2},{2,3},{4,5},{5,6},{6,7},{8,9},{9,10},{10,11},{12,13},{... | collective-permute-start | bytes 1572872 | tf_op jit(solution)/shard_map/ppermute | solution.py:240
  107.6 1.3 %collective-permute-start.23 = (f32[256,512]{1,0:T(8,128)S(1)}, f32[256,512]{1,0:T(8,128)}, u32[]{:S(2)}, u32[]{:S(2)}) collective-permute-start(f32[256,512]{1,0:T(8,128)S(1)} %get-tuple-element.93), channel_id=1, source_target_pairs={{1,0},{2,1},{3,2},{5,4},{6,5},{7,6},{9,8},{10,9},{11,10},{13,12},{... | collective-permute-start | bytes 1572872 | tf_op jit(solution)/shard_map/ppermute | solution.py:241
  108.9 2.9 %collective-permute-done.20 = f32[256,512]{1,0:T(8,128)S(1)} collective-permute-done((f32[256,512]{1,0:T(8,128)S(1)}, f32[256,512]{1,0:T(8,128)S(1)}, u32[]{:S(2)}, u32[]{:S(2)}) %collective-permute-start.20) | collective-permute-done | bytes 524320 | tf_op jit(solution)/shard_map/ppermute | solution.py:240
  111.8 0.0 collective-permute-done.21
  111.8 1.2 add_convert_fusion.1
  112.9 0.9 dynamic_update_slice.6
  113.8 8.4 %collective-permute-done.22 = f32[256,512]{1,0:T(8,128)} collective-permute-done((f32[256,512]{1,0:T(8,128)S(1)}, f32[256,512]{1,0:T(8,128)}, u32[]{:S(2)}, u32[]{:S(2)}) %collective-permute-start.22) | collective-permute-done | bytes 524320 | tf_op jit(solution)/shard_map/ppermute | solution.py:240
  122.2 0.0 collective-permute-done.23
  122.2 2.2 %fusion = bf16[256,1024]{1,0:T(8,128)(2,1)} fusion(bf16[256,1024]{1,0:T(8,128)(2,1)} %dynamic_update_slice.6, f32[256,512]{1,0:T(8,128)} %collective-permute-done.23, f32[256,512]{1,0:T(8,128)} %collective-permute-done.22, f32[256,4096]{1,0:T(8,128)} %copy-done.2, s32[]{:T(128)S(6)} %select_n.83), kind=kLoop, calls=%fused_computation.10 | loop fusion | flops 393216 | bytes 1835012 | tf_op jit(solution)/shard_map/dynamic_update_slice | solution.py:280
  (4 shorter events, 0.0 us)
Async XLA Ops:
  0.0 25.8 %copy-start = (bf16[512,768]{1,0:T(8,128)(2,1)S(1)}, bf16[512,768]{1,0:T(8,128)(2,1)}, u32[]{:S(2)}) copy-start(bf16[512,768]{1,0:T(8,128)(2,1)} %constant.48.clone.ahead_ref.refs_2_) | copy-start | bytes 2359300
  2.7 7.3 %collective-permute-start = (f32[256,256]{1,0:T(8,128)}, f32[256,256]{1,0:T(8,128)S(1)}, u32[]{:S(2)}, u32[]{:S(2)}) collective-permute-start(f32[256,256]{1,0:T(8,128)} %get-tuple-element.53), channel_id=1, source_target_pairs={{0,4},{4,0},{8,12},{12,8},{16,20},{20,16},{24,28},{28,24},{1,5},{5... | collective-permute-start | bytes 786440 | tf_op jit(solution)/shard_map/ppermute | solution.py:93
  3.2 11.0 %collective-permute-start.1 = (f32[256,256]{1,0:T(8,128)}, f32[256,256]{1,0:T(8,128)S(1)}, u32[]{:S(2)}, u32[]{:S(2)}) collective-permute-start(f32[256,256]{1,0:T(8,128)} %get-tuple-element.54), channel_id=1, source_target_pairs={{0,24},{4,28},{8,16},{12,20},{16,8},{20,12},{24,0},{28,4},{1,25},{... | collective-permute-start | bytes 786440 | tf_op jit(solution)/shard_map/ppermute | solution.py:93
  6.7 12.6 %collective-permute-start.2 = (f32[256,256]{1,0:T(8,128)}, f32[256,256]{1,0:T(8,128)S(1)}, u32[]{:S(2)}, u32[]{:S(2)}) collective-permute-start(f32[256,256]{1,0:T(8,128)} %get-tuple-element.55), channel_id=1, source_target_pairs={{0,28},{4,24},{8,20},{12,16},{16,12},{20,8},{24,4},{28,0},{1,29},{... | collective-permute-start | bytes 786440 | tf_op jit(solution)/shard_map/ppermute | solution.py:93
  6.8 19.0 %collective-permute-start.3 = (f32[256,256]{1,0:T(8,128)}, f32[256,256]{1,0:T(8,128)S(1)}, u32[]{:S(2)}, u32[]{:S(2)}) collective-permute-start(f32[256,256]{1,0:T(8,128)} %get-tuple-element.56), channel_id=1, source_target_pairs={{0,8},{4,12},{8,0},{12,4},{16,24},{20,28},{24,16},{28,20},{1,9},{5... | collective-permute-start | bytes 786440 | tf_op jit(solution)/shard_map/ppermute | solution.py:93
  8.5 17.4 %collective-permute-start.4 = (f32[256,256]{1,0:T(8,128)}, f32[256,256]{1,0:T(8,128)}, u32[]{:S(2)}, u32[]{:S(2)}) collective-permute-start(f32[256,256]{1,0:T(8,128)} %get-tuple-element.57), channel_id=1, source_target_pairs={{0,16},{4,20},{8,24},{12,28},{16,0},{20,4},{24,8},{28,12},{1,17},{... | collective-permute-start | bytes 786440 | tf_op jit(solution)/shard_map/ppermute | solution.py:93
  10.0 20.5 %collective-permute-start.5 = (f32[256,256]{1,0:T(8,128)}, f32[256,256]{1,0:T(8,128)S(1)}, u32[]{:S(2)}, u32[]{:S(2)}) collective-permute-start(f32[256,256]{1,0:T(8,128)} %get-tuple-element.58), channel_id=1, source_target_pairs={{0,12},{4,8},{8,4},{12,0},{16,28},{20,24},{24,20},{28,16},{1,13},{... | collective-permute-start | bytes 786440 | tf_op jit(solution)/shard_map/ppermute | solution.py:93
  14.2 16.4 %collective-permute-start.6 = (f32[256,256]{1,0:T(8,128)}, f32[256,256]{1,0:T(8,128)S(1)}, u32[]{:S(2)}, u32[]{:S(2)}) collective-permute-start(f32[256,256]{1,0:T(8,128)} %get-tuple-element.59), channel_id=1, source_target_pairs={{0,20},{4,16},{8,28},{12,24},{16,4},{20,0},{24,12},{28,8},{1,21},{... | collective-permute-start | bytes 786440 | tf_op jit(solution)/shard_map/ppermute | solution.py:93
  25.8 1.0 copy-start.1
  33.9 5.7 %collective-permute-start.10 = (f32[256,128]{1,0:T(8,128)S(1)}, f32[256,128]{1,0:T(8,128)S(1)}, u32[]{:S(2)}, u32[]{:S(2)}) collective-permute-start(f32[256,128]{1,0:T(8,128)S(1)} %get-tuple-element.64), channel_id=1, source_target_pairs={{0,8},{4,12},{8,0},{12,4},{16,24},{20,28},{24,16},{28,20},{1,9},{5... | collective-permute-start | bytes 393224 | tf_op jit(solution)/shard_map/ppermute | solution.py:93
  35.6 7.3 %collective-permute-start.11 = (f32[256,128]{1,0:T(8,128)S(1)}, f32[256,128]{1,0:T(8,128)S(1)}, u32[]{:S(2)}, u32[]{:S(2)}) collective-permute-start(f32[256,128]{1,0:T(8,128)S(1)} %get-tuple-element.65), channel_id=1, source_target_pairs={{0,16},{4,20},{8,24},{12,28},{16,0},{20,4},{24,8},{28,12},{1,17},{... | collective-permute-start | bytes 393224 | tf_op jit(solution)/shard_map/ppermute | solution.py:93
  37.2 5.8 %collective-permute-start.12 = (f32[256,128]{1,0:T(8,128)S(1)}, f32[256,128]{1,0:T(8,128)S(1)}, u32[]{:S(2)}, u32[]{:S(2)}) collective-permute-start(f32[256,128]{1,0:T(8,128)S(1)} %get-tuple-element.66), channel_id=1, source_target_pairs={{0,12},{4,8},{8,4},{12,0},{16,28},{20,24},{24,20},{28,16},{1,13},{... | collective-permute-start | bytes 393224 | tf_op jit(solution)/shard_map/ppermute | solution.py:93
  37.2 11.2 %collective-permute-start.13 = (f32[256,128]{1,0:T(8,128)S(1)}, f32[256,128]{1,0:T(8,128)S(1)}, u32[]{:S(2)}, u32[]{:S(2)}) collective-permute-start(f32[256,128]{1,0:T(8,128)S(1)} %get-tuple-element.67), channel_id=1, source_target_pairs={{0,20},{4,16},{8,28},{12,24},{16,4},{20,0},{24,12},{28,8},{1,21},{... | collective-permute-start | bytes 393224 | tf_op jit(solution)/shard_map/ppermute | solution.py:93
  37.7 10.7 %collective-permute-start.7 = (f32[256,128]{1,0:T(8,128)S(1)}, f32[256,128]{1,0:T(8,128)S(1)}, u32[]{:S(2)}, u32[]{:S(2)}) collective-permute-start(f32[256,128]{1,0:T(8,128)S(1)} %get-tuple-element.61), channel_id=1, source_target_pairs={{0,4},{4,0},{8,12},{12,8},{16,20},{20,16},{24,28},{28,24},{1,5},{5... | collective-permute-start | bytes 393224 | tf_op jit(solution)/shard_map/ppermute | solution.py:93
  39.6 8.8 %collective-permute-start.8 = (f32[256,128]{1,0:T(8,128)S(1)}, f32[256,128]{1,0:T(8,128)S(1)}, u32[]{:S(2)}, u32[]{:S(2)}) collective-permute-start(f32[256,128]{1,0:T(8,128)S(1)} %get-tuple-element.62), channel_id=1, source_target_pairs={{0,24},{4,28},{8,16},{12,20},{16,8},{20,12},{24,0},{28,4},{1,25},{... | collective-permute-start | bytes 393224 | tf_op jit(solution)/shard_map/ppermute | solution.py:93
  43.0 6.2 %collective-permute-start.9 = (f32[256,128]{1,0:T(8,128)S(1)}, f32[256,128]{1,0:T(8,128)S(1)}, u32[]{:S(2)}, u32[]{:S(2)}) collective-permute-start(f32[256,128]{1,0:T(8,128)S(1)} %get-tuple-element.63), channel_id=1, source_target_pairs={{0,28},{4,24},{8,20},{12,16},{16,12},{20,8},{24,4},{28,0},{1,29},{... | collective-permute-start | bytes 393224 | tf_op jit(solution)/shard_map/ppermute | solution.py:93
  51.1 15.8 %collective-permute-start.15 = (f32[256,512]{1,0:T(8,128)S(1)}, f32[256,512]{1,0:T(8,128)S(1)}, u32[]{:S(2)}, u32[]{:S(2)}) collective-permute-start(f32[256,512]{1,0:T(8,128)S(1)} %get-tuple-element.70), channel_id=1, source_target_pairs={{0,1},{3,2},{4,5},{7,6},{8,9},{11,10},{12,13},{15,14},{16,17},{19,... | collective-permute-start | bytes 1572872 | tf_op jit(solution)/shard_map/ppermute | solution.py:249
  60.3 2.0 %copy-start.2 = (f32[256,4096]{1,0:T(8,128)}, f32[256,4096]{1,0:T(8,128)S(1)}, u32[]{:S(2)}) copy-start(f32[256,4096]{1,0:T(8,128)S(1)} %fusion.1) | copy-start | bytes 12582916
  62.3 15.7 %collective-permute-start.14 = (f32[256,512]{1,0:T(8,128)S(1)}, f32[256,512]{1,0:T(8,128)}, u32[]{:S(2)}, u32[]{:S(2)}) collective-permute-start(f32[256,512]{1,0:T(8,128)S(1)} %constant_dynamic-slice_fusion), channel_id=1, source_target_pairs={{0,1},{3,2},{4,5},{7,6},{8,9},{11,10},{12,13},{15,14},{16,17},{19,... | collective-permute-start | bytes 1572872 | tf_op jit(solution)/shard_map/ppermute | solution.py:249
  68.2 21.1 %collective-permute-start.17 = (f32[256,512]{1,0:T(8,128)S(1)}, f32[256,512]{1,0:T(8,128)S(1)}, u32[]{:S(2)}, u32[]{:S(2)}) collective-permute-start(f32[256,512]{1,0:T(8,128)S(1)} %get-tuple-element.78), channel_id=1, source_target_pairs={{0,1},{1,2},{4,5},{5,6},{8,9},{9,10},{12,13},{13,14},{16,17},{17,1... | collective-permute-start | bytes 1572872 | tf_op jit(solution)/shard_map/ppermute | solution.py:240
  72.6 16.7 %collective-permute-start.18 = (f32[256,512]{1,0:T(8,128)S(1)}, f32[256,512]{1,0:T(8,128)S(1)}, u32[]{:S(2)}, u32[]{:S(2)}) collective-permute-start(f32[256,512]{1,0:T(8,128)S(1)} %get-tuple-element.80), channel_id=1, source_target_pairs={{2,1},{3,2},{6,5},{7,6},{10,9},{11,10},{14,13},{15,14},{18,17},{19... | collective-permute-start | bytes 1572872 | tf_op jit(solution)/shard_map/ppermute | solution.py:241
  79.6 20.9 %collective-permute-start.16 = (f32[256,512]{1,0:T(8,128)S(1)}, f32[256,512]{1,0:T(8,128)}, u32[]{:S(2)}, u32[]{:S(2)}) collective-permute-start(f32[256,512]{1,0:T(8,128)S(1)} %get-tuple-element.75), channel_id=1, source_target_pairs={{0,1},{1,2},{4,5},{5,6},{8,9},{9,10},{12,13},{13,14},{16,17},{17,1... | collective-permute-start | bytes 1572872 | tf_op jit(solution)/shard_map/ppermute | solution.py:240
  84.9 15.6 %collective-permute-start.19 = (f32[256,512]{1,0:T(8,128)S(1)}, f32[256,512]{1,0:T(8,128)}, u32[]{:S(2)}, u32[]{:S(2)}) collective-permute-start(f32[256,512]{1,0:T(8,128)S(1)} %get-tuple-element.82), channel_id=1, source_target_pairs={{2,1},{3,2},{6,5},{7,6},{10,9},{11,10},{14,13},{15,14},{18,17},{19... | collective-permute-start | bytes 1572872 | tf_op jit(solution)/shard_map/ppermute | solution.py:241
  90.7 21.1 %collective-permute-start.20 = (f32[256,512]{1,0:T(8,128)S(1)}, f32[256,512]{1,0:T(8,128)S(1)}, u32[]{:S(2)}, u32[]{:S(2)}) collective-permute-start(f32[256,512]{1,0:T(8,128)S(1)} %get-tuple-element.86), channel_id=1, source_target_pairs={{0,1},{1,2},{2,3},{4,5},{5,6},{6,7},{8,9},{9,10},{10,11},{12,13},{... | collective-permute-start | bytes 1572872 | tf_op jit(solution)/shard_map/ppermute | solution.py:240
  95.1 16.6 %collective-permute-start.21 = (f32[256,512]{1,0:T(8,128)S(1)}, f32[256,512]{1,0:T(8,128)S(1)}, u32[]{:S(2)}, u32[]{:S(2)}) collective-permute-start(f32[256,512]{1,0:T(8,128)S(1)} %get-tuple-element.87), channel_id=1, source_target_pairs={{1,0},{2,1},{3,2},{5,4},{6,5},{7,6},{9,8},{10,9},{11,10},{13,12},{... | collective-permute-start | bytes 1572872 | tf_op jit(solution)/shard_map/ppermute | solution.py:241
  102.3 19.9 %collective-permute-start.22 = (f32[256,512]{1,0:T(8,128)S(1)}, f32[256,512]{1,0:T(8,128)}, u32[]{:S(2)}, u32[]{:S(2)}) collective-permute-start(f32[256,512]{1,0:T(8,128)S(1)} %get-tuple-element.92), channel_id=1, source_target_pairs={{0,1},{1,2},{2,3},{4,5},{5,6},{6,7},{8,9},{9,10},{10,11},{12,13},{... | collective-permute-start | bytes 1572872 | tf_op jit(solution)/shard_map/ppermute | solution.py:240
  107.6 14.6 %collective-permute-start.23 = (f32[256,512]{1,0:T(8,128)S(1)}, f32[256,512]{1,0:T(8,128)}, u32[]{:S(2)}, u32[]{:S(2)}) collective-permute-start(f32[256,512]{1,0:T(8,128)S(1)} %get-tuple-element.93), channel_id=1, source_target_pairs={{1,0},{2,1},{3,2},{5,4},{6,5},{7,6},{9,8},{10,9},{11,10},{13,12},{... | collective-permute-start | bytes 1572872 | tf_op jit(solution)/shard_map/ppermute | solution.py:241

commit v6 on v5

--- a/solution.py
+++ b/solution.py
@@ -55,6 +55,14 @@
     chans = keys_ref.shape[1] // len(outs)
     origin = jnp.logical_and(place_ref[0] == 0, pl.program_id(0) == 0)
     rows = lax.broadcasted_iota(jnp.int32, (8, chans), 0)
+    if chans % 128 == 0:
+        for turn, out in zip(turns(len(outs)), outs):
+            cols = pl.ds(pl.multiple_of((turn ^ place_ref[0]) * chans, chans), chans)
+            out[:, :chans] = keys_ref[:, cols].astype(F32) * values_ref[:, cols].astype(F32)
+            out[:, chans:] = filt_ref[:, cols]
+            here = jnp.where(jnp.logical_and(rows == 0, origin), direct_ref[:, cols], 0.0)
+            out[:8, chans:] = filt_ref[:8, cols] + here
+        return
     for group in range(len(outs)):
         cols = slice(group * chans, (group + 1) * chans)
         slot = group ^ place_ref[0]
@@ -153,7 +161,7 @@
             mix_ref[j, real], mix_ref[j, imag] = sums[j]
         return carry
 
-    lax.fori_loop(0, rows // step, combine, 0)
+    lax.fori_loop(0, rows // step, combine, 0, unroll=2)
 
     back_in.wait()
     for j in range(0, count, 2):

time: 125 us -> 125 us (level)
  no operation moved by 1% of the time
where the time goes in v6:
time: 125 us; the launch traced here: 124 us
  waiting for transfers between devices  48.7 us (39%)
  starting transfers between devices  45.1 us (36%)
  Pallas kernels  10.2 us (8%)
  other arithmetic  9.36 us (7%)
  matrix products  5.72 us (5%)
  local copies, waits for them, and re-layouts  5.09 us (4%)
    ppermute x14, waiting for transfers between devices, swap(): lax.ppermute(arrays[j], 'ctx', pairs[j])  23.3 us
    ppermute x4, starting transfers between devices, pass_on(): up = lax.ppermute(up, 'tp', rise)  19.5 us
    ppermute x4, waiting for transfers between devices, pass_on(): up = lax.ppermute(up, 'tp', rise)  18.3 us
    ppermute x14, starting transfers between devices, swap(): lax.ppermute(arrays[j], 'ctx', pairs[j])  15.3 us
    ppermute x2, waiting for transfers between devices, first_step(): got = lax.ppermute(value, 'tp', [(0, 1), (size - 1, size - 2)])  7.13 us
    add x4, other arithmetic, scatter_dot(): down = sums[k][1] + own(place - size + step, k)  6.03 us
    dot_general x1, matrix products, scatter_dot(): terms = jnp.dot(lhs, rhs, preferred_element_type=F32)  5.72 us
    ppermute x2, starting transfers between devices, first_step(): got = lax.ppermute(value, 'tp', [(0, 1), (size - 1, size - 2)])  5.62 us
  transfers between devices with their start and end apart: 24, of which 14 were waited for; matrix products, arithmetic and copies ran while one was open for 12% of the time, Pallas kernels for 2%

profile of v6, /device:TPU:0, one launch (start us, length us, event | category | flops | bytes accessed | tf_op | source)
XLA Modules:
  0.0 124.3 jit_solution(11385257086295332501)
XLA Ops:
  0.0 2.8 %shard_map.82 = (f32[256,256]{1,0:T(8,128)}, f32[256,256]{1,0:T(8,128)}, f32[256,256]{1,0:T(8,128)}, f32[256,256]{1,0:T(8,128)}, f32[256,256]{1,0:T(8,128)}, /*i...) custom-call(s32[1]{0:T(128)} %bitcast.place_ref, bf16[256,1024]{1,0:T(8,128)(2,1)} %keys_ref.1, ...), custom_call_target="tpu_custom_call" | custom-call | tf_op jit(solution)/shard_map/pallas_call | solution.py:82
  2.8 0.5 collective-permute-start
  3.3 3.5 %collective-permute-start.1 = (f32[256,256]{1,0:T(8,128)}, f32[256,256]{1,0:T(8,128)S(1)}, u32[]{:S(2)}, u32[]{:S(2)}) collective-permute-start(f32[256,256]{1,0:T(8,128)} %get-tuple-element.54), channel_id=1, source_target_pairs={{0,24},{4,28},{8,16},{12,20},{16,8},{20,12},{24,0},{28,4},{1,25},{... | collective-permute-start | bytes 786440 | tf_op jit(solution)/shard_map/ppermute | solution.py:101
  6.8 0.1 collective-permute-start.2
  6.9 1.7 %collective-permute-start.3 = (f32[256,256]{1,0:T(8,128)}, f32[256,256]{1,0:T(8,128)S(1)}, u32[]{:S(2)}, u32[]{:S(2)}) collective-permute-start(f32[256,256]{1,0:T(8,128)} %get-tuple-element.56), channel_id=1, source_target_pairs={{0,8},{4,12},{8,0},{12,4},{16,24},{20,28},{24,16},{28,20},{1,9},{5... | collective-permute-start | bytes 786440 | tf_op jit(solution)/shard_map/ppermute | solution.py:101
  8.6 1.5 %collective-permute-start.4 = (f32[256,256]{1,0:T(8,128)}, f32[256,256]{1,0:T(8,128)}, u32[]{:S(2)}, u32[]{:S(2)}) collective-permute-start(f32[256,256]{1,0:T(8,128)} %get-tuple-element.57), channel_id=1, source_target_pairs={{0,16},{4,20},{8,24},{12,28},{16,0},{20,4},{24,8},{28,12},{1,17},{... | collective-permute-start | bytes 786440 | tf_op jit(solution)/shard_map/ppermute | solution.py:101
  10.1 0.0 collective-permute-done.refs_1_
  10.1 0.0 collective-permute-start.5
  10.1 4.2 %collective-permute-done.1.refs_2_ = f32[256,256]{1,0:T(8,128)S(1)} collective-permute-done((f32[256,256]{1,0:T(8,128)}, f32[256,256]{1,0:T(8,128)S(1)}, u32[]{:S(2)}, u32[]{:S(2)}) %collective-permute-start.1) | collective-permute-done | bytes 262176 | tf_op jit(solution)/shard_map/ppermute | solution.py:101
  14.3 0.7 collective-permute-start.6
  15.0 1.3 %constant_dynamic-slice_fusion.1.far_ref = bf16[1024,512]{1,0:T(8,128)(2,1)S(1)} fusion(bf16[1024,4096]{1,0:T(8,128)(2,1)} %param.13, s32[]{:T(128)S(6)} %select_n.67), kind=kLoop, calls=%fused_computation.12 | loop fusion | bytes 2097156 | tf_op jit(solution)/shard_map/dynamic_slice | solution.py:299
  16.3 3.2 %collective-permute-done.2.refs_3_ = f32[256,256]{1,0:T(8,128)S(1)} collective-permute-done((f32[256,256]{1,0:T(8,128)}, f32[256,256]{1,0:T(8,128)S(1)}, u32[]{:S(2)}, u32[]{:S(2)}) %collective-permute-start.2) | collective-permute-done | bytes 262176 | tf_op jit(solution)/shard_map/ppermute | solution.py:101
  19.4 6.5 %collective-permute-done.3.refs_4_ = f32[256,256]{1,0:T(8,128)S(1)} collective-permute-done((f32[256,256]{1,0:T(8,128)}, f32[256,256]{1,0:T(8,128)S(1)}, u32[]{:S(2)}, u32[]{:S(2)}) %collective-permute-start.3) | collective-permute-done | bytes 262176 | tf_op jit(solution)/shard_map/ppermute | solution.py:101
  25.9 0.0 collective-permute-done.4.refs_5_
  25.9 0.0 copy-done
  25.9 0.9 copy-done.1
  26.9 2.3 %shard_map.83.early_ref = f32[6,512,256]{2,1,0:T(8,128)S(1)} custom-call(bf16[512,768]{1,0:T(8,128)(2,1)S(1)} %copy-done, f32[256,256]{1,0:T(8,128)S(1)} %copy-done.1, f32[256,256]{1,0:T(8,128)S(1)} %collective-permute-done.refs_1_, f32[256,256]{1,0:T(8,128)S(1)} %collective-permute-done.1.refs_2_, f32[256,256]{1,0:T(8,128)S(1)} %collective-permute-done.2.refs_3_, ...), custom_call_target="tpu_custom_call" | custom-call | tf_op jit(solution)/shard_map/pallas_call | solution.py:112
  29.2 1.4 %collective-permute-done.5.refs_0_ = f32[256,256]{1,0:T(8,128)S(1)} collective-permute-done((f32[256,256]{1,0:T(8,128)}, f32[256,256]{1,0:T(8,128)S(1)}, u32[]{:S(2)}, u32[]{:S(2)}) %collective-permute-start.5) | collective-permute-done | bytes 262176 | tf_op jit(solution)/shard_map/ppermute | solution.py:101
  30.6 0.1 collective-permute-done.6.refs_1_
  30.7 3.2 %shard_map.84 = (f32[256,128]{1,0:T(8,128)S(1)}, f32[256,128]{1,0:T(8,128)S(1)}, f32[256,128]{1,0:T(8,128)S(1)}, f32[256,128]{1,0:T(8,128)S(1)}, f32[256,128]{1,...) custom-call(s32[1]{0:T(128)} %bitcast.place_ref, ...), custom_call_target="tpu_custom_call" | custom-call | tf_op jit(solution)/shard_map/pallas_call | solution.py:182
  33.9 1.8 %collective-permute-start.10 = (f32[256,128]{1,0:T(8,128)S(1)}, f32[256,128]{1,0:T(8,128)S(1)}, u32[]{:S(2)}, u32[]{:S(2)}) collective-permute-start(f32[256,128]{1,0:T(8,128)S(1)} %get-tuple-element.64), channel_id=1, source_target_pairs={{0,8},{4,12},{8,0},{12,4},{16,24},{20,28},{24,16},{28,20},{1,9},{5... | collective-permute-start | bytes 393224 | tf_op jit(solution)/shard_map/ppermute | solution.py:101
  35.6 1.5 %collective-permute-start.11 = (f32[256,128]{1,0:T(8,128)S(1)}, f32[256,128]{1,0:T(8,128)S(1)}, u32[]{:S(2)}, u32[]{:S(2)}) collective-permute-start(f32[256,128]{1,0:T(8,128)S(1)} %get-tuple-element.65), channel_id=1, source_target_pairs={{0,16},{4,20},{8,24},{12,28},{16,0},{20,4},{24,8},{28,12},{1,17},{... | collective-permute-start | bytes 393224 | tf_op jit(solution)/shard_map/ppermute | solution.py:101
  37.1 0.0 collective-permute-start.12
  37.1 0.5 collective-permute-start.13
  37.7 0.1 collective-permute-start.7
  37.8 1.8 %collective-permute-done.10.refs_4_ = f32[256,128]{1,0:T(8,128)S(1)} collective-permute-done((f32[256,128]{1,0:T(8,128)S(1)}, f32[256,128]{1,0:T(8,128)S(1)}, u32[]{:S(2)}, u32[]{:S(2)}) %collective-permute-start.10) | collective-permute-done | bytes 131104 | tf_op jit(solution)/shard_map/ppermute | solution.py:101
  39.5 3.4 %collective-permute-start.8 = (f32[256,128]{1,0:T(8,128)S(1)}, f32[256,128]{1,0:T(8,128)S(1)}, u32[]{:S(2)}, u32[]{:S(2)}) collective-permute-start(f32[256,128]{1,0:T(8,128)S(1)} %get-tuple-element.62), channel_id=1, source_target_pairs={{0,24},{4,28},{8,16},{12,20},{16,8},{20,12},{24,0},{28,4},{1,25},{... | collective-permute-start | bytes 393224 | tf_op jit(solution)/shard_map/ppermute | solution.py:101
  42.9 0.0 collective-permute-done.11.refs_5_
  42.9 0.0 collective-permute-start.9
  42.9 0.0 collective-permute-done.12.refs_6_
  42.9 5.4 %collective-permute-done.13.refs_7_ = f32[256,128]{1,0:T(8,128)S(1)} collective-permute-done((f32[256,128]{1,0:T(8,128)S(1)}, f32[256,128]{1,0:T(8,128)S(1)}, u32[]{:S(2)}, u32[]{:S(2)}) %collective-permute-start.13) | collective-permute-done | bytes 131104 | tf_op jit(solution)/shard_map/ppermute | solution.py:101
  48.4 0.0 collective-permute-done.7.refs_1_
  48.4 0.0 collective-permute-done.8.refs_2_
  48.4 0.8 collective-permute-done.9.refs_3_
  49.1 1.9 %shard_map.85 = (bf16[256,1024]{1,0:T(8,128)(2,1)S(1)}, f32[256,512]{1,0:T(8,128)S(1)}) custom-call(s32[1]{0:T(128)} %bitcast.place_ref, bf16[1024,512]{1,0:T(8,128)(2,1)S(1)} %constant_dynamic-slice_fusion.1.far_ref, bf16[256,1024]{1,0:T(8,128)(2,1)} %q_hbm.1, f32[256,128]{1,0:T(8,128)S(1)} %get-tuple-element.60.refs_0_, ...), custom_call_target="tpu_custom_call" | custom-call | tf_op jit(solution)/shard_map/pallas_call | solution.py:230
  51.0 3.5 %collective-permute-start.15 = (f32[256,512]{1,0:T(8,128)S(1)}, f32[256,512]{1,0:T(8,128)S(1)}, u32[]{:S(2)}, u32[]{:S(2)}) collective-permute-start(f32[256,512]{1,0:T(8,128)S(1)} %get-tuple-element.70), channel_id=1, source_target_pairs={{0,1},{3,2},{4,5},{7,6},{8,9},{11,10},{12,13},{15,14},{16,17},{19,... | collective-permute-start | bytes 1572872 | tf_op jit(solution)/shard_map/ppermute | solution.py:257
  54.5 5.7 %fusion.1 = f32[256,4096]{1,0:T(8,128)S(1)} fusion(bf16[256,1024]{1,0:T(8,128)(2,1)S(1)} %get-tuple-element.68, bf16[1024,4096]{1,0:T(8,128)(2,1)} %param.13), kind=kOutput, calls=%fused_computation.13 | convolution fusion | flops 2147483648 | bytes 13107200 | tf_op jit(solution)/shard_map/dot_general | solution.py:270
  60.3 1.9 %copy-done.2 = f32[256,4096]{1,0:T(8,128)} copy-done((f32[256,4096]{1,0:T(8,128)}, f32[256,4096]{1,0:T(8,128)S(1)}, u32[]{:S(2)}) %copy-start.2) | copy-done | bytes 4194328
  62.3 2.1 %collective-permute-start.14 = (f32[256,512]{1,0:T(8,128)S(1)}, f32[256,512]{1,0:T(8,128)}, u32[]{:S(2)}, u32[]{:S(2)}) collective-permute-start(f32[256,512]{1,0:T(8,128)S(1)} %constant_dynamic-slice_fusion), channel_id=1, source_target_pairs={{0,1},{3,2},{4,5},{7,6},{8,9},{11,10},{12,13},{15,14},{16,17},{19,... | collective-permute-start | bytes 1572872 | tf_op jit(solution)/shard_map/ppermute | solution.py:257
  64.4 2.4 %collective-permute-done.15 = f32[256,512]{1,0:T(8,128)S(1)} collective-permute-done((f32[256,512]{1,0:T(8,128)S(1)}, f32[256,512]{1,0:T(8,128)S(1)}, u32[]{:S(2)}, u32[]{:S(2)}) %collective-permute-start.15) | collective-permute-done | bytes 524320 | tf_op jit(solution)/shard_map/ppermute | solution.py:257
  66.8 1.4 %dynamic-slice_add_fusion.6 = (f32[256,512]{1,0:T(8,128)S(1)}, f32[256,512]{1,0:T(8,128)S(1)}) fusion(f32[256,4096]{1,0:T(8,128)} %copy-done.2, s32[]{:T(128)S(6)} %select_n.74, f32[256,512]{1,0:T(8,128)S(1)} %collective-permute-done.15, pred[]{:T(512)S(6)} %eq.14, s32[]{:T(128)S(6)} %select_n.71, pred[]{:T(512)S(6)} %eq.12), kind=kLoop, calls=%fused_computation.8 | loop fusion | flops 524288 | bytes 2621450 | tf_op jit(solution)/shard_map/add | solution.py:282
  68.2 4.4 %collective-permute-start.17 = (f32[256,512]{1,0:T(8,128)S(1)}, f32[256,512]{1,0:T(8,128)S(1)}, u32[]{:S(2)}, u32[]{:S(2)}) collective-permute-start(f32[256,512]{1,0:T(8,128)S(1)} %get-tuple-element.78), channel_id=1, source_target_pairs={{0,1},{1,2},{4,5},{5,6},{8,9},{9,10},{12,13},{13,14},{16,17},{17,1... | collective-permute-start | bytes 1572872 | tf_op jit(solution)/shard_map/ppermute | solution.py:248
  72.6 0.7 collective-permute-start.18
  73.3 4.7 %collective-permute-done.14 = f32[256,512]{1,0:T(8,128)} collective-permute-done((f32[256,512]{1,0:T(8,128)S(1)}, f32[256,512]{1,0:T(8,128)}, u32[]{:S(2)}, u32[]{:S(2)}) %collective-permute-start.14) | collective-permute-done | bytes 524320 | tf_op jit(solution)/shard_map/ppermute | solution.py:257
  78.0 1.5 %dynamic-slice_add_fusion.4 = (f32[256,512]{1,0:T(8,128)S(1)}, f32[256,512]{1,0:T(8,128)S(1)}) fusion(f32[256,4096]{1,0:T(8,128)} %copy-done.2, s32[]{:T(128)S(6)} %select_n.77, f32[256,512]{1,0:T(8,128)} %collective-permute-done.14, pred[]{:T(512)S(6)} %eq.14, s32[]{:T(128)S(6)} %select_n.75, pred[]{:T(512)S(6)} %eq.12), kind=kLoop, calls=%fused_computation.6 | loop fusion | flops 524288 | bytes 2621450 | tf_op jit(solution)/shard_map/add | solution.py:282
  79.5 5.3 %collective-permute-start.16 = (f32[256,512]{1,0:T(8,128)S(1)}, f32[256,512]{1,0:T(8,128)}, u32[]{:S(2)}, u32[]{:S(2)}) collective-permute-start(f32[256,512]{1,0:T(8,128)S(1)} %get-tuple-element.75), channel_id=1, source_target_pairs={{0,1},{1,2},{4,5},{5,6},{8,9},{9,10},{12,13},{13,14},{16,17},{17,1... | collective-permute-start | bytes 1572872 | tf_op jit(solution)/shard_map/ppermute | solution.py:248
  84.9 1.5 %collective-permute-start.19 = (f32[256,512]{1,0:T(8,128)S(1)}, f32[256,512]{1,0:T(8,128)}, u32[]{:S(2)}, u32[]{:S(2)}) collective-permute-start(f32[256,512]{1,0:T(8,128)S(1)} %get-tuple-element.82), channel_id=1, source_target_pairs={{2,1},{3,2},{6,5},{7,6},{10,9},{11,10},{14,13},{15,14},{18,17},{19... | collective-permute-start | bytes 1572872 | tf_op jit(solution)/shard_map/ppermute | solution.py:249
  86.3 2.9 %collective-permute-done.17 = f32[256,512]{1,0:T(8,128)S(1)} collective-permute-done((f32[256,512]{1,0:T(8,128)S(1)}, f32[256,512]{1,0:T(8,128)S(1)}, u32[]{:S(2)}, u32[]{:S(2)}) %collective-permute-start.17) | collective-permute-done | bytes 524320 | tf_op jit(solution)/shard_map/ppermute | solution.py:248
  89.3 0.0 collective-permute-done.18
  89.3 1.4 %dynamic-slice_add_fusion.2 = (f32[256,512]{1,0:T(8,128)S(1)}, f32[256,512]{1,0:T(8,128)S(1)}) fusion(f32[256,512]{1,0:T(8,128)S(1)} %collective-permute-done.18, f32[256,4096]{1,0:T(8,128)} %copy-done.2, s32[]{:T(128)S(6)} %select_n.79, f32[256,512]{1,0:T(8,128)S(1)} %collective-permute-done.17, s32[]{:T(128)S(6)} %select_n.78), kind=kLoop, calls=%fused_computation.4 | loop fusion | flops 262144 | bytes 3145736 | tf_op jit(solution)/shard_map/add | solution.py:282
  90.7 4.4 %collective-permute-start.20 = (f32[256,512]{1,0:T(8,128)S(1)}, f32[256,512]{1,0:T(8,128)S(1)}, u32[]{:S(2)}, u32[]{:S(2)}) collective-permute-start(f32[256,512]{1,0:T(8,128)S(1)} %get-tuple-element.86), channel_id=1, source_target_pairs={{0,1},{1,2},{2,3},{4,5},{5,6},{6,7},{8,9},{9,10},{10,11},{12,13},{... | collective-permute-start | bytes 1572872 | tf_op jit(solution)/shard_map/ppermute | solution.py:248
  95.1 1.3 %collective-permute-start.21 = (f32[256,512]{1,0:T(8,128)S(1)}, f32[256,512]{1,0:T(8,128)S(1)}, u32[]{:S(2)}, u32[]{:S(2)}) collective-permute-start(f32[256,512]{1,0:T(8,128)S(1)} %get-tuple-element.87), channel_id=1, source_target_pairs={{1,0},{2,1},{3,2},{5,4},{6,5},{7,6},{9,8},{10,9},{11,10},{13,12},{... | collective-permute-start | bytes 1572872 | tf_op jit(solution)/shard_map/ppermute | solution.py:249
  96.4 4.1 %collective-permute-done.16 = f32[256,512]{1,0:T(8,128)} collective-permute-done((f32[256,512]{1,0:T(8,128)S(1)}, f32[256,512]{1,0:T(8,128)}, u32[]{:S(2)}, u32[]{:S(2)}) %collective-permute-start.16) | collective-permute-done | bytes 524320 | tf_op jit(solution)/shard_map/ppermute | solution.py:248
  100.5 0.0 collective-permute-done.19
  100.5 1.7 %dynamic-slice_add_fusion = (f32[256,512]{1,0:T(8,128)S(1)}, f32[256,512]{1,0:T(8,128)S(1)}) fusion(f32[256,512]{1,0:T(8,128)} %collective-permute-done.19, f32[256,4096]{1,0:T(8,128)} %copy-done.2, s32[]{:T(128)S(6)} %select_n.81, f32[256,512]{1,0:T(8,128)} %collective-permute-done.16, s32[]{:T(128)S(6)} %select_n.80), kind=kLoop, calls=%fused_computation.2 | loop fusion | flops 262144 | bytes 3145736 | tf_op jit(solution)/shard_map/add | solution.py:282
  102.2 5.3 %collective-permute-start.22 = (f32[256,512]{1,0:T(8,128)S(1)}, f32[256,512]{1,0:T(8,128)}, u32[]{:S(2)}, u32[]{:S(2)}) collective-permute-start(f32[256,512]{1,0:T(8,128)S(1)} %get-tuple-element.92), channel_id=1, source_target_pairs={{0,1},{1,2},{2,3},{4,5},{5,6},{6,7},{8,9},{9,10},{10,11},{12,13},{... | collective-permute-start | bytes 1572872 | tf_op jit(solution)/shard_map/ppermute | solution.py:248
  107.5 1.3 %collective-permute-start.23 = (f32[256,512]{1,0:T(8,128)S(1)}, f32[256,512]{1,0:T(8,128)}, u32[]{:S(2)}, u32[]{:S(2)}) collective-permute-start(f32[256,512]{1,0:T(8,128)S(1)} %get-tuple-element.93), channel_id=1, source_target_pairs={{1,0},{2,1},{3,2},{5,4},{6,5},{7,6},{9,8},{10,9},{11,10},{13,12},{... | collective-permute-start | bytes 1572872 | tf_op jit(solution)/shard_map/ppermute | solution.py:249
  108.8 2.9 %collective-permute-done.20 = f32[256,512]{1,0:T(8,128)S(1)} collective-permute-done((f32[256,512]{1,0:T(8,128)S(1)}, f32[256,512]{1,0:T(8,128)S(1)}, u32[]{:S(2)}, u32[]{:S(2)}) %collective-permute-start.20) | collective-permute-done | bytes 524320 | tf_op jit(solution)/shard_map/ppermute | solution.py:248
  111.7 0.0 collective-permute-done.21
  111.7 1.2 add_convert_fusion.1
  112.9 0.9 dynamic_update_slice.6
  113.7 8.4 %collective-permute-done.22 = f32[256,512]{1,0:T(8,128)} collective-permute-done((f32[256,512]{1,0:T(8,128)S(1)}, f32[256,512]{1,0:T(8,128)}, u32[]{:S(2)}, u32[]{:S(2)}) %collective-permute-start.22) | collective-permute-done | bytes 524320 | tf_op jit(solution)/shard_map/ppermute | solution.py:248
  122.1 0.0 collective-permute-done.23
  122.1 2.2 %fusion = bf16[256,1024]{1,0:T(8,128)(2,1)} fusion(bf16[256,1024]{1,0:T(8,128)(2,1)} %dynamic_update_slice.6, f32[256,512]{1,0:T(8,128)} %collective-permute-done.23, f32[256,512]{1,0:T(8,128)} %collective-permute-done.22, f32[256,4096]{1,0:T(8,128)} %copy-done.2, s32[]{:T(128)S(6)} %select_n.83), kind=kLoop, calls=%fused_computation.10 | loop fusion | flops 393216 | bytes 1835012 | tf_op jit(solution)/shard_map/dynamic_update_slice | solution.py:288
  (4 shorter events, 0.0 us)
Async XLA Ops:
  0.0 25.9 %copy-start = (bf16[512,768]{1,0:T(8,128)(2,1)S(1)}, bf16[512,768]{1,0:T(8,128)(2,1)}, u32[]{:S(2)}) copy-start(bf16[512,768]{1,0:T(8,128)(2,1)} %constant.48.clone.ahead_ref.refs_2_) | copy-start | bytes 2359300
  2.8 7.3 %collective-permute-start = (f32[256,256]{1,0:T(8,128)}, f32[256,256]{1,0:T(8,128)S(1)}, u32[]{:S(2)}, u32[]{:S(2)}) collective-permute-start(f32[256,256]{1,0:T(8,128)} %get-tuple-element.53), channel_id=1, source_target_pairs={{0,4},{4,0},{8,12},{12,8},{16,20},{20,16},{24,28},{28,24},{1,5},{5... | collective-permute-start | bytes 786440 | tf_op jit(solution)/shard_map/ppermute | solution.py:101
  3.3 11.0 %collective-permute-start.1 = (f32[256,256]{1,0:T(8,128)}, f32[256,256]{1,0:T(8,128)S(1)}, u32[]{:S(2)}, u32[]{:S(2)}) collective-permute-start(f32[256,256]{1,0:T(8,128)} %get-tuple-element.54), channel_id=1, source_target_pairs={{0,24},{4,28},{8,16},{12,20},{16,8},{20,12},{24,0},{28,4},{1,25},{... | collective-permute-start | bytes 786440 | tf_op jit(solution)/shard_map/ppermute | solution.py:101
  6.8 12.6 %collective-permute-start.2 = (f32[256,256]{1,0:T(8,128)}, f32[256,256]{1,0:T(8,128)S(1)}, u32[]{:S(2)}, u32[]{:S(2)}) collective-permute-start(f32[256,256]{1,0:T(8,128)} %get-tuple-element.55), channel_id=1, source_target_pairs={{0,28},{4,24},{8,20},{12,16},{16,12},{20,8},{24,4},{28,0},{1,29},{... | collective-permute-start | bytes 786440 | tf_op jit(solution)/shard_map/ppermute | solution.py:101
  6.9 19.0 %collective-permute-start.3 = (f32[256,256]{1,0:T(8,128)}, f32[256,256]{1,0:T(8,128)S(1)}, u32[]{:S(2)}, u32[]{:S(2)}) collective-permute-start(f32[256,256]{1,0:T(8,128)} %get-tuple-element.56), channel_id=1, source_target_pairs={{0,8},{4,12},{8,0},{12,4},{16,24},{20,28},{24,16},{28,20},{1,9},{5... | collective-permute-start | bytes 786440 | tf_op jit(solution)/shard_map/ppermute | solution.py:101
  8.6 17.4 %collective-permute-start.4 = (f32[256,256]{1,0:T(8,128)}, f32[256,256]{1,0:T(8,128)}, u32[]{:S(2)}, u32[]{:S(2)}) collective-permute-start(f32[256,256]{1,0:T(8,128)} %get-tuple-element.57), channel_id=1, source_target_pairs={{0,16},{4,20},{8,24},{12,28},{16,0},{20,4},{24,8},{28,12},{1,17},{... | collective-permute-start | bytes 786440 | tf_op jit(solution)/shard_map/ppermute | solution.py:101
  10.1 20.6 %collective-permute-start.5 = (f32[256,256]{1,0:T(8,128)}, f32[256,256]{1,0:T(8,128)S(1)}, u32[]{:S(2)}, u32[]{:S(2)}) collective-permute-start(f32[256,256]{1,0:T(8,128)} %get-tuple-element.58), channel_id=1, source_target_pairs={{0,12},{4,8},{8,4},{12,0},{16,28},{20,24},{24,20},{28,16},{1,13},{... | collective-permute-start | bytes 786440 | tf_op jit(solution)/shard_map/ppermute | solution.py:101
  14.3 16.4 %collective-permute-start.6 = (f32[256,256]{1,0:T(8,128)}, f32[256,256]{1,0:T(8,128)S(1)}, u32[]{:S(2)}, u32[]{:S(2)}) collective-permute-start(f32[256,256]{1,0:T(8,128)} %get-tuple-element.59), channel_id=1, source_target_pairs={{0,20},{4,16},{8,28},{12,24},{16,4},{20,0},{24,12},{28,8},{1,21},{... | collective-permute-start | bytes 786440 | tf_op jit(solution)/shard_map/ppermute | solution.py:101
  25.9 1.0 copy-start.1
  33.9 5.7 %collective-permute-start.10 = (f32[256,128]{1,0:T(8,128)S(1)}, f32[256,128]{1,0:T(8,128)S(1)}, u32[]{:S(2)}, u32[]{:S(2)}) collective-permute-start(f32[256,128]{1,0:T(8,128)S(1)} %get-tuple-element.64), channel_id=1, source_target_pairs={{0,8},{4,12},{8,0},{12,4},{16,24},{20,28},{24,16},{28,20},{1,9},{5... | collective-permute-start | bytes 393224 | tf_op jit(solution)/shard_map/ppermute | solution.py:101
  35.6 7.3 %collective-permute-start.11 = (f32[256,128]{1,0:T(8,128)S(1)}, f32[256,128]{1,0:T(8,128)S(1)}, u32[]{:S(2)}, u32[]{:S(2)}) collective-permute-start(f32[256,128]{1,0:T(8,128)S(1)} %get-tuple-element.65), channel_id=1, source_target_pairs={{0,16},{4,20},{8,24},{12,28},{16,0},{20,4},{24,8},{28,12},{1,17},{... | collective-permute-start | bytes 393224 | tf_op jit(solution)/shard_map/ppermute | solution.py:101
  37.1 5.8 %collective-permute-start.12 = (f32[256,128]{1,0:T(8,128)S(1)}, f32[256,128]{1,0:T(8,128)S(1)}, u32[]{:S(2)}, u32[]{:S(2)}) collective-permute-start(f32[256,128]{1,0:T(8,128)S(1)} %get-tuple-element.66), channel_id=1, source_target_pairs={{0,12},{4,8},{8,4},{12,0},{16,28},{20,24},{24,20},{28,16},{1,13},{... | collective-permute-start | bytes 393224 | tf_op jit(solution)/shard_map/ppermute | solution.py:101
  37.1 11.2 %collective-permute-start.13 = (f32[256,128]{1,0:T(8,128)S(1)}, f32[256,128]{1,0:T(8,128)S(1)}, u32[]{:S(2)}, u32[]{:S(2)}) collective-permute-start(f32[256,128]{1,0:T(8,128)S(1)} %get-tuple-element.67), channel_id=1, source_target_pairs={{0,20},{4,16},{8,28},{12,24},{16,4},{20,0},{24,12},{28,8},{1,21},{... | collective-permute-start | bytes 393224 | tf_op jit(solution)/shard_map/ppermute | solution.py:101
  37.7 10.7 %collective-permute-start.7 = (f32[256,128]{1,0:T(8,128)S(1)}, f32[256,128]{1,0:T(8,128)S(1)}, u32[]{:S(2)}, u32[]{:S(2)}) collective-permute-start(f32[256,128]{1,0:T(8,128)S(1)} %get-tuple-element.61), channel_id=1, source_target_pairs={{0,4},{4,0},{8,12},{12,8},{16,20},{20,16},{24,28},{28,24},{1,5},{5... | collective-permute-start | bytes 393224 | tf_op jit(solution)/shard_map/ppermute | solution.py:101
  39.5 8.8 %collective-permute-start.8 = (f32[256,128]{1,0:T(8,128)S(1)}, f32[256,128]{1,0:T(8,128)S(1)}, u32[]{:S(2)}, u32[]{:S(2)}) collective-permute-start(f32[256,128]{1,0:T(8,128)S(1)} %get-tuple-element.62), channel_id=1, source_target_pairs={{0,24},{4,28},{8,16},{12,20},{16,8},{20,12},{24,0},{28,4},{1,25},{... | collective-permute-start | bytes 393224 | tf_op jit(solution)/shard_map/ppermute | solution.py:101
  42.9 6.2 %collective-permute-start.9 = (f32[256,128]{1,0:T(8,128)S(1)}, f32[256,128]{1,0:T(8,128)S(1)}, u32[]{:S(2)}, u32[]{:S(2)}) collective-permute-start(f32[256,128]{1,0:T(8,128)S(1)} %get-tuple-element.63), channel_id=1, source_target_pairs={{0,28},{4,24},{8,20},{12,16},{16,12},{20,8},{24,4},{28,0},{1,29},{... | collective-permute-start | bytes 393224 | tf_op jit(solution)/shard_map/ppermute | solution.py:101
  51.0 15.8 %collective-permute-start.15 = (f32[256,512]{1,0:T(8,128)S(1)}, f32[256,512]{1,0:T(8,128)S(1)}, u32[]{:S(2)}, u32[]{:S(2)}) collective-permute-start(f32[256,512]{1,0:T(8,128)S(1)} %get-tuple-element.70), channel_id=1, source_target_pairs={{0,1},{3,2},{4,5},{7,6},{8,9},{11,10},{12,13},{15,14},{16,17},{19,... | collective-permute-start | bytes 1572872 | tf_op jit(solution)/shard_map/ppermute | solution.py:257
  60.3 2.0 %copy-start.2 = (f32[256,4096]{1,0:T(8,128)}, f32[256,4096]{1,0:T(8,128)S(1)}, u32[]{:S(2)}) copy-start(f32[256,4096]{1,0:T(8,128)S(1)} %fusion.1) | copy-start | bytes 12582916
  62.3 15.7 %collective-permute-start.14 = (f32[256,512]{1,0:T(8,128)S(1)}, f32[256,512]{1,0:T(8,128)}, u32[]{:S(2)}, u32[]{:S(2)}) collective-permute-start(f32[256,512]{1,0:T(8,128)S(1)} %constant_dynamic-slice_fusion), channel_id=1, source_target_pairs={{0,1},{3,2},{4,5},{7,6},{8,9},{11,10},{12,13},{15,14},{16,17},{19,... | collective-permute-start | bytes 1572872 | tf_op jit(solution)/shard_map/ppermute | solution.py:257
  68.2 21.1 %collective-permute-start.17 = (f32[256,512]{1,0:T(8,128)S(1)}, f32[256,512]{1,0:T(8,128)S(1)}, u32[]{:S(2)}, u32[]{:S(2)}) collective-permute-start(f32[256,512]{1,0:T(8,128)S(1)} %get-tuple-element.78), channel_id=1, source_target_pairs={{0,1},{1,2},{4,5},{5,6},{8,9},{9,10},{12,13},{13,14},{16,17},{17,1... | collective-permute-start | bytes 1572872 | tf_op jit(solution)/shard_map/ppermute | solution.py:248
  72.6 16.7 %collective-permute-start.18 = (f32[256,512]{1,0:T(8,128)S(1)}, f32[256,512]{1,0:T(8,128)S(1)}, u32[]{:S(2)}, u32[]{:S(2)}) collective-permute-start(f32[256,512]{1,0:T(8,128)S(1)} %get-tuple-element.80), channel_id=1, source_target_pairs={{2,1},{3,2},{6,5},{7,6},{10,9},{11,10},{14,13},{15,14},{18,17},{19... | collective-permute-start | bytes 1572872 | tf_op jit(solution)/shard_map/ppermute | solution.py:249
  79.5 20.9 %collective-permute-start.16 = (f32[256,512]{1,0:T(8,128)S(1)}, f32[256,512]{1,0:T(8,128)}, u32[]{:S(2)}, u32[]{:S(2)}) collective-permute-start(f32[256,512]{1,0:T(8,128)S(1)} %get-tuple-element.75), channel_id=1, source_target_pairs={{0,1},{1,2},{4,5},{5,6},{8,9},{9,10},{12,13},{13,14},{16,17},{17,1... | collective-permute-start | bytes 1572872 | tf_op jit(solution)/shard_map/ppermute | solution.py:248
  84.9 15.6 %collective-permute-start.19 = (f32[256,512]{1,0:T(8,128)S(1)}, f32[256,512]{1,0:T(8,128)}, u32[]{:S(2)}, u32[]{:S(2)}) collective-permute-start(f32[256,512]{1,0:T(8,128)S(1)} %get-tuple-element.82), channel_id=1, source_target_pairs={{2,1},{3,2},{6,5},{7,6},{10,9},{11,10},{14,13},{15,14},{18,17},{19... | collective-permute-start | bytes 1572872 | tf_op jit(solution)/shard_map/ppermute | solution.py:249
  90.7 21.1 %collective-permute-start.20 = (f32[256,512]{1,0:T(8,128)S(1)}, f32[256,512]{1,0:T(8,128)S(1)}, u32[]{:S(2)}, u32[]{:S(2)}) collective-permute-start(f32[256,512]{1,0:T(8,128)S(1)} %get-tuple-element.86), channel_id=1, source_target_pairs={{0,1},{1,2},{2,3},{4,5},{5,6},{6,7},{8,9},{9,10},{10,11},{12,13},{... | collective-permute-start | bytes 1572872 | tf_op jit(solution)/shard_map/ppermute | solution.py:248
  95.1 16.6 %collective-permute-start.21 = (f32[256,512]{1,0:T(8,128)S(1)}, f32[256,512]{1,0:T(8,128)S(1)}, u32[]{:S(2)}, u32[]{:S(2)}) collective-permute-start(f32[256,512]{1,0:T(8,128)S(1)} %get-tuple-element.87), channel_id=1, source_target_pairs={{1,0},{2,1},{3,2},{5,4},{6,5},{7,6},{9,8},{10,9},{11,10},{13,12},{... | collective-permute-start | bytes 1572872 | tf_op jit(solution)/shard_map/ppermute | solution.py:249
  102.2 19.9 %collective-permute-start.22 = (f32[256,512]{1,0:T(8,128)S(1)}, f32[256,512]{1,0:T(8,128)}, u32[]{:S(2)}, u32[]{:S(2)}) collective-permute-start(f32[256,512]{1,0:T(8,128)S(1)} %get-tuple-element.92), channel_id=1, source_target_pairs={{0,1},{1,2},{2,3},{4,5},{5,6},{6,7},{8,9},{9,10},{10,11},{12,13},{... | collective-permute-start | bytes 1572872 | tf_op jit(solution)/shard_map/ppermute | solution.py:248
  107.5 14.6 %collective-permute-start.23 = (f32[256,512]{1,0:T(8,128)S(1)}, f32[256,512]{1,0:T(8,128)}, u32[]{:S(2)}, u32[]{:S(2)}) collective-permute-start(f32[256,512]{1,0:T(8,128)S(1)} %get-tuple-element.93), channel_id=1, source_target_pairs={{1,0},{2,1},{3,2},{5,4},{6,5},{7,6},{9,8},{10,9},{11,10},{13,12},{... | collective-permute-start | bytes 1572872 | tf_op jit(solution)/shard_map/ppermute | solution.py:249

commit v7 on v5

--- a/solution.py
+++ b/solution.py
@@ -209,7 +209,10 @@
     for group in range(count):
         cols = slice(group * chans, (group + 1) * chans)
         gated_ref[:, cols] = (q_ref[:, cols].astype(F32) * conv_ref[group]).astype(BF16)
-    first_ref[...] = jnp.dot(gated_ref[...], far_ref[...], preferred_element_type=F32)
+
+    @pl.when(place_ref[1] == 1)
+    def _():
+        first_ref[...] = jnp.dot(gated_ref[...], far_ref[...], preferred_element_type=F32)
 
 
 def gate(place, query, far, convs):
@@ -291,7 +294,9 @@
     far = lax.dynamic_slice_in_dim(w_out, far_end(size) * (part * CHAINS), part, 1)
     xs[0], far = lax.optimization_barrier((xs[0], far))
     convs = swap(convolve(place, xs))
-    gated, first = gate(place, query, far, convs)
+    line = lax.axis_index("tp")
+    ends = jnp.logical_or(line == 0, line == size - 1).astype(jnp.int32).reshape(1)
+    gated, first = gate(jnp.concatenate([place, ends]), query, far, convs)
     return scatter_dot(gated, w_out, first)
 
 

time: 125 us -> 125 us (level)
  no operation moved by 1% of the time
where the time goes in v7:
time: 125 us
  waiting for transfers between devices  48.6 us (39%)
  starting transfers between devices  44.7 us (36%)
  Pallas kernels  10.9 us (9%)
  other arithmetic  9.44 us (8%)
  matrix products  5.72 us (5%)
  local copies, waits for them, and re-layouts  5.09 us (4%)
    ppermute x14, waiting for transfers between devices, swap(): lax.ppermute(arrays[j], 'ctx', pairs[j])  23.2 us
    ppermute x4, starting transfers between devices, pass_on(): up = lax.ppermute(up, 'tp', rise)  19.5 us
    ppermute x4, waiting for transfers between devices, pass_on(): up = lax.ppermute(up, 'tp', rise)  18.3 us
    ppermute x14, starting transfers between devices, swap(): lax.ppermute(arrays[j], 'ctx', pairs[j])  15.3 us
    ppermute x2, waiting for transfers between devices, first_step(): got = lax.ppermute(value, 'tp', [(0, 1), (size - 1, size - 2)])  7.14 us
    add x4, other arithmetic, scatter_dot(): down = sums[k][1] + own(place - size + step, k)  6.03 us
    dot_general x1, matrix products, scatter_dot(): terms = jnp.dot(lhs, rhs, preferred_element_type=F32)  5.72 us
    ppermute x2, starting transfers between devices, first_step(): got = lax.ppermute(value, 'tp', [(0, 1), (size - 1, size - 2)])  5.19 us
  transfers between devices with their start and end apart: 24, of which 14 were waited for; matrix products, arithmetic and copies ran while one was open for 12% of the time, Pallas kernels for 2%

profile of v7, /device:TPU:0, one launch (start us, length us, event | category | flops | bytes accessed | tf_op | source)
XLA Modules:
  0.0 124.6 jit_solution(703490372593812507)
XLA Ops:
  0.0 2.7 %shard_map.82 = (f32[256,256]{1,0:T(8,128)}, f32[256,256]{1,0:T(8,128)}, f32[256,256]{1,0:T(8,128)}, f32[256,256]{1,0:T(8,128)}, f32[256,256]{1,0:T(8,128)}, /*i...) custom-call(s32[1]{0:T(128)} %bitcast.place_ref, bf16[256,1024]{1,0:T(8,128)(2,1)} %keys_ref.1, ...), custom_call_target="tpu_custom_call" | custom-call | tf_op jit(solution)/shard_map/pallas_call | solution.py:74
  2.7 0.5 collective-permute-start
  3.2 3.5 %collective-permute-start.1 = (f32[256,256]{1,0:T(8,128)}, f32[256,256]{1,0:T(8,128)S(1)}, u32[]{:S(2)}, u32[]{:S(2)}) collective-permute-start(f32[256,256]{1,0:T(8,128)} %get-tuple-element.54), channel_id=1, source_target_pairs={{0,24},{4,28},{8,16},{12,20},{16,8},{20,12},{24,0},{28,4},{1,25},{... | collective-permute-start | bytes 786440 | tf_op jit(solution)/shard_map/ppermute | solution.py:93
  6.7 0.1 collective-permute-start.2
  6.8 1.7 %collective-permute-start.3 = (f32[256,256]{1,0:T(8,128)}, f32[256,256]{1,0:T(8,128)S(1)}, u32[]{:S(2)}, u32[]{:S(2)}) collective-permute-start(f32[256,256]{1,0:T(8,128)} %get-tuple-element.56), channel_id=1, source_target_pairs={{0,8},{4,12},{8,0},{12,4},{16,24},{20,28},{24,16},{28,20},{1,9},{5... | collective-permute-start | bytes 786440 | tf_op jit(solution)/shard_map/ppermute | solution.py:93
  8.5 1.5 %collective-permute-start.4 = (f32[256,256]{1,0:T(8,128)}, f32[256,256]{1,0:T(8,128)}, u32[]{:S(2)}, u32[]{:S(2)}) collective-permute-start(f32[256,256]{1,0:T(8,128)} %get-tuple-element.57), channel_id=1, source_target_pairs={{0,16},{4,20},{8,24},{12,28},{16,0},{20,4},{24,8},{28,12},{1,17},{... | collective-permute-start | bytes 786440 | tf_op jit(solution)/shard_map/ppermute | solution.py:93
  10.0 0.0 collective-permute-done.refs_1_
  10.0 0.0 collective-permute-start.5
  10.0 4.2 %collective-permute-done.1.refs_2_ = f32[256,256]{1,0:T(8,128)S(1)} collective-permute-done((f32[256,256]{1,0:T(8,128)}, f32[256,256]{1,0:T(8,128)S(1)}, u32[]{:S(2)}, u32[]{:S(2)}) %collective-permute-start.1) | collective-permute-done | bytes 262176 | tf_op jit(solution)/shard_map/ppermute | solution.py:93
  14.2 0.7 collective-permute-start.6
  14.9 1.3 %constant_dynamic-slice_fusion.1.far_ref = bf16[1024,512]{1,0:T(8,128)(2,1)S(1)} fusion(bf16[1024,4096]{1,0:T(8,128)(2,1)} %param.13, s32[]{:T(128)S(6)} %select_n.67), kind=kLoop, calls=%fused_computation.12 | loop fusion | bytes 2097156 | tf_op jit(solution)/shard_map/dynamic_slice | solution.py:294
  16.2 3.2 %collective-permute-done.2.refs_3_ = f32[256,256]{1,0:T(8,128)S(1)} collective-permute-done((f32[256,256]{1,0:T(8,128)}, f32[256,256]{1,0:T(8,128)S(1)}, u32[]{:S(2)}, u32[]{:S(2)}) %collective-permute-start.2) | collective-permute-done | bytes 262176 | tf_op jit(solution)/shard_map/ppermute | solution.py:93
  19.3 6.5 %collective-permute-done.3.refs_4_ = f32[256,256]{1,0:T(8,128)S(1)} collective-permute-done((f32[256,256]{1,0:T(8,128)}, f32[256,256]{1,0:T(8,128)S(1)}, u32[]{:S(2)}, u32[]{:S(2)}) %collective-permute-start.3) | collective-permute-done | bytes 262176 | tf_op jit(solution)/shard_map/ppermute | solution.py:93
  25.8 0.0 collective-permute-done.4.refs_5_
  25.8 0.9 copy-done.1
  26.8 2.3 %shard_map.83.early_ref = f32[6,512,256]{2,1,0:T(8,128)S(1)} custom-call(bf16[512,768]{1,0:T(8,128)(2,1)S(1)} %copy-done, f32[256,256]{1,0:T(8,128)S(1)} %copy-done.1, f32[256,256]{1,0:T(8,128)S(1)} %collective-permute-done.refs_1_, f32[256,256]{1,0:T(8,128)S(1)} %collective-permute-done.1.refs_2_, f32[256,256]{1,0:T(8,128)S(1)} %collective-permute-done.2.refs_3_, ...), custom_call_target="tpu_custom_call" | custom-call | tf_op jit(solution)/shard_map/pallas_call | solution.py:104
  29.1 1.4 %collective-permute-done.5.refs_0_ = f32[256,256]{1,0:T(8,128)S(1)} collective-permute-done((f32[256,256]{1,0:T(8,128)}, f32[256,256]{1,0:T(8,128)S(1)}, u32[]{:S(2)}, u32[]{:S(2)}) %collective-permute-start.5) | collective-permute-done | bytes 262176 | tf_op jit(solution)/shard_map/ppermute | solution.py:93
  30.5 0.1 collective-permute-done.6.refs_1_
  30.6 3.3 %shard_map.84 = (f32[256,128]{1,0:T(8,128)S(1)}, f32[256,128]{1,0:T(8,128)S(1)}, f32[256,128]{1,0:T(8,128)S(1)}, f32[256,128]{1,0:T(8,128)S(1)}, f32[256,128]{1,...) custom-call(s32[1]{0:T(128)} %bitcast.place_ref, ...), custom_call_target="tpu_custom_call" | custom-call | tf_op jit(solution)/shard_map/pallas_call | solution.py:174
  33.9 1.8 %collective-permute-start.10 = (f32[256,128]{1,0:T(8,128)S(1)}, f32[256,128]{1,0:T(8,128)S(1)}, u32[]{:S(2)}, u32[]{:S(2)}) collective-permute-start(f32[256,128]{1,0:T(8,128)S(1)} %get-tuple-element.64), channel_id=1, source_target_pairs={{0,8},{4,12},{8,0},{12,4},{16,24},{20,28},{24,16},{28,20},{1,9},{5... | collective-permute-start | bytes 393224 | tf_op jit(solution)/shard_map/ppermute | solution.py:93
  35.6 1.5 %collective-permute-start.11 = (f32[256,128]{1,0:T(8,128)S(1)}, f32[256,128]{1,0:T(8,128)S(1)}, u32[]{:S(2)}, u32[]{:S(2)}) collective-permute-start(f32[256,128]{1,0:T(8,128)S(1)} %get-tuple-element.65), channel_id=1, source_target_pairs={{0,16},{4,20},{8,24},{12,28},{16,0},{20,4},{24,8},{28,12},{1,17},{... | collective-permute-start | bytes 393224 | tf_op jit(solution)/shard_map/ppermute | solution.py:93
  37.2 0.0 collective-permute-start.12
  37.2 0.6 collective-permute-start.13
  37.7 0.1 collective-permute-start.7
  37.8 1.7 %collective-permute-done.10.refs_4_ = f32[256,128]{1,0:T(8,128)S(1)} collective-permute-done((f32[256,128]{1,0:T(8,128)S(1)}, f32[256,128]{1,0:T(8,128)S(1)}, u32[]{:S(2)}, u32[]{:S(2)}) %collective-permute-start.10) | collective-permute-done | bytes 131104 | tf_op jit(solution)/shard_map/ppermute | solution.py:93
  39.6 3.4 %collective-permute-start.8 = (f32[256,128]{1,0:T(8,128)S(1)}, f32[256,128]{1,0:T(8,128)S(1)}, u32[]{:S(2)}, u32[]{:S(2)}) collective-permute-start(f32[256,128]{1,0:T(8,128)S(1)} %get-tuple-element.62), channel_id=1, source_target_pairs={{0,24},{4,28},{8,16},{12,20},{16,8},{20,12},{24,0},{28,4},{1,25},{... | collective-permute-start | bytes 393224 | tf_op jit(solution)/shard_map/ppermute | solution.py:93
  43.0 0.0 collective-permute-done.11.refs_5_
  43.0 0.0 collective-permute-start.9
  43.0 0.1 pad_add_fusion.place_ref
  43.0 0.0 collective-permute-done.12.refs_6_
  43.0 5.3 %collective-permute-done.13.refs_7_ = f32[256,128]{1,0:T(8,128)S(1)} collective-permute-done((f32[256,128]{1,0:T(8,128)S(1)}, f32[256,128]{1,0:T(8,128)S(1)}, u32[]{:S(2)}, u32[]{:S(2)}) %collective-permute-start.13) | collective-permute-done | bytes 131104 | tf_op jit(solution)/shard_map/ppermute | solution.py:93
  48.4 0.0 collective-permute-done.7.refs_1_
  48.4 0.0 collective-permute-done.8.refs_2_
  48.4 0.8 collective-permute-done.9.refs_3_
  49.2 2.6 %shard_map.85 = (bf16[256,1024]{1,0:T(8,128)(2,1)S(1)}, f32[256,512]{1,0:T(8,128)S(1)}) custom-call(s32[2]{0:T(128)S(1)} %pad_add_fusion.place_ref, bf16[1024,512]{1,0:T(8,128)(2,1)S(1)} %constant_dynamic-slice_fusion.1.far_ref, bf16[256,1024]{1,0:T(8,128)(2,1)} %q_hbm.1, f32[256,128]{1,0:T(8,128)S(1)} %get-tuple-element.60.refs_0_, ...), custom_call_target="tpu_custom_call" | custom-call | tf_op jit(solution)/shard_map/pallas_call | solution.py:225
  51.7 3.1 %collective-permute-start.15 = (f32[256,512]{1,0:T(8,128)S(1)}, f32[256,512]{1,0:T(8,128)S(1)}, u32[]{:S(2)}, u32[]{:S(2)}) collective-permute-start(f32[256,512]{1,0:T(8,128)S(1)} %get-tuple-element.70), channel_id=1, source_target_pairs={{0,1},{3,2},{4,5},{7,6},{8,9},{11,10},{12,13},{15,14},{16,17},{19,... | collective-permute-start | bytes 1572872 | tf_op jit(solution)/shard_map/ppermute | solution.py:252
  54.8 5.7 %fusion.1 = f32[256,4096]{1,0:T(8,128)S(1)} fusion(bf16[256,1024]{1,0:T(8,128)(2,1)S(1)} %get-tuple-element.68, bf16[1024,4096]{1,0:T(8,128)(2,1)} %param.13), kind=kOutput, calls=%fused_computation.14 | convolution fusion | flops 2147483648 | bytes 13107200 | tf_op jit(solution)/shard_map/dot_general | solution.py:265
  60.6 1.9 %copy-done.2 = f32[256,4096]{1,0:T(8,128)} copy-done((f32[256,4096]{1,0:T(8,128)}, f32[256,4096]{1,0:T(8,128)S(1)}, u32[]{:S(2)}) %copy-start.2) | copy-done | bytes 4194328
  62.6 2.1 %collective-permute-start.14 = (f32[256,512]{1,0:T(8,128)S(1)}, f32[256,512]{1,0:T(8,128)}, u32[]{:S(2)}, u32[]{:S(2)}) collective-permute-start(f32[256,512]{1,0:T(8,128)S(1)} %constant_dynamic-slice_fusion), channel_id=1, source_target_pairs={{0,1},{3,2},{4,5},{7,6},{8,9},{11,10},{12,13},{15,14},{16,17},{19,... | collective-permute-start | bytes 1572872 | tf_op jit(solution)/shard_map/ppermute | solution.py:252
  64.7 2.4 %collective-permute-done.15 = f32[256,512]{1,0:T(8,128)S(1)} collective-permute-done((f32[256,512]{1,0:T(8,128)S(1)}, f32[256,512]{1,0:T(8,128)S(1)}, u32[]{:S(2)}, u32[]{:S(2)}) %collective-permute-start.15) | collective-permute-done | bytes 524320 | tf_op jit(solution)/shard_map/ppermute | solution.py:252
  67.1 1.4 %dynamic-slice_add_fusion.6 = (f32[256,512]{1,0:T(8,128)S(1)}, f32[256,512]{1,0:T(8,128)S(1)}) fusion(f32[256,4096]{1,0:T(8,128)} %copy-done.2, s32[]{:T(128)S(6)} %select_n.74, f32[256,512]{1,0:T(8,128)S(1)} %collective-permute-done.15, pred[]{:T(512)S(6)} %eq.19, s32[]{:T(128)S(6)} %select_n.71, pred[]{:T(512)S(6)} %eq.16), kind=kLoop, calls=%fused_computation.8 | loop fusion | flops 524288 | bytes 2621450 | tf_op jit(solution)/shard_map/add | solution.py:277
  68.4 4.4 %collective-permute-start.17 = (f32[256,512]{1,0:T(8,128)S(1)}, f32[256,512]{1,0:T(8,128)S(1)}, u32[]{:S(2)}, u32[]{:S(2)}) collective-permute-start(f32[256,512]{1,0:T(8,128)S(1)} %get-tuple-element.78), channel_id=1, source_target_pairs={{0,1},{1,2},{4,5},{5,6},{8,9},{9,10},{12,13},{13,14},{16,17},{17,1... | collective-permute-start | bytes 1572872 | tf_op jit(solution)/shard_map/ppermute | solution.py:243
  72.9 0.7 collective-permute-start.18
  73.6 4.7 %collective-permute-done.14 = f32[256,512]{1,0:T(8,128)} collective-permute-done((f32[256,512]{1,0:T(8,128)S(1)}, f32[256,512]{1,0:T(8,128)}, u32[]{:S(2)}, u32[]{:S(2)}) %collective-permute-start.14) | collective-permute-done | bytes 524320 | tf_op jit(solution)/shard_map/ppermute | solution.py:252
  78.3 1.5 %dynamic-slice_add_fusion.4 = (f32[256,512]{1,0:T(8,128)S(1)}, f32[256,512]{1,0:T(8,128)S(1)}) fusion(f32[256,4096]{1,0:T(8,128)} %copy-done.2, s32[]{:T(128)S(6)} %select_n.77, f32[256,512]{1,0:T(8,128)} %collective-permute-done.14, pred[]{:T(512)S(6)} %eq.19, s32[]{:T(128)S(6)} %select_n.75, pred[]{:T(512)S(6)} %eq.16), kind=kLoop, calls=%fused_computation.6 | loop fusion | flops 524288 | bytes 2621450 | tf_op jit(solution)/shard_map/add | solution.py:277
  79.8 5.3 %collective-permute-start.16 = (f32[256,512]{1,0:T(8,128)S(1)}, f32[256,512]{1,0:T(8,128)}, u32[]{:S(2)}, u32[]{:S(2)}) collective-permute-start(f32[256,512]{1,0:T(8,128)S(1)} %get-tuple-element.75), channel_id=1, source_target_pairs={{0,1},{1,2},{4,5},{5,6},{8,9},{9,10},{12,13},{13,14},{16,17},{17,1... | collective-permute-start | bytes 1572872 | tf_op jit(solution)/shard_map/ppermute | solution.py:243
  85.2 1.5 %collective-permute-start.19 = (f32[256,512]{1,0:T(8,128)S(1)}, f32[256,512]{1,0:T(8,128)}, u32[]{:S(2)}, u32[]{:S(2)}) collective-permute-start(f32[256,512]{1,0:T(8,128)S(1)} %get-tuple-element.82), channel_id=1, source_target_pairs={{2,1},{3,2},{6,5},{7,6},{10,9},{11,10},{14,13},{15,14},{18,17},{19... | collective-permute-start | bytes 1572872 | tf_op jit(solution)/shard_map/ppermute | solution.py:244
  86.6 2.9 %collective-permute-done.17 = f32[256,512]{1,0:T(8,128)S(1)} collective-permute-done((f32[256,512]{1,0:T(8,128)S(1)}, f32[256,512]{1,0:T(8,128)S(1)}, u32[]{:S(2)}, u32[]{:S(2)}) %collective-permute-start.17) | collective-permute-done | bytes 524320 | tf_op jit(solution)/shard_map/ppermute | solution.py:243
  89.5 0.0 collective-permute-done.18
  89.6 1.4 %dynamic-slice_add_fusion.2 = (f32[256,512]{1,0:T(8,128)S(1)}, f32[256,512]{1,0:T(8,128)S(1)}) fusion(f32[256,512]{1,0:T(8,128)S(1)} %collective-permute-done.18, f32[256,4096]{1,0:T(8,128)} %copy-done.2, s32[]{:T(128)S(6)} %select_n.79, f32[256,512]{1,0:T(8,128)S(1)} %collective-permute-done.17, s32[]{:T(128)S(6)} %select_n.78), kind=kLoop, calls=%fused_computation.4 | loop fusion | flops 262144 | bytes 3145736 | tf_op jit(solution)/shard_map/add | solution.py:277
  91.0 4.4 %collective-permute-start.20 = (f32[256,512]{1,0:T(8,128)S(1)}, f32[256,512]{1,0:T(8,128)S(1)}, u32[]{:S(2)}, u32[]{:S(2)}) collective-permute-start(f32[256,512]{1,0:T(8,128)S(1)} %get-tuple-element.86), channel_id=1, source_target_pairs={{0,1},{1,2},{2,3},{4,5},{5,6},{6,7},{8,9},{9,10},{10,11},{12,13},{... | collective-permute-start | bytes 1572872 | tf_op jit(solution)/shard_map/ppermute | solution.py:243
  95.4 1.3 %collective-permute-start.21 = (f32[256,512]{1,0:T(8,128)S(1)}, f32[256,512]{1,0:T(8,128)S(1)}, u32[]{:S(2)}, u32[]{:S(2)}) collective-permute-start(f32[256,512]{1,0:T(8,128)S(1)} %get-tuple-element.87), channel_id=1, source_target_pairs={{1,0},{2,1},{3,2},{5,4},{6,5},{7,6},{9,8},{10,9},{11,10},{13,12},{... | collective-permute-start | bytes 1572872 | tf_op jit(solution)/shard_map/ppermute | solution.py:244
  96.7 4.1 %collective-permute-done.16 = f32[256,512]{1,0:T(8,128)} collective-permute-done((f32[256,512]{1,0:T(8,128)S(1)}, f32[256,512]{1,0:T(8,128)}, u32[]{:S(2)}, u32[]{:S(2)}) %collective-permute-start.16) | collective-permute-done | bytes 524320 | tf_op jit(solution)/shard_map/ppermute | solution.py:243
  100.8 0.0 collective-permute-done.19
  100.8 1.7 %dynamic-slice_add_fusion = (f32[256,512]{1,0:T(8,128)S(1)}, f32[256,512]{1,0:T(8,128)S(1)}) fusion(f32[256,512]{1,0:T(8,128)} %collective-permute-done.19, f32[256,4096]{1,0:T(8,128)} %copy-done.2, s32[]{:T(128)S(6)} %select_n.81, f32[256,512]{1,0:T(8,128)} %collective-permute-done.16, s32[]{:T(128)S(6)} %select_n.80), kind=kLoop, calls=%fused_computation.2 | loop fusion | flops 262144 | bytes 3145736 | tf_op jit(solution)/shard_map/add | solution.py:277
  102.5 5.3 %collective-permute-start.22 = (f32[256,512]{1,0:T(8,128)S(1)}, f32[256,512]{1,0:T(8,128)}, u32[]{:S(2)}, u32[]{:S(2)}) collective-permute-start(f32[256,512]{1,0:T(8,128)S(1)} %get-tuple-element.92), channel_id=1, source_target_pairs={{0,1},{1,2},{2,3},{4,5},{5,6},{6,7},{8,9},{9,10},{10,11},{12,13},{... | collective-permute-start | bytes 1572872 | tf_op jit(solution)/shard_map/ppermute | solution.py:243
  107.8 1.3 %collective-permute-start.23 = (f32[256,512]{1,0:T(8,128)S(1)}, f32[256,512]{1,0:T(8,128)}, u32[]{:S(2)}, u32[]{:S(2)}) collective-permute-start(f32[256,512]{1,0:T(8,128)S(1)} %get-tuple-element.93), channel_id=1, source_target_pairs={{1,0},{2,1},{3,2},{5,4},{6,5},{7,6},{9,8},{10,9},{11,10},{13,12},{... | collective-permute-start | bytes 1572872 | tf_op jit(solution)/shard_map/ppermute | solution.py:244
  109.1 2.9 %collective-permute-done.20 = f32[256,512]{1,0:T(8,128)S(1)} collective-permute-done((f32[256,512]{1,0:T(8,128)S(1)}, f32[256,512]{1,0:T(8,128)S(1)}, u32[]{:S(2)}, u32[]{:S(2)}) %collective-permute-start.20) | collective-permute-done | bytes 524320 | tf_op jit(solution)/shard_map/ppermute | solution.py:243
  112.0 0.0 collective-permute-done.21
  112.0 1.2 add_convert_fusion.1
  113.2 0.9 dynamic_update_slice.6
  114.0 8.3 %collective-permute-done.22 = f32[256,512]{1,0:T(8,128)} collective-permute-done((f32[256,512]{1,0:T(8,128)S(1)}, f32[256,512]{1,0:T(8,128)}, u32[]{:S(2)}, u32[]{:S(2)}) %collective-permute-start.22) | collective-permute-done | bytes 524320 | tf_op jit(solution)/shard_map/ppermute | solution.py:243
  122.4 0.0 collective-permute-done.23
  122.4 2.2 %fusion = bf16[256,1024]{1,0:T(8,128)(2,1)} fusion(bf16[256,1024]{1,0:T(8,128)(2,1)} %dynamic_update_slice.6, f32[256,512]{1,0:T(8,128)} %collective-permute-done.23, f32[256,512]{1,0:T(8,128)} %collective-permute-done.22, f32[256,4096]{1,0:T(8,128)} %copy-done.2, s32[]{:T(128)S(6)} %select_n.83), kind=kLoop, calls=%fused_computation.10 | loop fusion | flops 393216 | bytes 1835012 | tf_op jit(solution)/shard_map/dynamic_update_slice | solution.py:283
  (5 shorter events, 0.0 us)
Async XLA Ops:
  0.0 25.8 %copy-start = (bf16[512,768]{1,0:T(8,128)(2,1)S(1)}, bf16[512,768]{1,0:T(8,128)(2,1)}, u32[]{:S(2)}) copy-start(bf16[512,768]{1,0:T(8,128)(2,1)} %constant.48.clone.ahead_ref.refs_2_) | copy-start | bytes 2359300
  2.7 7.3 %collective-permute-start = (f32[256,256]{1,0:T(8,128)}, f32[256,256]{1,0:T(8,128)S(1)}, u32[]{:S(2)}, u32[]{:S(2)}) collective-permute-start(f32[256,256]{1,0:T(8,128)} %get-tuple-element.53), channel_id=1, source_target_pairs={{0,4},{4,0},{8,12},{12,8},{16,20},{20,16},{24,28},{28,24},{1,5},{5... | collective-permute-start | bytes 786440 | tf_op jit(solution)/shard_map/ppermute | solution.py:93
  3.2 11.0 %collective-permute-start.1 = (f32[256,256]{1,0:T(8,128)}, f32[256,256]{1,0:T(8,128)S(1)}, u32[]{:S(2)}, u32[]{:S(2)}) collective-permute-start(f32[256,256]{1,0:T(8,128)} %get-tuple-element.54), channel_id=1, source_target_pairs={{0,24},{4,28},{8,16},{12,20},{16,8},{20,12},{24,0},{28,4},{1,25},{... | collective-permute-start | bytes 786440 | tf_op jit(solution)/shard_map/ppermute | solution.py:93
  6.7 12.6 %collective-permute-start.2 = (f32[256,256]{1,0:T(8,128)}, f32[256,256]{1,0:T(8,128)S(1)}, u32[]{:S(2)}, u32[]{:S(2)}) collective-permute-start(f32[256,256]{1,0:T(8,128)} %get-tuple-element.55), channel_id=1, source_target_pairs={{0,28},{4,24},{8,20},{12,16},{16,12},{20,8},{24,4},{28,0},{1,29},{... | collective-permute-start | bytes 786440 | tf_op jit(solution)/shard_map/ppermute | solution.py:93
  6.8 19.0 %collective-permute-start.3 = (f32[256,256]{1,0:T(8,128)}, f32[256,256]{1,0:T(8,128)S(1)}, u32[]{:S(2)}, u32[]{:S(2)}) collective-permute-start(f32[256,256]{1,0:T(8,128)} %get-tuple-element.56), channel_id=1, source_target_pairs={{0,8},{4,12},{8,0},{12,4},{16,24},{20,28},{24,16},{28,20},{1,9},{5... | collective-permute-start | bytes 786440 | tf_op jit(solution)/shard_map/ppermute | solution.py:93
  8.5 17.4 %collective-permute-start.4 = (f32[256,256]{1,0:T(8,128)}, f32[256,256]{1,0:T(8,128)}, u32[]{:S(2)}, u32[]{:S(2)}) collective-permute-start(f32[256,256]{1,0:T(8,128)} %get-tuple-element.57), channel_id=1, source_target_pairs={{0,16},{4,20},{8,24},{12,28},{16,0},{20,4},{24,8},{28,12},{1,17},{... | collective-permute-start | bytes 786440 | tf_op jit(solution)/shard_map/ppermute | solution.py:93
  10.0 20.5 %collective-permute-start.5 = (f32[256,256]{1,0:T(8,128)}, f32[256,256]{1,0:T(8,128)S(1)}, u32[]{:S(2)}, u32[]{:S(2)}) collective-permute-start(f32[256,256]{1,0:T(8,128)} %get-tuple-element.58), channel_id=1, source_target_pairs={{0,12},{4,8},{8,4},{12,0},{16,28},{20,24},{24,20},{28,16},{1,13},{... | collective-permute-start | bytes 786440 | tf_op jit(solution)/shard_map/ppermute | solution.py:93
  14.2 16.4 %collective-permute-start.6 = (f32[256,256]{1,0:T(8,128)}, f32[256,256]{1,0:T(8,128)S(1)}, u32[]{:S(2)}, u32[]{:S(2)}) collective-permute-start(f32[256,256]{1,0:T(8,128)} %get-tuple-element.59), channel_id=1, source_target_pairs={{0,20},{4,16},{8,28},{12,24},{16,4},{20,0},{24,12},{28,8},{1,21},{... | collective-permute-start | bytes 786440 | tf_op jit(solution)/shard_map/ppermute | solution.py:93
  25.8 1.0 copy-start.1
  33.9 5.7 %collective-permute-start.10 = (f32[256,128]{1,0:T(8,128)S(1)}, f32[256,128]{1,0:T(8,128)S(1)}, u32[]{:S(2)}, u32[]{:S(2)}) collective-permute-start(f32[256,128]{1,0:T(8,128)S(1)} %get-tuple-element.64), channel_id=1, source_target_pairs={{0,8},{4,12},{8,0},{12,4},{16,24},{20,28},{24,16},{28,20},{1,9},{5... | collective-permute-start | bytes 393224 | tf_op jit(solution)/shard_map/ppermute | solution.py:93
  35.6 7.3 %collective-permute-start.11 = (f32[256,128]{1,0:T(8,128)S(1)}, f32[256,128]{1,0:T(8,128)S(1)}, u32[]{:S(2)}, u32[]{:S(2)}) collective-permute-start(f32[256,128]{1,0:T(8,128)S(1)} %get-tuple-element.65), channel_id=1, source_target_pairs={{0,16},{4,20},{8,24},{12,28},{16,0},{20,4},{24,8},{28,12},{1,17},{... | collective-permute-start | bytes 393224 | tf_op jit(solution)/shard_map/ppermute | solution.py:93
  37.2 5.9 %collective-permute-start.12 = (f32[256,128]{1,0:T(8,128)S(1)}, f32[256,128]{1,0:T(8,128)S(1)}, u32[]{:S(2)}, u32[]{:S(2)}) collective-permute-start(f32[256,128]{1,0:T(8,128)S(1)} %get-tuple-element.66), channel_id=1, source_target_pairs={{0,12},{4,8},{8,4},{12,0},{16,28},{20,24},{24,20},{28,16},{1,13},{... | collective-permute-start | bytes 393224 | tf_op jit(solution)/shard_map/ppermute | solution.py:93
  37.2 11.2 %collective-permute-start.13 = (f32[256,128]{1,0:T(8,128)S(1)}, f32[256,128]{1,0:T(8,128)S(1)}, u32[]{:S(2)}, u32[]{:S(2)}) collective-permute-start(f32[256,128]{1,0:T(8,128)S(1)} %get-tuple-element.67), channel_id=1, source_target_pairs={{0,20},{4,16},{8,28},{12,24},{16,4},{20,0},{24,12},{28,8},{1,21},{... | collective-permute-start | bytes 393224 | tf_op jit(solution)/shard_map/ppermute | solution.py:93
  37.7 10.7 %collective-permute-start.7 = (f32[256,128]{1,0:T(8,128)S(1)}, f32[256,128]{1,0:T(8,128)S(1)}, u32[]{:S(2)}, u32[]{:S(2)}) collective-permute-start(f32[256,128]{1,0:T(8,128)S(1)} %get-tuple-element.61), channel_id=1, source_target_pairs={{0,4},{4,0},{8,12},{12,8},{16,20},{20,16},{24,28},{28,24},{1,5},{5... | collective-permute-start | bytes 393224 | tf_op jit(solution)/shard_map/ppermute | solution.py:93
  39.6 8.8 %collective-permute-start.8 = (f32[256,128]{1,0:T(8,128)S(1)}, f32[256,128]{1,0:T(8,128)S(1)}, u32[]{:S(2)}, u32[]{:S(2)}) collective-permute-start(f32[256,128]{1,0:T(8,128)S(1)} %get-tuple-element.62), channel_id=1, source_target_pairs={{0,24},{4,28},{8,16},{12,20},{16,8},{20,12},{24,0},{28,4},{1,25},{... | collective-permute-start | bytes 393224 | tf_op jit(solution)/shard_map/ppermute | solution.py:93
  43.0 6.2 %collective-permute-start.9 = (f32[256,128]{1,0:T(8,128)S(1)}, f32[256,128]{1,0:T(8,128)S(1)}, u32[]{:S(2)}, u32[]{:S(2)}) collective-permute-start(f32[256,128]{1,0:T(8,128)S(1)} %get-tuple-element.63), channel_id=1, source_target_pairs={{0,28},{4,24},{8,20},{12,16},{16,12},{20,8},{24,4},{28,0},{1,29},{... | collective-permute-start | bytes 393224 | tf_op jit(solution)/shard_map/ppermute | solution.py:93
  51.7 15.3 %collective-permute-start.15 = (f32[256,512]{1,0:T(8,128)S(1)}, f32[256,512]{1,0:T(8,128)S(1)}, u32[]{:S(2)}, u32[]{:S(2)}) collective-permute-start(f32[256,512]{1,0:T(8,128)S(1)} %get-tuple-element.70), channel_id=1, source_target_pairs={{0,1},{3,2},{4,5},{7,6},{8,9},{11,10},{12,13},{15,14},{16,17},{19,... | collective-permute-start | bytes 1572872 | tf_op jit(solution)/shard_map/ppermute | solution.py:252
  60.6 2.0 %copy-start.2 = (f32[256,4096]{1,0:T(8,128)}, f32[256,4096]{1,0:T(8,128)S(1)}, u32[]{:S(2)}) copy-start(f32[256,4096]{1,0:T(8,128)S(1)} %fusion.1) | copy-start | bytes 12582916
  62.6 15.8 %collective-permute-start.14 = (f32[256,512]{1,0:T(8,128)S(1)}, f32[256,512]{1,0:T(8,128)}, u32[]{:S(2)}, u32[]{:S(2)}) collective-permute-start(f32[256,512]{1,0:T(8,128)S(1)} %constant_dynamic-slice_fusion), channel_id=1, source_target_pairs={{0,1},{3,2},{4,5},{7,6},{8,9},{11,10},{12,13},{15,14},{16,17},{19,... | collective-permute-start | bytes 1572872 | tf_op jit(solution)/shard_map/ppermute | solution.py:252
  68.4 21.1 %collective-permute-start.17 = (f32[256,512]{1,0:T(8,128)S(1)}, f32[256,512]{1,0:T(8,128)S(1)}, u32[]{:S(2)}, u32[]{:S(2)}) collective-permute-start(f32[256,512]{1,0:T(8,128)S(1)} %get-tuple-element.78), channel_id=1, source_target_pairs={{0,1},{1,2},{4,5},{5,6},{8,9},{9,10},{12,13},{13,14},{16,17},{17,1... | collective-permute-start | bytes 1572872 | tf_op jit(solution)/shard_map/ppermute | solution.py:243
  72.9 16.7 %collective-permute-start.18 = (f32[256,512]{1,0:T(8,128)S(1)}, f32[256,512]{1,0:T(8,128)S(1)}, u32[]{:S(2)}, u32[]{:S(2)}) collective-permute-start(f32[256,512]{1,0:T(8,128)S(1)} %get-tuple-element.80), channel_id=1, source_target_pairs={{2,1},{3,2},{6,5},{7,6},{10,9},{11,10},{14,13},{15,14},{18,17},{19... | collective-permute-start | bytes 1572872 | tf_op jit(solution)/shard_map/ppermute | solution.py:244
  79.8 20.9 %collective-permute-start.16 = (f32[256,512]{1,0:T(8,128)S(1)}, f32[256,512]{1,0:T(8,128)}, u32[]{:S(2)}, u32[]{:S(2)}) collective-permute-start(f32[256,512]{1,0:T(8,128)S(1)} %get-tuple-element.75), channel_id=1, source_target_pairs={{0,1},{1,2},{4,5},{5,6},{8,9},{9,10},{12,13},{13,14},{16,17},{17,1... | collective-permute-start | bytes 1572872 | tf_op jit(solution)/shard_map/ppermute | solution.py:243
  85.2 15.6 %collective-permute-start.19 = (f32[256,512]{1,0:T(8,128)S(1)}, f32[256,512]{1,0:T(8,128)}, u32[]{:S(2)}, u32[]{:S(2)}) collective-permute-start(f32[256,512]{1,0:T(8,128)S(1)} %get-tuple-element.82), channel_id=1, source_target_pairs={{2,1},{3,2},{6,5},{7,6},{10,9},{11,10},{14,13},{15,14},{18,17},{19... | collective-permute-start | bytes 1572872 | tf_op jit(solution)/shard_map/ppermute | solution.py:244
  91.0 21.1 %collective-permute-start.20 = (f32[256,512]{1,0:T(8,128)S(1)}, f32[256,512]{1,0:T(8,128)S(1)}, u32[]{:S(2)}, u32[]{:S(2)}) collective-permute-start(f32[256,512]{1,0:T(8,128)S(1)} %get-tuple-element.86), channel_id=1, source_target_pairs={{0,1},{1,2},{2,3},{4,5},{5,6},{6,7},{8,9},{9,10},{10,11},{12,13},{... | collective-permute-start | bytes 1572872 | tf_op jit(solution)/shard_map/ppermute | solution.py:243
  95.4 16.6 %collective-permute-start.21 = (f32[256,512]{1,0:T(8,128)S(1)}, f32[256,512]{1,0:T(8,128)S(1)}, u32[]{:S(2)}, u32[]{:S(2)}) collective-permute-start(f32[256,512]{1,0:T(8,128)S(1)} %get-tuple-element.87), channel_id=1, source_target_pairs={{1,0},{2,1},{3,2},{5,4},{6,5},{7,6},{9,8},{10,9},{11,10},{13,12},{... | collective-permute-start | bytes 1572872 | tf_op jit(solution)/shard_map/ppermute | solution.py:244
  102.5 19.9 %collective-permute-start.22 = (f32[256,512]{1,0:T(8,128)S(1)}, f32[256,512]{1,0:T(8,128)}, u32[]{:S(2)}, u32[]{:S(2)}) collective-permute-start(f32[256,512]{1,0:T(8,128)S(1)} %get-tuple-element.92), channel_id=1, source_target_pairs={{0,1},{1,2},{2,3},{4,5},{5,6},{6,7},{8,9},{9,10},{10,11},{12,13},{... | collective-permute-start | bytes 1572872 | tf_op jit(solution)/shard_map/ppermute | solution.py:243
  107.8 14.6 %collective-permute-start.23 = (f32[256,512]{1,0:T(8,128)S(1)}, f32[256,512]{1,0:T(8,128)}, u32[]{:S(2)}, u32[]{:S(2)}) collective-permute-start(f32[256,512]{1,0:T(8,128)S(1)} %get-tuple-element.93), channel_id=1, source_target_pairs={{1,0},{2,1},{3,2},{5,4},{6,5},{7,6},{9,8},{10,9},{11,10},{13,12},{... | collective-permute-start | bytes 1572872 | tf_op jit(solution)/shard_map/ppermute | solution.py:244

commit v8 on v5

--- a/solution.py
+++ b/solution.py
@@ -190,7 +190,9 @@
     )(place, early, *xs[first:], ahead, stay(back))
 
 
-CHAINS = 2
+def chain_widths(width):
+    first = -(-width * 5 // 8 // 128) * 128
+    return [first, width - first]
 
 
 def gate_kernel(place_ref, far_ref, q_hbm, *refs):
@@ -257,27 +259,29 @@
 def scatter_dot(lhs, rhs, first):
     size = lax.axis_size("tp")
     place = lax.axis_index("tp")
-    rows, width = first.shape
+    rows = first.shape[0]
+    width = rhs.shape[1] // size
+    widths = chain_widths(width)
     lhs, first = lax.optimization_barrier((lhs, first))
     terms = jnp.dot(lhs, rhs, preferred_element_type=F32)
 
     def own(index, k):
-        start = jnp.clip(index, 0, size - 1) * (width * CHAINS) + k * width
-        return lax.dynamic_slice_in_dim(terms, start, width, 1)
-
-    firsts = [first] + [own(far_end(size), k) for k in range(1, CHAINS)]
+        start = jnp.clip(index, 0, size - 1) * width + sum(widths[:k])
+        return lax.dynamic_slice_in_dim(terms, start, widths[k], 1)
+
+    firsts = [first] + [own(far_end(size), k) for k in range(1, len(widths))]
     firsts[1:], terms = lax.optimization_barrier((firsts[1:], terms))
     sums = [first_step(value, size) for value in firsts]
     for step in range(2, size):
-        for k in range(CHAINS):
+        for k in range(len(widths)):
             up = sums[k][0] + own(place + size - step, k)
             down = sums[k][1] + own(place - size + step, k)
             up, down, terms = lax.optimization_barrier((up, down, terms))
             sums[k] = pass_on(up, down, step, size)
-    out = jnp.zeros((rows, width * CHAINS), BF16)
-    for k in range(CHAINS):
+    out = jnp.zeros((rows, width), BF16)
+    for k in range(len(widths)):
         part = (own(place, k) + sums[k][0] + sums[k][1]).astype(BF16)
-        out = lax.dynamic_update_slice(out, part, (0, k * width))
+        out = lax.dynamic_update_slice(out, part, (0, sum(widths[:k])))
         out, terms = lax.optimization_barrier((out, terms))
     return out
 
@@ -287,8 +291,8 @@
     size = lax.axis_size("tp")
     place = lax.axis_index("ctx").reshape(1)
     xs = swap(pack(place, keys, values, filt, direct.reshape(1, -1), count))
-    part = w_out.shape[1] // (size * CHAINS)
-    far = lax.dynamic_slice_in_dim(w_out, far_end(size) * (part * CHAINS), part, 1)
+    part = w_out.shape[1] // size
+    far = lax.dynamic_slice_in_dim(w_out, far_end(size) * part, chain_widths(part)[0], 1)
     xs[0], far = lax.optimization_barrier((xs[0], far))
     convs = swap(convolve(place, xs))
     gated, first = gate(place, query, far, convs)

time: 125 us -> 139 us (1.11); the launches traced: 124 us -> 137 us
  waiting for transfers between devices: 48.7 us -> 57.2 us
  starting transfers between devices: 45.1 us -> 50.9 us
  local copies, waits for them, and re-layouts: 5.09 us -> 3.29 us
    ppermute x2, waiting for transfers between devices: 7.13 us -> 24.7 us  [first_step(): got = lax.ppermute(value, 'tp', [(0, 1), (size - 1, size - 2)])]
    ppermute x4, waiting for transfers between devices: 18.3 us -> 1.14 us  [pass_on(): up = lax.ppermute(up, 'tp', rise)]
    ppermute x4, waiting for transfers between devices: 0.01 us -> 8.28 us  [pass_on(): down = lax.ppermute(down, 'tp', fall)]
    ppermute x4, starting transfers between devices: 19.5 us -> 22.6 us  [pass_on(): up = lax.ppermute(up, 'tp', rise)]
    ppermute x2, starting transfers between devices: 5.62 us -> 8.32 us  [first_step(): got = lax.ppermute(value, 'tp', [(0, 1), (size - 1, size - 2)])]
    unnamed x6, local copies, waits for them, and re-layouts: 2.9 us -> 0.96 us
  transfers between devices with their start and end apart: 24 -> 24, of which waited for: 14 -> 13; matrix products, arithmetic and copies ran while one was open for 12% -> 11% of each run, Pallas kernels for 2% -> 2%
where the time goes in v8:
time: 139 us; the launch traced here: 137 us
  waiting for transfers between devices  57.2 us (41%)
  starting transfers between devices  50.9 us (37%)
  Pallas kernels  10.4 us (7%)
  other arithmetic  9.21 us (7%)
  matrix products  5.72 us (4%)
  local copies, waits for them, and re-layouts  3.29 us (2%)
    ppermute x2, waiting for transfers between devices, first_step(): got = lax.ppermute(value, 'tp', [(0, 1), (size - 1, size - 2)])  24.7 us
    ppermute x14, waiting for transfers between devices, swap(): lax.ppermute(arrays[j], 'ctx', pairs[j])  23.1 us
    ppermute x4, starting transfers between devices, pass_on(): up = lax.ppermute(up, 'tp', rise)  22.6 us
    ppermute x14, starting transfers between devices, swap(): lax.ppermute(arrays[j], 'ctx', pairs[j])  15.3 us
    ppermute x2, starting transfers between devices, first_step(): got = lax.ppermute(value, 'tp', [(0, 1), (size - 1, size - 2)])  8.32 us
    ppermute x4, waiting for transfers between devices, pass_on(): down = lax.ppermute(down, 'tp', fall)  8.28 us
    add x4, other arithmetic, scatter_dot(): down = sums[k][1] + own(place - size + step, k)  6.18 us
    dot_general x1, matrix products, scatter_dot(): terms = jnp.dot(lhs, rhs, preferred_element_type=F32)  5.72 us
  transfers between devices with their start and end apart: 24, of which 13 were waited for; matrix products, arithmetic and copies ran while one was open for 11% of the time, Pallas kernels for 2%

profile of v8, /device:TPU:0, one launch (start us, length us, event | category | flops | bytes accessed | tf_op | source)
XLA Modules:
  0.0 136.9 jit_solution(18210080978854184349)
XLA Ops:
  0.0 2.7 %shard_map.82 = (f32[256,256]{1,0:T(8,128)}, f32[256,256]{1,0:T(8,128)}, f32[256,256]{1,0:T(8,128)}, f32[256,256]{1,0:T(8,128)}, f32[256,256]{1,0:T(8,128)}, /*i...) custom-call(s32[1]{0:T(128)} %bitcast.place_ref, bf16[256,1024]{1,0:T(8,128)(2,1)} %keys_ref.1, ...), custom_call_target="tpu_custom_call" | custom-call | tf_op jit(solution)/shard_map/pallas_call | solution.py:74
  2.7 0.5 collective-permute-start
  3.2 3.5 %collective-permute-start.1 = (f32[256,256]{1,0:T(8,128)}, f32[256,256]{1,0:T(8,128)S(1)}, u32[]{:S(2)}, u32[]{:S(2)}) collective-permute-start(f32[256,256]{1,0:T(8,128)} %get-tuple-element.54), channel_id=1, source_target_pairs={{0,24},{4,28},{8,16},{12,20},{16,8},{20,12},{24,0},{28,4},{1,25},{... | collective-permute-start | bytes 786440 | tf_op jit(solution)/shard_map/ppermute | solution.py:93
  6.7 0.1 collective-permute-start.2
  6.8 1.7 %collective-permute-start.3 = (f32[256,256]{1,0:T(8,128)}, f32[256,256]{1,0:T(8,128)}, u32[]{:S(2)}, u32[]{:S(2)}) collective-permute-start(f32[256,256]{1,0:T(8,128)} %get-tuple-element.56), channel_id=1, source_target_pairs={{0,8},{4,12},{8,0},{12,4},{16,24},{20,28},{24,16},{28,20},{1,9},{5... | collective-permute-start | bytes 786440 | tf_op jit(solution)/shard_map/ppermute | solution.py:93
  8.5 1.5 %collective-permute-start.4 = (f32[256,256]{1,0:T(8,128)}, f32[256,256]{1,0:T(8,128)}, u32[]{:S(2)}, u32[]{:S(2)}) collective-permute-start(f32[256,256]{1,0:T(8,128)} %get-tuple-element.57), channel_id=1, source_target_pairs={{0,16},{4,20},{8,24},{12,28},{16,0},{20,4},{24,8},{28,12},{1,17},{... | collective-permute-start | bytes 786440 | tf_op jit(solution)/shard_map/ppermute | solution.py:93
  10.0 0.0 collective-permute-done.refs_1_
  10.0 0.0 collective-permute-start.5
  10.0 4.2 %collective-permute-done.1.refs_2_ = f32[256,256]{1,0:T(8,128)S(1)} collective-permute-done((f32[256,256]{1,0:T(8,128)}, f32[256,256]{1,0:T(8,128)S(1)}, u32[]{:S(2)}, u32[]{:S(2)}) %collective-permute-start.1) | collective-permute-done | bytes 262176 | tf_op jit(solution)/shard_map/ppermute | solution.py:93
  14.2 0.7 collective-permute-start.6
  14.9 1.4 %constant_dynamic-slice_fusion.1.far_ref = bf16[1024,640]{1,0:T(8,128)(2,1)S(1)} fusion(bf16[1024,4096]{1,0:T(8,128)(2,1)} %param.13, s32[]{:T(128)S(6)} %select_n.71), kind=kLoop, calls=%fused_computation.12 | loop fusion | bytes 2621444 | tf_op jit(solution)/shard_map/dynamic_slice | solution.py:295
  16.3 3.0 %collective-permute-done.2.refs_3_ = f32[256,256]{1,0:T(8,128)S(1)} collective-permute-done((f32[256,256]{1,0:T(8,128)}, f32[256,256]{1,0:T(8,128)S(1)}, u32[]{:S(2)}, u32[]{:S(2)}) %collective-permute-start.2) | collective-permute-done | bytes 262176 | tf_op jit(solution)/shard_map/ppermute | solution.py:93
  19.3 6.6 %collective-permute-done.3.refs_4_ = f32[256,256]{1,0:T(8,128)} collective-permute-done((f32[256,256]{1,0:T(8,128)}, f32[256,256]{1,0:T(8,128)}, u32[]{:S(2)}, u32[]{:S(2)}) %collective-permute-start.3) | collective-permute-done | bytes 262176 | tf_op jit(solution)/shard_map/ppermute | solution.py:93
  25.9 0.0 collective-permute-done.4.refs_5_
  25.9 0.0 copy-done
  25.9 0.9 copy-done.1
  26.9 2.4 %shard_map.83.early_ref = f32[6,512,256]{2,1,0:T(8,128)S(1)} custom-call(bf16[512,768]{1,0:T(8,128)(2,1)S(1)} %copy-done, f32[256,256]{1,0:T(8,128)S(1)} %copy-done.1, f32[256,256]{1,0:T(8,128)S(1)} %collective-permute-done.refs_1_, f32[256,256]{1,0:T(8,128)S(1)} %collective-permute-done.1.refs_2_, f32[256,256]{1,0:T(8,128)S(1)} %collective-permute-done.2.refs_3_, ...), custom_call_target="tpu_custom_call" | custom-call | tf_op jit(solution)/shard_map/pallas_call | solution.py:104
  29.3 1.2 collective-permute-done.5.refs_0_
  30.5 0.1 collective-permute-done.6.refs_1_
  30.6 3.3 %shard_map.84 = (f32[256,128]{1,0:T(8,128)S(1)}, f32[256,128]{1,0:T(8,128)S(1)}, f32[256,128]{1,0:T(8,128)S(1)}, f32[256,128]{1,0:T(8,128)S(1)}, f32[256,128]{1,...) custom-call(s32[1]{0:T(128)} %bitcast.place_ref, ...), custom_call_target="tpu_custom_call" | custom-call | tf_op jit(solution)/shard_map/pallas_call | solution.py:174
  33.9 1.8 %collective-permute-start.10 = (f32[256,128]{1,0:T(8,128)S(1)}, f32[256,128]{1,0:T(8,128)S(1)}, u32[]{:S(2)}, u32[]{:S(2)}) collective-permute-start(f32[256,128]{1,0:T(8,128)S(1)} %get-tuple-element.64), channel_id=1, source_target_pairs={{0,8},{4,12},{8,0},{12,4},{16,24},{20,28},{24,16},{28,20},{1,9},{5... | collective-permute-start | bytes 393224 | tf_op jit(solution)/shard_map/ppermute | solution.py:93
  35.6 1.5 %collective-permute-start.11 = (f32[256,128]{1,0:T(8,128)S(1)}, f32[256,128]{1,0:T(8,128)S(1)}, u32[]{:S(2)}, u32[]{:S(2)}) collective-permute-start(f32[256,128]{1,0:T(8,128)S(1)} %get-tuple-element.65), channel_id=1, source_target_pairs={{0,16},{4,20},{8,24},{12,28},{16,0},{20,4},{24,8},{28,12},{1,17},{... | collective-permute-start | bytes 393224 | tf_op jit(solution)/shard_map/ppermute | solution.py:93
  37.2 0.0 collective-permute-start.12
  37.2 0.6 collective-permute-start.13
  37.7 0.1 collective-permute-start.7
  37.8 1.7 %collective-permute-done.10.refs_4_ = f32[256,128]{1,0:T(8,128)S(1)} collective-permute-done((f32[256,128]{1,0:T(8,128)S(1)}, f32[256,128]{1,0:T(8,128)S(1)}, u32[]{:S(2)}, u32[]{:S(2)}) %collective-permute-start.10) | collective-permute-done | bytes 131104 | tf_op jit(solution)/shard_map/ppermute | solution.py:93
  39.6 3.4 %collective-permute-start.8 = (f32[256,128]{1,0:T(8,128)S(1)}, f32[256,128]{1,0:T(8,128)S(1)}, u32[]{:S(2)}, u32[]{:S(2)}) collective-permute-start(f32[256,128]{1,0:T(8,128)S(1)} %get-tuple-element.62), channel_id=1, source_target_pairs={{0,24},{4,28},{8,16},{12,20},{16,8},{20,12},{24,0},{28,4},{1,25},{... | collective-permute-start | bytes 393224 | tf_op jit(solution)/shard_map/ppermute | solution.py:93
  43.0 0.0 collective-permute-done.11.refs_5_
  43.0 0.0 collective-permute-start.9
  43.0 0.0 collective-permute-done.12.refs_6_
  43.0 5.4 %collective-permute-done.13.refs_7_ = f32[256,128]{1,0:T(8,128)S(1)} collective-permute-done((f32[256,128]{1,0:T(8,128)S(1)}, f32[256,128]{1,0:T(8,128)S(1)}, u32[]{:S(2)}, u32[]{:S(2)}) %collective-permute-start.13) | collective-permute-done | bytes 131104 | tf_op jit(solution)/shard_map/ppermute | solution.py:93
  48.4 0.0 collective-permute-done.7.refs_1_
  48.4 0.0 collective-permute-done.8.refs_2_
  48.4 0.8 collective-permute-done.9.refs_3_
  49.2 2.0 %shard_map.85 = (bf16[256,1024]{1,0:T(8,128)(2,1)S(1)}, f32[256,640]{1,0:T(8,128)S(1)}) custom-call(s32[1]{0:T(128)} %bitcast.place_ref, bf16[1024,640]{1,0:T(8,128)(2,1)S(1)} %constant_dynamic-slice_fusion.1.far_ref, bf16[256,1024]{1,0:T(8,128)(2,1)} %q_hbm.1, f32[256,128]{1,0:T(8,128)S(1)} %get-tuple-element.60.refs_0_, ...), custom_call_target="tpu_custom_call" | custom-call | tf_op jit(solution)/shard_map/pallas_call | solution.py:224
  51.2 3.5 %collective-permute-start.15 = (f32[256,640]{1,0:T(8,128)S(1)}, f32[256,640]{1,0:T(8,128)S(1)}, u32[]{:S(2)}, u32[]{:S(2)}) collective-permute-start(f32[256,640]{1,0:T(8,128)S(1)} %get-tuple-element.70), channel_id=1, source_target_pairs={{0,1},{3,2},{4,5},{7,6},{8,9},{11,10},{12,13},{15,14},{16,17},{19,... | collective-permute-start | bytes 1966088 | tf_op jit(solution)/shard_map/ppermute | solution.py:251
  54.7 5.7 %fusion.1 = f32[256,4096]{1,0:T(8,128)S(1)} fusion(bf16[256,1024]{1,0:T(8,128)(2,1)S(1)} %get-tuple-element.68, bf16[1024,4096]{1,0:T(8,128)(2,1)} %param.13), kind=kOutput, calls=%fused_computation.13 | convolution fusion | flops 2147483648 | bytes 13107200 | tf_op jit(solution)/shard_map/dot_general | solution.py:266
  60.4 0.0 copy-start.2
  60.5 8.4 %collective-permute-done.15 = f32[256,640]{1,0:T(8,128)S(1)} collective-permute-done((f32[256,640]{1,0:T(8,128)S(1)}, f32[256,640]{1,0:T(8,128)S(1)}, u32[]{:S(2)}, u32[]{:S(2)}) %collective-permute-start.15) | collective-permute-done | bytes 655392 | tf_op jit(solution)/shard_map/ppermute | solution.py:251
  68.9 0.2 dynamic-slice_add_fusion.2
  69.1 4.4 %collective-permute-start.17 = (f32[256,640]{1,0:T(8,128)S(1)}, f32[256,640]{1,0:T(8,128)S(1)}, u32[]{:S(2)}, u32[]{:S(2)}) collective-permute-start(f32[256,640]{1,0:T(8,128)S(1)} %get-tuple-element.78), channel_id=1, source_target_pairs={{0,1},{1,2},{4,5},{5,6},{8,9},{9,10},{12,13},{13,14},{16,17},{17,1... | collective-permute-start | bytes 1966088 | tf_op jit(solution)/shard_map/ppermute | solution.py:242
  73.5 0.7 collective-permute-start.18
  74.3 4.8 %collective-permute-start.14 = (f32[256,384]{1,0:T(8,128)S(1)}, f32[256,384]{1,0:T(8,128)}, u32[]{:S(2)}, u32[]{:S(2)}) collective-permute-start(f32[256,384]{1,0:T(8,128)S(1)} %constant_dynamic-slice_fusion), channel_id=1, source_target_pairs={{0,1},{3,2},{4,5},{7,6},{8,9},{11,10},{12,13},{15,14},{16,17},{19,... | collective-permute-start | bytes 1179656 | tf_op jit(solution)/shard_map/ppermute | solution.py:251
  79.1 16.3 %collective-permute-done.14 = f32[256,384]{1,0:T(8,128)} collective-permute-done((f32[256,384]{1,0:T(8,128)S(1)}, f32[256,384]{1,0:T(8,128)}, u32[]{:S(2)}, u32[]{:S(2)}) %collective-permute-start.14) | collective-permute-done | bytes 393248 | tf_op jit(solution)/shard_map/ppermute | solution.py:251
  95.3 2.2 %dynamic-slice_add_fusion.6 = (f32[256,384]{1,0:T(8,128)}, f32[256,384]{1,0:T(8,128)}) fusion(f32[256,4096]{1,0:T(8,128)} %copy-done.2, s32[]{:T(128)S(6)} %select_n.83, f32[256,384]{1,0:T(8,128)} %collective-permute-done.14, pred[]{:T(512)S(6)} %eq.14, s32[]{:T(128)S(6)} %select_n.80, pred[]{:T(512)S(6)} %eq.12), kind=kLoop, calls=%fused_computation.8 | loop fusion | flops 393216 | bytes 1966090 | tf_op jit(solution)/shard_map/add | solution.py:278
  97.6 5.3 %collective-permute-start.16 = (f32[256,384]{1,0:T(8,128)}, f32[256,384]{1,0:T(8,128)}, u32[]{:S(2)}, u32[]{:S(2)}) collective-permute-start(f32[256,384]{1,0:T(8,128)} %get-tuple-element.75), channel_id=1, source_target_pairs={{0,1},{1,2},{4,5},{5,6},{8,9},{9,10},{12,13},{13,14},{16,17},{17,1... | collective-permute-start | bytes 1179656 | tf_op jit(solution)/shard_map/ppermute | solution.py:242
  102.8 1.4 %collective-permute-start.19 = (f32[256,384]{1,0:T(8,128)}, f32[256,384]{1,0:T(8,128)}, u32[]{:S(2)}, u32[]{:S(2)}) collective-permute-start(f32[256,384]{1,0:T(8,128)} %get-tuple-element.82), channel_id=1, source_target_pairs={{2,1},{3,2},{6,5},{7,6},{10,9},{11,10},{14,13},{15,14},{18,17},{19... | collective-permute-start | bytes 1179656 | tf_op jit(solution)/shard_map/ppermute | solution.py:243
  104.2 0.0 collective-permute-done.17
  104.2 0.0 collective-permute-done.18
  104.2 1.4 %dynamic-slice_add_fusion = (f32[256,640]{1,0:T(8,128)S(1)}, f32[256,640]{1,0:T(8,128)S(1)}) fusion(f32[256,640]{1,0:T(8,128)S(1)} %collective-permute-done.18, f32[256,4096]{1,0:T(8,128)} %copy-done.2, s32[]{:T(128)S(6)} %select_n.85, f32[256,640]{1,0:T(8,128)S(1)} %collective-permute-done.17, s32[]{:T(128)S(6)} %select_n.84), kind=kLoop, calls=%fused_computation.1 | loop fusion | flops 327680 | bytes 3932168 | tf_op jit(solution)/shard_map/add | solution.py:278
  105.6 4.0 %collective-permute-start.20 = (f32[256,640]{1,0:T(8,128)S(1)}, f32[256,640]{1,0:T(8,128)S(1)}, u32[]{:S(2)}, u32[]{:S(2)}) collective-permute-start(f32[256,640]{1,0:T(8,128)S(1)} %get-tuple-element.86), channel_id=1, source_target_pairs={{0,1},{1,2},{2,3},{4,5},{5,6},{6,7},{8,9},{9,10},{10,11},{12,13},{... | collective-permute-start | bytes 1966088 | tf_op jit(solution)/shard_map/ppermute | solution.py:242
  109.6 1.3 collective-permute-start.21
  110.9 0.0 collective-permute-done.16
  110.9 0.0 collective-permute-done.19
  111.0 2.4 %dynamic-slice_add_fusion.4 = (f32[256,384]{1,0:T(8,128)}, f32[256,384]{1,0:T(8,128)}) fusion(f32[256,384]{1,0:T(8,128)} %collective-permute-done.19, f32[256,4096]{1,0:T(8,128)} %copy-done.2, s32[]{:T(128)S(6)} %select_n.87, f32[256,384]{1,0:T(8,128)} %collective-permute-done.16, s32[]{:T(128)S(6)} %select_n.86), kind=kLoop, calls=%fused_computation.6 | loop fusion | flops 196608 | bytes 2359304 | tf_op jit(solution)/shard_map/add | solution.py:278
  113.3 9.0 %collective-permute-start.22 = (f32[256,384]{1,0:T(8,128)}, f32[256,384]{1,0:T(8,128)S(1)}, u32[]{:S(2)}, u32[]{:S(2)}) collective-permute-start(f32[256,384]{1,0:T(8,128)} %get-tuple-element.92), channel_id=1, source_target_pairs={{0,1},{1,2},{2,3},{4,5},{5,6},{6,7},{8,9},{9,10},{10,11},{12,13},{... | collective-permute-start | bytes 1179656 | tf_op jit(solution)/shard_map/ppermute | solution.py:242
  122.3 1.3 collective-permute-start.23
  123.6 1.1 collective-permute-done.20
  124.8 5.0 %collective-permute-done.21 = f32[256,640]{1,0:T(8,128)S(1)} collective-permute-done((f32[256,640]{1,0:T(8,128)S(1)}, f32[256,640]{1,0:T(8,128)S(1)}, u32[]{:S(2)}, u32[]{:S(2)}) %collective-permute-start.21) | collective-permute-done | bytes 655392 | tf_op jit(solution)/shard_map/ppermute | solution.py:243
  129.8 1.2 add_convert_fusion
  131.0 0.9 dynamic_update_slice.6
  131.8 0.0 collective-permute-done.22
  131.8 3.2 %collective-permute-done.23 = f32[256,384]{1,0:T(8,128)} collective-permute-done((f32[256,384]{1,0:T(8,128)}, f32[256,384]{1,0:T(8,128)}, u32[]{:S(2)}, u32[]{:S(2)}) %collective-permute-start.23) | collective-permute-done | bytes 393248 | tf_op jit(solution)/shard_map/ppermute | solution.py:243
  135.1 1.8 %fusion = bf16[256,1024]{1,0:T(8,128)(2,1)} fusion(bf16[256,1024]{1,0:T(8,128)(2,1)} %dynamic_update_slice.6, f32[256,384]{1,0:T(8,128)} %collective-permute-done.23, f32[256,384]{1,0:T(8,128)S(1)} %collective-permute-done.22, f32[256,4096]{1,0:T(8,128)} %copy-done.2, s32[]{:T(128)S(6)} %select_n.89), kind=kLoop, calls=%fused_computation.10 | loop fusion | flops 294912 | bytes 1376260 | tf_op jit(solution)/shard_map/dynamic_update_slice | solution.py:284
  (4 shorter events, 0.0 us)
Async XLA Ops:
  0.0 25.9 %copy-start = (bf16[512,768]{1,0:T(8,128)(2,1)S(1)}, bf16[512,768]{1,0:T(8,128)(2,1)}, u32[]{:S(2)}) copy-start(bf16[512,768]{1,0:T(8,128)(2,1)} %constant.48.clone.ahead_ref.refs_2_) | copy-start | bytes 2359300
  2.7 7.3 %collective-permute-start = (f32[256,256]{1,0:T(8,128)}, f32[256,256]{1,0:T(8,128)S(1)}, u32[]{:S(2)}, u32[]{:S(2)}) collective-permute-start(f32[256,256]{1,0:T(8,128)} %get-tuple-element.53), channel_id=1, source_target_pairs={{0,4},{4,0},{8,12},{12,8},{16,20},{20,16},{24,28},{28,24},{1,5},{5... | collective-permute-start | bytes 786440 | tf_op jit(solution)/shard_map/ppermute | solution.py:93
  3.2 11.0 %collective-permute-start.1 = (f32[256,256]{1,0:T(8,128)}, f32[256,256]{1,0:T(8,128)S(1)}, u32[]{:S(2)}, u32[]{:S(2)}) collective-permute-start(f32[256,256]{1,0:T(8,128)} %get-tuple-element.54), channel_id=1, source_target_pairs={{0,24},{4,28},{8,16},{12,20},{16,8},{20,12},{24,0},{28,4},{1,25},{... | collective-permute-start | bytes 786440 | tf_op jit(solution)/shard_map/ppermute | solution.py:93
  6.7 12.6 %collective-permute-start.2 = (f32[256,256]{1,0:T(8,128)}, f32[256,256]{1,0:T(8,128)S(1)}, u32[]{:S(2)}, u32[]{:S(2)}) collective-permute-start(f32[256,256]{1,0:T(8,128)} %get-tuple-element.55), channel_id=1, source_target_pairs={{0,28},{4,24},{8,20},{12,16},{16,12},{20,8},{24,4},{28,0},{1,29},{... | collective-permute-start | bytes 786440 | tf_op jit(solution)/shard_map/ppermute | solution.py:93
  6.8 19.1 %collective-permute-start.3 = (f32[256,256]{1,0:T(8,128)}, f32[256,256]{1,0:T(8,128)}, u32[]{:S(2)}, u32[]{:S(2)}) collective-permute-start(f32[256,256]{1,0:T(8,128)} %get-tuple-element.56), channel_id=1, source_target_pairs={{0,8},{4,12},{8,0},{12,4},{16,24},{20,28},{24,16},{28,20},{1,9},{5... | collective-permute-start | bytes 786440 | tf_op jit(solution)/shard_map/ppermute | solution.py:93
  8.5 17.5 %collective-permute-start.4 = (f32[256,256]{1,0:T(8,128)}, f32[256,256]{1,0:T(8,128)}, u32[]{:S(2)}, u32[]{:S(2)}) collective-permute-start(f32[256,256]{1,0:T(8,128)} %get-tuple-element.57), channel_id=1, source_target_pairs={{0,16},{4,20},{8,24},{12,28},{16,0},{20,4},{24,8},{28,12},{1,17},{... | collective-permute-start | bytes 786440 | tf_op jit(solution)/shard_map/ppermute | solution.py:93
  10.0 20.5 %collective-permute-start.5 = (f32[256,256]{1,0:T(8,128)}, f32[256,256]{1,0:T(8,128)S(1)}, u32[]{:S(2)}, u32[]{:S(2)}) collective-permute-start(f32[256,256]{1,0:T(8,128)} %get-tuple-element.58), channel_id=1, source_target_pairs={{0,12},{4,8},{8,4},{12,0},{16,28},{20,24},{24,20},{28,16},{1,13},{... | collective-permute-start | bytes 786440 | tf_op jit(solution)/shard_map/ppermute | solution.py:93
  14.2 16.4 %collective-permute-start.6 = (f32[256,256]{1,0:T(8,128)}, f32[256,256]{1,0:T(8,128)S(1)}, u32[]{:S(2)}, u32[]{:S(2)}) collective-permute-start(f32[256,256]{1,0:T(8,128)} %get-tuple-element.59), channel_id=1, source_target_pairs={{0,20},{4,16},{8,28},{12,24},{16,4},{20,0},{24,12},{28,8},{1,21},{... | collective-permute-start | bytes 786440 | tf_op jit(solution)/shard_map/ppermute | solution.py:93
  25.9 1.0 copy-start.1
  33.9 5.7 %collective-permute-start.10 = (f32[256,128]{1,0:T(8,128)S(1)}, f32[256,128]{1,0:T(8,128)S(1)}, u32[]{:S(2)}, u32[]{:S(2)}) collective-permute-start(f32[256,128]{1,0:T(8,128)S(1)} %get-tuple-element.64), channel_id=1, source_target_pairs={{0,8},{4,12},{8,0},{12,4},{16,24},{20,28},{24,16},{28,20},{1,9},{5... | collective-permute-start | bytes 393224 | tf_op jit(solution)/shard_map/ppermute | solution.py:93
  35.6 7.3 %collective-permute-start.11 = (f32[256,128]{1,0:T(8,128)S(1)}, f32[256,128]{1,0:T(8,128)S(1)}, u32[]{:S(2)}, u32[]{:S(2)}) collective-permute-start(f32[256,128]{1,0:T(8,128)S(1)} %get-tuple-element.65), channel_id=1, source_target_pairs={{0,16},{4,20},{8,24},{12,28},{16,0},{20,4},{24,8},{28,12},{1,17},{... | collective-permute-start | bytes 393224 | tf_op jit(solution)/shard_map/ppermute | solution.py:93
  37.2 5.8 %collective-permute-start.12 = (f32[256,128]{1,0:T(8,128)S(1)}, f32[256,128]{1,0:T(8,128)S(1)}, u32[]{:S(2)}, u32[]{:S(2)}) collective-permute-start(f32[256,128]{1,0:T(8,128)S(1)} %get-tuple-element.66), channel_id=1, source_target_pairs={{0,12},{4,8},{8,4},{12,0},{16,28},{20,24},{24,20},{28,16},{1,13},{... | collective-permute-start | bytes 393224 | tf_op jit(solution)/shard_map/ppermute | solution.py:93
  37.2 11.2 %collective-permute-start.13 = (f32[256,128]{1,0:T(8,128)S(1)}, f32[256,128]{1,0:T(8,128)S(1)}, u32[]{:S(2)}, u32[]{:S(2)}) collective-permute-start(f32[256,128]{1,0:T(8,128)S(1)} %get-tuple-element.67), channel_id=1, source_target_pairs={{0,20},{4,16},{8,28},{12,24},{16,4},{20,0},{24,12},{28,8},{1,21},{... | collective-permute-start | bytes 393224 | tf_op jit(solution)/shard_map/ppermute | solution.py:93
  37.7 10.7 %collective-permute-start.7 = (f32[256,128]{1,0:T(8,128)S(1)}, f32[256,128]{1,0:T(8,128)S(1)}, u32[]{:S(2)}, u32[]{:S(2)}) collective-permute-start(f32[256,128]{1,0:T(8,128)S(1)} %get-tuple-element.61), channel_id=1, source_target_pairs={{0,4},{4,0},{8,12},{12,8},{16,20},{20,16},{24,28},{28,24},{1,5},{5... | collective-permute-start | bytes 393224 | tf_op jit(solution)/shard_map/ppermute | solution.py:93
  39.6 8.8 %collective-permute-start.8 = (f32[256,128]{1,0:T(8,128)S(1)}, f32[256,128]{1,0:T(8,128)S(1)}, u32[]{:S(2)}, u32[]{:S(2)}) collective-permute-start(f32[256,128]{1,0:T(8,128)S(1)} %get-tuple-element.62), channel_id=1, source_target_pairs={{0,24},{4,28},{8,16},{12,20},{16,8},{20,12},{24,0},{28,4},{1,25},{... | collective-permute-start | bytes 393224 | tf_op jit(solution)/shard_map/ppermute | solution.py:93
  43.0 6.2 %collective-permute-start.9 = (f32[256,128]{1,0:T(8,128)S(1)}, f32[256,128]{1,0:T(8,128)S(1)}, u32[]{:S(2)}, u32[]{:S(2)}) collective-permute-start(f32[256,128]{1,0:T(8,128)S(1)} %get-tuple-element.63), channel_id=1, source_target_pairs={{0,28},{4,24},{8,20},{12,16},{16,12},{20,8},{24,4},{28,0},{1,29},{... | collective-permute-start | bytes 393224 | tf_op jit(solution)/shard_map/ppermute | solution.py:93
  51.2 17.7 %collective-permute-start.15 = (f32[256,640]{1,0:T(8,128)S(1)}, f32[256,640]{1,0:T(8,128)S(1)}, u32[]{:S(2)}, u32[]{:S(2)}) collective-permute-start(f32[256,640]{1,0:T(8,128)S(1)} %get-tuple-element.70), channel_id=1, source_target_pairs={{0,1},{3,2},{4,5},{7,6},{8,9},{11,10},{12,13},{15,14},{16,17},{19,... | collective-permute-start | bytes 1966088 | tf_op jit(solution)/shard_map/ppermute | solution.py:251
  60.4 8.5 %copy-start.2 = (f32[256,4096]{1,0:T(8,128)}, f32[256,4096]{1,0:T(8,128)S(1)}, u32[]{:S(2)}) copy-start(f32[256,4096]{1,0:T(8,128)S(1)} %fusion.1) | copy-start | bytes 12582916
  69.1 35.1 %collective-permute-start.17 = (f32[256,640]{1,0:T(8,128)S(1)}, f32[256,640]{1,0:T(8,128)S(1)}, u32[]{:S(2)}, u32[]{:S(2)}) collective-permute-start(f32[256,640]{1,0:T(8,128)S(1)} %get-tuple-element.78), channel_id=1, source_target_pairs={{0,1},{1,2},{4,5},{5,6},{8,9},{9,10},{12,13},{13,14},{16,17},{17,1... | collective-permute-start | bytes 1966088 | tf_op jit(solution)/shard_map/ppermute | solution.py:242
  73.5 30.7 %collective-permute-start.18 = (f32[256,640]{1,0:T(8,128)S(1)}, f32[256,640]{1,0:T(8,128)S(1)}, u32[]{:S(2)}, u32[]{:S(2)}) collective-permute-start(f32[256,640]{1,0:T(8,128)S(1)} %get-tuple-element.80), channel_id=1, source_target_pairs={{2,1},{3,2},{6,5},{7,6},{10,9},{11,10},{14,13},{15,14},{18,17},{19... | collective-permute-start | bytes 1966088 | tf_op jit(solution)/shard_map/ppermute | solution.py:243
  74.3 21.1 %collective-permute-start.14 = (f32[256,384]{1,0:T(8,128)S(1)}, f32[256,384]{1,0:T(8,128)}, u32[]{:S(2)}, u32[]{:S(2)}) collective-permute-start(f32[256,384]{1,0:T(8,128)S(1)} %constant_dynamic-slice_fusion), channel_id=1, source_target_pairs={{0,1},{3,2},{4,5},{7,6},{8,9},{11,10},{12,13},{15,14},{16,17},{19,... | collective-permute-start | bytes 1179656 | tf_op jit(solution)/shard_map/ppermute | solution.py:251
  97.6 13.4 %collective-permute-start.16 = (f32[256,384]{1,0:T(8,128)}, f32[256,384]{1,0:T(8,128)}, u32[]{:S(2)}, u32[]{:S(2)}) collective-permute-start(f32[256,384]{1,0:T(8,128)} %get-tuple-element.75), channel_id=1, source_target_pairs={{0,1},{1,2},{4,5},{5,6},{8,9},{9,10},{12,13},{13,14},{16,17},{17,1... | collective-permute-start | bytes 1179656 | tf_op jit(solution)/shard_map/ppermute | solution.py:242
  102.8 8.1 %collective-permute-start.19 = (f32[256,384]{1,0:T(8,128)}, f32[256,384]{1,0:T(8,128)}, u32[]{:S(2)}, u32[]{:S(2)}) collective-permute-start(f32[256,384]{1,0:T(8,128)} %get-tuple-element.82), channel_id=1, source_target_pairs={{2,1},{3,2},{6,5},{7,6},{10,9},{11,10},{14,13},{15,14},{18,17},{19... | collective-permute-start | bytes 1179656 | tf_op jit(solution)/shard_map/ppermute | solution.py:243
  105.6 19.1 %collective-permute-start.20 = (f32[256,640]{1,0:T(8,128)S(1)}, f32[256,640]{1,0:T(8,128)S(1)}, u32[]{:S(2)}, u32[]{:S(2)}) collective-permute-start(f32[256,640]{1,0:T(8,128)S(1)} %get-tuple-element.86), channel_id=1, source_target_pairs={{0,1},{1,2},{2,3},{4,5},{5,6},{6,7},{8,9},{9,10},{10,11},{12,13},{... | collective-permute-start | bytes 1966088 | tf_op jit(solution)/shard_map/ppermute | solution.py:242
  109.6 20.2 %collective-permute-start.21 = (f32[256,640]{1,0:T(8,128)S(1)}, f32[256,640]{1,0:T(8,128)S(1)}, u32[]{:S(2)}, u32[]{:S(2)}) collective-permute-start(f32[256,640]{1,0:T(8,128)S(1)} %get-tuple-element.87), channel_id=1, source_target_pairs={{1,0},{2,1},{3,2},{5,4},{6,5},{7,6},{9,8},{10,9},{11,10},{13,12},{... | collective-permute-start | bytes 1966088 | tf_op jit(solution)/shard_map/ppermute | solution.py:243
  113.3 18.5 %collective-permute-start.22 = (f32[256,384]{1,0:T(8,128)}, f32[256,384]{1,0:T(8,128)S(1)}, u32[]{:S(2)}, u32[]{:S(2)}) collective-permute-start(f32[256,384]{1,0:T(8,128)} %get-tuple-element.92), channel_id=1, source_target_pairs={{0,1},{1,2},{2,3},{4,5},{5,6},{6,7},{8,9},{9,10},{10,11},{12,13},{... | collective-permute-start | bytes 1179656 | tf_op jit(solution)/shard_map/ppermute | solution.py:242
  122.3 12.7 %collective-permute-start.23 = (f32[256,384]{1,0:T(8,128)}, f32[256,384]{1,0:T(8,128)}, u32[]{:S(2)}, u32[]{:S(2)}) collective-permute-start(f32[256,384]{1,0:T(8,128)} %get-tuple-element.93), channel_id=1, source_target_pairs={{1,0},{2,1},{3,2},{5,4},{6,5},{7,6},{9,8},{10,9},{11,10},{13,12},{... | collective-permute-start | bytes 1179656 | tf_op jit(solution)/shard_map/ppermute | solution.py:243

commit v9 on v5

--- a/solution.py
+++ b/solution.py
@@ -68,7 +68,7 @@
 
 def pack(place, keys, values, filt, direct, count):
     rows, width = keys.shape
-    step = math.gcd(rows, 128)
+    step = math.gcd(rows, 256)
     spec = pl.BlockSpec((step, width), lambda i: (i, 0))
     wide = 2 * width // count
     return pl.pallas_call(

time: 125 us -> 125 us (level)
  transfers between devices with their start and end apart: 24 -> 24, of which waited for: 14 -> 13; matrix products, arithmetic and copies ran while one was open for 12% -> 12% of each run, Pallas kernels for 2% -> 2%
where the time goes in v9:
time: 125 us
  waiting for transfers between devices  48.6 us (39%)
  starting transfers between devices  45.1 us (36%)
  Pallas kernels  10.7 us (9%)
  other arithmetic  9.36 us (7%)
  matrix products  5.72 us (5%)
  local copies, waits for them, and re-layouts  5.09 us (4%)
    ppermute x14, waiting for transfers between devices, swap(): lax.ppermute(arrays[j], 'ctx', pairs[j])  23.2 us
    ppermute x4, starting transfers between devices, pass_on(): up = lax.ppermute(up, 'tp', rise)  19.5 us
    ppermute x4, waiting for transfers between devices, pass_on(): up = lax.ppermute(up, 'tp', rise)  18.3 us
    ppermute x14, starting transfers between devices, swap(): lax.ppermute(arrays[j], 'ctx', pairs[j])  15.3 us
    ppermute x2, waiting for transfers between devices, first_step(): got = lax.ppermute(value, 'tp', [(0, 1), (size - 1, size - 2)])  7.13 us
    add x4, other arithmetic, scatter_dot(): down = sums[k][1] + own(place - size + step, k)  6.03 us
    dot_general x1, matrix products, scatter_dot(): terms = jnp.dot(lhs, rhs, preferred_element_type=F32)  5.72 us
    ppermute x2, starting transfers between devices, first_step(): got = lax.ppermute(value, 'tp', [(0, 1), (size - 1, size - 2)])  5.62 us
  transfers between devices with their start and end apart: 24, of which 13 were waited for; matrix products, arithmetic and copies ran while one was open for 12% of the time, Pallas kernels for 2%

profile of v9, /device:TPU:0, one launch (start us, length us, event | category | flops | bytes accessed | tf_op | source)
XLA Modules:
  0.0 124.8 jit_solution(14642197739608340001)
XLA Ops:
  0.0 3.2 %shard_map.82 = (f32[256,256]{1,0:T(8,128)}, f32[256,256]{1,0:T(8,128)}, f32[256,256]{1,0:T(8,128)}, f32[256,256]{1,0:T(8,128)}, f32[256,256]{1,0:T(8,128)}, /*i...) custom-call(s32[1]{0:T(128)} %bitcast.place_ref, bf16[256,1024]{1,0:T(8,128)(2,1)} %keys_ref.1, ...), custom_call_target="tpu_custom_call" | custom-call | tf_op jit(solution)/shard_map/pallas_call | solution.py:74
  3.2 0.5 collective-permute-start
  3.7 3.5 %collective-permute-start.1 = (f32[256,256]{1,0:T(8,128)}, f32[256,256]{1,0:T(8,128)S(1)}, u32[]{:S(2)}, u32[]{:S(2)}) collective-permute-start(f32[256,256]{1,0:T(8,128)} %get-tuple-element.54), channel_id=1, source_target_pairs={{0,24},{4,28},{8,16},{12,20},{16,8},{20,12},{24,0},{28,4},{1,25},{... | collective-permute-start | bytes 786440 | tf_op jit(solution)/shard_map/ppermute | solution.py:93
  7.1 0.1 collective-permute-start.2
  7.3 1.7 %collective-permute-start.3 = (f32[256,256]{1,0:T(8,128)}, f32[256,256]{1,0:T(8,128)S(1)}, u32[]{:S(2)}, u32[]{:S(2)}) collective-permute-start(f32[256,256]{1,0:T(8,128)} %get-tuple-element.56), channel_id=1, source_target_pairs={{0,8},{4,12},{8,0},{12,4},{16,24},{20,28},{24,16},{28,20},{1,9},{5... | collective-permute-start | bytes 786440 | tf_op jit(solution)/shard_map/ppermute | solution.py:93
  8.9 1.5 %collective-permute-start.4 = (f32[256,256]{1,0:T(8,128)}, f32[256,256]{1,0:T(8,128)}, u32[]{:S(2)}, u32[]{:S(2)}) collective-permute-start(f32[256,256]{1,0:T(8,128)} %get-tuple-element.57), channel_id=1, source_target_pairs={{0,16},{4,20},{8,24},{12,28},{16,0},{20,4},{24,8},{28,12},{1,17},{... | collective-permute-start | bytes 786440 | tf_op jit(solution)/shard_map/ppermute | solution.py:93
  10.4 0.0 collective-permute-done.refs_1_
  10.4 0.0 collective-permute-start.5
  10.4 4.1 %collective-permute-done.1.refs_2_ = f32[256,256]{1,0:T(8,128)S(1)} collective-permute-done((f32[256,256]{1,0:T(8,128)}, f32[256,256]{1,0:T(8,128)S(1)}, u32[]{:S(2)}, u32[]{:S(2)}) %collective-permute-start.1) | collective-permute-done | bytes 262176 | tf_op jit(solution)/shard_map/ppermute | solution.py:93
  14.6 0.8 collective-permute-start.6
  15.4 1.3 %constant_dynamic-slice_fusion.1.far_ref = bf16[1024,512]{1,0:T(8,128)(2,1)S(1)} fusion(bf16[1024,4096]{1,0:T(8,128)(2,1)} %param.13, s32[]{:T(128)S(6)} %select_n.67), kind=kLoop, calls=%fused_computation.12 | loop fusion | bytes 2097156 | tf_op jit(solution)/shard_map/dynamic_slice | solution.py:291
  16.7 3.1 %collective-permute-done.2.refs_3_ = f32[256,256]{1,0:T(8,128)S(1)} collective-permute-done((f32[256,256]{1,0:T(8,128)}, f32[256,256]{1,0:T(8,128)S(1)}, u32[]{:S(2)}, u32[]{:S(2)}) %collective-permute-start.2) | collective-permute-done | bytes 262176 | tf_op jit(solution)/shard_map/ppermute | solution.py:93
  19.8 6.4 %collective-permute-done.3.refs_4_ = f32[256,256]{1,0:T(8,128)S(1)} collective-permute-done((f32[256,256]{1,0:T(8,128)}, f32[256,256]{1,0:T(8,128)S(1)}, u32[]{:S(2)}, u32[]{:S(2)}) %collective-permute-start.3) | collective-permute-done | bytes 262176 | tf_op jit(solution)/shard_map/ppermute | solution.py:93
  26.2 0.0 collective-permute-done.4.refs_5_
  26.2 0.0 copy-done
  26.2 0.9 copy-done.1
  27.2 2.3 %shard_map.83.early_ref = f32[6,512,256]{2,1,0:T(8,128)S(1)} custom-call(bf16[512,768]{1,0:T(8,128)(2,1)S(1)} %copy-done, f32[256,256]{1,0:T(8,128)S(1)} %copy-done.1, f32[256,256]{1,0:T(8,128)S(1)} %collective-permute-done.refs_1_, f32[256,256]{1,0:T(8,128)S(1)} %collective-permute-done.1.refs_2_, f32[256,256]{1,0:T(8,128)S(1)} %collective-permute-done.2.refs_3_, ...), custom_call_target="tpu_custom_call" | custom-call | tf_op jit(solution)/shard_map/pallas_call | solution.py:104
  29.5 1.5 %collective-permute-done.5.refs_0_ = f32[256,256]{1,0:T(8,128)S(1)} collective-permute-done((f32[256,256]{1,0:T(8,128)}, f32[256,256]{1,0:T(8,128)S(1)}, u32[]{:S(2)}, u32[]{:S(2)}) %collective-permute-start.5) | collective-permute-done | bytes 262176 | tf_op jit(solution)/shard_map/ppermute | solution.py:93
  31.0 0.0 collective-permute-done.6.refs_1_
  31.1 3.3 %shard_map.84 = (f32[256,128]{1,0:T(8,128)S(1)}, f32[256,128]{1,0:T(8,128)S(1)}, f32[256,128]{1,0:T(8,128)S(1)}, f32[256,128]{1,0:T(8,128)S(1)}, f32[256,128]{1,...) custom-call(s32[1]{0:T(128)} %bitcast.place_ref, ...), custom_call_target="tpu_custom_call" | custom-call | tf_op jit(solution)/shard_map/pallas_call | solution.py:174
  34.4 1.7 %collective-permute-start.10 = (f32[256,128]{1,0:T(8,128)S(1)}, f32[256,128]{1,0:T(8,128)S(1)}, u32[]{:S(2)}, u32[]{:S(2)}) collective-permute-start(f32[256,128]{1,0:T(8,128)S(1)} %get-tuple-element.64), channel_id=1, source_target_pairs={{0,8},{4,12},{8,0},{12,4},{16,24},{20,28},{24,16},{28,20},{1,9},{5... | collective-permute-start | bytes 393224 | tf_op jit(solution)/shard_map/ppermute | solution.py:93
  36.1 1.5 %collective-permute-start.11 = (f32[256,128]{1,0:T(8,128)S(1)}, f32[256,128]{1,0:T(8,128)S(1)}, u32[]{:S(2)}, u32[]{:S(2)}) collective-permute-start(f32[256,128]{1,0:T(8,128)S(1)} %get-tuple-element.65), channel_id=1, source_target_pairs={{0,16},{4,20},{8,24},{12,28},{16,0},{20,4},{24,8},{28,12},{1,17},{... | collective-permute-start | bytes 393224 | tf_op jit(solution)/shard_map/ppermute | solution.py:93
  37.6 0.0 collective-permute-start.12
  37.6 0.6 collective-permute-start.13
  38.2 0.1 collective-permute-start.7
  38.3 1.8 %collective-permute-done.10.refs_4_ = f32[256,128]{1,0:T(8,128)S(1)} collective-permute-done((f32[256,128]{1,0:T(8,128)S(1)}, f32[256,128]{1,0:T(8,128)S(1)}, u32[]{:S(2)}, u32[]{:S(2)}) %collective-permute-start.10) | collective-permute-done | bytes 131104 | tf_op jit(solution)/shard_map/ppermute | solution.py:93
  40.0 3.4 %collective-permute-start.8 = (f32[256,128]{1,0:T(8,128)S(1)}, f32[256,128]{1,0:T(8,128)S(1)}, u32[]{:S(2)}, u32[]{:S(2)}) collective-permute-start(f32[256,128]{1,0:T(8,128)S(1)} %get-tuple-element.62), channel_id=1, source_target_pairs={{0,24},{4,28},{8,16},{12,20},{16,8},{20,12},{24,0},{28,4},{1,25},{... | collective-permute-start | bytes 393224 | tf_op jit(solution)/shard_map/ppermute | solution.py:93
  43.4 0.0 collective-permute-done.11.refs_5_
  43.4 0.0 collective-permute-start.9
  43.4 0.0 collective-permute-done.12.refs_6_
  43.4 5.4 %collective-permute-done.13.refs_7_ = f32[256,128]{1,0:T(8,128)S(1)} collective-permute-done((f32[256,128]{1,0:T(8,128)S(1)}, f32[256,128]{1,0:T(8,128)S(1)}, u32[]{:S(2)}, u32[]{:S(2)}) %collective-permute-start.13) | collective-permute-done | bytes 131104 | tf_op jit(solution)/shard_map/ppermute | solution.py:93
  48.9 0.0 collective-permute-done.7.refs_1_
  48.9 0.0 collective-permute-done.8.refs_2_
  48.9 0.8 collective-permute-done.9.refs_3_
  49.6 1.9 %shard_map.85 = (bf16[256,1024]{1,0:T(8,128)(2,1)S(1)}, f32[256,512]{1,0:T(8,128)S(1)}) custom-call(s32[1]{0:T(128)} %bitcast.place_ref, bf16[1024,512]{1,0:T(8,128)(2,1)S(1)} %constant_dynamic-slice_fusion.1.far_ref, bf16[256,1024]{1,0:T(8,128)(2,1)} %q_hbm.1, f32[256,128]{1,0:T(8,128)S(1)} %get-tuple-element.60.refs_0_, ...), custom_call_target="tpu_custom_call" | custom-call | tf_op jit(solution)/shard_map/pallas_call | solution.py:222
  51.5 3.5 %collective-permute-start.15 = (f32[256,512]{1,0:T(8,128)S(1)}, f32[256,512]{1,0:T(8,128)S(1)}, u32[]{:S(2)}, u32[]{:S(2)}) collective-permute-start(f32[256,512]{1,0:T(8,128)S(1)} %get-tuple-element.70), channel_id=1, source_target_pairs={{0,1},{3,2},{4,5},{7,6},{8,9},{11,10},{12,13},{15,14},{16,17},{19,... | collective-permute-start | bytes 1572872 | tf_op jit(solution)/shard_map/ppermute | solution.py:249
  55.0 5.7 %fusion.1 = f32[256,4096]{1,0:T(8,128)S(1)} fusion(bf16[256,1024]{1,0:T(8,128)(2,1)S(1)} %get-tuple-element.68, bf16[1024,4096]{1,0:T(8,128)(2,1)} %param.13), kind=kOutput, calls=%fused_computation.13 | convolution fusion | flops 2147483648 | bytes 13107200 | tf_op jit(solution)/shard_map/dot_general | solution.py:262
  60.8 1.9 %copy-done.2 = f32[256,4096]{1,0:T(8,128)} copy-done((f32[256,4096]{1,0:T(8,128)}, f32[256,4096]{1,0:T(8,128)S(1)}, u32[]{:S(2)}) %copy-start.2) | copy-done | bytes 4194328
  62.8 2.1 %collective-permute-start.14 = (f32[256,512]{1,0:T(8,128)S(1)}, f32[256,512]{1,0:T(8,128)}, u32[]{:S(2)}, u32[]{:S(2)}) collective-permute-start(f32[256,512]{1,0:T(8,128)S(1)} %constant_dynamic-slice_fusion), channel_id=1, source_target_pairs={{0,1},{3,2},{4,5},{7,6},{8,9},{11,10},{12,13},{15,14},{16,17},{19,... | collective-permute-start | bytes 1572872 | tf_op jit(solution)/shard_map/ppermute | solution.py:249
  64.9 2.4 %collective-permute-done.15 = f32[256,512]{1,0:T(8,128)S(1)} collective-permute-done((f32[256,512]{1,0:T(8,128)S(1)}, f32[256,512]{1,0:T(8,128)S(1)}, u32[]{:S(2)}, u32[]{:S(2)}) %collective-permute-start.15) | collective-permute-done | bytes 524320 | tf_op jit(solution)/shard_map/ppermute | solution.py:249
  67.3 1.4 %dynamic-slice_add_fusion.6 = (f32[256,512]{1,0:T(8,128)S(1)}, f32[256,512]{1,0:T(8,128)S(1)}) fusion(f32[256,4096]{1,0:T(8,128)} %copy-done.2, s32[]{:T(128)S(6)} %select_n.74, f32[256,512]{1,0:T(8,128)S(1)} %collective-permute-done.15, pred[]{:T(512)S(6)} %eq.14, s32[]{:T(128)S(6)} %select_n.71, pred[]{:T(512)S(6)} %eq.12), kind=kLoop, calls=%fused_computation.8 | loop fusion | flops 524288 | bytes 2621450 | tf_op jit(solution)/shard_map/add | solution.py:274
  68.6 4.4 %collective-permute-start.17 = (f32[256,512]{1,0:T(8,128)S(1)}, f32[256,512]{1,0:T(8,128)S(1)}, u32[]{:S(2)}, u32[]{:S(2)}) collective-permute-start(f32[256,512]{1,0:T(8,128)S(1)} %get-tuple-element.78), channel_id=1, source_target_pairs={{0,1},{1,2},{4,5},{5,6},{8,9},{9,10},{12,13},{13,14},{16,17},{17,1... | collective-permute-start | bytes 1572872 | tf_op jit(solution)/shard_map/ppermute | solution.py:240
  73.1 0.7 collective-permute-start.18
  73.8 4.7 %collective-permute-done.14 = f32[256,512]{1,0:T(8,128)} collective-permute-done((f32[256,512]{1,0:T(8,128)S(1)}, f32[256,512]{1,0:T(8,128)}, u32[]{:S(2)}, u32[]{:S(2)}) %collective-permute-start.14) | collective-permute-done | bytes 524320 | tf_op jit(solution)/shard_map/ppermute | solution.py:249
  78.5 1.5 %dynamic-slice_add_fusion.4 = (f32[256,512]{1,0:T(8,128)S(1)}, f32[256,512]{1,0:T(8,128)S(1)}) fusion(f32[256,4096]{1,0:T(8,128)} %copy-done.2, s32[]{:T(128)S(6)} %select_n.77, f32[256,512]{1,0:T(8,128)} %collective-permute-done.14, pred[]{:T(512)S(6)} %eq.14, s32[]{:T(128)S(6)} %select_n.75, pred[]{:T(512)S(6)} %eq.12), kind=kLoop, calls=%fused_computation.6 | loop fusion | flops 524288 | bytes 2621450 | tf_op jit(solution)/shard_map/add | solution.py:274
  80.0 5.3 %collective-permute-start.16 = (f32[256,512]{1,0:T(8,128)S(1)}, f32[256,512]{1,0:T(8,128)}, u32[]{:S(2)}, u32[]{:S(2)}) collective-permute-start(f32[256,512]{1,0:T(8,128)S(1)} %get-tuple-element.75), channel_id=1, source_target_pairs={{0,1},{1,2},{4,5},{5,6},{8,9},{9,10},{12,13},{13,14},{16,17},{17,1... | collective-permute-start | bytes 1572872 | tf_op jit(solution)/shard_map/ppermute | solution.py:240
  85.3 1.5 %collective-permute-start.19 = (f32[256,512]{1,0:T(8,128)S(1)}, f32[256,512]{1,0:T(8,128)}, u32[]{:S(2)}, u32[]{:S(2)}) collective-permute-start(f32[256,512]{1,0:T(8,128)S(1)} %get-tuple-element.82), channel_id=1, source_target_pairs={{2,1},{3,2},{6,5},{7,6},{10,9},{11,10},{14,13},{15,14},{18,17},{19... | collective-permute-start | bytes 1572872 | tf_op jit(solution)/shard_map/ppermute | solution.py:241
  86.8 2.9 %collective-permute-done.17 = f32[256,512]{1,0:T(8,128)S(1)} collective-permute-done((f32[256,512]{1,0:T(8,128)S(1)}, f32[256,512]{1,0:T(8,128)S(1)}, u32[]{:S(2)}, u32[]{:S(2)}) %collective-permute-start.17) | collective-permute-done | bytes 524320 | tf_op jit(solution)/shard_map/ppermute | solution.py:240
  89.7 0.0 collective-permute-done.18
  89.7 1.4 %dynamic-slice_add_fusion.2 = (f32[256,512]{1,0:T(8,128)S(1)}, f32[256,512]{1,0:T(8,128)S(1)}) fusion(f32[256,512]{1,0:T(8,128)S(1)} %collective-permute-done.18, f32[256,4096]{1,0:T(8,128)} %copy-done.2, s32[]{:T(128)S(6)} %select_n.79, f32[256,512]{1,0:T(8,128)S(1)} %collective-permute-done.17, s32[]{:T(128)S(6)} %select_n.78), kind=kLoop, calls=%fused_computation.4 | loop fusion | flops 262144 | bytes 3145736 | tf_op jit(solution)/shard_map/add | solution.py:274
  91.2 4.4 %collective-permute-start.20 = (f32[256,512]{1,0:T(8,128)S(1)}, f32[256,512]{1,0:T(8,128)S(1)}, u32[]{:S(2)}, u32[]{:S(2)}) collective-permute-start(f32[256,512]{1,0:T(8,128)S(1)} %get-tuple-element.86), channel_id=1, source_target_pairs={{0,1},{1,2},{2,3},{4,5},{5,6},{6,7},{8,9},{9,10},{10,11},{12,13},{... | collective-permute-start | bytes 1572872 | tf_op jit(solution)/shard_map/ppermute | solution.py:240
  95.6 1.3 %collective-permute-start.21 = (f32[256,512]{1,0:T(8,128)S(1)}, f32[256,512]{1,0:T(8,128)S(1)}, u32[]{:S(2)}, u32[]{:S(2)}) collective-permute-start(f32[256,512]{1,0:T(8,128)S(1)} %get-tuple-element.87), channel_id=1, source_target_pairs={{1,0},{2,1},{3,2},{5,4},{6,5},{7,6},{9,8},{10,9},{11,10},{13,12},{... | collective-permute-start | bytes 1572872 | tf_op jit(solution)/shard_map/ppermute | solution.py:241
  96.9 4.1 %collective-permute-done.16 = f32[256,512]{1,0:T(8,128)} collective-permute-done((f32[256,512]{1,0:T(8,128)S(1)}, f32[256,512]{1,0:T(8,128)}, u32[]{:S(2)}, u32[]{:S(2)}) %collective-permute-start.16) | collective-permute-done | bytes 524320 | tf_op jit(solution)/shard_map/ppermute | solution.py:240
  101.0 0.0 collective-permute-done.19
  101.0 1.7 %dynamic-slice_add_fusion = (f32[256,512]{1,0:T(8,128)S(1)}, f32[256,512]{1,0:T(8,128)S(1)}) fusion(f32[256,512]{1,0:T(8,128)} %collective-permute-done.19, f32[256,4096]{1,0:T(8,128)} %copy-done.2, s32[]{:T(128)S(6)} %select_n.81, f32[256,512]{1,0:T(8,128)} %collective-permute-done.16, s32[]{:T(128)S(6)} %select_n.80), kind=kLoop, calls=%fused_computation.2 | loop fusion | flops 262144 | bytes 3145736 | tf_op jit(solution)/shard_map/add | solution.py:274
  102.7 5.3 %collective-permute-start.22 = (f32[256,512]{1,0:T(8,128)S(1)}, f32[256,512]{1,0:T(8,128)}, u32[]{:S(2)}, u32[]{:S(2)}) collective-permute-start(f32[256,512]{1,0:T(8,128)S(1)} %get-tuple-element.92), channel_id=1, source_target_pairs={{0,1},{1,2},{2,3},{4,5},{5,6},{6,7},{8,9},{9,10},{10,11},{12,13},{... | collective-permute-start | bytes 1572872 | tf_op jit(solution)/shard_map/ppermute | solution.py:240
  108.0 1.3 %collective-permute-start.23 = (f32[256,512]{1,0:T(8,128)S(1)}, f32[256,512]{1,0:T(8,128)}, u32[]{:S(2)}, u32[]{:S(2)}) collective-permute-start(f32[256,512]{1,0:T(8,128)S(1)} %get-tuple-element.93), channel_id=1, source_target_pairs={{1,0},{2,1},{3,2},{5,4},{6,5},{7,6},{9,8},{10,9},{11,10},{13,12},{... | collective-permute-start | bytes 1572872 | tf_op jit(solution)/shard_map/ppermute | solution.py:241
  109.3 2.9 %collective-permute-done.20 = f32[256,512]{1,0:T(8,128)S(1)} collective-permute-done((f32[256,512]{1,0:T(8,128)S(1)}, f32[256,512]{1,0:T(8,128)S(1)}, u32[]{:S(2)}, u32[]{:S(2)}) %collective-permute-start.20) | collective-permute-done | bytes 524320 | tf_op jit(solution)/shard_map/ppermute | solution.py:240
  112.2 0.0 collective-permute-done.21
  112.2 1.2 add_convert_fusion.1
  113.4 0.9 dynamic_update_slice.6
  114.2 8.4 %collective-permute-done.22 = f32[256,512]{1,0:T(8,128)} collective-permute-done((f32[256,512]{1,0:T(8,128)S(1)}, f32[256,512]{1,0:T(8,128)}, u32[]{:S(2)}, u32[]{:S(2)}) %collective-permute-start.22) | collective-permute-done | bytes 524320 | tf_op jit(solution)/shard_map/ppermute | solution.py:240
  122.6 0.0 collective-permute-done.23
  122.6 2.2 %fusion = bf16[256,1024]{1,0:T(8,128)(2,1)} fusion(bf16[256,1024]{1,0:T(8,128)(2,1)} %dynamic_update_slice.6, f32[256,512]{1,0:T(8,128)} %collective-permute-done.23, f32[256,512]{1,0:T(8,128)} %collective-permute-done.22, f32[256,4096]{1,0:T(8,128)} %copy-done.2, s32[]{:T(128)S(6)} %select_n.83), kind=kLoop, calls=%fused_computation.10 | loop fusion | flops 393216 | bytes 1835012 | tf_op jit(solution)/shard_map/dynamic_update_slice | solution.py:280
  (4 shorter events, 0.0 us)
Async XLA Ops:
  0.0 26.2 %copy-start = (bf16[512,768]{1,0:T(8,128)(2,1)S(1)}, bf16[512,768]{1,0:T(8,128)(2,1)}, u32[]{:S(2)}) copy-start(bf16[512,768]{1,0:T(8,128)(2,1)} %constant.48.clone.ahead_ref.refs_2_) | copy-start | bytes 2359300
  3.2 7.2 %collective-permute-start = (f32[256,256]{1,0:T(8,128)}, f32[256,256]{1,0:T(8,128)S(1)}, u32[]{:S(2)}, u32[]{:S(2)}) collective-permute-start(f32[256,256]{1,0:T(8,128)} %get-tuple-element.53), channel_id=1, source_target_pairs={{0,4},{4,0},{8,12},{12,8},{16,20},{20,16},{24,28},{28,24},{1,5},{5... | collective-permute-start | bytes 786440 | tf_op jit(solution)/shard_map/ppermute | solution.py:93
  3.7 10.9 %collective-permute-start.1 = (f32[256,256]{1,0:T(8,128)}, f32[256,256]{1,0:T(8,128)S(1)}, u32[]{:S(2)}, u32[]{:S(2)}) collective-permute-start(f32[256,256]{1,0:T(8,128)} %get-tuple-element.54), channel_id=1, source_target_pairs={{0,24},{4,28},{8,16},{12,20},{16,8},{20,12},{24,0},{28,4},{1,25},{... | collective-permute-start | bytes 786440 | tf_op jit(solution)/shard_map/ppermute | solution.py:93
  7.1 12.7 %collective-permute-start.2 = (f32[256,256]{1,0:T(8,128)}, f32[256,256]{1,0:T(8,128)S(1)}, u32[]{:S(2)}, u32[]{:S(2)}) collective-permute-start(f32[256,256]{1,0:T(8,128)} %get-tuple-element.55), channel_id=1, source_target_pairs={{0,28},{4,24},{8,20},{12,16},{16,12},{20,8},{24,4},{28,0},{1,29},{... | collective-permute-start | bytes 786440 | tf_op jit(solution)/shard_map/ppermute | solution.py:93
  7.3 19.0 %collective-permute-start.3 = (f32[256,256]{1,0:T(8,128)}, f32[256,256]{1,0:T(8,128)S(1)}, u32[]{:S(2)}, u32[]{:S(2)}) collective-permute-start(f32[256,256]{1,0:T(8,128)} %get-tuple-element.56), channel_id=1, source_target_pairs={{0,8},{4,12},{8,0},{12,4},{16,24},{20,28},{24,16},{28,20},{1,9},{5... | collective-permute-start | bytes 786440 | tf_op jit(solution)/shard_map/ppermute | solution.py:93
  8.9 17.3 %collective-permute-start.4 = (f32[256,256]{1,0:T(8,128)}, f32[256,256]{1,0:T(8,128)}, u32[]{:S(2)}, u32[]{:S(2)}) collective-permute-start(f32[256,256]{1,0:T(8,128)} %get-tuple-element.57), channel_id=1, source_target_pairs={{0,16},{4,20},{8,24},{12,28},{16,0},{20,4},{24,8},{28,12},{1,17},{... | collective-permute-start | bytes 786440 | tf_op jit(solution)/shard_map/ppermute | solution.py:93
  10.4 20.6 %collective-permute-start.5 = (f32[256,256]{1,0:T(8,128)}, f32[256,256]{1,0:T(8,128)S(1)}, u32[]{:S(2)}, u32[]{:S(2)}) collective-permute-start(f32[256,256]{1,0:T(8,128)} %get-tuple-element.58), channel_id=1, source_target_pairs={{0,12},{4,8},{8,4},{12,0},{16,28},{20,24},{24,20},{28,16},{1,13},{... | collective-permute-start | bytes 786440 | tf_op jit(solution)/shard_map/ppermute | solution.py:93
  14.6 16.5 %collective-permute-start.6 = (f32[256,256]{1,0:T(8,128)}, f32[256,256]{1,0:T(8,128)S(1)}, u32[]{:S(2)}, u32[]{:S(2)}) collective-permute-start(f32[256,256]{1,0:T(8,128)} %get-tuple-element.59), channel_id=1, source_target_pairs={{0,20},{4,16},{8,28},{12,24},{16,4},{20,0},{24,12},{28,8},{1,21},{... | collective-permute-start | bytes 786440 | tf_op jit(solution)/shard_map/ppermute | solution.py:93
  26.2 1.0 copy-start.1
  34.4 5.7 %collective-permute-start.10 = (f32[256,128]{1,0:T(8,128)S(1)}, f32[256,128]{1,0:T(8,128)S(1)}, u32[]{:S(2)}, u32[]{:S(2)}) collective-permute-start(f32[256,128]{1,0:T(8,128)S(1)} %get-tuple-element.64), channel_id=1, source_target_pairs={{0,8},{4,12},{8,0},{12,4},{16,24},{20,28},{24,16},{28,20},{1,9},{5... | collective-permute-start | bytes 393224 | tf_op jit(solution)/shard_map/ppermute | solution.py:93
  36.1 7.3 %collective-permute-start.11 = (f32[256,128]{1,0:T(8,128)S(1)}, f32[256,128]{1,0:T(8,128)S(1)}, u32[]{:S(2)}, u32[]{:S(2)}) collective-permute-start(f32[256,128]{1,0:T(8,128)S(1)} %get-tuple-element.65), channel_id=1, source_target_pairs={{0,16},{4,20},{8,24},{12,28},{16,0},{20,4},{24,8},{28,12},{1,17},{... | collective-permute-start | bytes 393224 | tf_op jit(solution)/shard_map/ppermute | solution.py:93
  37.6 5.8 %collective-permute-start.12 = (f32[256,128]{1,0:T(8,128)S(1)}, f32[256,128]{1,0:T(8,128)S(1)}, u32[]{:S(2)}, u32[]{:S(2)}) collective-permute-start(f32[256,128]{1,0:T(8,128)S(1)} %get-tuple-element.66), channel_id=1, source_target_pairs={{0,12},{4,8},{8,4},{12,0},{16,28},{20,24},{24,20},{28,16},{1,13},{... | collective-permute-start | bytes 393224 | tf_op jit(solution)/shard_map/ppermute | solution.py:93
  37.6 11.2 %collective-permute-start.13 = (f32[256,128]{1,0:T(8,128)S(1)}, f32[256,128]{1,0:T(8,128)S(1)}, u32[]{:S(2)}, u32[]{:S(2)}) collective-permute-start(f32[256,128]{1,0:T(8,128)S(1)} %get-tuple-element.67), channel_id=1, source_target_pairs={{0,20},{4,16},{8,28},{12,24},{16,4},{20,0},{24,12},{28,8},{1,21},{... | collective-permute-start | bytes 393224 | tf_op jit(solution)/shard_map/ppermute | solution.py:93
  38.2 10.7 %collective-permute-start.7 = (f32[256,128]{1,0:T(8,128)S(1)}, f32[256,128]{1,0:T(8,128)S(1)}, u32[]{:S(2)}, u32[]{:S(2)}) collective-permute-start(f32[256,128]{1,0:T(8,128)S(1)} %get-tuple-element.61), channel_id=1, source_target_pairs={{0,4},{4,0},{8,12},{12,8},{16,20},{20,16},{24,28},{28,24},{1,5},{5... | collective-permute-start | bytes 393224 | tf_op jit(solution)/shard_map/ppermute | solution.py:93
  40.0 8.8 %collective-permute-start.8 = (f32[256,128]{1,0:T(8,128)S(1)}, f32[256,128]{1,0:T(8,128)S(1)}, u32[]{:S(2)}, u32[]{:S(2)}) collective-permute-start(f32[256,128]{1,0:T(8,128)S(1)} %get-tuple-element.62), channel_id=1, source_target_pairs={{0,24},{4,28},{8,16},{12,20},{16,8},{20,12},{24,0},{28,4},{1,25},{... | collective-permute-start | bytes 393224 | tf_op jit(solution)/shard_map/ppermute | solution.py:93
  43.4 6.2 %collective-permute-start.9 = (f32[256,128]{1,0:T(8,128)S(1)}, f32[256,128]{1,0:T(8,128)S(1)}, u32[]{:S(2)}, u32[]{:S(2)}) collective-permute-start(f32[256,128]{1,0:T(8,128)S(1)} %get-tuple-element.63), channel_id=1, source_target_pairs={{0,28},{4,24},{8,20},{12,16},{16,12},{20,8},{24,4},{28,0},{1,29},{... | collective-permute-start | bytes 393224 | tf_op jit(solution)/shard_map/ppermute | solution.py:93
  51.5 15.8 %collective-permute-start.15 = (f32[256,512]{1,0:T(8,128)S(1)}, f32[256,512]{1,0:T(8,128)S(1)}, u32[]{:S(2)}, u32[]{:S(2)}) collective-permute-start(f32[256,512]{1,0:T(8,128)S(1)} %get-tuple-element.70), channel_id=1, source_target_pairs={{0,1},{3,2},{4,5},{7,6},{8,9},{11,10},{12,13},{15,14},{16,17},{19,... | collective-permute-start | bytes 1572872 | tf_op jit(solution)/shard_map/ppermute | solution.py:249
  60.7 2.0 %copy-start.2 = (f32[256,4096]{1,0:T(8,128)}, f32[256,4096]{1,0:T(8,128)S(1)}, u32[]{:S(2)}) copy-start(f32[256,4096]{1,0:T(8,128)S(1)} %fusion.1) | copy-start | bytes 12582916
  62.8 15.7 %collective-permute-start.14 = (f32[256,512]{1,0:T(8,128)S(1)}, f32[256,512]{1,0:T(8,128)}, u32[]{:S(2)}, u32[]{:S(2)}) collective-permute-start(f32[256,512]{1,0:T(8,128)S(1)} %constant_dynamic-slice_fusion), channel_id=1, source_target_pairs={{0,1},{3,2},{4,5},{7,6},{8,9},{11,10},{12,13},{15,14},{16,17},{19,... | collective-permute-start | bytes 1572872 | tf_op jit(solution)/shard_map/ppermute | solution.py:249
  68.6 21.1 %collective-permute-start.17 = (f32[256,512]{1,0:T(8,128)S(1)}, f32[256,512]{1,0:T(8,128)S(1)}, u32[]{:S(2)}, u32[]{:S(2)}) collective-permute-start(f32[256,512]{1,0:T(8,128)S(1)} %get-tuple-element.78), channel_id=1, source_target_pairs={{0,1},{1,2},{4,5},{5,6},{8,9},{9,10},{12,13},{13,14},{16,17},{17,1... | collective-permute-start | bytes 1572872 | tf_op jit(solution)/shard_map/ppermute | solution.py:240
  73.1 16.7 %collective-permute-start.18 = (f32[256,512]{1,0:T(8,128)S(1)}, f32[256,512]{1,0:T(8,128)S(1)}, u32[]{:S(2)}, u32[]{:S(2)}) collective-permute-start(f32[256,512]{1,0:T(8,128)S(1)} %get-tuple-element.80), channel_id=1, source_target_pairs={{2,1},{3,2},{6,5},{7,6},{10,9},{11,10},{14,13},{15,14},{18,17},{19... | collective-permute-start | bytes 1572872 | tf_op jit(solution)/shard_map/ppermute | solution.py:241
  80.0 20.9 %collective-permute-start.16 = (f32[256,512]{1,0:T(8,128)S(1)}, f32[256,512]{1,0:T(8,128)}, u32[]{:S(2)}, u32[]{:S(2)}) collective-permute-start(f32[256,512]{1,0:T(8,128)S(1)} %get-tuple-element.75), channel_id=1, source_target_pairs={{0,1},{1,2},{4,5},{5,6},{8,9},{9,10},{12,13},{13,14},{16,17},{17,1... | collective-permute-start | bytes 1572872 | tf_op jit(solution)/shard_map/ppermute | solution.py:240
  85.3 15.6 %collective-permute-start.19 = (f32[256,512]{1,0:T(8,128)S(1)}, f32[256,512]{1,0:T(8,128)}, u32[]{:S(2)}, u32[]{:S(2)}) collective-permute-start(f32[256,512]{1,0:T(8,128)S(1)} %get-tuple-element.82), channel_id=1, source_target_pairs={{2,1},{3,2},{6,5},{7,6},{10,9},{11,10},{14,13},{15,14},{18,17},{19... | collective-permute-start | bytes 1572872 | tf_op jit(solution)/shard_map/ppermute | solution.py:241
  91.2 21.1 %collective-permute-start.20 = (f32[256,512]{1,0:T(8,128)S(1)}, f32[256,512]{1,0:T(8,128)S(1)}, u32[]{:S(2)}, u32[]{:S(2)}) collective-permute-start(f32[256,512]{1,0:T(8,128)S(1)} %get-tuple-element.86), channel_id=1, source_target_pairs={{0,1},{1,2},{2,3},{4,5},{5,6},{6,7},{8,9},{9,10},{10,11},{12,13},{... | collective-permute-start | bytes 1572872 | tf_op jit(solution)/shard_map/ppermute | solution.py:240
  95.6 16.6 %collective-permute-start.21 = (f32[256,512]{1,0:T(8,128)S(1)}, f32[256,512]{1,0:T(8,128)S(1)}, u32[]{:S(2)}, u32[]{:S(2)}) collective-permute-start(f32[256,512]{1,0:T(8,128)S(1)} %get-tuple-element.87), channel_id=1, source_target_pairs={{1,0},{2,1},{3,2},{5,4},{6,5},{7,6},{9,8},{10,9},{11,10},{13,12},{... | collective-permute-start | bytes 1572872 | tf_op jit(solution)/shard_map/ppermute | solution.py:241
  102.7 19.9 %collective-permute-start.22 = (f32[256,512]{1,0:T(8,128)S(1)}, f32[256,512]{1,0:T(8,128)}, u32[]{:S(2)}, u32[]{:S(2)}) collective-permute-start(f32[256,512]{1,0:T(8,128)S(1)} %get-tuple-element.92), channel_id=1, source_target_pairs={{0,1},{1,2},{2,3},{4,5},{5,6},{6,7},{8,9},{9,10},{10,11},{12,13},{... | collective-permute-start | bytes 1572872 | tf_op jit(solution)/shard_map/ppermute | solution.py:240
  108.0 14.6 %collective-permute-start.23 = (f32[256,512]{1,0:T(8,128)S(1)}, f32[256,512]{1,0:T(8,128)}, u32[]{:S(2)}, u32[]{:S(2)}) collective-permute-start(f32[256,512]{1,0:T(8,128)S(1)} %get-tuple-element.93), channel_id=1, source_target_pairs={{1,0},{2,1},{3,2},{5,4},{6,5},{7,6},{9,8},{10,9},{11,10},{13,12},{... | collective-permute-start | bytes 1572872 | tf_op jit(solution)/shard_map/ppermute | solution.py:241
